TPU v7x, 32 devices: a whole 2x2x4 slice. The times are simulated.
32 devices in a mesh: dp: 2 (over x), seq: 16 (over z, y, core).
Axes of the slice: x: 2, y: 2, z: 4, core: 2. Of those that a mesh axis runs over, the one named last changes fastest.
Arguments:
- head_queries: bfloat16 [2, 2048, 3072], P('dp', 'seq')
- head_keys: bfloat16 [2, 2048, 3072], P('dp', 'seq')
- head_values: bfloat16 [2, 2048, 3072], P('dp', 'seq'), may hold values from -6 to 6
- output_gradient: bfloat16 [2, 2048, 3072], P('dp', 'seq'), may hold values from -96 to 96
- key_adapter_input: bfloat16 [2, 2048, 64], P('dp', 'seq'), may hold values from -0.09375 to 0.09375
- value_adapter_input: bfloat16 [2, 2048, 64], P('dp', 'seq'), may hold values from -0.09375 to 0.09375
- key_block_lists: int32 [24, 16, 5], replicated, may hold values from 0 to 15, as said below
- live_block_counts: int32 [24, 16], replicated, may hold values from 1 to 5, as said below
Outputs:
- key_gradient: bfloat16 [2, 2048, 3072], P('dp', 'seq')
- value_gradient: bfloat16 [2, 2048, 3072], P('dp', 'seq')
- key_adapter_gradient: float32 [3072, 64], P(('dp', 'seq'))
- value_adapter_gradient: float32 [3072, 64], P(('dp', 'seq'))
Inputs may be any that keep to these rules, and one draw needn't show every extreme that they name: Entry 0 of key_block_lists[h, b] is b; the first live_block_counts[h, b] entries are distinct blocks within 2 of b; later entries equal b. live_block_counts[h, b] is the smaller of a count of head h and the number of blocks within 2 of b.
All inputs are finite; a program needn't handle non-finite values.
Results may differ from a plain program's by a relative error of at most 0.04.
Values may be sent and summed in bfloat16 or wider, within the bound.
No kernel may reach another device: no remote copies, remote signals or barrier semaphores. Data moves between devices by JAX's collectives and lax.ppermute only.
A program may use at most 64 MiB of HBM per device.

v0:
```python
import functools

import jax
import jax.numpy as jnp
from jax import lax
from jax.experimental import pallas as pl
from jax.experimental.pallas import tpu as pltpu
from jax.sharding import PartitionSpec as P

HEAD_COUNT = 24
HEAD_WIDTH = 128
BLK = 128
REACH = 2
TILES = 5
RANK = 64
TEAM = 4
HEADS = HEAD_COUNT // TEAM
CHUNKS = (3, 3)
WINDOW = TEAM + 2 * REACH
SCALING = HEAD_WIDTH**-0.5
LOG2E = 1.4426950408889634
ANY = pl.BlockSpec(memory_space=pl.ANY)
VMEM = pl.BlockSpec(memory_space=pltpu.VMEM)
SMEM = pl.BlockSpec(memory_space=pltpu.SMEM)


def cols(first, count):
    if isinstance(first, int):
        return pl.ds(first * HEAD_WIDTH, count * HEAD_WIDTH)
    return pl.ds(pl.multiple_of(first * HEAD_WIDTH, HEAD_WIDTH), count * HEAD_WIDTH)


def rows(first, count):
    if isinstance(first, int):
        return pl.ds(first * BLK, count * BLK)
    return pl.ds(pl.multiple_of(first * BLK, BLK), count * BLK)


def first_heads():
    return [sum(CHUNKS[:c]) for c in range(len(CHUNKS))]


def pack_kernel(with_adapters, *refs):
    a_ref, b_ref = refs[:2]
    ins = 4 if with_adapters else 2
    outs = refs[ins : ins + TEAM * len(CHUNKS)]
    sems = refs[ins + len(outs)]
    member = lax.rem(lax.axis_index("seq"), TEAM)
    copies = []

    def start(source, target):
        copy = pltpu.make_async_copy(source, target, sems.at[len(copies)])
        copy.start()
        copies.append(copy)

    for c, (first, count) in enumerate(zip(first_heads(), CHUNKS)):
        for k in (2, 3, 1, 0):
            owner = jnp.bitwise_xor(member, k)
            out = outs[c * TEAM + k]
            head = owner * HEADS + first
            start(a_ref.at[0, :, cols(head, count)], out.at[:, cols(0, count)])
            start(b_ref.at[0, :, cols(head, count)], out.at[:, cols(count, count)])
    if with_adapters:
        tile = refs[ins + len(outs) + 1]
        tile[:, :RANK] = refs[2][0]
        tile[:, RANK:] = refs[3][0]
        for k in range(TEAM):
            start(tile, outs[k].at[:, cols(2 * CHUNKS[0], 1)])
    for copy in copies:
        copy.wait()


def pack(first, second, adapters=()):
    tokens = first.shape[1]
    out_shape = []
    for c, count in enumerate(CHUNKS):
        tiles = 2 * count + (1 if adapters and c == 0 else 0)
        out_shape += [jax.ShapeDtypeStruct((tokens, tiles * HEAD_WIDTH), first.dtype)] * TEAM
    copies = 2 * len(out_shape) + (TEAM if adapters else 0)
    scratch = [pltpu.SemaphoreType.DMA((copies,))]
    if adapters:
        scratch.append(pltpu.VMEM((tokens, 2 * RANK), first.dtype))
    outs = pl.pallas_call(
        functools.partial(pack_kernel, bool(adapters)),
        out_shape=out_shape,
        in_specs=[ANY, ANY] + [VMEM] * len(adapters),
        out_specs=[ANY] * len(out_shape),
        scratch_shapes=scratch,
        name="pack_kv" if adapters else "pack_qg",
    )(first, second, *adapters)
    return [outs[c * TEAM : (c + 1) * TEAM] for c in range(len(CHUNKS))]


def compute_kernel(count, first, leading, *refs):
    bias_ref = refs[0]
    kv = refs[1 : 1 + TEAM]
    halo = refs[1 + TEAM : 1 + 2 * TEAM]
    qg = refs[1 + 2 * TEAM : 1 + 3 * TEAM]
    rest = refs[1 + 3 * TEAM :]
    if leading:
        own_ref, a_ref, b_ref, term_ref, adapt_ref = rest[:5]
        rest = rest[5:]
    else:
        adapt_ref, own_ref, a_ref, b_ref, term_ref = rest[:5]
        rest = rest[5:]
    kw, vw, qs, gs, acc_k, acc_v, pm, dm = rest
    position = lax.axis_index("seq")
    member = lax.rem(position, TEAM)
    even = lax.rem(position // TEAM, 2) == 0

    places = []
    for j in range(TEAM):
        owner = jnp.bitwise_xor(member, j)
        places.append((owner, owner + REACH, lax.rem(owner + REACH + TEAM, WINDOW)))

    if leading:
        column = cols(2 * count, 1)
        for j, (_, near, far) in enumerate(places):
            acc_k[rows(near, 1), :] = kv[j][:, column].astype(jnp.float32)
            acc_k[rows(far, 1), :] = halo[j][:, column].astype(jnp.float32)
        adapt_ref[...] = acc_k[...].T.astype(adapt_ref.dtype)

    zero = jnp.zeros((BLK, BLK), pm.dtype)
    pm[rows(TEAM + 1, 1), :BLK] = zero
    dm[rows(TEAM + 1, 1), :BLK] = zero
    pm[rows(0, 1), BLK:] = zero
    dm[rows(0, 1), BLK:] = zero

    def one_head(h, carry):
        for j, (owner, near, far) in enumerate(places):
            kw[rows(near, 1), :] = kv[j][:, cols(h, 1)]
            vw[rows(near, 1), :] = kv[j][:, cols(count + h, 1)]
            kw[rows(far, 1), :] = halo[j][:, cols(h, 1)]
            vw[rows(far, 1), :] = halo[j][:, cols(count + h, 1)]
            qs[rows(owner, 1), :] = qg[j][:, cols(h, 1)]
            gs[rows(owner, 1), :] = qg[j][:, cols(count + h, 1)]
        for pair in range(TEAM // 2):
            span = rows(2 * pair, TILES + 1)
            queries = qs[rows(2 * pair, 2), :]
            grads = gs[rows(2 * pair, 2), :]
            on_last = (((1,), (1,)), ((), ()))
            scores = lax.dot_general(kw[span, :], queries, on_last, preferred_element_type=jnp.float32)
            dprobs = lax.dot_general(vw[span, :], grads, on_last, preferred_element_type=jnp.float32)
            for u in range(2):
                base = ((first + h) * TEAM + 2 * pair + u) * TILES
                lanes = slice(u * BLK, (u + 1) * BLK)
                logits = []
                for t in range(TILES):
                    tile = scores[(u + t) * BLK : (u + t + 1) * BLK, lanes]
                    logits.append(tile * (SCALING * LOG2E) + bias_ref[base + t])
                logits = jnp.concatenate(logits, axis=0)
                top = jnp.max(logits, axis=0, keepdims=True)
                weights = jnp.exp2(logits - top)
                inverse = 1.0 / jnp.sum(weights, axis=0, keepdims=True)
                probs = weights * inverse
                dp = dprobs[u * BLK : (u + TILES) * BLK, lanes]
                delta = jnp.sum(probs * dp, axis=0, keepdims=True)
                pm[rows(u, TILES), lanes] = probs.astype(pm.dtype)
                dm[rows(u, TILES), lanes] = (probs * (dp - delta)).astype(dm.dtype)
            value_add = jnp.dot(pm[...], grads, preferred_element_type=jnp.float32)
            key_add = jnp.dot(dm[...], queries, preferred_element_type=jnp.float32) * SCALING
            if pair == 0:
                acc_v[rows(0, TILES + 1), :] = value_add
                acc_k[rows(0, TILES + 1), :] = key_add
            else:
                split = TEAM * BLK
                acc_v[rows(2, TEAM), :] += value_add[:split]
                acc_k[rows(2, TEAM), :] += key_add[:split]
                acc_v[rows(2 + TEAM, 2), :] = value_add[split:]
                acc_k[rows(2 + TEAM, 2), :] = key_add[split:]
        for acc, place, half in ((acc_k, cols(h, 1), 0), (acc_v, cols(count + h, 1), RANK)):
            own_ref[:, place] = acc[rows(REACH, TEAM), :]
            lower = acc[rows(0, REACH), :].astype(a_ref.dtype)
            upper = acc[rows(REACH + TEAM, REACH), :].astype(a_ref.dtype)
            a_ref[:, place] = jnp.where(even, upper, lower)
            b_ref[:, place] = jnp.where(even, lower, upper)
            term_ref[half : half + RANK, cols(h, 1)] = jnp.dot(
                adapt_ref[half : half + RANK, :],
                acc[...].astype(adapt_ref.dtype),
                preferred_element_type=jnp.float32,
            )
        return carry

    lax.fori_loop(0, count, one_head, 0)


def compute(c, bias, kv, halo, qg, adapt):
    count, first = CHUNKS[c], first_heads()[c]
    leading = c == 0
    kind = qg[0].dtype
    width = 2 * count * HEAD_WIDTH
    out_shape = [
        jax.ShapeDtypeStruct((TEAM * BLK, width), jnp.float32),
        jax.ShapeDtypeStruct((REACH * BLK, width), kind),
        jax.ShapeDtypeStruct((REACH * BLK, width), kind),
        jax.ShapeDtypeStruct((2 * RANK, count * HEAD_WIDTH), jnp.float32),
    ]
    inputs = [bias, *kv, *halo, *qg]
    if leading:
        out_shape.append(jax.ShapeDtypeStruct((2 * RANK, WINDOW * BLK), kind))
    else:
        inputs.append(adapt)
    tall, team = WINDOW * BLK, TEAM * BLK
    return pl.pallas_call(
        functools.partial(compute_kernel, count, first, leading),
        out_shape=out_shape,
        in_specs=[SMEM] + [VMEM] * (len(inputs) - 1),
        out_specs=[VMEM] * len(out_shape),
        scratch_shapes=[
            pltpu.VMEM((tall, HEAD_WIDTH), kind),
            pltpu.VMEM((tall, HEAD_WIDTH), kind),
            pltpu.VMEM((team, HEAD_WIDTH), kind),
            pltpu.VMEM((team, HEAD_WIDTH), kind),
            pltpu.VMEM((tall, HEAD_WIDTH), jnp.float32),
            pltpu.VMEM((tall, HEAD_WIDTH), jnp.float32),
            pltpu.VMEM(((TILES + 1) * BLK, 2 * BLK), kind),
            pltpu.VMEM(((TILES + 1) * BLK, 2 * BLK), kind),
        ],
        compiler_params=pltpu.CompilerParams(vmem_limit_bytes=24 << 20),
        cost_estimate=pl.CostEstimate(
            flops=count * 4 * 2 * 2 * 6 * BLK * 2 * BLK * HEAD_WIDTH, bytes_accessed=8 << 20, transcendentals=0
        ),
        name=f"gradients_{c}",
    )(*inputs)


def combine_kernel(own_ref, a_ref, b_ref, *outs):
    position = lax.axis_index("seq")
    member = lax.rem(position, TEAM)
    even = lax.rem(position // TEAM, 2)
    for k in range(TEAM):
        owner = jnp.bitwise_xor(member, k)
        from_a = owner // 2 != even
        row = rows(lax.rem(owner, 2), 1)
        part = jnp.where(from_a, a_ref[row, :], b_ref[row, :]).astype(jnp.float32)
        outs[k][...] = (own_ref[rows(owner, 1), :] + part).astype(outs[k].dtype)


def combine(c, own, a, b):
    shape = jax.ShapeDtypeStruct((BLK, own.shape[1]), a.dtype)
    return pl.pallas_call(
        combine_kernel,
        out_shape=[shape] * TEAM,
        in_specs=[VMEM] * 3,
        out_specs=[VMEM] * TEAM,
        compiler_params=pltpu.CompilerParams(vmem_limit_bytes=16 << 20),
        name=f"combine_{c}",
    )(own, a, b)


def unpack_kernel(*refs):
    ins = refs[: TEAM * len(CHUNKS)]
    key_ref, value_ref, sems = refs[len(ins) :]
    member = lax.rem(lax.axis_index("seq"), TEAM)
    copies = []
    for c, (first, count) in enumerate(zip(first_heads(), CHUNKS)):
        for k in range(TEAM):
            head = jnp.bitwise_xor(member, k) * HEADS + first
            for part, out in enumerate((key_ref, value_ref)):
                copy = pltpu.make_async_copy(
                    ins[c * TEAM + k].at[:, cols(part * count, count)],
                    out.at[0, :, cols(head, count)],
                    sems.at[len(copies)],
                )
                copy.start()
                copies.append(copy)
    for copy in copies:
        copy.wait()


def unpack(home):
    flat = [block for chunk in home for block in chunk]
    shape = jax.ShapeDtypeStruct((1, flat[0].shape[0], HEAD_COUNT * HEAD_WIDTH), flat[0].dtype)
    return pl.pallas_call(
        unpack_kernel,
        out_shape=[shape, shape],
        in_specs=[ANY] * len(flat),
        out_specs=[ANY, ANY],
        scratch_shapes=[pltpu.SemaphoreType.DMA((2 * len(flat),))],
        name="unpack",
    )(*flat)


def pieces_kernel(pieces, bit_of, *refs):
    terms = refs[: len(CHUNKS)]
    keep_ref, send_ref, whole = refs[len(CHUNKS) :]
    for first, term in zip(first_heads(), terms):
        whole[:, cols(first, term.shape[1] // HEAD_WIDTH)] = term[...]
    upper = bit_of() == 1
    width = whole.shape[1] // pieces
    half = pieces // 2
    for j in range(half):
        low = whole[:, j * width : (j + 1) * width]
        high = whole[:, (half + j) * width : (half + j + 1) * width]
        keep_ref[j] = jnp.where(upper, high, low)
        send_ref[j] = jnp.where(upper, low, high)


def reduce_terms(terms):
    clips, seq = lax.axis_size("dp"), lax.axis_size("seq")
    teams = seq // TEAM
    pieces = clips * teams
    rounds = [("dp", clips >> s, 1) for s in range(1, clips.bit_length())]
    rounds += [("seq", teams >> s, TEAM) for s in range(1, teams.bit_length())]

    def bit_value(axis, bit, unit):
        return lax.axis_index(axis) // (bit * unit) % 2

    def first_bit():
        axis, bit, unit = rounds[0]
        return lax.rem(lax.axis_index(axis) // (bit * unit), 2)

    width = HEADS * HEAD_WIDTH // pieces
    shape = jax.ShapeDtypeStruct((pieces // 2, 2 * RANK, width), jnp.float32)
    held, sent = pl.pallas_call(
        functools.partial(pieces_kernel, pieces, first_bit),
        out_shape=[shape, shape],
        in_specs=[VMEM] * len(terms),
        out_specs=[VMEM, VMEM],
        scratch_shapes=[pltpu.VMEM((2 * RANK, HEADS * HEAD_WIDTH), jnp.float32)],
        compiler_params=pltpu.CompilerParams(vmem_limit_bytes=16 << 20),
        name="pieces",
    )(*terms)
    for index, (axis, bit, unit) in enumerate(rounds):
        if index > 0:
            half = held.shape[0] // 2
            value = bit_value(axis, bit, unit)
            sent = lax.dynamic_slice_in_dim(held, (1 - value) * half, half, 0)
            held = lax.dynamic_slice_in_dim(held, value * half, half, 0)
        route = [(i, i ^ (bit * unit)) for i in range(lax.axis_size(axis))]
        held = held + lax.ppermute(sent, axis, route)
    route = []
    for clip in range(clips):
        for position in range(seq):
            piece = clip * teams + position // TEAM
            route.append((clip * seq + position, position % TEAM * pieces + piece))
    return lax.ppermute(held[0], ("dp", "seq"), route)


def body(
    head_queries,
    head_keys,
    head_values,
    output_gradient,
    key_adapter_input,
    value_adapter_input,
    key_block_lists,
    live_block_counts,
):
    seq = lax.axis_size("seq")
    teams = seq // TEAM
    position = lax.axis_index("seq")
    member = position % TEAM
    team = position // TEAM

    def partner(block, k):
        return lax.ppermute(block, "seq", [(i, i ^ k) for i in range(seq)]) if k else block

    near = []
    for p in range(seq):
        t = p // TEAM + (1 if p % TEAM >= TEAM // 2 else -1)
        if 0 <= t < teams:
            near.append((p, t * TEAM + p % TEAM))
    far = [(target, source) for source, target in near]
    swaps = []
    for start in (0, 1):
        pairs = []
        for t in range(start, teams - 1, 2):
            for m in range(TEAM):
                pairs += [(t * TEAM + m, (t + 1) * TEAM + m), ((t + 1) * TEAM + m, t * TEAM + m)]
        swaps.append(pairs)

    kv_sent = pack(head_keys, head_values, (key_adapter_input, value_adapter_input))
    kv = [[partner(chunk[k], k) for k in range(TEAM)] for chunk in kv_sent]
    qg_sent = pack(head_queries, output_gradient)
    qg = [[partner(chunk[k], k) for k in range(TEAM)] for chunk in qg_sent]
    halo = [[lax.ppermute(chunk[k], "seq", near if k < 2 else far) for k in range(TEAM)] for chunk in kv]

    lists = lax.dynamic_slice(key_block_lists, (member * HEADS, team * TEAM, 0), (HEADS, TEAM, TILES))
    counts = lax.dynamic_slice(live_block_counts, (member * HEADS, team * TEAM), (HEADS, TEAM))
    own_block = team * TEAM + jnp.arange(TEAM, dtype=jnp.int32)
    window = own_block[:, None] - REACH + jnp.arange(TILES, dtype=jnp.int32)
    listed = lists[:, :, :, None] == window[None, :, None, :]
    in_use = jnp.arange(TILES, dtype=jnp.int32) < counts[:, :, None]
    live = jnp.any(listed & in_use[:, :, :, None], axis=2)
    bias = jnp.where(live, 0.0, -jnp.inf).astype(jnp.float32).reshape(-1)

    adapt = None
    home, terms = [], []
    for c in range(len(CHUNKS)):
        results = compute(c, bias, kv[c], halo[c], qg[c], adapt)
        own, to_a, to_b, term = results[:4]
        if c == 0:
            adapt = results[4]
        terms.append(term)
        from_a = lax.ppermute(to_a, "seq", swaps[0])
        from_b = lax.ppermute(to_b, "seq", swaps[1])
        blocks = combine(c, own, from_a, from_b)
        home.append([partner(block, k) for k, block in enumerate(blocks)])
    summed = reduce_terms(terms)
    key_gradient, value_gradient = unpack(home)
    return key_gradient, value_gradient, summed[:RANK].T, summed[RANK:].T


def solution(mesh):
    tokens = P("dp", "seq", None)
    shares = P(("dp", "seq"), None)
    return jax.shard_map(
        body,
        mesh=mesh,
        in_specs=(tokens,) * 6 + (P(), P()),
        out_specs=(tokens, tokens, shares, shares),
        check_vma=False,
    )
```

profile of v0, /device:TPU:5, one launch (start us, length us, event | category | flops | bytes accessed | tf_op | source)
XLA Modules:
  0.0 281.5 jit_solution(11416783527354119499)
XLA Ops:
  0.7 48.9 %pack_qg.1 = (bf16[128,768]{1,0:T(8,128)(2,1)}, bf16[128,768]{1,0:T(8,128)(2,1)}, bf16[128,768]{1,0:T(8,128)(2,1)}, bf16[128,768]{1,0:T(8,128)(2,1)}, bf16[128,7...) custom-call(bf16[1,128,3072]{2,1,0:T(8,128)(2,1)} %refs_0_.3, ...), custom_call_target="tpu_custom_call" | custom-call | tf_op jit(solution)/shard_map/pack_qg/pallas_call | solution.py:83
  50.3 1.7 collective-permute-start.9
  53.5 49.7 %pack_kv.1 = (bf16[128,896]{1,0:T(8,128)(2,1)}, bf16[128,896]{1,0:T(8,128)(2,1)}, bf16[128,896]{1,0:T(8,128)(2,1)}, bf16[128,896]{1,0:T(8,128)(2,1)}, bf16[128,7...) custom-call(bf16[1,128,3072]{2,1,0:T(8,128)(2,1)} %refs_0_.2, ...), custom_call_target="tpu_custom_call" | custom-call | tf_op jit(solution)/shard_map/pack_kv/pallas_call | solution.py:83
  105.2 1.8 collective-permute-start.2
  110.1 10.9 %collective-permute-done.16.refs_3_ = bf16[128,768]{1,0:T(8,128)(2,1)} collective-permute-done((bf16[128,768]{1,0:T(8,128)(2,1)}, bf16[128,768]{1,0:T(8,128)(2,1)}, u32[]{:S(2)}, u32[]{:S(2)}) %collective-permute-start.16) | collective-permute-done | bytes 196640 | tf_op jit(solution)/shard_map/ppermute | solution.py:357
  121.0 3.2 %collective-permute-start.3 = (bf16[128,896]{1,0:T(8,128)(2,1)}, bf16[128,896]{1,0:T(8,128)(2,1)S(1)}, u32[]{:S(2)}, u32[]{:S(2)}) collective-permute-start(bf16[128,896]{1,0:T(8,128)(2,1)} %get-tuple-element.41.refs_1_), channel_id=1, source_target_pairs={{2,6},{3,7},{4,0},{5,1},{6,10},{7,11},{8,4},{9,5},{10,14},{11,15},... | collective-permute-start | bytes 688136 | tf_op jit(solution)/shard_map/ppermute | solution.py:377
  125.5 3.2 %collective-permute-start.18 = (bf16[128,768]{1,0:T(8,128)(2,1)}, bf16[128,768]{1,0:T(8,128)(2,1)S(1)}, u32[]{:S(2)}, u32[]{:S(2)}) collective-permute-start(bf16[128,768]{1,0:T(8,128)(2,1)} %get-tuple-element.56.refs_1_), channel_id=1, source_target_pairs={{2,6},{3,7},{4,0},{5,1},{6,10},{7,11},{8,4},{9,5},{10,14},{11,15},... | collective-permute-start | bytes 589832 | tf_op jit(solution)/shard_map/ppermute | solution.py:377
  128.7 3.2 %collective-permute-start.4 = (bf16[128,896]{1,0:T(8,128)(2,1)S(1)}, bf16[128,896]{1,0:T(8,128)(2,1)S(1)}, u32[]{:S(2)}, u32[]{:S(2)}) collective-permute-start(bf16[128,896]{1,0:T(8,128)(2,1)S(1)} %collective-permute-done.refs_2_), channel_id=1, source_target_pairs={{2,6},{3,7},{4,0},{5,1},{6,10},{7,11},{8,4},{9,5},{10,14},{11,15},... | collective-permute-start | bytes 688136 | tf_op jit(solution)/shard_map/ppermute | solution.py:377
  138.1 1.7 collective-permute-start.23
  140.1 5.6 %collective-permute-start.19 = (bf16[128,768]{1,0:T(8,128)(2,1)S(1)}, bf16[128,768]{1,0:T(8,128)(2,1)}, u32[]{:S(2)}, u32[]{:S(2)}) collective-permute-start(bf16[128,768]{1,0:T(8,128)(2,1)S(1)} %collective-permute-done.15.refs_2_), channel_id=1, source_target_pairs={{2,6},{3,7},{4,0},{5,1},{6,10},{7,11},{8,4},{9,5},{10,14},{11,15},... | collective-permute-start | bytes 589832 | tf_op jit(solution)/shard_map/ppermute | solution.py:377
  153.2 6.6 %gradients_0.1 = (f32[512,768]{1,0:T(8,128)S(1)}, bf16[256,768]{1,0:T(8,128)(2,1)S(1)}, bf16[256,768]{1,0:T(8,128)(2,1)S(1)}, f32[128,384]{1,0:T(8,128)S(1)}, bf16[128,1024]{1,0:T(8,128)(2,1)S(1)}) custom-call(f32[120]{0:T(128)S(1)} %select_n.56.refs_0_, bf16[128,896]{1,0:T(8,128)(2,1)S(1)} %copy-done.7, bf16[128,896]{1,0:T(8,128)(2,1)S(1)} %collective-permute-done.refs_2_, ...), custom_call_target="tpu_custom_call" | custom-call | flops 1207959552 | bytes 8388608 | tf_op jit(solution)/shard_map/gradients_0/pallas_call | solution.py:204
  162.3 7.2 %gradients_1.1 = (f32[512,768]{1,0:T(8,128)S(1)}, bf16[256,768]{1,0:T(8,128)(2,1)S(1)}, bf16[256,768]{1,0:T(8,128)(2,1)S(1)}, f32[128,384]{1,0:T(8,128)S(1)}) custom-call(f32[120]{0:T(128)S(1)} %select_n.56.refs_0_, bf16[128,768]{1,0:T(8,128)(2,1)S(1)} %copy-done.9, bf16[128,768]{1,0:T(8,128)(2,1)S(1)} %copy-done.11, ...), custom_call_target="tpu_custom_call" | custom-call | flops 1207959552 | bytes 8388608 | tf_op jit(solution)/shard_map/gradients_1/pallas_call | solution.py:204
  172.4 6.9 %collective-permute-done.30 = f32[4,128,96]{2,1,0:T(8,128)} collective-permute-done((f32[4,128,96]{2,1,0:T(8,128)}, f32[4,128,96]{2,1,0:T(8,128)}, u32[]{:S(2)}, u32[]{:S(2)}) %collective-permute-start.30) | collective-permute-done | bytes 196640 | tf_op jit(solution)/shard_map/ppermute | solution.py:331
  181.0 3.3 %collective-permute-start.31 = (f32[2,128,96]{2,1,0:T(8,128)S(1)}, f32[2,128,96]{2,1,0:T(8,128)S(1)}, u32[]{:S(2)}, u32[]{:S(2)}) collective-permute-start(f32[2,128,96]{2,1,0:T(8,128)S(1)} %constant_dynamic-slice_fusion.1), channel_id=1, source_target_pairs={{0,8},{1,9},{2,10},{3,11},{4,12},{5,13},{6,14},{7,15},{8,0},{9,1},... | collective-permute-start | bytes 294920 | tf_op jit(solution)/shard_map/ppermute | solution.py:331
  184.3 1.7 collective-permute-start.10
  192.4 3.6 %collective-permute-done.10.a_ref = bf16[256,768]{1,0:T(8,128)(2,1)} collective-permute-done((bf16[256,768]{1,0:T(8,128)(2,1)}, bf16[256,768]{1,0:T(8,128)(2,1)}, u32[]{:S(2)}, u32[]{:S(2)}) %collective-permute-start.10) | collective-permute-done | bytes 393248 | tf_op jit(solution)/shard_map/ppermute | solution.py:396
  198.0 3.1 %collective-permute-start.12 = (bf16[128,768]{1,0:T(8,128)(2,1)S(1)}, bf16[128,768]{1,0:T(8,128)(2,1)S(1)}, u32[]{:S(2)}, u32[]{:S(2)}) collective-permute-start(bf16[128,768]{1,0:T(8,128)(2,1)S(1)} %get-tuple-element.53), channel_id=1, source_target_pairs={{0,1},{1,0},{2,3},{3,2},{4,5},{5,4},{6,7},{7,6},{8,9},{9,8},{10,11... | collective-permute-start | bytes 589832 | tf_op jit(solution)/shard_map/ppermute | solution.py:357
  201.1 4.8 %collective-permute-done.32 = f32[1,128,96]{2,1,0:T(8,128)S(1)} collective-permute-done((f32[1,128,96]{2,1,0:T(8,128)S(1)}, f32[1,128,96]{2,1,0:T(8,128)S(1)}, u32[]{:S(2)}, u32[]{:S(2)}) %collective-permute-start.32) | collective-permute-done | bytes 49184 | tf_op jit(solution)/shard_map/ppermute | solution.py:331
  205.9 5.7 %collective-permute-start.33 = (f32[128,96]{1,0:T(8,128)S(1)}, f32[128,96]{1,0:T(8,128)S(1)}, u32[]{:S(2)}, u32[]{:S(2)}) collective-permute-start(f32[128,96]{1,0:T(8,128)S(1)} %add_bitcast_fusion), channel_id=1, source_target_pairs={{0,0},{1,8},{2,16},{3,24},{4,1},{5,9},{6,17},{7,25},{8,2},{9,10},{... | collective-permute-start | bytes 147464 | tf_op jit(solution)/shard_map/ppermute | solution.py:337
  215.6 1.7 collective-permute-start.29
  219.3 4.2 %collective-permute-done.14.refs_3_ = bf16[128,768]{1,0:T(8,128)(2,1)S(1)} collective-permute-done((bf16[128,768]{1,0:T(8,128)(2,1)S(1)}, bf16[128,768]{1,0:T(8,128)(2,1)S(1)}, u32[]{:S(2)}, u32[]{:S(2)}) %collective-permute-start.14) | collective-permute-done | bytes 196640 | tf_op jit(solution)/shard_map/ppermute | solution.py:357
  223.5 4.2 %collective-permute-done.28.refs_6_ = bf16[128,768]{1,0:T(8,128)(2,1)S(1)} collective-permute-done((bf16[128,768]{1,0:T(8,128)(2,1)S(1)}, bf16[128,768]{1,0:T(8,128)(2,1)S(1)}, u32[]{:S(2)}, u32[]{:S(2)}) %collective-permute-start.28) | collective-permute-done | bytes 196640 | tf_op jit(solution)/shard_map/ppermute | solution.py:357
  227.8 4.2 %collective-permute-done.29.refs_7_ = bf16[128,768]{1,0:T(8,128)(2,1)S(1)} collective-permute-done((bf16[128,768]{1,0:T(8,128)(2,1)S(1)}, bf16[128,768]{1,0:T(8,128)(2,1)S(1)}, u32[]{:S(2)}, u32[]{:S(2)}) %collective-permute-start.29) | collective-permute-done | bytes 196640 | tf_op jit(solution)/shard_map/ppermute | solution.py:357
  232.6 48.9 %unpack.1 = (bf16[1,128,3072]{2,1,0:T(8,128)(2,1)}, bf16[1,128,3072]{2,1,0:T(8,128)(2,1)}) custom-call(bf16[128,768]{1,0:T(8,128)(2,1)} %copy-done.1, bf16[128,768]{1,0:T(8,128)(2,1)} %copy-done.24, bf16[128,768]{1,0:T(8,128)(2,1)} %copy-done.25, bf16[128,768]{1,0:T(8,128)(2,1)} %copy-done.26, bf16[128,768]{1,0:T(8,128)(2,1)} %copy-done.2, ...), custom_call_target="tpu_custom_call" | custom-call | tf_op jit(solution)/shard_map/unpack/pallas_call | solution.py:274
  (135 shorter events, 44.5 us)
Async XLA Ops:
  49.6 54.2 %collective-permute-start.7 = (bf16[128,768]{1,0:T(8,128)(2,1)}, bf16[128,768]{1,0:T(8,128)(2,1)S(1)}, u32[]{:S(2)}, u32[]{:S(2)}) collective-permute-start(bf16[128,768]{1,0:T(8,128)(2,1)} %get-tuple-element.46), channel_id=1, source_target_pairs={{0,1},{1,0},{2,3},{3,2},{4,5},{5,4},{6,7},{7,6},{8,9},{9,8},{10,11... | collective-permute-start | bytes 589832 | tf_op jit(solution)/shard_map/ppermute | solution.py:357
  50.3 54.1 %collective-permute-start.8 = (bf16[128,768]{1,0:T(8,128)(2,1)}, bf16[128,768]{1,0:T(8,128)(2,1)S(1)}, u32[]{:S(2)}, u32[]{:S(2)}) collective-permute-start(bf16[128,768]{1,0:T(8,128)(2,1)} %get-tuple-element.47), channel_id=1, source_target_pairs={{0,2},{1,3},{2,0},{3,1},{4,6},{5,7},{6,4},{7,5},{8,10},{9,11},{10,... | collective-permute-start | bytes 589832 | tf_op jit(solution)/shard_map/ppermute | solution.py:357
  50.3 57.4 %collective-permute-start.9 = (bf16[128,768]{1,0:T(8,128)(2,1)}, bf16[128,768]{1,0:T(8,128)(2,1)S(1)}, u32[]{:S(2)}, u32[]{:S(2)}) collective-permute-start(bf16[128,768]{1,0:T(8,128)(2,1)} %get-tuple-element.48), channel_id=1, source_target_pairs={{0,3},{1,2},{2,1},{3,0},{4,7},{5,6},{6,5},{7,4},{8,11},{9,10},{10,... | collective-permute-start | bytes 589832 | tf_op jit(solution)/shard_map/ppermute | solution.py:357
  103.4 25.2 %collective-permute-start = (bf16[128,896]{1,0:T(8,128)(2,1)}, bf16[128,896]{1,0:T(8,128)(2,1)S(1)}, u32[]{:S(2)}, u32[]{:S(2)}) collective-permute-start(bf16[128,896]{1,0:T(8,128)(2,1)} %get-tuple-element.42), channel_id=1, source_target_pairs={{0,1},{1,0},{2,3},{3,2},{4,5},{5,4},{6,7},{7,6},{8,9},{9,8},{10,11... | collective-permute-start | bytes 688136 | tf_op jit(solution)/shard_map/ppermute | solution.py:357
  104.5 27.4 %collective-permute-start.1 = (bf16[128,896]{1,0:T(8,128)(2,1)}, bf16[128,896]{1,0:T(8,128)(2,1)S(1)}, u32[]{:S(2)}, u32[]{:S(2)}) collective-permute-start(bf16[128,896]{1,0:T(8,128)(2,1)} %get-tuple-element.43), channel_id=1, source_target_pairs={{0,2},{1,3},{2,0},{3,1},{4,6},{5,7},{6,4},{7,5},{8,10},{9,11},{10,... | collective-permute-start | bytes 688136 | tf_op jit(solution)/shard_map/ppermute | solution.py:357
  105.2 28.0 %collective-permute-start.2 = (bf16[128,896]{1,0:T(8,128)(2,1)}, bf16[128,896]{1,0:T(8,128)(2,1)S(1)}, u32[]{:S(2)}, u32[]{:S(2)}) collective-permute-start(bf16[128,896]{1,0:T(8,128)(2,1)} %get-tuple-element.44), channel_id=1, source_target_pairs={{0,3},{1,2},{2,1},{3,0},{4,7},{5,6},{6,5},{7,4},{8,11},{9,10},{10,... | collective-permute-start | bytes 688136 | tf_op jit(solution)/shard_map/ppermute | solution.py:357
  108.4 12.6 %collective-permute-start.16 = (bf16[128,768]{1,0:T(8,128)(2,1)}, bf16[128,768]{1,0:T(8,128)(2,1)}, u32[]{:S(2)}, u32[]{:S(2)}) collective-permute-start(bf16[128,768]{1,0:T(8,128)(2,1)} %get-tuple-element.58), channel_id=1, source_target_pairs={{0,2},{1,3},{2,0},{3,1},{4,6},{5,7},{6,4},{7,5},{8,10},{9,11},{10,... | collective-permute-start | bytes 589832 | tf_op jit(solution)/shard_map/ppermute | solution.py:357
  108.5 17.0 %collective-permute-start.17 = (bf16[128,768]{1,0:T(8,128)(2,1)}, bf16[128,768]{1,0:T(8,128)(2,1)}, u32[]{:S(2)}, u32[]{:S(2)}) collective-permute-start(bf16[128,768]{1,0:T(8,128)(2,1)} %get-tuple-element.59), channel_id=1, source_target_pairs={{0,3},{1,2},{2,1},{3,0},{4,7},{5,6},{6,5},{7,4},{8,11},{9,10},{10,... | collective-permute-start | bytes 589832 | tf_op jit(solution)/shard_map/ppermute | solution.py:357
  121.0 18.8 %collective-permute-start.3 = (bf16[128,896]{1,0:T(8,128)(2,1)}, bf16[128,896]{1,0:T(8,128)(2,1)S(1)}, u32[]{:S(2)}, u32[]{:S(2)}) collective-permute-start(bf16[128,896]{1,0:T(8,128)(2,1)} %get-tuple-element.41.refs_1_), channel_id=1, source_target_pairs={{2,6},{3,7},{4,0},{5,1},{6,10},{7,11},{8,4},{9,5},{10,14},{11,15},... | collective-permute-start | bytes 688136 | tf_op jit(solution)/shard_map/ppermute | solution.py:377
  131.9 13.8 %collective-permute-start.5 = (bf16[128,896]{1,0:T(8,128)(2,1)S(1)}, bf16[128,896]{1,0:T(8,128)(2,1)S(1)}, u32[]{:S(2)}, u32[]{:S(2)}) collective-permute-start(bf16[128,896]{1,0:T(8,128)(2,1)S(1)} %collective-permute-done.1.refs_3_), channel_id=1, source_target_pairs={{6,2},{7,3},{0,4},{1,5},{10,6},{11,7},{4,8},{5,9},{14,10},{15,11},... | collective-permute-start | bytes 688136 | tf_op jit(solution)/shard_map/ppermute | solution.py:377
  133.2 13.8 %collective-permute-start.6 = (bf16[128,896]{1,0:T(8,128)(2,1)S(1)}, bf16[128,896]{1,0:T(8,128)(2,1)S(1)}, u32[]{:S(2)}, u32[]{:S(2)}) collective-permute-start(bf16[128,896]{1,0:T(8,128)(2,1)S(1)} %collective-permute-done.2.refs_4_), channel_id=1, source_target_pairs={{6,2},{7,3},{0,4},{1,5},{10,6},{11,7},{4,8},{5,9},{14,10},{15,11},... | collective-permute-start | bytes 688136 | tf_op jit(solution)/shard_map/ppermute | solution.py:377
  138.1 23.2 %collective-permute-start.23 = (bf16[128,768]{1,0:T(8,128)(2,1)}, bf16[128,768]{1,0:T(8,128)(2,1)}, u32[]{:S(2)}, u32[]{:S(2)}) collective-permute-start(bf16[128,768]{1,0:T(8,128)(2,1)} %get-tuple-element.62), channel_id=1, source_target_pairs={{0,2},{1,3},{2,0},{3,1},{4,6},{5,7},{6,4},{7,5},{8,10},{9,11},{10,... | collective-permute-start | bytes 589832 | tf_op jit(solution)/shard_map/ppermute | solution.py:357
  139.8 21.5 %collective-permute-start.24 = (bf16[128,768]{1,0:T(8,128)(2,1)}, bf16[128,768]{1,0:T(8,128)(2,1)}, u32[]{:S(2)}, u32[]{:S(2)}) collective-permute-start(bf16[128,768]{1,0:T(8,128)(2,1)} %get-tuple-element.63), channel_id=1, source_target_pairs={{0,3},{1,2},{2,1},{3,0},{4,7},{5,6},{6,5},{7,4},{8,11},{9,10},{10,... | collective-permute-start | bytes 589832 | tf_op jit(solution)/shard_map/ppermute | solution.py:357
  140.1 21.2 %collective-permute-start.19 = (bf16[128,768]{1,0:T(8,128)(2,1)S(1)}, bf16[128,768]{1,0:T(8,128)(2,1)}, u32[]{:S(2)}, u32[]{:S(2)}) collective-permute-start(bf16[128,768]{1,0:T(8,128)(2,1)S(1)} %collective-permute-done.15.refs_2_), channel_id=1, source_target_pairs={{2,6},{3,7},{4,0},{5,1},{6,10},{7,11},{8,4},{9,5},{10,14},{11,15},... | collective-permute-start | bytes 589832 | tf_op jit(solution)/shard_map/ppermute | solution.py:377
  145.7 15.6 %collective-permute-start.20 = (bf16[128,768]{1,0:T(8,128)(2,1)}, bf16[128,768]{1,0:T(8,128)(2,1)}, u32[]{:S(2)}, u32[]{:S(2)}) collective-permute-start(bf16[128,768]{1,0:T(8,128)(2,1)} %collective-permute-done.16.refs_3_), channel_id=1, source_target_pairs={{6,2},{7,3},{0,4},{1,5},{10,6},{11,7},{4,8},{5,9},{14,10},{15,11},... | collective-permute-start | bytes 589832 | tf_op jit(solution)/shard_map/ppermute | solution.py:377
  147.0 14.3 %collective-permute-start.21 = (bf16[128,768]{1,0:T(8,128)(2,1)}, bf16[128,768]{1,0:T(8,128)(2,1)}, u32[]{:S(2)}, u32[]{:S(2)}) collective-permute-start(bf16[128,768]{1,0:T(8,128)(2,1)} %collective-permute-done.17.refs_4_), channel_id=1, source_target_pairs={{6,2},{7,3},{0,4},{1,5},{10,6},{11,7},{4,8},{5,9},{14,10},{15,11},... | collective-permute-start | bytes 589832 | tf_op jit(solution)/shard_map/ppermute | solution.py:377
  184.3 11.7 %collective-permute-start.10 = (bf16[256,768]{1,0:T(8,128)(2,1)}, bf16[256,768]{1,0:T(8,128)(2,1)}, u32[]{:S(2)}, u32[]{:S(2)}) collective-permute-start(bf16[256,768]{1,0:T(8,128)(2,1)} %copy-done.6), channel_id=1, source_target_pairs={{0,4},{4,0},{1,5},{5,1},{2,6},{6,2},{3,7},{7,3},{8,12},{12,8},{9,1... | collective-permute-start | bytes 1179656 | tf_op jit(solution)/shard_map/ppermute | solution.py:396
  187.4 24.3 %collective-permute-start.25 = (bf16[256,768]{1,0:T(8,128)(2,1)}, bf16[256,768]{1,0:T(8,128)(2,1)}, u32[]{:S(2)}, u32[]{:S(2)}) collective-permute-start(bf16[256,768]{1,0:T(8,128)(2,1)} %copy-done.5), channel_id=1, source_target_pairs={{0,4},{4,0},{1,5},{5,1},{2,6},{6,2},{3,7},{7,3},{8,12},{12,8},{9,1... | collective-permute-start | bytes 1179656 | tf_op jit(solution)/shard_map/ppermute | solution.py:396
  188.4 24.8 %collective-permute-start.26 = (bf16[256,768]{1,0:T(8,128)(2,1)}, bf16[256,768]{1,0:T(8,128)(2,1)}, u32[]{:S(2)}, u32[]{:S(2)}) collective-permute-start(bf16[256,768]{1,0:T(8,128)(2,1)} %copy-done.3), channel_id=1, source_target_pairs={{4,8},{8,4},{5,9},{9,5},{6,10},{10,6},{7,11},{11,7},{20,24},{24,20... | collective-permute-start | bytes 1179656 | tf_op jit(solution)/shard_map/ppermute | solution.py:397
  190.7 15.1 %collective-permute-start.32 = (f32[1,128,96]{2,1,0:T(8,128)S(1)}, f32[1,128,96]{2,1,0:T(8,128)S(1)}, u32[]{:S(2)}, u32[]{:S(2)}) collective-permute-start(f32[1,128,96]{2,1,0:T(8,128)S(1)} %constant_dynamic-slice_fusion), channel_id=1, source_target_pairs={{0,4},{1,5},{2,6},{3,7},{4,0},{5,1},{6,2},{7,3},{8,12},{9,13},{10,... | collective-permute-start | bytes 147464 | tf_op jit(solution)/shard_map/ppermute | solution.py:331
  198.0 17.6 %collective-permute-start.12 = (bf16[128,768]{1,0:T(8,128)(2,1)S(1)}, bf16[128,768]{1,0:T(8,128)(2,1)S(1)}, u32[]{:S(2)}, u32[]{:S(2)}) collective-permute-start(bf16[128,768]{1,0:T(8,128)(2,1)S(1)} %get-tuple-element.53), channel_id=1, source_target_pairs={{0,1},{1,0},{2,3},{3,2},{4,5},{5,4},{6,7},{7,6},{8,9},{9,8},{10,11... | collective-permute-start | bytes 589832 | tf_op jit(solution)/shard_map/ppermute | solution.py:357
  211.7 11.8 %collective-permute-start.14 = (bf16[128,768]{1,0:T(8,128)(2,1)S(1)}, bf16[128,768]{1,0:T(8,128)(2,1)S(1)}, u32[]{:S(2)}, u32[]{:S(2)}) collective-permute-start(bf16[128,768]{1,0:T(8,128)(2,1)S(1)} %get-tuple-element.55), channel_id=1, source_target_pairs={{0,3},{1,2},{2,1},{3,0},{4,7},{5,6},{6,5},{7,4},{8,11},{9,10},{10,... | collective-permute-start | bytes 589832 | tf_op jit(solution)/shard_map/ppermute | solution.py:357
  215.5 12.3 %collective-permute-start.28 = (bf16[128,768]{1,0:T(8,128)(2,1)S(1)}, bf16[128,768]{1,0:T(8,128)(2,1)S(1)}, u32[]{:S(2)}, u32[]{:S(2)}) collective-permute-start(bf16[128,768]{1,0:T(8,128)(2,1)S(1)} %get-tuple-element.70), channel_id=1, source_target_pairs={{0,2},{1,3},{2,0},{3,1},{4,6},{5,7},{6,4},{7,5},{8,10},{9,11},{10,... | collective-permute-start | bytes 589832 | tf_op jit(solution)/shard_map/ppermute | solution.py:357
  215.6 16.4 %collective-permute-start.29 = (bf16[128,768]{1,0:T(8,128)(2,1)S(1)}, bf16[128,768]{1,0:T(8,128)(2,1)S(1)}, u32[]{:S(2)}, u32[]{:S(2)}) collective-permute-start(bf16[128,768]{1,0:T(8,128)(2,1)S(1)} %get-tuple-element.71), channel_id=1, source_target_pairs={{0,3},{1,2},{2,1},{3,0},{4,7},{5,6},{6,5},{7,4},{8,11},{9,10},{10,... | collective-permute-start | bytes 589832 | tf_op jit(solution)/shard_map/ppermute | solution.py:357
  (43 other events, 554.3 us)
where the time goes:
time: 283 us; the launch traced here: 282 us
  Pallas kernels  165 us (58%)
  starting transfers between devices  54.2 us (19%)
  waiting for transfers between devices  42.4 us (15%)
  local copies, waits for them, and re-layouts  17.1 us (6%)
    pallas_call x2, Pallas kernels, pack(): pl.pallas_call(functools.partial(pack_kernel, bool(adapters)), out_shape=...  98.6 us
    pallas_call x1, Pallas kernels, unpack(): pl.pallas_call(unpack_kernel, out_shape=[shape, shape], in_specs=[ANY] *...  48.9 us
    ppermute x18, waiting for transfers between devices, partner(): lax.ppermute(block, 'seq', [(i, i ^ k) for i in range(seq)])  27.1 us
    ppermute x8, starting transfers between devices, body(): lax.ppermute(chunk[k], 'seq', near if k < 2 else far)  20.3 us
    ppermute x18, starting transfers between devices, partner(): lax.ppermute(block, 'seq', [(i, i ^ k) for i in range(seq)])  16.4 us
    unnamed x68, local copies, waits for them, and re-layouts  15.4 us
    pallas_call x2, Pallas kernels, compute(): pl.pallas_call(functools.partial(compute_kernel, count, first, leading),...  13.8 us
    ppermute x3, waiting for transfers between devices, reduce_terms(): held = held + lax.ppermute(sent, axis, route)  11.7 us
  transfers between devices with their start and end apart: 34, of which 10 were waited for; matrix products, arithmetic and copies ran while one was open for 1% of the time, Pallas kernels for 21%

commit v1 on v0

v1 whole, which is shorter than its diff:
```python
import functools

import jax
import jax.numpy as jnp
from jax import lax
from jax.experimental import pallas as pl
from jax.experimental.pallas import tpu as pltpu
from jax.sharding import PartitionSpec as P

HEAD_COUNT = 24
HEAD_WIDTH = 128
BLK = 128
REACH = 2
TILES = 5
RANK = 64
TEAM = 4
HEADS = HEAD_COUNT // TEAM
CHUNKS = (3, 3)
WINDOW = TEAM + 2 * REACH
SCALING = HEAD_WIDTH**-0.5
LOG2E = 1.4426950408889634
ANY = pl.BlockSpec(memory_space=pl.ANY)
VMEM = pl.BlockSpec(memory_space=pltpu.VMEM)
SMEM = pl.BlockSpec(memory_space=pltpu.SMEM)


def call(kernel, name, out_shape, inputs, in_specs=None, scratch=(), vmem=4):
    return pl.pallas_call(
        kernel,
        out_shape=out_shape,
        in_specs=in_specs or [VMEM] * len(inputs),
        out_specs=[VMEM] * len(out_shape),
        scratch_shapes=list(scratch),
        compiler_params=pltpu.CompilerParams(vmem_limit_bytes=vmem << 20),
        cost_estimate=pl.CostEstimate(flops=1, bytes_accessed=1, transcendentals=0),
        name=name,
    )(*inputs)


def cols(first, count):
    if not isinstance(first, int):
        first = pl.multiple_of(first * HEAD_WIDTH, HEAD_WIDTH)
    else:
        first = first * HEAD_WIDTH
    return pl.ds(first, count * HEAD_WIDTH)


def rows(first, count):
    if not isinstance(first, int):
        first = pl.multiple_of(first * BLK, BLK)
    else:
        first = first * BLK
    return pl.ds(first, count * BLK)


def place():
    position = lax.axis_index("seq")
    return lax.rem(position, TEAM), position // TEAM


def pack_kernel(adapters, *refs):
    a_ref, b_ref = refs[:2]
    outs = refs[-TEAM:]
    member, _ = place()
    for k in range(TEAM):
        head = jnp.bitwise_xor(member, k) * HEADS
        outs[k][:, cols(0, HEADS)] = a_ref[0, :, cols(head, HEADS)]
        outs[k][:, cols(HEADS, HEADS)] = b_ref[0, :, cols(head, HEADS)]
    if adapters:
        for k in range(TEAM):
            outs[k][:RANK, cols(2 * HEADS, 1)] = refs[2][0]
            outs[k][RANK:, cols(2 * HEADS, 1)] = refs[3][0]


def pack(first, second, adapters=(), after=()):
    tiles = 2 * HEADS + (1 if adapters else 0)
    shape = jax.ShapeDtypeStruct((BLK, tiles * HEAD_WIDTH), first.dtype)
    inputs = [first, second, *adapters, *after]
    specs = [VMEM] * (2 + len(adapters)) + [ANY] * len(after)
    name = "pack_kv" if adapters else "pack_qg"
    return call(functools.partial(pack_kernel, bool(adapters)), name, [shape] * TEAM, inputs, specs)


def stack_kernel(first_ref, second_ref, out_ref):
    out_ref[rows(0, 1), :] = first_ref[...]
    out_ref[rows(1, 1), :] = second_ref[...]


def stack(first, second, name):
    shape = jax.ShapeDtypeStruct((2 * BLK, first.shape[1]), first.dtype)
    return call(stack_kernel, name, [shape], [first, second])[0]


def compute_kernel(first, count, lists_ref, counts_ref, *refs):
    kv, near_ref, far_ref, qg = refs[:TEAM], refs[TEAM], refs[TEAM + 1], refs[TEAM + 2 : 2 * TEAM + 2]
    own_ref, a_ref, b_ref, term_ref, kw, vw, qs, gs, acc_k, acc_v, pm, dm, adapt = refs[2 * TEAM + 2 :]
    member, team = place()
    even = lax.rem(team, 2) == 0

    places = []
    for j in range(TEAM):
        owner = jnp.bitwise_xor(member, j)
        halo = (near_ref if j < 2 else far_ref, rows(j % 2, 1))
        places.append((owner, owner + REACH, lax.rem(owner + REACH + TEAM, WINDOW), halo))

    for j, (_, near, far, (halo, row)) in enumerate(places):
        adapt[:, rows(near, 1)] = kv[j][:, cols(2 * HEADS, 1)]
        adapt[:, rows(far, 1)] = halo[row, cols(2 * HEADS, 1)]

    zero = jnp.zeros((BLK, BLK), pm.dtype)
    for matrix in (pm, dm):
        matrix[rows(TILES, 1), :BLK] = zero
        matrix[rows(0, 1), BLK:] = zero

    def one_head(h, carry):
        head = first + h
        for j, (owner, near, far, (halo, row)) in enumerate(places):
            kw[rows(near, 1), :] = kv[j][:, cols(head, 1)]
            vw[rows(near, 1), :] = kv[j][:, cols(HEADS + head, 1)]
            kw[rows(far, 1), :] = halo[row, cols(head, 1)]
            vw[rows(far, 1), :] = halo[row, cols(HEADS + head, 1)]
            qs[rows(owner, 1), :] = qg[j][:, cols(head, 1)]
            gs[rows(owner, 1), :] = qg[j][:, cols(HEADS + head, 1)]
        for pair in range(TEAM // 2):
            span = rows(2 * pair, TILES + 1)
            queries = qs[rows(2 * pair, 2), :]
            grads = gs[rows(2 * pair, 2), :]
            on_last = (((1,), (1,)), ((), ()))
            scores = lax.dot_general(kw[span, :], queries, on_last, preferred_element_type=jnp.float32)
            dprobs = lax.dot_general(vw[span, :], grads, on_last, preferred_element_type=jnp.float32)
            for u in range(2):
                block = team * TEAM + 2 * pair + u
                whole_head = member * HEADS + head
                used = counts_ref[block, whole_head]
                live = jnp.int32(0)
                for t in range(TILES):
                    offset = lists_ref[t, block, whole_head] - block + REACH
                    live = live | jnp.where(t < used, jnp.left_shift(1, offset), 0)
                lanes = slice(u * BLK, (u + 1) * BLK)
                logits = []
                for t in range(TILES):
                    tile = scores[(u + t) * BLK : (u + t + 1) * BLK, lanes]
                    masked = jnp.where((live >> t) & 1 == 1, 0.0, -jnp.inf)
                    logits.append(tile * (SCALING * LOG2E) + masked)
                logits = jnp.concatenate(logits, axis=0)
                top = jnp.max(logits, axis=0, keepdims=True)
                weights = jnp.exp2(logits - top)
                inverse = 1.0 / jnp.sum(weights, axis=0, keepdims=True)
                probs = weights * inverse
                dp = dprobs[u * BLK : (u + TILES) * BLK, lanes]
                delta = jnp.sum(probs * dp, axis=0, keepdims=True)
                pm[rows(u, TILES), lanes] = probs.astype(pm.dtype)
                dm[rows(u, TILES), lanes] = (probs * (dp - delta)).astype(dm.dtype)
            value_add = jnp.dot(pm[...], grads, preferred_element_type=jnp.float32)
            key_add = jnp.dot(dm[...], queries, preferred_element_type=jnp.float32) * SCALING
            if pair == 0:
                acc_v[rows(0, TILES + 1), :] = value_add
                acc_k[rows(0, TILES + 1), :] = key_add
            else:
                split = TEAM * BLK
                acc_v[rows(2, TEAM), :] += value_add[:split]
                acc_k[rows(2, TEAM), :] += key_add[:split]
                acc_v[rows(2 + TEAM, 2), :] = value_add[split:]
                acc_k[rows(2 + TEAM, 2), :] = key_add[split:]
        for acc, column, half in ((acc_k, cols(h, 1), 0), (acc_v, cols(count + h, 1), RANK)):
            own_ref[:, column] = acc[rows(REACH, TEAM), :]
            lower = acc[rows(0, REACH), :].astype(a_ref.dtype)
            upper = acc[rows(REACH + TEAM, REACH), :].astype(a_ref.dtype)
            a_ref[:, column] = jnp.where(even, upper, lower)
            b_ref[:, column] = jnp.where(even, lower, upper)
            term_ref[half : half + RANK, cols(h, 1)] = jnp.dot(
                adapt[half : half + RANK, :], acc[...].astype(adapt.dtype), preferred_element_type=jnp.float32
            )
        return carry

    if UNROLL:
        for h in range(count):
            one_head(h, 0)
    else:
        lax.fori_loop(0, count, one_head, 0)


UNROLL = True


def compute(c, lists, counts, kv, near, far, qg):
    first, count = sum(CHUNKS[:c]), CHUNKS[c]
    kind = qg[0].dtype
    width = 2 * count * HEAD_WIDTH
    out_shape = [
        jax.ShapeDtypeStruct((TEAM * BLK, width), jnp.float32),
        jax.ShapeDtypeStruct((REACH * BLK, width), kind),
        jax.ShapeDtypeStruct((REACH * BLK, width), kind),
        jax.ShapeDtypeStruct((2 * RANK, count * HEAD_WIDTH), jnp.float32),
    ]
    inputs = [lists, counts, *kv, near, far, *qg]
    tall, team = WINDOW * BLK, TEAM * BLK
    scratch = [
        pltpu.VMEM((tall, HEAD_WIDTH), kind),
        pltpu.VMEM((tall, HEAD_WIDTH), kind),
        pltpu.VMEM((team, HEAD_WIDTH), kind),
        pltpu.VMEM((team, HEAD_WIDTH), kind),
        pltpu.VMEM((tall, HEAD_WIDTH), jnp.float32),
        pltpu.VMEM((tall, HEAD_WIDTH), jnp.float32),
        pltpu.VMEM(((TILES + 1) * BLK, 2 * BLK), kind),
        pltpu.VMEM(((TILES + 1) * BLK, 2 * BLK), kind),
        pltpu.VMEM((2 * RANK, tall), kind),
    ]
    specs = [SMEM] * 2 + [VMEM] * (len(inputs) - 2)
    kernel = functools.partial(compute_kernel, first, count)
    return call(kernel, f"gradients_{c}", out_shape, inputs, specs, scratch, 8)


def combine_kernel(own_ref, a_ref, b_ref, *outs):
    member, team = place()
    even = lax.rem(team, 2)
    for k in range(TEAM):
        owner = jnp.bitwise_xor(member, k)
        row = rows(lax.rem(owner, 2), 1)
        from_a = owner // 2 != even

        def add(part_ref, k=k, owner=owner, row=row):
            part = part_ref[row, :].astype(jnp.float32)
            outs[k][...] = (own_ref[rows(owner, 1), :] + part).astype(outs[k].dtype)

        pl.when(from_a)(functools.partial(add, a_ref))
        pl.when(jnp.logical_not(from_a))(functools.partial(add, b_ref))


def combine(c, own, a, b):
    shape = jax.ShapeDtypeStruct((BLK, own.shape[1]), a.dtype)
    return call(combine_kernel, f"combine_{c}", [shape] * TEAM, [own, a, b])


def unpack_kernel(*refs):
    ins, outs = refs[: TEAM * len(CHUNKS)], refs[TEAM * len(CHUNKS) :]
    member, _ = place()
    for c, count in enumerate(CHUNKS):
        for k in range(TEAM):
            head = jnp.bitwise_xor(member, k) * HEADS + sum(CHUNKS[:c])
            for part, out in enumerate(outs):
                out[0, :, cols(head, count)] = ins[c * TEAM + k][:, cols(part * count, count)]


def unpack(home):
    flat = [block for chunk in home for block in chunk]
    shape = jax.ShapeDtypeStruct((1, BLK, HEAD_COUNT * HEAD_WIDTH), flat[0].dtype)
    return call(unpack_kernel, "unpack", [shape, shape], flat)


def bit_value(axis, bit, unit):
    return lax.rem(lax.axis_index(axis) // (bit * unit), 2)


def pieces_kernel(pieces, bit, *refs):
    terms = refs[: len(CHUNKS)]
    keep_ref, send_ref, whole = refs[len(CHUNKS) :]
    for c, term in enumerate(terms):
        whole[:, cols(sum(CHUNKS[:c]), CHUNKS[c])] = term[...]
    upper = bit_value(*bit) == 1
    width = whole.shape[1] // pieces
    half = pieces // 2
    for j in range(half):
        low = whole[:, j * width : (j + 1) * width]
        high = whole[:, (half + j) * width : (half + j + 1) * width]
        keep_ref[j] = jnp.where(upper, high, low)
        send_ref[j] = jnp.where(upper, low, high)


def fold_kernel(bit, held_ref, got_ref, *outs):
    half = held_ref.shape[0] // 2
    if bit is None:
        outs[0][...] = held_ref[0] + got_ref[0]
        return
    value = bit_value(*bit)
    for out, first in ((outs[0], value * half), (outs[1], (1 - value) * half)):
        out[...] = held_ref[pl.ds(first, half)] + got_ref[pl.ds(first, half)]


def split_kernel(in_ref, key_ref, value_ref):
    key_ref[...] = in_ref[:RANK, :]
    value_ref[...] = in_ref[RANK:, :]


def reduce_terms(terms):
    clips, seq = lax.axis_size("dp"), lax.axis_size("seq")
    teams = seq // TEAM
    pieces = clips * teams
    rounds = [("dp", clips >> s, 1) for s in range(1, clips.bit_length())]
    rounds += [("seq", teams >> s, TEAM) for s in range(1, teams.bit_length())]
    width = HEADS * HEAD_WIDTH // pieces
    shape = jax.ShapeDtypeStruct((pieces // 2, 2 * RANK, width), jnp.float32)
    scratch = [pltpu.VMEM((2 * RANK, HEADS * HEAD_WIDTH), jnp.float32)]
    kernel = functools.partial(pieces_kernel, pieces, rounds[0])
    held, sent = call(kernel, "pieces", [shape, shape], terms, scratch=scratch)
    for index, (axis, bit, unit) in enumerate(rounds):
        route = [(i, i ^ (bit * unit)) for i in range(lax.axis_size(axis))]
        got = lax.ppermute(sent, axis, route)
        following = rounds[index + 1] if index + 1 < len(rounds) else None
        if following:
            shape = jax.ShapeDtypeStruct((held.shape[0] // 2, 2 * RANK, width), jnp.float32)
            out_shape = [shape, shape]
        else:
            out_shape = [jax.ShapeDtypeStruct((2 * RANK, width), jnp.float32)]
        folded = call(functools.partial(fold_kernel, following), f"fold_{index}", out_shape, [held, got])
        held, sent = folded[0], folded[-1]
    route = []
    for clip in range(clips):
        for position in range(seq):
            piece = clip * teams + position // TEAM
            route.append((clip * seq + position, position % TEAM * pieces + piece))
    shape = jax.ShapeDtypeStruct((RANK, width), jnp.float32)
    return call(split_kernel, "split", [shape, shape], [lax.ppermute(held, ("dp", "seq"), route)])


def body(
    head_queries,
    head_keys,
    head_values,
    output_gradient,
    key_adapter_input,
    value_adapter_input,
    key_block_lists,
    live_block_counts,
):
    seq = lax.axis_size("seq")
    teams = seq // TEAM

    def partner(block, k):
        return lax.ppermute(block, "seq", [(i, i ^ k) for i in range(seq)]) if k else block

    near_route = []
    for p in range(seq):
        t = p // TEAM + (1 if p % TEAM >= TEAM // 2 else -1)
        if 0 <= t < teams:
            near_route.append((p, t * TEAM + p % TEAM))
    far_route = [(target, source) for source, target in near_route]
    swaps = []
    for start in (0, 1):
        pairs = []
        for t in range(start, teams - 1, 2):
            for m in range(TEAM):
                pairs += [(t * TEAM + m, (t + 1) * TEAM + m), ((t + 1) * TEAM + m, t * TEAM + m)]
        swaps.append(pairs)

    lists = key_block_lists.transpose(2, 1, 0)
    counts = live_block_counts.T
    adapters = (key_adapter_input.transpose(0, 2, 1), value_adapter_input.transpose(0, 2, 1))
    kv_out = pack(head_keys, head_values, adapters)
    kv = [partner(block, k) for k, block in enumerate(kv_out)]
    qg_out = pack(head_queries, output_gradient, after=kv_out[:1])
    qg = [partner(block, k) for k, block in enumerate(qg_out)]
    near = lax.ppermute(stack(kv[0], kv[1], "near"), "seq", near_route)
    far = lax.ppermute(stack(kv[2], kv[3], "far"), "seq", far_route)

    home, terms = [], []
    for c in range(len(CHUNKS)):
        own, to_a, to_b, term = compute(c, lists, counts, kv, near, far, qg)
        terms.append(term)
        from_a = lax.ppermute(to_a, "seq", swaps[0])
        from_b = lax.ppermute(to_b, "seq", swaps[1])
        blocks = combine(c, own, from_a, from_b)
        home.append([partner(block, k) for k, block in enumerate(blocks)])
    key_term, value_term = reduce_terms(terms)
    key_gradient, value_gradient = unpack(home)
    return key_gradient, value_gradient, key_term.T, value_term.T


def solution(mesh):
    tokens = P("dp", "seq", None)
    shares = P(("dp", "seq"), None)
    return jax.shard_map(
        body,
        mesh=mesh,
        in_specs=(tokens,) * 6 + (P(), P()),
        out_specs=(tokens, tokens, shares, shares),
        check_vma=False,
    )
```

time: 283 us -> 117 us (0.41)
  Pallas kernels: 165 us -> 16.4 us
  starting transfers between devices: 54.2 us -> 34.2 us
  waiting for transfers between devices: 42.4 us -> 60.4 us
  local copies, waits for them, and re-layouts: 17.1 us -> 3.71 us
    pallas_call x8 -> x14, Pallas kernels: 165 us -> 16.4 us  [call(): pl.pallas_call(kernel, out_shape=out_shape, in_specs=in_specs or [VMEM] *...]
    ppermute x12 -> x6, starting transfers between devices: 32.3 us -> 13.3 us  [the longest x3 4.45 us: reduce_terms(): got = lax.ppermute(sent, axis, route)]
    ppermute x18 -> x12, waiting for transfers between devices: 27.1 us -> 45.1 us  [partner(): lax.ppermute(block, 'seq', [(i, i ^ k) for i in range(seq)])]
    unnamed x68 -> x16, local copies, waits for them, and re-layouts: 15.4 us -> 3.71 us
    ppermute x12 -> x6, waiting for transfers between devices: 11.7 us -> 15.3 us  [the longest x3 14.1 us: reduce_terms(): got = lax.ppermute(sent, axis, route)]
    ppermute x2, waiting for transfers between devices: 3.63 us -> 0.01 us  [body(): from_a = lax.ppermute(to_a, 'seq', swaps[0])]
    ppermute x18 -> x12, starting transfers between devices: 16.4 us -> 14.6 us  [partner(): lax.ppermute(block, 'seq', [(i, i ^ k) for i in range(seq)])]
  transfers between devices with their start and end apart: 34 -> 22, of which waited for: 10 -> 12; matrix products, arithmetic and copies ran while one was open for 1% -> 0% of each run, Pallas kernels for 21% -> 7%
where the time goes in v1:
time: 117 us; the launch traced here: 116 us
  waiting for transfers between devices  60.4 us (52%)
  starting transfers between devices  34.2 us (29%)
  Pallas kernels  16.4 us (14%)
  local copies, waits for them, and re-layouts  3.71 us (3%)
    ppermute x12, waiting for transfers between devices, partner(): lax.ppermute(block, 'seq', [(i, i ^ k) for i in range(seq)])  45.1 us
    pallas_call x14, Pallas kernels, call(): pl.pallas_call(kernel, out_shape=out_shape, in_specs=in_specs or [VMEM] *...  16.4 us
    ppermute x12, starting transfers between devices, partner(): lax.ppermute(block, 'seq', [(i, i ^ k) for i in range(seq)])  14.6 us
    ppermute x3, waiting for transfers between devices, reduce_terms(): got = lax.ppermute(sent, axis, route)  14.1 us
    ppermute x2, starting transfers between devices, body(): from_a = lax.ppermute(to_a, 'seq', swaps[0])  4.84 us
    ppermute x3, starting transfers between devices, reduce_terms(): got = lax.ppermute(sent, axis, route)  4.45 us
    ppermute x1, starting transfers between devices, reduce_terms(): lax.ppermute(held, ('dp', 'seq'), route)  4.15 us
    unnamed x16, local copies, waits for them, and re-layouts  3.71 us
  transfers between devices with their start and end apart: 22, of which 12 were waited for; matrix products, arithmetic and copies ran while one was open for 0% of the time, Pallas kernels for 7%

profile of v1, /device:TPU:5, one launch (start us, length us, event | category | flops | bytes accessed | tf_op | source)
XLA Modules:
  0.0 115.6 jit_solution(12964581186988638208)
XLA Ops:
  5.2 1.7 %collective-permute-start.2 = (bf16[128,1664]{1,0:T(8,128)(2,1)S(1)}, bf16[128,1664]{1,0:T(8,128)(2,1)S(1)}, u32[]{:S(2)}, u32[]{:S(2)}) collective-permute-start(bf16[128,1664]{1,0:T(8,128)(2,1)S(1)} %get-tuple-element.41), channel_id=1, source_target_pairs={{0,3},{1,2},{2,1},{3,0},{4,7},{5,6},{6,5},{7,4},{8,11},{9,10},{10,... | collective-permute-start | bytes 1277960 | tf_op jit(solution)/shard_map/ppermute | solution.py:330
  7.0 3.4 %collective-permute-start.3 = (bf16[256,1664]{1,0:T(8,128)(2,1)S(1)}, bf16[256,1664]{1,0:T(8,128)(2,1)S(1)}, u32[]{:S(2)}, u32[]{:S(2)}) collective-permute-start(bf16[256,1664]{1,0:T(8,128)(2,1)S(1)} %near.1), channel_id=1, source_target_pairs={{2,6},{3,7},{4,0},{5,1},{6,10},{7,11},{8,4},{9,5},{10,14},{11,15},... | collective-permute-start | bytes 2555912 | tf_op jit(solution)/shard_map/ppermute | solution.py:353
  10.4 6.2 %collective-permute-done.1.first_ref.refs_2_ = bf16[128,1664]{1,0:T(8,128)(2,1)S(1)} collective-permute-done((bf16[128,1664]{1,0:T(8,128)(2,1)S(1)}, bf16[128,1664]{1,0:T(8,128)(2,1)S(1)}, u32[]{:S(2)}, u32[]{:S(2)}) %collective-permute-start.1) | collective-permute-done | bytes 426016 | tf_op jit(solution)/shard_map/ppermute | solution.py:330
  16.6 9.3 %collective-permute-done.2.second_ref.refs_3_ = bf16[128,1664]{1,0:T(8,128)(2,1)S(1)} collective-permute-done((bf16[128,1664]{1,0:T(8,128)(2,1)S(1)}, bf16[128,1664]{1,0:T(8,128)(2,1)S(1)}, u32[]{:S(2)}, u32[]{:S(2)}) %collective-permute-start.2) | collective-permute-done | bytes 426016 | tf_op jit(solution)/shard_map/ppermute | solution.py:330
  26.0 1.3 %collective-permute-start.4 = (bf16[256,1664]{1,0:T(8,128)(2,1)S(1)}, bf16[256,1664]{1,0:T(8,128)(2,1)S(1)}, u32[]{:S(2)}, u32[]{:S(2)}) collective-permute-start(bf16[256,1664]{1,0:T(8,128)(2,1)S(1)} %far.1), channel_id=1, source_target_pairs={{6,2},{7,3},{0,4},{1,5},{10,6},{11,7},{4,8},{5,9},{14,10},{15,11},... | collective-permute-start | bytes 2555912 | tf_op jit(solution)/shard_map/ppermute | solution.py:354
  27.7 2.5 %collective-permute-start.6 = (bf16[128,1536]{1,0:T(8,128)(2,1)S(1)}, bf16[128,1536]{1,0:T(8,128)(2,1)S(1)}, u32[]{:S(2)}, u32[]{:S(2)}) collective-permute-start(bf16[128,1536]{1,0:T(8,128)(2,1)S(1)} %get-tuple-element.44), channel_id=1, source_target_pairs={{0,2},{1,3},{2,0},{3,1},{4,6},{5,7},{6,4},{7,5},{8,10},{9,11},{10,... | collective-permute-start | bytes 1179656 | tf_op jit(solution)/shard_map/ppermute | solution.py:330
  30.4 9.1 %collective-permute-done.6.refs_8_ = bf16[128,1536]{1,0:T(8,128)(2,1)S(1)} collective-permute-done((bf16[128,1536]{1,0:T(8,128)(2,1)S(1)}, bf16[128,1536]{1,0:T(8,128)(2,1)S(1)}, u32[]{:S(2)}, u32[]{:S(2)}) %collective-permute-start.6) | collective-permute-done | bytes 393248 | tf_op jit(solution)/shard_map/ppermute | solution.py:330
  39.4 8.8 %collective-permute-done.7.refs_9_ = bf16[128,1536]{1,0:T(8,128)(2,1)S(1)} collective-permute-done((bf16[128,1536]{1,0:T(8,128)(2,1)S(1)}, bf16[128,1536]{1,0:T(8,128)(2,1)S(1)}, u32[]{:S(2)}, u32[]{:S(2)}) %collective-permute-start.7) | collective-permute-done | bytes 393248 | tf_op jit(solution)/shard_map/ppermute | solution.py:330
  48.5 6.7 %gradients_0.1 = (f32[512,768]{1,0:T(8,128)S(1)}, bf16[256,768]{1,0:T(8,128)(2,1)S(1)}, bf16[256,768]{1,0:T(8,128)(2,1)S(1)}, f32[128,384]{1,0:T(8,128)S(1)}) custom-call(s32[5,16,24]{2,1,0:T(8,128)S(1)} %bitcast.6, s32[16,24]{1,0:T(8,128)S(1)} %bitcast.8, bf16[128,1664]{1,0:T(8,128)(2,1)S(1)} %get-tuple-element.38.first_ref.refs_2_.refs_0_, ...), custom_call_target="tpu_custom_call" | custom-call | flops 1 | bytes 1 | tf_op jit(solution)/shard_map/gradients_0/pallas_call | solution.py:28
  55.2 1.7 %collective-permute-start.8 = (bf16[256,768]{1,0:T(8,128)(2,1)S(1)}, bf16[256,768]{1,0:T(8,128)(2,1)S(1)}, u32[]{:S(2)}, u32[]{:S(2)}) collective-permute-start(bf16[256,768]{1,0:T(8,128)(2,1)S(1)} %get-tuple-element.47), channel_id=1, source_target_pairs={{0,4},{4,0},{1,5},{5,1},{2,6},{6,2},{3,7},{7,3},{8,12},{12,8},{9,1... | collective-permute-start | bytes 1179656 | tf_op jit(solution)/shard_map/ppermute | solution.py:360
  57.8 6.7 %gradients_1.1 = (f32[512,768]{1,0:T(8,128)S(1)}, bf16[256,768]{1,0:T(8,128)(2,1)S(1)}, bf16[256,768]{1,0:T(8,128)(2,1)S(1)}, f32[128,384]{1,0:T(8,128)S(1)}) custom-call(s32[5,16,24]{2,1,0:T(8,128)S(1)} %bitcast.7, s32[16,24]{1,0:T(8,128)S(1)} %bitcast.9, bf16[128,1664]{1,0:T(8,128)(2,1)S(1)} %get-tuple-element.38.first_ref.refs_2_.refs_0_, ...), custom_call_target="tpu_custom_call" | custom-call | flops 1 | bytes 1 | tf_op jit(solution)/shard_map/gradients_1/pallas_call | solution.py:28
  66.0 3.1 %collective-permute-start.13 = (bf16[256,768]{1,0:T(8,128)(2,1)S(1)}, bf16[256,768]{1,0:T(8,128)(2,1)S(1)}, u32[]{:S(2)}, u32[]{:S(2)}) collective-permute-start(bf16[256,768]{1,0:T(8,128)(2,1)S(1)} %get-tuple-element.54), channel_id=1, source_target_pairs={{0,4},{4,0},{1,5},{5,1},{2,6},{6,2},{3,7},{7,3},{8,12},{12,8},{9,1... | collective-permute-start | bytes 1179656 | tf_op jit(solution)/shard_map/ppermute | solution.py:360
  69.8 1.8 %collective-permute-done.18.got_ref = f32[4,128,96]{2,1,0:T(8,128)S(1)} collective-permute-done((f32[4,128,96]{2,1,0:T(8,128)S(1)}, f32[4,128,96]{2,1,0:T(8,128)S(1)}, u32[]{:S(2)}, u32[]{:S(2)}) %collective-permute-start.18) | collective-permute-done | bytes 196640 | tf_op jit(solution)/shard_map/ppermute | solution.py:298
  71.7 3.1 %collective-permute-start.19 = (f32[2,128,96]{2,1,0:T(8,128)S(1)}, f32[2,128,96]{2,1,0:T(8,128)S(1)}, u32[]{:S(2)}, u32[]{:S(2)}) collective-permute-start(f32[2,128,96]{2,1,0:T(8,128)S(1)} %get-tuple-element.67), channel_id=1, source_target_pairs={{0,8},{1,9},{2,10},{3,11},{4,12},{5,13},{6,14},{7,15},{8,0},{9,1},... | collective-permute-start | bytes 294920 | tf_op jit(solution)/shard_map/ppermute | solution.py:298
  75.0 2.1 %collective-permute-start.10 = (bf16[128,768]{1,0:T(8,128)(2,1)S(1)}, bf16[128,768]{1,0:T(8,128)(2,1)S(1)}, u32[]{:S(2)}, u32[]{:S(2)}) collective-permute-start(bf16[128,768]{1,0:T(8,128)(2,1)S(1)} %get-tuple-element.50), channel_id=1, source_target_pairs={{0,1},{1,0},{2,3},{3,2},{4,5},{5,4},{6,7},{7,6},{8,9},{9,8},{10,11... | collective-permute-start | bytes 589832 | tf_op jit(solution)/shard_map/ppermute | solution.py:330
  77.0 9.2 %collective-permute-done.19.got_ref = f32[2,128,96]{2,1,0:T(8,128)S(1)} collective-permute-done((f32[2,128,96]{2,1,0:T(8,128)S(1)}, f32[2,128,96]{2,1,0:T(8,128)S(1)}, u32[]{:S(2)}, u32[]{:S(2)}) %collective-permute-start.19) | collective-permute-done | bytes 98336 | tf_op jit(solution)/shard_map/ppermute | solution.py:298
  86.3 3.1 %collective-permute-done.20.got_ref = f32[1,128,96]{2,1,0:T(8,128)S(1)} collective-permute-done((f32[1,128,96]{2,1,0:T(8,128)S(1)}, f32[1,128,96]{2,1,0:T(8,128)S(1)}, u32[]{:S(2)}, u32[]{:S(2)}) %collective-permute-start.20) | collective-permute-done | bytes 49184 | tf_op jit(solution)/shard_map/ppermute | solution.py:298
  89.4 4.2 %collective-permute-start.21 = (f32[128,96]{1,0:T(8,128)S(1)}, f32[128,96]{1,0:T(8,128)S(1)}, u32[]{:S(2)}, u32[]{:S(2)}) collective-permute-start(f32[128,96]{1,0:T(8,128)S(1)} %fold_2.1), channel_id=1, source_target_pairs={{0,0},{1,8},{2,16},{3,24},{4,1},{5,9},{6,17},{7,25},{8,2},{9,10},{... | collective-permute-start | bytes 147464 | tf_op jit(solution)/shard_map/ppermute | solution.py:313
  94.0 2.5 %collective-permute-start.12 = (bf16[128,768]{1,0:T(8,128)(2,1)S(1)}, bf16[128,768]{1,0:T(8,128)(2,1)S(1)}, u32[]{:S(2)}, u32[]{:S(2)}) collective-permute-start(bf16[128,768]{1,0:T(8,128)(2,1)S(1)} %get-tuple-element.52), channel_id=1, source_target_pairs={{0,3},{1,2},{2,1},{3,0},{4,7},{5,6},{6,5},{7,4},{8,11},{9,10},{10,... | collective-permute-start | bytes 589832 | tf_op jit(solution)/shard_map/ppermute | solution.py:330
  97.8 4.2 %collective-permute-start.17 = (bf16[128,768]{1,0:T(8,128)(2,1)S(1)}, bf16[128,768]{1,0:T(8,128)(2,1)S(1)}, u32[]{:S(2)}, u32[]{:S(2)}) collective-permute-start(bf16[128,768]{1,0:T(8,128)(2,1)S(1)} %get-tuple-element.59), channel_id=1, source_target_pairs={{0,3},{1,2},{2,1},{3,0},{4,7},{5,6},{6,5},{7,4},{8,11},{9,10},{10,... | collective-permute-start | bytes 589832 | tf_op jit(solution)/shard_map/ppermute | solution.py:330
  102.6 4.4 %collective-permute-done.12.refs_3_ = bf16[128,768]{1,0:T(8,128)(2,1)S(1)} collective-permute-done((bf16[128,768]{1,0:T(8,128)(2,1)S(1)}, bf16[128,768]{1,0:T(8,128)(2,1)S(1)}, u32[]{:S(2)}, u32[]{:S(2)}) %collective-permute-start.12) | collective-permute-done | bytes 196640 | tf_op jit(solution)/shard_map/ppermute | solution.py:330
  107.0 2.3 %collective-permute-done.16.refs_6_ = bf16[128,768]{1,0:T(8,128)(2,1)S(1)} collective-permute-done((bf16[128,768]{1,0:T(8,128)(2,1)S(1)}, bf16[128,768]{1,0:T(8,128)(2,1)S(1)}, u32[]{:S(2)}, u32[]{:S(2)}) %collective-permute-start.16) | collective-permute-done | bytes 196640 | tf_op jit(solution)/shard_map/ppermute | solution.py:330
  109.3 5.0 %collective-permute-done.17.refs_7_ = bf16[128,768]{1,0:T(8,128)(2,1)S(1)} collective-permute-done((bf16[128,768]{1,0:T(8,128)(2,1)S(1)}, bf16[128,768]{1,0:T(8,128)(2,1)S(1)}, u32[]{:S(2)}, u32[]{:S(2)}) %collective-permute-start.17) | collective-permute-done | bytes 196640 | tf_op jit(solution)/shard_map/ppermute | solution.py:330
  114.3 1.3 %unpack.1 = (bf16[1,128,3072]{2,1,0:T(8,128)(2,1)}, bf16[1,128,3072]{2,1,0:T(8,128)(2,1)}) custom-call(bf16[128,768]{1,0:T(8,128)(2,1)S(1)} %get-tuple-element.49.refs_0_, bf16[128,768]{1,0:T(8,128)(2,1)S(1)} %collective-permute-done.10.refs_1_, bf16[128,768]{1,0:T(8,128)(2,1)S(1)} %collective-permute-done.11.refs_2_, ...), custom_call_target="tpu_custom_call" | custom-call | flops 1 | bytes 1 | tf_op jit(solution)/shard_map/unpack/pallas_call | solution.py:28
  (50 shorter events, 11.3 us)
Async XLA Ops:
  4.5 2.5 %collective-permute-start = (bf16[128,1664]{1,0:T(8,128)(2,1)S(1)}, bf16[128,1664]{1,0:T(8,128)(2,1)S(1)}, u32[]{:S(2)}, u32[]{:S(2)}) collective-permute-start(bf16[128,1664]{1,0:T(8,128)(2,1)S(1)} %get-tuple-element.39), channel_id=1, source_target_pairs={{0,1},{1,0},{2,3},{3,2},{4,5},{5,4},{6,7},{7,6},{8,9},{9,8},{10,11... | collective-permute-start | bytes 1277960 | tf_op jit(solution)/shard_map/ppermute | solution.py:330
  5.2 11.4 %collective-permute-start.1 = (bf16[128,1664]{1,0:T(8,128)(2,1)S(1)}, bf16[128,1664]{1,0:T(8,128)(2,1)S(1)}, u32[]{:S(2)}, u32[]{:S(2)}) collective-permute-start(bf16[128,1664]{1,0:T(8,128)(2,1)S(1)} %get-tuple-element.40), channel_id=1, source_target_pairs={{0,2},{1,3},{2,0},{3,1},{4,6},{5,7},{6,4},{7,5},{8,10},{9,11},{10,... | collective-permute-start | bytes 1277960 | tf_op jit(solution)/shard_map/ppermute | solution.py:330
  5.2 20.7 %collective-permute-start.2 = (bf16[128,1664]{1,0:T(8,128)(2,1)S(1)}, bf16[128,1664]{1,0:T(8,128)(2,1)S(1)}, u32[]{:S(2)}, u32[]{:S(2)}) collective-permute-start(bf16[128,1664]{1,0:T(8,128)(2,1)S(1)} %get-tuple-element.41), channel_id=1, source_target_pairs={{0,3},{1,2},{2,1},{3,0},{4,7},{5,6},{6,5},{7,4},{8,11},{9,10},{10,... | collective-permute-start | bytes 1277960 | tf_op jit(solution)/shard_map/ppermute | solution.py:330
  7.0 41.5 %copy-start.4 = (s32[24,16,5]{0,1,2:T(8,128)S(1)}, s32[24,16,5]{0,1,2:T(8,128)}, u32[]{:S(2)}) copy-start(s32[24,16,5]{0,1,2:T(8,128)} %param.14) | copy-start | bytes 23044
  7.0 41.5 %copy-start.5 = (s32[24,16]{0,1:T(8,128)S(1)}, s32[24,16]{0,1:T(8,128)}, u32[]{:S(2)}) copy-start(s32[24,16]{0,1:T(8,128)} %param.15) | copy-start | bytes 4612
  7.0 41.3 %collective-permute-start.3 = (bf16[256,1664]{1,0:T(8,128)(2,1)S(1)}, bf16[256,1664]{1,0:T(8,128)(2,1)S(1)}, u32[]{:S(2)}, u32[]{:S(2)}) collective-permute-start(bf16[256,1664]{1,0:T(8,128)(2,1)S(1)} %near.1), channel_id=1, source_target_pairs={{2,6},{3,7},{4,0},{5,1},{6,10},{7,11},{8,4},{9,5},{10,14},{11,15},... | collective-permute-start | bytes 2555912 | tf_op jit(solution)/shard_map/ppermute | solution.py:353
  26.0 22.5 %collective-permute-start.4 = (bf16[256,1664]{1,0:T(8,128)(2,1)S(1)}, bf16[256,1664]{1,0:T(8,128)(2,1)S(1)}, u32[]{:S(2)}, u32[]{:S(2)}) collective-permute-start(bf16[256,1664]{1,0:T(8,128)(2,1)S(1)} %far.1), channel_id=1, source_target_pairs={{6,2},{7,3},{0,4},{1,5},{10,6},{11,7},{4,8},{5,9},{14,10},{15,11},... | collective-permute-start | bytes 2555912 | tf_op jit(solution)/shard_map/ppermute | solution.py:354
  27.4 3.0 %collective-permute-start.5 = (bf16[128,1536]{1,0:T(8,128)(2,1)S(1)}, bf16[128,1536]{1,0:T(8,128)(2,1)S(1)}, u32[]{:S(2)}, u32[]{:S(2)}) collective-permute-start(bf16[128,1536]{1,0:T(8,128)(2,1)S(1)} %get-tuple-element.43), channel_id=1, source_target_pairs={{0,1},{1,0},{2,3},{3,2},{4,5},{5,4},{6,7},{7,6},{8,9},{9,8},{10,11... | collective-permute-start | bytes 1179656 | tf_op jit(solution)/shard_map/ppermute | solution.py:330
  27.7 11.7 %collective-permute-start.6 = (bf16[128,1536]{1,0:T(8,128)(2,1)S(1)}, bf16[128,1536]{1,0:T(8,128)(2,1)S(1)}, u32[]{:S(2)}, u32[]{:S(2)}) collective-permute-start(bf16[128,1536]{1,0:T(8,128)(2,1)S(1)} %get-tuple-element.44), channel_id=1, source_target_pairs={{0,2},{1,3},{2,0},{3,1},{4,6},{5,7},{6,4},{7,5},{8,10},{9,11},{10,... | collective-permute-start | bytes 1179656 | tf_op jit(solution)/shard_map/ppermute | solution.py:330
  30.2 18.1 %collective-permute-start.7 = (bf16[128,1536]{1,0:T(8,128)(2,1)S(1)}, bf16[128,1536]{1,0:T(8,128)(2,1)S(1)}, u32[]{:S(2)}, u32[]{:S(2)}) collective-permute-start(bf16[128,1536]{1,0:T(8,128)(2,1)S(1)} %get-tuple-element.45), channel_id=1, source_target_pairs={{0,3},{1,2},{2,1},{3,0},{4,7},{5,6},{6,5},{7,4},{8,11},{9,10},{10,... | collective-permute-start | bytes 1179656 | tf_op jit(solution)/shard_map/ppermute | solution.py:330
  55.2 19.6 %collective-permute-start.8 = (bf16[256,768]{1,0:T(8,128)(2,1)S(1)}, bf16[256,768]{1,0:T(8,128)(2,1)S(1)}, u32[]{:S(2)}, u32[]{:S(2)}) collective-permute-start(bf16[256,768]{1,0:T(8,128)(2,1)S(1)} %get-tuple-element.47), channel_id=1, source_target_pairs={{0,4},{4,0},{1,5},{5,1},{2,6},{6,2},{3,7},{7,3},{8,12},{12,8},{9,1... | collective-permute-start | bytes 1179656 | tf_op jit(solution)/shard_map/ppermute | solution.py:360
  56.9 17.9 %collective-permute-start.9 = (bf16[256,768]{1,0:T(8,128)(2,1)S(1)}, bf16[256,768]{1,0:T(8,128)(2,1)S(1)}, u32[]{:S(2)}, u32[]{:S(2)}) collective-permute-start(bf16[256,768]{1,0:T(8,128)(2,1)S(1)} %get-tuple-element.48), channel_id=1, source_target_pairs={{4,8},{8,4},{5,9},{9,5},{6,10},{10,6},{7,11},{11,7},{20,24},{24,20... | collective-permute-start | bytes 1179656 | tf_op jit(solution)/shard_map/ppermute | solution.py:361
  64.7 6.9 %collective-permute-start.18 = (f32[4,128,96]{2,1,0:T(8,128)S(1)}, f32[4,128,96]{2,1,0:T(8,128)S(1)}, u32[]{:S(2)}, u32[]{:S(2)}) collective-permute-start(f32[4,128,96]{2,1,0:T(8,128)S(1)} %get-tuple-element.65), channel_id=1, source_target_pairs={{0,16},{16,0},{1,17},{17,1},{2,18},{18,2},{3,19},{19,3},{4,20},{20... | collective-permute-start | bytes 589832 | tf_op jit(solution)/shard_map/ppermute | solution.py:298
  66.0 28.0 %collective-permute-start.13 = (bf16[256,768]{1,0:T(8,128)(2,1)S(1)}, bf16[256,768]{1,0:T(8,128)(2,1)S(1)}, u32[]{:S(2)}, u32[]{:S(2)}) collective-permute-start(bf16[256,768]{1,0:T(8,128)(2,1)S(1)} %get-tuple-element.54), channel_id=1, source_target_pairs={{0,4},{4,0},{1,5},{5,1},{2,6},{6,2},{3,7},{7,3},{8,12},{12,8},{9,1... | collective-permute-start | bytes 1179656 | tf_op jit(solution)/shard_map/ppermute | solution.py:360
  69.2 27.3 %collective-permute-start.14 = (bf16[256,768]{1,0:T(8,128)(2,1)S(1)}, bf16[256,768]{1,0:T(8,128)(2,1)S(1)}, u32[]{:S(2)}, u32[]{:S(2)}) collective-permute-start(bf16[256,768]{1,0:T(8,128)(2,1)S(1)} %get-tuple-element.55), channel_id=1, source_target_pairs={{4,8},{8,4},{5,9},{9,5},{6,10},{10,6},{7,11},{11,7},{20,24},{24,20... | collective-permute-start | bytes 1179656 | tf_op jit(solution)/shard_map/ppermute | solution.py:361
  71.7 14.6 %collective-permute-start.19 = (f32[2,128,96]{2,1,0:T(8,128)S(1)}, f32[2,128,96]{2,1,0:T(8,128)S(1)}, u32[]{:S(2)}, u32[]{:S(2)}) collective-permute-start(f32[2,128,96]{2,1,0:T(8,128)S(1)} %get-tuple-element.67), channel_id=1, source_target_pairs={{0,8},{1,9},{2,10},{3,11},{4,12},{5,13},{6,14},{7,15},{8,0},{9,1},... | collective-permute-start | bytes 294920 | tf_op jit(solution)/shard_map/ppermute | solution.py:298
  75.0 22.9 %collective-permute-start.10 = (bf16[128,768]{1,0:T(8,128)(2,1)S(1)}, bf16[128,768]{1,0:T(8,128)(2,1)S(1)}, u32[]{:S(2)}, u32[]{:S(2)}) collective-permute-start(bf16[128,768]{1,0:T(8,128)(2,1)S(1)} %get-tuple-element.50), channel_id=1, source_target_pairs={{0,1},{1,0},{2,3},{3,2},{4,5},{5,4},{6,7},{7,6},{8,9},{9,8},{10,11... | collective-permute-start | bytes 589832 | tf_op jit(solution)/shard_map/ppermute | solution.py:330
  86.2 3.2 %collective-permute-start.20 = (f32[1,128,96]{2,1,0:T(8,128)S(1)}, f32[1,128,96]{2,1,0:T(8,128)S(1)}, u32[]{:S(2)}, u32[]{:S(2)}) collective-permute-start(f32[1,128,96]{2,1,0:T(8,128)S(1)} %get-tuple-element.69), channel_id=1, source_target_pairs={{0,4},{1,5},{2,6},{3,7},{4,0},{5,1},{6,2},{7,3},{8,12},{9,13},{10,... | collective-permute-start | bytes 147464 | tf_op jit(solution)/shard_map/ppermute | solution.py:298
  89.4 8.4 %collective-permute-start.21 = (f32[128,96]{1,0:T(8,128)S(1)}, f32[128,96]{1,0:T(8,128)S(1)}, u32[]{:S(2)}, u32[]{:S(2)}) collective-permute-start(f32[128,96]{1,0:T(8,128)S(1)} %fold_2.1), channel_id=1, source_target_pairs={{0,0},{1,8},{2,16},{3,24},{4,1},{5,9},{6,17},{7,25},{8,2},{9,10},{... | collective-permute-start | bytes 147464 | tf_op jit(solution)/shard_map/ppermute | solution.py:313
  93.6 9.0 %collective-permute-start.11 = (bf16[128,768]{1,0:T(8,128)(2,1)S(1)}, bf16[128,768]{1,0:T(8,128)(2,1)S(1)}, u32[]{:S(2)}, u32[]{:S(2)}) collective-permute-start(bf16[128,768]{1,0:T(8,128)(2,1)S(1)} %get-tuple-element.51), channel_id=1, source_target_pairs={{0,2},{1,3},{2,0},{3,1},{4,6},{5,7},{6,4},{7,5},{8,10},{9,11},{10,... | collective-permute-start | bytes 589832 | tf_op jit(solution)/shard_map/ppermute | solution.py:330
  94.0 13.0 %collective-permute-start.12 = (bf16[128,768]{1,0:T(8,128)(2,1)S(1)}, bf16[128,768]{1,0:T(8,128)(2,1)S(1)}, u32[]{:S(2)}, u32[]{:S(2)}) collective-permute-start(bf16[128,768]{1,0:T(8,128)(2,1)S(1)} %get-tuple-element.52), channel_id=1, source_target_pairs={{0,3},{1,2},{2,1},{3,0},{4,7},{5,6},{6,5},{7,4},{8,11},{9,10},{10,... | collective-permute-start | bytes 589832 | tf_op jit(solution)/shard_map/ppermute | solution.py:330
  96.6 10.4 %collective-permute-start.15 = (bf16[128,768]{1,0:T(8,128)(2,1)S(1)}, bf16[128,768]{1,0:T(8,128)(2,1)S(1)}, u32[]{:S(2)}, u32[]{:S(2)}) collective-permute-start(bf16[128,768]{1,0:T(8,128)(2,1)S(1)} %get-tuple-element.57), channel_id=1, source_target_pairs={{0,1},{1,0},{2,3},{3,2},{4,5},{5,4},{6,7},{7,6},{8,9},{9,8},{10,11... | collective-permute-start | bytes 589832 | tf_op jit(solution)/shard_map/ppermute | solution.py:330
  97.8 11.5 %collective-permute-start.16 = (bf16[128,768]{1,0:T(8,128)(2,1)S(1)}, bf16[128,768]{1,0:T(8,128)(2,1)S(1)}, u32[]{:S(2)}, u32[]{:S(2)}) collective-permute-start(bf16[128,768]{1,0:T(8,128)(2,1)S(1)} %get-tuple-element.58), channel_id=1, source_target_pairs={{0,2},{1,3},{2,0},{3,1},{4,6},{5,7},{6,4},{7,5},{8,10},{9,11},{10,... | collective-permute-start | bytes 589832 | tf_op jit(solution)/shard_map/ppermute | solution.py:330
  97.8 16.5 %collective-permute-start.17 = (bf16[128,768]{1,0:T(8,128)(2,1)S(1)}, bf16[128,768]{1,0:T(8,128)(2,1)S(1)}, u32[]{:S(2)}, u32[]{:S(2)}) collective-permute-start(bf16[128,768]{1,0:T(8,128)(2,1)S(1)} %get-tuple-element.59), channel_id=1, source_target_pairs={{0,3},{1,2},{2,1},{3,0},{4,7},{5,6},{6,5},{7,4},{8,11},{9,10},{10,... | collective-permute-start | bytes 589832 | tf_op jit(solution)/shard_map/ppermute | solution.py:330
  (6 other events, 44.4 us)

commit v2 on v1

v2 whole, which is shorter than its diff:
```python
import functools

import jax
import jax.numpy as jnp
from jax import lax
from jax.experimental import pallas as pl
from jax.experimental.pallas import tpu as pltpu
from jax.sharding import PartitionSpec as P

HEAD_COUNT = 24
HEAD_WIDTH = 128
BLK = 128
REACH = 2
TILES = 5
RANK = 64
TEAM = 4
HEADS = HEAD_COUNT // TEAM
CHUNKS = (3, 3)
LOADS = 4
WINDOW = TEAM + 2 * REACH
SCALING = HEAD_WIDTH**-0.5
LOG2E = 1.4426950408889634
ANY = pl.BlockSpec(memory_space=pl.ANY)
PACK_VMEM = 62
VMEM = pl.BlockSpec(memory_space=pltpu.VMEM)
SMEM = pl.BlockSpec(memory_space=pltpu.SMEM)


def call(kernel, name, out_shape, inputs, in_specs=None, scratch=(), vmem=4):
    return pl.pallas_call(
        kernel,
        out_shape=out_shape,
        in_specs=in_specs or [VMEM] * len(inputs),
        out_specs=[VMEM] * len(out_shape),
        scratch_shapes=list(scratch),
        compiler_params=pltpu.CompilerParams(vmem_limit_bytes=vmem << 20),
        cost_estimate=pl.CostEstimate(flops=1, bytes_accessed=1, transcendentals=0),
        name=name,
    )(*inputs)


def cols(first, count):
    if not isinstance(first, int):
        first = pl.multiple_of(first * HEAD_WIDTH, HEAD_WIDTH)
    else:
        first = first * HEAD_WIDTH
    return pl.ds(first, count * HEAD_WIDTH)


def rows(first, count):
    if not isinstance(first, int):
        first = pl.multiple_of(first * BLK, BLK)
    else:
        first = first * BLK
    return pl.ds(first, count * BLK)


def place():
    position = lax.axis_index("seq")
    return lax.rem(position, TEAM), position // TEAM


def spans():
    return [(sum(CHUNKS[:c]), count) for c, count in enumerate(CHUNKS)]


class Tiles:
    def __init__(self, ref, span=(0, HEADS), row=0):
        self.ref, (self.first, self.count), self.row = ref, span, row

    def tile(self, head, part):
        place = 2 * self.count if part == 2 else part * self.count + head - self.first
        return self.ref[rows(self.row, 1), cols(place, 1)]


def pack_spans(adapters):
    plan = []
    for k in range(TEAM):
        for span in [(0, HEADS)] if k < 2 else spans():
            plan.append((k, span, bool(adapters) and span[0] == 0))
    return plan


def fill(plan, a_ref, b_ref, adapter_refs, outs, part):
    member, _ = place()
    for (k, (first, count), adapted), out in zip(plan, outs):
        head = jnp.bitwise_xor(member, k) * HEADS + first
        out[part, cols(0, count)] = a_ref[part, cols(head, count)]
        out[part, cols(count, count)] = b_ref[part, cols(head, count)]
    return adapter_refs


def pack_kv_kernel(plan, keys, values, key_in, value_in, *refs):
    outs, (tall, small, sems) = refs[:-3], refs[-3:]
    size = BLK // LOADS
    copies = []
    for part in range(LOADS):
        for index, source in enumerate((keys, values)):
            piece = pl.ds(part * size, size)
            copies.append((source.at[0, piece, :], tall.at[index, piece, :]))
    copies += [(key_in.at[0], small.at[0]), (value_in.at[0], small.at[1])]
    copies = [pltpu.make_async_copy(*pair, sems.at[i]) for i, pair in enumerate(copies)]
    for copy in copies:
        copy.start()
    for part in range(LOADS):
        for copy in copies[2 * part : 2 * part + 2]:
            copy.wait()
        fill(plan, tall.at[0], tall.at[1], None, outs, pl.ds(part * size, size))
    for copy in copies[2 * LOADS :]:
        copy.wait()
    for (k, (_, count), adapted), out in zip(plan, outs):
        if adapted:
            out[:RANK, cols(2 * count, 1)] = small[0]
            out[RANK:, cols(2 * count, 1)] = small[1]


def pack_qg_kernel(plan, queries, grads, _, *outs):
    fill(plan, queries.at[0], grads.at[0], None, outs, slice(None))


def pack(first, second, adapters=(), after=()):
    plan = pack_spans(adapters)
    kind = first.dtype
    out_shape = [
        jax.ShapeDtypeStruct((BLK, (2 * count + adapted) * HEAD_WIDTH), kind) for _, (_, count), adapted in plan
    ]
    if adapters:
        scratch = [
            pltpu.VMEM((2, BLK, HEAD_COUNT * HEAD_WIDTH), kind),
            pltpu.VMEM((2, RANK, BLK), kind),
            pltpu.SemaphoreType.DMA((2 * LOADS + 2,)),
        ]
        kernel = functools.partial(pack_kv_kernel, plan)
        outs = call(kernel, "pack_kv", out_shape, [first, second, *adapters], [ANY] * 4, scratch, PACK_VMEM)
    else:
        kernel = functools.partial(pack_qg_kernel, plan)
        outs = call(kernel, "pack_qg", out_shape, [first, second, *after], [VMEM, VMEM, ANY])
    chunks = len(CHUNKS)
    return [outs[0], outs[1], outs[2 : 2 + chunks], outs[2 + chunks :]]


def stack_kernel(span, first_ref, second_ref, *refs):
    out = refs[-1]
    for row, ref in enumerate((first_ref, second_ref)):
        if span is None:
            out[rows(row, 1), :] = ref[...]
            continue
        first, count = span
        out[rows(row, 1), cols(0, count)] = ref[:, cols(first, count)]
        out[rows(row, 1), cols(count, count)] = ref[:, cols(HEADS + first, count)]
        if first == 0:
            out[rows(row, 1), cols(2 * count, 1)] = ref[:, cols(2 * HEADS, 1)]


def stack(first, second, name, span=None, after=()):
    width = (2 * span[1] + (span[0] == 0)) * HEAD_WIDTH if span else first.shape[1]
    shape = jax.ShapeDtypeStruct((2 * BLK, width), first.dtype)
    specs = [VMEM] * 2 + [ANY] * len(after)
    kernel = functools.partial(stack_kernel, span)
    return call(kernel, name, [shape], [first, second, *after], specs)[0]


def mask_kernel(lists_ref, counts_ref, _, mask_ref):
    member, team = place()
    for h in range(HEADS):
        head = member * HEADS + h
        for b in range(TEAM):
            block = team * TEAM + b
            used = counts_ref[block, head]
            live = jnp.int32(0)
            for t in range(TILES):
                offset = lists_ref[t, block, head] - block + REACH
                live = live | jnp.where(t < used, jnp.left_shift(1, offset), 0)
            for t in range(TILES):
                value = jnp.where((live >> t) & 1 == 1, 0.0, -jnp.inf)
                row = (h * TEAM + b) * TILES + t
                mask_ref[row : row + 1, :] = jnp.full((1, BLK), value, jnp.float32)


def make_mask(lists, counts, after):
    shape = jax.ShapeDtypeStruct((HEADS * TEAM * TILES, BLK), jnp.float32)
    return call(mask_kernel, "mask", [shape], [lists, counts, after], [SMEM, SMEM, ANY])[0]


def compute_kernel(c, mask_ref, *refs):
    first, count = spans()[c]
    kv_refs, qg_refs, (near_ref, far_ref) = refs[:TEAM], refs[TEAM : 2 * TEAM], refs[2 * TEAM : 2 * TEAM + 2]
    if c == 0:
        own_ref, a_ref, b_ref, term_ref, adapt, kw, vw, qs, gs, pm, dm = refs[2 * TEAM + 2 :]
    else:
        adapt, own_ref, a_ref, b_ref, term_ref, kw, vw, qs, gs, pm, dm = refs[2 * TEAM + 2 :]
    kind = adapt.dtype
    member, team = place()
    even = lax.rem(team, 2) == 0
    kv, qg, halo, places = [], [], [], []
    for j in range(TEAM):
        span = (0, HEADS) if j < 2 else (first, count)
        kv.append(Tiles(kv_refs[j], span))
        qg.append(Tiles(qg_refs[j], span))
        halo.append(Tiles(near_ref if j < 2 else far_ref, (first, count), j % 2))
        owner = jnp.bitwise_xor(member, j)
        places.append((owner, owner + REACH, lax.rem(owner + REACH + TEAM, WINDOW)))

    if c == 0:
        for j, (_, near, far) in enumerate(places):
            adapt[:, rows(near, 1)] = kv[j].tile(0, 2)
            adapt[:, rows(far, 1)] = halo[j].tile(0, 2)

    zero = jnp.zeros((BLK, BLK), kind)
    for index in range(count * 2):
        for matrix in (pm, dm):
            matrix[index, rows(TILES, 1), :BLK] = zero
            matrix[index, rows(0, 1), BLK:] = zero

    on_last = (((1,), (1,)), ((), ()))

    def product(left, right, dims=(((1,), (0,)), ((), ()))):
        return lax.dot_general(left, right, dims, preferred_element_type=jnp.float32)

    def load(h):
        head = first + h
        for j, (owner, near, far) in enumerate(places):
            kw[h, rows(near, 1), :] = kv[j].tile(head, 0)
            vw[h, rows(near, 1), :] = kv[j].tile(head, 1)
            kw[h, rows(far, 1), :] = halo[j].tile(head, 0)
            vw[h, rows(far, 1), :] = halo[j].tile(head, 1)
            qs[h, rows(owner, 1), :] = qg[j].tile(head, 0)
            gs[h, rows(owner, 1), :] = qg[j].tile(head, 1)

    def scored(h, pair):
        span, two = rows(2 * pair, TILES + 1), rows(2 * pair, 2)
        return product(kw[h, span, :], qs[h, two, :], on_last), product(vw[h, span, :], gs[h, two, :], on_last)

    def soften(h, pair, scores, dprobs):
        index = h * 2 + pair
        for u in range(2):
            base = ((first + h) * TEAM + 2 * pair + u) * TILES
            masks = [mask_ref[base + t : base + t + 1, :] for t in range(TILES)]
            lanes = slice(u * BLK, (u + 1) * BLK)
            tiles = [slice((u + t) * BLK, (u + t + 1) * BLK) for t in range(TILES)]
            top = jnp.full((1, BLK), -jnp.inf, jnp.float32)
            for mask, tile in zip(masks, tiles):
                top = jnp.maximum(top, jnp.max(scores[tile, lanes], axis=0, keepdims=True) + mask)
            top = top * (SCALING * LOG2E)
            weights = []
            for mask, tile in zip(masks, tiles):
                weights.append(jnp.exp2(scores[tile, lanes] * (SCALING * LOG2E) - (top - mask)))
            total = sum(jnp.sum(weight, axis=0, keepdims=True) for weight in weights)
            mixed = sum(
                jnp.sum(weight * dprobs[tile, lanes], axis=0, keepdims=True) for weight, tile in zip(weights, tiles)
            )
            inverse = 1.0 / total
            delta = mixed * inverse
            for weight, tile in zip(weights, tiles):
                probs = weight * inverse
                pm[index, tile, lanes] = probs.astype(kind)
                dm[index, tile, lanes] = (probs * (dprobs[tile, lanes] - delta)).astype(kind)

    def spread(h, pair):
        index, two = h * 2 + pair, rows(2 * pair, 2)
        return product(dm[index], qs[h, two, :]) * SCALING, product(pm[index], gs[h, two, :])

    def finish(h, adds):
        split, edge = TEAM * BLK, REACH * BLK
        for part, column, half in ((0, cols(h, 1), 0), (1, cols(count + h, 1), RANK)):
            low, high = adds[0][part], adds[1][part]
            middle = low[edge:] + high[:split]
            lower, upper = low[:edge].astype(kind), high[split:].astype(kind)
            own_ref[:, column] = middle
            a_ref[:, column] = jnp.where(even, upper, lower)
            b_ref[:, column] = jnp.where(even, lower, upper)
            window = jnp.concatenate([lower, middle.astype(kind), upper], axis=0)
            term_ref[half : half + RANK, cols(h, 1)] = product(adapt[half : half + RANK, :], window)

    items = [(h, pair) for h in range(count) for pair in range(TEAM // 2)]
    for h in range(count):
        load(h)
    waiting, adds = scored(*items[0]), []
    for index, item in enumerate(items):
        current = waiting
        if index + 1 < len(items):
            waiting = scored(*items[index + 1])
        soften(*item, *current)
        adds.append(spread(*item))
        if len(adds) == TEAM // 2:
            finish(item[0], adds)
            adds = []


def compute(c, mask, kv, qg, near, far, adapt):
    count = CHUNKS[c]
    kind = near.dtype
    width = 2 * count * HEAD_WIDTH
    tall, team = WINDOW * BLK, TEAM * BLK
    out_shape = [
        jax.ShapeDtypeStruct((team, width), jnp.float32),
        jax.ShapeDtypeStruct((REACH * BLK, width), kind),
        jax.ShapeDtypeStruct((REACH * BLK, width), kind),
        jax.ShapeDtypeStruct((2 * RANK, count * HEAD_WIDTH), jnp.float32),
    ]
    inputs = [mask, *kv, *qg, near, far]
    if c == 0:
        out_shape.append(jax.ShapeDtypeStruct((2 * RANK, tall), kind))
    else:
        inputs.append(adapt)
    scratch = [
        pltpu.VMEM((count, tall, HEAD_WIDTH), kind),
        pltpu.VMEM((count, tall, HEAD_WIDTH), kind),
        pltpu.VMEM((count, team, HEAD_WIDTH), kind),
        pltpu.VMEM((count, team, HEAD_WIDTH), kind),
        pltpu.VMEM((count * 2, (TILES + 1) * BLK, 2 * BLK), kind),
        pltpu.VMEM((count * 2, (TILES + 1) * BLK, 2 * BLK), kind),
    ]
    return call(
        functools.partial(compute_kernel, c), f"gradients_{c}", out_shape, inputs, scratch=scratch, vmem=16
    )


def combine_kernel(earlier, own_ref, a_ref, b_ref, *refs):
    outs = refs[-TEAM:]
    member, team = place()
    even = lax.rem(team, 2)
    width = own_ref.shape[1]
    start = outs[1].shape[1] - width
    for index in range(earlier):
        ref = refs[index]
        before = sum(refs[i].shape[1] for i in range(index))
        outs[1][:, before : before + ref.shape[1]] = ref[...]
    for k in range(TEAM):
        owner = jnp.bitwise_xor(member, k)
        row = rows(lax.rem(owner, 2), 1)
        from_a = owner // 2 != even
        column = slice(start, start + width) if k == 1 else slice(None)

        def add(part_ref, out=outs[k], owner=owner, row=row, column=column):
            part = part_ref[row, :].astype(jnp.float32)
            out[:, column] = (own_ref[rows(owner, 1), :] + part).astype(out.dtype)

        pl.when(from_a)(functools.partial(add, a_ref))
        pl.when(jnp.logical_not(from_a))(functools.partial(add, b_ref))


def combine(c, own, a, b, earlier, after):
    block = jax.ShapeDtypeStruct((BLK, own.shape[1]), a.dtype)
    wide = jax.ShapeDtypeStruct((BLK, own.shape[1] + sum(x.shape[1] for x in earlier)), a.dtype)
    specs = [VMEM] * (3 + len(earlier)) + [ANY] * len(after)
    kernel = functools.partial(combine_kernel, len(earlier))
    inputs = [own, a, b, *earlier, *after]
    return call(kernel, f"combine_{c}", [block, wide, block, block], inputs, specs)


def unpack_kernel(*refs):
    outs, other, blocks = refs[-2:], refs[-3], refs[:-3]
    member, _ = place()
    before = 0
    for c, (first, count) in enumerate(spans()):
        sources = [(0, blocks[3 * c], 0), (1, other, before), (2, blocks[3 * c + 1], 0), (3, blocks[3 * c + 2], 0)]
        for k, ref, column in sources:
            head = jnp.bitwise_xor(member, k) * HEADS + first
            for part, out in enumerate(outs):
                out[0, :, cols(head, count)] = ref[:, cols(column + part * count, count)]
        before += 2 * count


def unpack(home, other):
    flat = [block for chunk in home for block in chunk] + [other]
    shape = jax.ShapeDtypeStruct((1, BLK, HEAD_COUNT * HEAD_WIDTH), other.dtype)
    return call(unpack_kernel, "unpack", [shape, shape], flat)


def bit_value(axis, bit, unit):
    return lax.rem(lax.axis_index(axis) // (bit * unit), 2)


def pieces_kernel(bit, *refs):
    terms = refs[: len(CHUNKS)]
    keep_ref, send_ref, whole = refs[len(CHUNKS) :]
    for (first, count), term in zip(spans(), terms):
        whole[:, cols(first, count)] = term[...]
    upper = bit_value(*bit) == 1
    half = whole.shape[1] // 2
    low, high = whole[:, :half], whole[:, half:]
    keep_ref[...] = jnp.where(upper, high, low)
    send_ref[...] = jnp.where(upper, low, high)


def fold_kernel(bit, held_ref, got_ref, *refs):
    keep_ref, send_ref = refs[-2:]
    half, width = keep_ref.shape[0], keep_ref.shape[2]
    value = bit_value(*bit)
    if len(held_ref.shape) == 2:
        total = held_ref[...] + got_ref[...]
        for j in range(half):
            low = total[:, j * width : (j + 1) * width]
            high = total[:, (half + j) * width : (half + j + 1) * width]
            keep_ref[j] = jnp.where(value == 1, high, low)
            send_ref[j] = jnp.where(value == 1, low, high)
    else:
        for out, first in ((keep_ref, value * half), (send_ref, (1 - value) * half)):
            out[...] = held_ref[pl.ds(first, half)] + got_ref[pl.ds(first, half)]


def final_kernel(first_ref, second_ref, key_ref, value_ref):
    key_ref[...] = first_ref[0, :RANK, :] + second_ref[0, :RANK, :]
    value_ref[...] = first_ref[0, RANK:, :] + second_ref[0, RANK:, :]


class Reduction:
    def __init__(self, terms):
        self.clips, seq = lax.axis_size("dp"), lax.axis_size("seq")
        self.teams = seq // TEAM
        self.pieces = self.clips * self.teams
        self.rounds = [("dp", self.clips >> s, 1) for s in range(1, self.clips.bit_length())]
        self.rounds += [("seq", self.teams >> s, TEAM) for s in range(1, self.teams.bit_length())]
        self.width = HEADS * HEAD_WIDTH // self.pieces
        shape = jax.ShapeDtypeStruct((2 * RANK, HEADS * HEAD_WIDTH // 2), jnp.float32)
        scratch = [pltpu.VMEM((2 * RANK, HEADS * HEAD_WIDTH), jnp.float32)]
        kernel = functools.partial(pieces_kernel, self.rounds[0])
        self.held, self.sent = call(kernel, "pieces", [shape, shape], terms, scratch=scratch)
        self.index = 0

    def step(self, after=()):
        index = self.index
        axis, bit, unit = self.rounds[index]
        route = [(i, i ^ (bit * unit)) for i in range(lax.axis_size(axis))]
        got = lax.ppermute(self.sent, axis, route)
        shape = jax.ShapeDtypeStruct((self.pieces >> (index + 2), 2 * RANK, self.width), jnp.float32)
        specs = [VMEM] * 2 + [ANY] * len(after)
        kernel = functools.partial(fold_kernel, self.rounds[index + 1])
        inputs = [self.held, got, *after]
        self.held, self.sent = call(kernel, f"fold_{index}", [shape, shape], inputs, specs)
        self.index += 1

    def finish(self):
        arrived = []
        for flip, piece in enumerate((self.held, self.sent)):
            route = []
            for clip in range(self.clips):
                for position in range(self.teams * TEAM):
                    index = (clip * self.teams + position // TEAM) ^ flip
                    source = clip * self.teams * TEAM + position
                    route.append((source, position % TEAM * self.pieces + index))
            arrived.append(lax.ppermute(piece, ("dp", "seq"), route))
        shape = jax.ShapeDtypeStruct((RANK, self.width), jnp.float32)
        return call(final_kernel, "final", [shape, shape], arrived)


def body(
    head_queries,
    head_keys,
    head_values,
    output_gradient,
    key_adapter_input,
    value_adapter_input,
    key_block_lists,
    live_block_counts,
):
    seq = lax.axis_size("seq")
    teams = seq // TEAM

    def partner(block, k):
        return lax.ppermute(block, "seq", [(i, i ^ k) for i in range(seq)]) if k else block

    near_route = []
    for p in range(seq):
        t = p // TEAM + (1 if p % TEAM >= TEAM // 2 else -1)
        if 0 <= t < teams:
            near_route.append((p, t * TEAM + p % TEAM))
    far_route = [(target, source) for source, target in near_route]
    swaps = []
    for start in (0, 1):
        pairs = []
        for t in range(start, teams - 1, 2):
            for m in range(TEAM):
                pairs += [(t * TEAM + m, (t + 1) * TEAM + m), ((t + 1) * TEAM + m, t * TEAM + m)]
        swaps.append(pairs)

    lists = key_block_lists.transpose(2, 1, 0)
    counts = live_block_counts.T
    adapters = (key_adapter_input.transpose(0, 2, 1), value_adapter_input.transpose(0, 2, 1))
    def spread(packed):
        own, other, across, diagonal = packed
        return [own, partner(other, 1), [partner(x, 2) for x in across], [partner(x, 3) for x in diagonal]]

    kv_out = pack(head_keys, head_values, adapters)
    kv = spread(kv_out)
    qg_out = pack(head_queries, output_gradient, after=kv_out[:1])
    qg = spread(qg_out)
    mask = make_mask(lists, counts, kv_out[0])
    near, far = [], []
    for c, span in enumerate(spans()):
        near.append(lax.ppermute(stack(kv[0], kv[1], f"near_{c}", span, [mask, qg[1]]), "seq", near_route))
        far.append(lax.ppermute(stack(kv[2][c], kv[3][c], f"far_{c}"), "seq", far_route))

    adapt, parts, terms = None, [], []
    for c in range(len(CHUNKS)):
        kv_c, qg_c = ([x[0], x[1], x[2][c], x[3][c]] for x in (kv, qg))
        own, to_a, to_b, term, *more = compute(c, mask, kv_c, qg_c, near[c], far[c], adapt)
        adapt = more[0] if more else adapt
        terms.append(term)
        parts.append((own, lax.ppermute(to_a, "seq", swaps[0]), lax.ppermute(to_b, "seq", swaps[1])))
    reduction = Reduction(terms)
    home, others, after = [], [], []
    for c, part in enumerate(parts):
        last = c + 1 == len(CHUNKS)
        blocks = combine(c, *part, others if last else [], after)
        others.append(blocks[1])
        home.append([blocks[0], partner(blocks[2], 2), partner(blocks[3], 3)])
        after = home[-1][1:]
        for _ in range(2):
            if not last and reduction.index + 1 < len(reduction.rounds):
                reduction.step(blocks[:1])
                after.append(reduction.held)
    while reduction.index + 1 < len(reduction.rounds):
        reduction.step()
    key_term, value_term = reduction.finish()
    key_gradient, value_gradient = unpack(home, partner(others[-1], 1))
    return key_gradient, value_gradient, key_term.T, value_term.T


def solution(mesh):
    tokens = P("dp", "seq", None)
    shares = P(("dp", "seq"), None)
    return jax.shard_map(
        body,
        mesh=mesh,
        in_specs=(tokens,) * 6 + (P(), P()),
        out_specs=(tokens, tokens, shares, shares),
        check_vma=False,
    )
```

time: 117 us -> 94.4 us (0.81)
  waiting for transfers between devices: 60.4 us -> 33.4 us
  starting transfers between devices: 34.2 us -> 39.3 us
  local copies, waits for them, and re-layouts: 3.71 us -> 1.83 us
    ppermute x12 -> x15, waiting for transfers between devices: 45.1 us -> 23.7 us  [partner(): lax.ppermute(block, 'seq', [(i, i ^ k) for i in range(seq)])]
    ppermute x10 -> x12, waiting for transfers between devices: 15.4 us -> 9.78 us  [the longest x2 5.81 us: step(): got = lax.ppermute(self.sent, axis, route)]
    ppermute x10 -> x12, starting transfers between devices: 19.6 us -> 24.9 us  [the longest x2 7.2 us: body(): lax.ppermute(stack(kv[0], kv[1], f'near_{c}', span, [mask, qg[1]]), 'seq'...]
    unnamed x16 -> x20, local copies, waits for them, and re-layouts: 3.71 us -> 1.83 us
    pallas_call x14 -> x16, Pallas kernels: 16.4 us -> 17.2 us  [call(): pl.pallas_call(kernel, out_shape=out_shape, in_specs=in_specs or [VMEM] *...]
    ppermute x12 -> x15, starting transfers between devices: 14.6 us -> 14.4 us  [partner(): lax.ppermute(block, 'seq', [(i, i ^ k) for i in range(seq)])]
  transfers between devices with their start and end apart: 22 -> 27, of which waited for: 12 -> 11; matrix products, arithmetic and copies ran while one was open for 0% -> 0% of each run, Pallas kernels for 7% -> 14%
where the time goes in v2:
time: 94.4 us; the launch traced here: 92.7 us
  starting transfers between devices  39.3 us (42%)
  waiting for transfers between devices  33.4 us (35%)
  Pallas kernels  17.2 us (18%)
  local copies, waits for them, and re-layouts  1.83 us (2%)
  between operations  0.96 us (1%)
    ppermute x15, waiting for transfers between devices, partner(): lax.ppermute(block, 'seq', [(i, i ^ k) for i in range(seq)])  23.7 us
    pallas_call x16, Pallas kernels, call(): pl.pallas_call(kernel, out_shape=out_shape, in_specs=in_specs or [VMEM] *...  17.2 us
    ppermute x15, starting transfers between devices, partner(): lax.ppermute(block, 'seq', [(i, i ^ k) for i in range(seq)])  14.4 us
    ppermute x2, starting transfers between devices, body(): lax.ppermute(stack(kv[0], kv[1], f'near_{c}', span, [mask, qg[1]]), 'seq'...  7.2 us
    ppermute x2, starting transfers between devices, finish(): arrived.append(lax.ppermute(piece, ('dp', 'seq'), route))  6.34 us
    ppermute x2, waiting for transfers between devices, step(): got = lax.ppermute(self.sent, axis, route)  5.81 us
    ppermute x2, starting transfers between devices, step(): got = lax.ppermute(self.sent, axis, route)  3.77 us
    ppermute x2, starting transfers between devices, body(): lax.ppermute(to_a, 'seq', swaps[0])  3.62 us
  transfers between devices with their start and end apart: 27, of which 11 were waited for; matrix products, arithmetic and copies ran while one was open for 0% of the time, Pallas kernels for 14%

profile of v2, /device:TPU:5, one launch (start us, length us, event | category | flops | bytes accessed | tf_op | source)
XLA Modules:
  0.0 92.7 jit_solution(8651934016165846588)
XLA Ops:
  0.7 2.9 %pack_kv.1 = (bf16[128,1664]{1,0:T(8,128)(2,1)}, bf16[128,1664]{1,0:T(8,128)(2,1)}, bf16[128,896]{1,0:T(8,128)(2,1)}, bf16[128,768]{1,0:T(8,128)(2,1)}, bf16[128...) custom-call(bf16[1,128,3072]{2,1,0:T(8,128)(2,1)} %keys.1, bf16[1,128,3072]{2,1,0:T(8,128)(2,1)} %values.1, ...), custom_call_target="tpu_custom_call" | custom-call | flops 1 | bytes 1 | tf_op jit(solution)/shard_map/pack_kv/pallas_call | solution.py:30
  6.3 1.6 %collective-permute-start.2 = (bf16[128,896]{1,0:T(8,128)(2,1)S(1)}, bf16[128,896]{1,0:T(8,128)(2,1)S(1)}, u32[]{:S(2)}, u32[]{:S(2)}) collective-permute-start(bf16[128,896]{1,0:T(8,128)(2,1)S(1)} %copy-done.6), channel_id=1, source_target_pairs={{0,3},{1,2},{2,1},{3,0},{4,7},{5,6},{6,5},{7,4},{8,11},{9,10},{10,... | collective-permute-start | bytes 688136 | tf_op jit(solution)/shard_map/ppermute | solution.py:462
  7.9 1.8 %mask.1.refs_0_.mask_ref = f32[120,128]{1,0:T(8,128)S(1)} custom-call(s32[5,16,24]{2,1,0:T(8,128)S(1)} %bitcast.6, s32[16,24]{1,0:T(8,128)S(1)} %bitcast.7, bf16[128,1664]{1,0:T(8,128)(2,1)S(1)} %copy-done), custom_call_target="tpu_custom_call" | custom-call | flops 1 | bytes 1 | tf_op jit(solution)/shard_map/mask/pallas_call | solution.py:30
  9.7 3.7 %collective-permute-done.1.first_ref.refs_2_ = bf16[128,896]{1,0:T(8,128)(2,1)S(1)} collective-permute-done((bf16[128,896]{1,0:T(8,128)(2,1)S(1)}, bf16[128,896]{1,0:T(8,128)(2,1)S(1)}, u32[]{:S(2)}, u32[]{:S(2)}) %collective-permute-start.1) | collective-permute-done | bytes 229408 | tf_op jit(solution)/shard_map/ppermute | solution.py:462
  13.4 5.5 %collective-permute-done.2.second_ref.refs_3_ = bf16[128,896]{1,0:T(8,128)(2,1)S(1)} collective-permute-done((bf16[128,896]{1,0:T(8,128)(2,1)S(1)}, bf16[128,896]{1,0:T(8,128)(2,1)S(1)}, u32[]{:S(2)}, u32[]{:S(2)}) %collective-permute-start.2) | collective-permute-done | bytes 229408 | tf_op jit(solution)/shard_map/ppermute | solution.py:462
  20.3 4.0 %collective-permute-start.6 = (bf16[256,896]{1,0:T(8,128)(2,1)S(1)}, bf16[256,896]{1,0:T(8,128)(2,1)S(1)}, u32[]{:S(2)}, u32[]{:S(2)}) collective-permute-start(bf16[256,896]{1,0:T(8,128)(2,1)S(1)} %near_0.1), channel_id=1, source_target_pairs={{2,6},{3,7},{4,0},{5,1},{6,10},{7,11},{8,4},{9,5},{10,14},{11,15},... | collective-permute-start | bytes 1376264 | tf_op jit(solution)/shard_map/ppermute | solution.py:492
  24.4 1.8 %collective-permute-start.4 = (bf16[128,768]{1,0:T(8,128)(2,1)S(1)}, bf16[128,768]{1,0:T(8,128)(2,1)S(1)}, u32[]{:S(2)}, u32[]{:S(2)}) collective-permute-start(bf16[128,768]{1,0:T(8,128)(2,1)S(1)} %get-tuple-element.49), channel_id=1, source_target_pairs={{0,2},{1,3},{2,0},{3,1},{4,6},{5,7},{6,4},{7,5},{8,10},{9,11},{10,... | collective-permute-start | bytes 589832 | tf_op jit(solution)/shard_map/ppermute | solution.py:462
  26.6 5.4 %collective-permute-done.13.second_ref.refs_3_ = bf16[128,768]{1,0:T(8,128)(2,1)S(1)} collective-permute-done((bf16[128,768]{1,0:T(8,128)(2,1)S(1)}, bf16[128,768]{1,0:T(8,128)(2,1)S(1)}, u32[]{:S(2)}, u32[]{:S(2)}) %collective-permute-start.13) | collective-permute-done | bytes 196640 | tf_op jit(solution)/shard_map/ppermute | solution.py:462
  32.0 3.6 %collective-permute-done.4.refs_6_ = bf16[128,768]{1,0:T(8,128)(2,1)S(1)} collective-permute-done((bf16[128,768]{1,0:T(8,128)(2,1)S(1)}, bf16[128,768]{1,0:T(8,128)(2,1)S(1)}, u32[]{:S(2)}, u32[]{:S(2)}) %collective-permute-start.4) | collective-permute-done | bytes 196640 | tf_op jit(solution)/shard_map/ppermute | solution.py:462
  36.9 3.2 %collective-permute-done.5.refs_7_ = bf16[128,768]{1,0:T(8,128)(2,1)S(1)} collective-permute-done((bf16[128,768]{1,0:T(8,128)(2,1)S(1)}, bf16[128,768]{1,0:T(8,128)(2,1)S(1)}, u32[]{:S(2)}, u32[]{:S(2)}) %collective-permute-start.5) | collective-permute-done | bytes 196640 | tf_op jit(solution)/shard_map/ppermute | solution.py:462
  40.0 3.2 %collective-permute-start.16 = (bf16[256,768]{1,0:T(8,128)(2,1)S(1)}, bf16[256,768]{1,0:T(8,128)(2,1)S(1)}, u32[]{:S(2)}, u32[]{:S(2)}) collective-permute-start(bf16[256,768]{1,0:T(8,128)(2,1)S(1)} %near_1.1), channel_id=1, source_target_pairs={{2,6},{3,7},{4,0},{5,1},{6,10},{7,11},{8,4},{9,5},{10,14},{11,15},... | collective-permute-start | bytes 1179656 | tf_op jit(solution)/shard_map/ppermute | solution.py:492
  43.3 4.8 %gradients_0.1 = (f32[512,768]{1,0:T(8,128)S(1)}, bf16[256,768]{1,0:T(8,128)(2,1)S(1)}, bf16[256,768]{1,0:T(8,128)(2,1)S(1)}, f32[128,384]{1,0:T(8,128)S(1)}, bf16[128,1024]{1,0:T(8,128)(2,1)S(1)}) custom-call(f32[120,128]{1,0:T(8,128)S(1)} %mask.1.refs_0_.mask_ref, bf16[128,1664]{1,0:T(8,128)(2,1)S(1)} %copy-done.1, ...), custom_call_target="tpu_custom_call" | custom-call | flops 1 | bytes 1 | tf_op jit(solution)/shard_map/gradients_0/pallas_call | solution.py:30
  48.1 1.4 %collective-permute-start.8 = (bf16[256,768]{1,0:T(8,128)(2,1)S(1)}, bf16[256,768]{1,0:T(8,128)(2,1)S(1)}, u32[]{:S(2)}, u32[]{:S(2)}) collective-permute-start(bf16[256,768]{1,0:T(8,128)(2,1)S(1)} %get-tuple-element.52), channel_id=1, source_target_pairs={{0,4},{4,0},{1,5},{5,1},{2,6},{6,2},{3,7},{7,3},{8,12},{12,8},{9,1... | collective-permute-start | bytes 1179656 | tf_op jit(solution)/shard_map/ppermute | solution.py:501
  51.6 4.7 %gradients_1.1 = (f32[512,768]{1,0:T(8,128)S(1)}, bf16[256,768]{1,0:T(8,128)(2,1)S(1)}, bf16[256,768]{1,0:T(8,128)(2,1)S(1)}, f32[128,384]{1,0:T(8,128)S(1)}) custom-call(f32[120,128]{1,0:T(8,128)S(1)} %mask.1.refs_0_.mask_ref, bf16[128,1664]{1,0:T(8,128)(2,1)S(1)} %copy-done.1, bf16[128,1664]{1,0:T(8,128)(2,1)S(1)} %collective-permute-done.second_ref.refs_1_, ...), custom_call_target="tpu_custom_call" | custom-call | flops 1 | bytes 1 | tf_op jit(solution)/shard_map/gradients_1/pallas_call | solution.py:30
  56.3 2.3 %collective-permute-start.18 = (bf16[256,768]{1,0:T(8,128)(2,1)S(1)}, bf16[256,768]{1,0:T(8,128)(2,1)S(1)}, u32[]{:S(2)}, u32[]{:S(2)}) collective-permute-start(bf16[256,768]{1,0:T(8,128)(2,1)S(1)} %get-tuple-element.63), channel_id=1, source_target_pairs={{0,4},{4,0},{1,5},{5,1},{2,6},{6,2},{3,7},{7,3},{8,12},{12,8},{9,1... | collective-permute-start | bytes 1179656 | tf_op jit(solution)/shard_map/ppermute | solution.py:501
  61.4 3.1 %collective-permute-start.11 = (bf16[128,768]{1,0:T(8,128)(2,1)S(1)}, bf16[128,768]{1,0:T(8,128)(2,1)S(1)}, u32[]{:S(2)}, u32[]{:S(2)}) collective-permute-start(bf16[128,768]{1,0:T(8,128)(2,1)S(1)} %get-tuple-element.56), channel_id=1, source_target_pairs={{0,3},{1,2},{2,1},{3,0},{4,7},{5,6},{6,5},{7,4},{8,11},{9,10},{10,... | collective-permute-start | bytes 589832 | tf_op jit(solution)/shard_map/ppermute | solution.py:462
  64.9 2.5 %collective-permute-start.21 = (f32[2,128,96]{2,1,0:T(8,128)S(1)}, f32[2,128,96]{2,1,0:T(8,128)S(1)}, u32[]{:S(2)}, u32[]{:S(2)}) collective-permute-start(f32[2,128,96]{2,1,0:T(8,128)S(1)} %get-tuple-element.71), channel_id=1, source_target_pairs={{0,8},{1,9},{2,10},{3,11},{4,12},{5,13},{6,14},{7,15},{8,0},{9,1},... | collective-permute-start | bytes 294920 | tf_op jit(solution)/shard_map/ppermute | solution.py:426
  67.4 5.8 %collective-permute-done.21.got_ref = f32[2,128,96]{2,1,0:T(8,128)S(1)} collective-permute-done((f32[2,128,96]{2,1,0:T(8,128)S(1)}, f32[2,128,96]{2,1,0:T(8,128)S(1)}, u32[]{:S(2)}, u32[]{:S(2)}) %collective-permute-start.21) | collective-permute-done | bytes 98336 | tf_op jit(solution)/shard_map/ppermute | solution.py:426
  73.5 4.2 %collective-permute-start.24 = (bf16[128,1536]{1,0:T(8,128)(2,1)S(1)}, bf16[128,1536]{1,0:T(8,128)(2,1)S(1)}, u32[]{:S(2)}, u32[]{:S(2)}) collective-permute-start(bf16[128,1536]{1,0:T(8,128)(2,1)S(1)} %get-tuple-element.76), channel_id=1, source_target_pairs={{0,1},{1,0},{2,3},{3,2},{4,5},{5,4},{6,7},{7,6},{8,9},{9,8},{10,11... | collective-permute-start | bytes 1179656 | tf_op jit(solution)/shard_map/ppermute | solution.py:462
  77.7 1.3 %collective-permute-start.22 = (bf16[128,768]{1,0:T(8,128)(2,1)S(1)}, bf16[128,768]{1,0:T(8,128)(2,1)S(1)}, u32[]{:S(2)}, u32[]{:S(2)}) collective-permute-start(bf16[128,768]{1,0:T(8,128)(2,1)S(1)} %get-tuple-element.74), channel_id=1, source_target_pairs={{0,2},{1,3},{2,0},{3,1},{4,6},{5,7},{6,4},{7,5},{8,10},{9,11},{10,... | collective-permute-start | bytes 589832 | tf_op jit(solution)/shard_map/ppermute | solution.py:462
  79.4 3.1 %collective-permute-start.25 = (f32[1,128,96]{2,1,0:T(8,128)S(1)}, f32[1,128,96]{2,1,0:T(8,128)S(1)}, u32[]{:S(2)}, u32[]{:S(2)}) collective-permute-start(f32[1,128,96]{2,1,0:T(8,128)S(1)} %get-tuple-element.72.refs_4_), channel_id=1, source_target_pairs={{0,0},{1,8},{2,16},{3,24},{4,1},{5,9},{6,17},{7,25},{8,2},{9,10},{... | collective-permute-start | bytes 147464 | tf_op jit(solution)/shard_map/ppermute | solution.py:443
  82.6 3.2 %collective-permute-start.26 = (f32[1,128,96]{2,1,0:T(8,128)S(1)}, f32[1,128,96]{2,1,0:T(8,128)S(1)}, u32[]{:S(2)}, u32[]{:S(2)}) collective-permute-start(f32[1,128,96]{2,1,0:T(8,128)S(1)} %get-tuple-element.79), channel_id=1, source_target_pairs={{0,1},{1,9},{2,17},{3,25},{4,0},{5,8},{6,16},{7,24},{8,3},{9,11},{... | collective-permute-start | bytes 147464 | tf_op jit(solution)/shard_map/ppermute | solution.py:443
  85.8 2.0 %collective-permute-done.25.first_ref = f32[1,128,96]{2,1,0:T(8,128)S(1)} collective-permute-done((f32[1,128,96]{2,1,0:T(8,128)S(1)}, f32[1,128,96]{2,1,0:T(8,128)S(1)}, u32[]{:S(2)}, u32[]{:S(2)}) %collective-permute-start.25) | collective-permute-done | bytes 49184 | tf_op jit(solution)/shard_map/ppermute | solution.py:443
  89.1 2.2 %collective-permute-done.23.refs_5_ = bf16[128,768]{1,0:T(8,128)(2,1)S(1)} collective-permute-done((bf16[128,768]{1,0:T(8,128)(2,1)S(1)}, bf16[128,768]{1,0:T(8,128)(2,1)S(1)}, u32[]{:S(2)}, u32[]{:S(2)}) %collective-permute-start.23) | collective-permute-done | bytes 196640 | tf_op jit(solution)/shard_map/ppermute | solution.py:462
  (66 shorter events, 14.5 us)
Async XLA Ops:
  3.5 16.7 %collective-permute-start = (bf16[128,1664]{1,0:T(8,128)(2,1)}, bf16[128,1664]{1,0:T(8,128)(2,1)S(1)}, u32[]{:S(2)}, u32[]{:S(2)}) collective-permute-start(bf16[128,1664]{1,0:T(8,128)(2,1)} %get-tuple-element.44), channel_id=1, source_target_pairs={{0,1},{1,0},{2,3},{3,2},{4,5},{5,4},{6,7},{7,6},{8,9},{9,8},{10,11... | collective-permute-start | bytes 1277960 | tf_op jit(solution)/shard_map/ppermute | solution.py:462
  5.5 14.8 %collective-permute-start.3 = (bf16[128,1536]{1,0:T(8,128)(2,1)S(1)}, bf16[128,1536]{1,0:T(8,128)(2,1)S(1)}, u32[]{:S(2)}, u32[]{:S(2)}) collective-permute-start(bf16[128,1536]{1,0:T(8,128)(2,1)S(1)} %get-tuple-element.48), channel_id=1, source_target_pairs={{0,1},{1,0},{2,3},{3,2},{4,5},{5,4},{6,7},{7,6},{8,9},{9,8},{10,11... | collective-permute-start | bytes 1179656 | tf_op jit(solution)/shard_map/ppermute | solution.py:462
  6.2 7.2 %collective-permute-start.1 = (bf16[128,896]{1,0:T(8,128)(2,1)S(1)}, bf16[128,896]{1,0:T(8,128)(2,1)S(1)}, u32[]{:S(2)}, u32[]{:S(2)}) collective-permute-start(bf16[128,896]{1,0:T(8,128)(2,1)S(1)} %copy-done.7), channel_id=1, source_target_pairs={{0,2},{1,3},{2,0},{3,1},{4,6},{5,7},{6,4},{7,5},{8,10},{9,11},{10,... | collective-permute-start | bytes 688136 | tf_op jit(solution)/shard_map/ppermute | solution.py:462
  6.3 12.6 %collective-permute-start.2 = (bf16[128,896]{1,0:T(8,128)(2,1)S(1)}, bf16[128,896]{1,0:T(8,128)(2,1)S(1)}, u32[]{:S(2)}, u32[]{:S(2)}) collective-permute-start(bf16[128,896]{1,0:T(8,128)(2,1)S(1)} %copy-done.6), channel_id=1, source_target_pairs={{0,3},{1,2},{2,1},{3,0},{4,7},{5,6},{6,5},{7,4},{8,11},{9,10},{10,... | collective-permute-start | bytes 688136 | tf_op jit(solution)/shard_map/ppermute | solution.py:462
  7.9 18.3 %collective-permute-start.12 = (bf16[128,768]{1,0:T(8,128)(2,1)S(1)}, bf16[128,768]{1,0:T(8,128)(2,1)S(1)}, u32[]{:S(2)}, u32[]{:S(2)}) collective-permute-start(bf16[128,768]{1,0:T(8,128)(2,1)S(1)} %copy-done.9), channel_id=1, source_target_pairs={{0,2},{1,3},{2,0},{3,1},{4,6},{5,7},{6,4},{7,5},{8,10},{9,11},{10,... | collective-permute-start | bytes 589832 | tf_op jit(solution)/shard_map/ppermute | solution.py:462
  18.9 24.3 %collective-permute-start.7 = (bf16[256,896]{1,0:T(8,128)(2,1)S(1)}, bf16[256,896]{1,0:T(8,128)(2,1)S(1)}, u32[]{:S(2)}, u32[]{:S(2)}) collective-permute-start(bf16[256,896]{1,0:T(8,128)(2,1)S(1)} %far_0.1), channel_id=1, source_target_pairs={{6,2},{7,3},{0,4},{1,5},{10,6},{11,7},{4,8},{5,9},{14,10},{15,11},... | collective-permute-start | bytes 1376264 | tf_op jit(solution)/shard_map/ppermute | solution.py:493
  20.3 23.0 %collective-permute-start.6 = (bf16[256,896]{1,0:T(8,128)(2,1)S(1)}, bf16[256,896]{1,0:T(8,128)(2,1)S(1)}, u32[]{:S(2)}, u32[]{:S(2)}) collective-permute-start(bf16[256,896]{1,0:T(8,128)(2,1)S(1)} %near_0.1), channel_id=1, source_target_pairs={{2,6},{3,7},{4,0},{5,1},{6,10},{7,11},{8,4},{9,5},{10,14},{11,15},... | collective-permute-start | bytes 1376264 | tf_op jit(solution)/shard_map/ppermute | solution.py:492
  24.3 7.6 %collective-permute-start.13 = (bf16[128,768]{1,0:T(8,128)(2,1)S(1)}, bf16[128,768]{1,0:T(8,128)(2,1)S(1)}, u32[]{:S(2)}, u32[]{:S(2)}) collective-permute-start(bf16[128,768]{1,0:T(8,128)(2,1)S(1)} %copy-done.8), channel_id=1, source_target_pairs={{0,3},{1,2},{2,1},{3,0},{4,7},{5,6},{6,5},{7,4},{8,11},{9,10},{10,... | collective-permute-start | bytes 589832 | tf_op jit(solution)/shard_map/ppermute | solution.py:462
  24.4 11.2 %collective-permute-start.4 = (bf16[128,768]{1,0:T(8,128)(2,1)S(1)}, bf16[128,768]{1,0:T(8,128)(2,1)S(1)}, u32[]{:S(2)}, u32[]{:S(2)}) collective-permute-start(bf16[128,768]{1,0:T(8,128)(2,1)S(1)} %get-tuple-element.49), channel_id=1, source_target_pairs={{0,2},{1,3},{2,0},{3,1},{4,6},{5,7},{6,4},{7,5},{8,10},{9,11},{10,... | collective-permute-start | bytes 589832 | tf_op jit(solution)/shard_map/ppermute | solution.py:462
  26.2 13.8 %collective-permute-start.5 = (bf16[128,768]{1,0:T(8,128)(2,1)S(1)}, bf16[128,768]{1,0:T(8,128)(2,1)S(1)}, u32[]{:S(2)}, u32[]{:S(2)}) collective-permute-start(bf16[128,768]{1,0:T(8,128)(2,1)S(1)} %get-tuple-element.50), channel_id=1, source_target_pairs={{0,3},{1,2},{2,1},{3,0},{4,7},{5,6},{6,5},{7,4},{8,11},{9,10},{10,... | collective-permute-start | bytes 589832 | tf_op jit(solution)/shard_map/ppermute | solution.py:462
  31.9 17.6 %collective-permute-start.14 = (bf16[128,768]{1,0:T(8,128)(2,1)S(1)}, bf16[128,768]{1,0:T(8,128)(2,1)S(1)}, u32[]{:S(2)}, u32[]{:S(2)}) collective-permute-start(bf16[128,768]{1,0:T(8,128)(2,1)S(1)} %get-tuple-element.59), channel_id=1, source_target_pairs={{0,2},{1,3},{2,0},{3,1},{4,6},{5,7},{6,4},{7,5},{8,10},{9,11},{10,... | collective-permute-start | bytes 589832 | tf_op jit(solution)/shard_map/ppermute | solution.py:462
  35.6 14.7 %collective-permute-start.17 = (bf16[256,768]{1,0:T(8,128)(2,1)S(1)}, bf16[256,768]{1,0:T(8,128)(2,1)S(1)}, u32[]{:S(2)}, u32[]{:S(2)}) collective-permute-start(bf16[256,768]{1,0:T(8,128)(2,1)S(1)} %far_1.1), channel_id=1, source_target_pairs={{6,2},{7,3},{0,4},{1,5},{10,6},{11,7},{4,8},{5,9},{14,10},{15,11},... | collective-permute-start | bytes 1179656 | tf_op jit(solution)/shard_map/ppermute | solution.py:493
  40.0 11.5 %collective-permute-start.16 = (bf16[256,768]{1,0:T(8,128)(2,1)S(1)}, bf16[256,768]{1,0:T(8,128)(2,1)S(1)}, u32[]{:S(2)}, u32[]{:S(2)}) collective-permute-start(bf16[256,768]{1,0:T(8,128)(2,1)S(1)} %near_1.1), channel_id=1, source_target_pairs={{2,6},{3,7},{4,0},{5,1},{6,10},{7,11},{8,4},{9,5},{10,14},{11,15},... | collective-permute-start | bytes 1179656 | tf_op jit(solution)/shard_map/ppermute | solution.py:492
  48.1 12.4 %collective-permute-start.8 = (bf16[256,768]{1,0:T(8,128)(2,1)S(1)}, bf16[256,768]{1,0:T(8,128)(2,1)S(1)}, u32[]{:S(2)}, u32[]{:S(2)}) collective-permute-start(bf16[256,768]{1,0:T(8,128)(2,1)S(1)} %get-tuple-element.52), channel_id=1, source_target_pairs={{0,4},{4,0},{1,5},{5,1},{2,6},{6,2},{3,7},{7,3},{8,12},{12,8},{9,1... | collective-permute-start | bytes 1179656 | tf_op jit(solution)/shard_map/ppermute | solution.py:501
  49.5 11.1 %collective-permute-start.9 = (bf16[256,768]{1,0:T(8,128)(2,1)S(1)}, bf16[256,768]{1,0:T(8,128)(2,1)S(1)}, u32[]{:S(2)}, u32[]{:S(2)}) collective-permute-start(bf16[256,768]{1,0:T(8,128)(2,1)S(1)} %get-tuple-element.53), channel_id=1, source_target_pairs={{4,8},{8,4},{5,9},{9,5},{6,10},{10,6},{7,11},{11,7},{20,24},{24,20... | collective-permute-start | bytes 1179656 | tf_op jit(solution)/shard_map/ppermute | solution.py:501
  56.3 16.9 %collective-permute-start.18 = (bf16[256,768]{1,0:T(8,128)(2,1)S(1)}, bf16[256,768]{1,0:T(8,128)(2,1)S(1)}, u32[]{:S(2)}, u32[]{:S(2)}) collective-permute-start(bf16[256,768]{1,0:T(8,128)(2,1)S(1)} %get-tuple-element.63), channel_id=1, source_target_pairs={{0,4},{4,0},{1,5},{5,1},{2,6},{6,2},{3,7},{7,3},{8,12},{12,8},{9,1... | collective-permute-start | bytes 1179656 | tf_op jit(solution)/shard_map/ppermute | solution.py:501
  58.6 14.6 %collective-permute-start.19 = (bf16[256,768]{1,0:T(8,128)(2,1)S(1)}, bf16[256,768]{1,0:T(8,128)(2,1)S(1)}, u32[]{:S(2)}, u32[]{:S(2)}) collective-permute-start(bf16[256,768]{1,0:T(8,128)(2,1)S(1)} %get-tuple-element.64), channel_id=1, source_target_pairs={{4,8},{8,4},{5,9},{9,5},{6,10},{10,6},{7,11},{11,7},{20,24},{24,20... | collective-permute-start | bytes 1179656 | tf_op jit(solution)/shard_map/ppermute | solution.py:501
  60.8 12.4 %collective-permute-start.10 = (bf16[128,768]{1,0:T(8,128)(2,1)S(1)}, bf16[128,768]{1,0:T(8,128)(2,1)S(1)}, u32[]{:S(2)}, u32[]{:S(2)}) collective-permute-start(bf16[128,768]{1,0:T(8,128)(2,1)S(1)} %get-tuple-element.55), channel_id=1, source_target_pairs={{0,2},{1,3},{2,0},{3,1},{4,6},{5,7},{6,4},{7,5},{8,10},{9,11},{10,... | collective-permute-start | bytes 589832 | tf_op jit(solution)/shard_map/ppermute | solution.py:462
  61.4 11.8 %collective-permute-start.11 = (bf16[128,768]{1,0:T(8,128)(2,1)S(1)}, bf16[128,768]{1,0:T(8,128)(2,1)S(1)}, u32[]{:S(2)}, u32[]{:S(2)}) collective-permute-start(bf16[128,768]{1,0:T(8,128)(2,1)S(1)} %get-tuple-element.56), channel_id=1, source_target_pairs={{0,3},{1,2},{2,1},{3,0},{4,7},{5,6},{6,5},{7,4},{8,11},{9,10},{10,... | collective-permute-start | bytes 589832 | tf_op jit(solution)/shard_map/ppermute | solution.py:462
  64.9 8.3 %collective-permute-start.21 = (f32[2,128,96]{2,1,0:T(8,128)S(1)}, f32[2,128,96]{2,1,0:T(8,128)S(1)}, u32[]{:S(2)}, u32[]{:S(2)}) collective-permute-start(f32[2,128,96]{2,1,0:T(8,128)S(1)} %get-tuple-element.71), channel_id=1, source_target_pairs={{0,8},{1,9},{2,10},{3,11},{4,12},{5,13},{6,14},{7,15},{8,0},{9,1},... | collective-permute-start | bytes 294920 | tf_op jit(solution)/shard_map/ppermute | solution.py:426
  73.5 17.9 %collective-permute-start.24 = (bf16[128,1536]{1,0:T(8,128)(2,1)S(1)}, bf16[128,1536]{1,0:T(8,128)(2,1)S(1)}, u32[]{:S(2)}, u32[]{:S(2)}) collective-permute-start(bf16[128,1536]{1,0:T(8,128)(2,1)S(1)} %get-tuple-element.76), channel_id=1, source_target_pairs={{0,1},{1,0},{2,3},{3,2},{4,5},{5,4},{6,7},{7,6},{8,9},{9,8},{10,11... | collective-permute-start | bytes 1179656 | tf_op jit(solution)/shard_map/ppermute | solution.py:462
  77.7 11.4 %collective-permute-start.22 = (bf16[128,768]{1,0:T(8,128)(2,1)S(1)}, bf16[128,768]{1,0:T(8,128)(2,1)S(1)}, u32[]{:S(2)}, u32[]{:S(2)}) collective-permute-start(bf16[128,768]{1,0:T(8,128)(2,1)S(1)} %get-tuple-element.74), channel_id=1, source_target_pairs={{0,2},{1,3},{2,0},{3,1},{4,6},{5,7},{6,4},{7,5},{8,10},{9,11},{10,... | collective-permute-start | bytes 589832 | tf_op jit(solution)/shard_map/ppermute | solution.py:462
  79.0 12.4 %collective-permute-start.23 = (bf16[128,768]{1,0:T(8,128)(2,1)S(1)}, bf16[128,768]{1,0:T(8,128)(2,1)S(1)}, u32[]{:S(2)}, u32[]{:S(2)}) collective-permute-start(bf16[128,768]{1,0:T(8,128)(2,1)S(1)} %get-tuple-element.75), channel_id=1, source_target_pairs={{0,3},{1,2},{2,1},{3,0},{4,7},{5,6},{6,5},{7,4},{8,11},{9,10},{10,... | collective-permute-start | bytes 589832 | tf_op jit(solution)/shard_map/ppermute | solution.py:462
  79.4 8.4 %collective-permute-start.25 = (f32[1,128,96]{2,1,0:T(8,128)S(1)}, f32[1,128,96]{2,1,0:T(8,128)S(1)}, u32[]{:S(2)}, u32[]{:S(2)}) collective-permute-start(f32[1,128,96]{2,1,0:T(8,128)S(1)} %get-tuple-element.72.refs_4_), channel_id=1, source_target_pairs={{0,0},{1,8},{2,16},{3,24},{4,1},{5,9},{6,17},{7,25},{8,2},{9,10},{... | collective-permute-start | bytes 147464 | tf_op jit(solution)/shard_map/ppermute | solution.py:443
  (13 other events, 72.4 us)

commit v3 on v2

--- a/solution.py
+++ b/solution.py
@@ -21,9 +21,10 @@
 SCALING = HEAD_WIDTH**-0.5
 LOG2E = 1.4426950408889634
 ANY = pl.BlockSpec(memory_space=pl.ANY)
-PACK_VMEM = 62
+PACK_VMEM = 56
 VMEM = pl.BlockSpec(memory_space=pltpu.VMEM)
 SMEM = pl.BlockSpec(memory_space=pltpu.SMEM)
+MARK = jax.ShapeDtypeStruct((8, HEAD_WIDTH), jnp.float32)
 
 
 def call(kernel, name, out_shape, inputs, in_specs=None, scratch=(), vmem=4):
@@ -64,34 +65,33 @@
     return [(sum(CHUNKS[:c]), count) for c, count in enumerate(CHUNKS)]
 
 
-class Tiles:
-    def __init__(self, ref, span=(0, HEADS), row=0):
-        self.ref, (self.first, self.count), self.row = ref, span, row
-
-    def tile(self, head, part):
-        place = 2 * self.count if part == 2 else part * self.count + head - self.first
-        return self.ref[rows(self.row, 1), cols(place, 1)]
-
-
-def pack_spans(adapters):
-    plan = []
-    for k in range(TEAM):
-        for span in [(0, HEADS)] if k < 2 else spans():
-            plan.append((k, span, bool(adapters) and span[0] == 0))
-    return plan
-
-
-def fill(plan, a_ref, b_ref, adapter_refs, outs, part):
+SIDE, OWN, ACROSS = (1, 3), (0,), (2,)
+
+
+def pack_plan(kinds, adapters):
+    return [(span, owners, bool(adapters) and span[0] == 0) for span in spans() for owners in kinds]
+
+
+def fill(plan, a_ref, b_ref, outs, part):
     member, _ = place()
-    for (k, (first, count), adapted), out in zip(plan, outs):
-        head = jnp.bitwise_xor(member, k) * HEADS + first
-        out[part, cols(0, count)] = a_ref[part, cols(head, count)]
-        out[part, cols(count, count)] = b_ref[part, cols(head, count)]
-    return adapter_refs
-
-
-def pack_kv_kernel(plan, keys, values, key_in, value_in, *refs):
-    outs, (tall, small, sems) = refs[:-3], refs[-3:]
+    for ((first, count), owners, _), out in zip(plan, outs):
+        for index, k in enumerate(owners):
+            head = jnp.bitwise_xor(member, k) * HEADS + first
+            out[part, cols(2 * index * count, count)] = a_ref[part, cols(head, count)]
+            out[part, cols((2 * index + 1) * count, count)] = b_ref[part, cols(head, count)]
+
+
+def fill_adapters(plan, key_tile, value_tile, outs):
+    for (_, _, adapted), out in zip(plan, outs):
+        if adapted:
+            column = cols(out.shape[1] // HEAD_WIDTH - 1, 1)
+            out[:RANK, column] = key_tile
+            out[RANK:, column] = value_tile
+
+
+def pack_first_kernel(plan, keys, values, key_in, value_in, *refs):
+    outs, (mark, tall, small, sems) = refs[:-4], refs[-4:]
+    mark[...] = jnp.zeros_like(mark)
     size = BLK // LOADS
     copies = []
     for part in range(LOADS):
@@ -105,59 +105,60 @@
     for part in range(LOADS):
         for copy in copies[2 * part : 2 * part + 2]:
             copy.wait()
-        fill(plan, tall.at[0], tall.at[1], None, outs, pl.ds(part * size, size))
+        fill(plan, tall.at[0], tall.at[1], outs, pl.ds(part * size, size))
     for copy in copies[2 * LOADS :]:
         copy.wait()
-    for (k, (_, count), adapted), out in zip(plan, outs):
-        if adapted:
-            out[:RANK, cols(2 * count, 1)] = small[0]
-            out[RANK:, cols(2 * count, 1)] = small[1]
-
-
-def pack_qg_kernel(plan, queries, grads, _, *outs):
-    fill(plan, queries.at[0], grads.at[0], None, outs, slice(None))
-
-
-def pack(first, second, adapters=(), after=()):
-    plan = pack_spans(adapters)
+    fill_adapters(plan, small[0], small[1], outs)
+
+
+def pack_kernel(plan, adapters, a_ref, b_ref, *refs):
+    outs = refs[-len(plan) :]
+    fill(plan, a_ref.at[0], b_ref.at[0], outs, slice(None))
+    if adapters:
+        fill_adapters(plan, refs[0][0], refs[1][0], outs)
+
+
+def pack(name, kinds, first, second, adapters=(), after=(), at_once=False):
+    plan = pack_plan(kinds, adapters)
     kind = first.dtype
     out_shape = [
-        jax.ShapeDtypeStruct((BLK, (2 * count + adapted) * HEAD_WIDTH), kind) for _, (_, count), adapted in plan
+        jax.ShapeDtypeStruct((BLK, (2 * count * len(owners) + adapted) * HEAD_WIDTH), kind)
+        for (_, count), owners, adapted in plan
     ]
-    if adapters:
+    inputs = [first, second, *adapters, *after]
+    if at_once:
         scratch = [
             pltpu.VMEM((2, BLK, HEAD_COUNT * HEAD_WIDTH), kind),
             pltpu.VMEM((2, RANK, BLK), kind),
             pltpu.SemaphoreType.DMA((2 * LOADS + 2,)),
         ]
-        kernel = functools.partial(pack_kv_kernel, plan)
-        outs = call(kernel, "pack_kv", out_shape, [first, second, *adapters], [ANY] * 4, scratch, PACK_VMEM)
+        kernel = functools.partial(pack_first_kernel, plan)
+        out_shape.append(MARK)
+        outs = call(kernel, name, out_shape, inputs, [ANY] * 4, scratch, PACK_VMEM)
     else:
-        kernel = functools.partial(pack_qg_kernel, plan)
-        outs = call(kernel, "pack_qg", out_shape, [first, second, *after], [VMEM, VMEM, ANY])
-    chunks = len(CHUNKS)
-    return [outs[0], outs[1], outs[2 : 2 + chunks], outs[2 + chunks :]]
-
-
-def stack_kernel(span, first_ref, second_ref, *refs):
-    out = refs[-1]
-    for row, ref in enumerate((first_ref, second_ref)):
-        if span is None:
-            out[rows(row, 1), :] = ref[...]
-            continue
-        first, count = span
-        out[rows(row, 1), cols(0, count)] = ref[:, cols(first, count)]
-        out[rows(row, 1), cols(count, count)] = ref[:, cols(HEADS + first, count)]
-        if first == 0:
-            out[rows(row, 1), cols(2 * count, 1)] = ref[:, cols(2 * HEADS, 1)]
-
-
-def stack(first, second, name, span=None, after=()):
-    width = (2 * span[1] + (span[0] == 0)) * HEAD_WIDTH if span else first.shape[1]
-    shape = jax.ShapeDtypeStruct((2 * BLK, width), first.dtype)
-    specs = [VMEM] * 2 + [ANY] * len(after)
-    kernel = functools.partial(stack_kernel, span)
-    return call(kernel, name, [shape], [first, second, *after], specs)[0]
+        kernel = functools.partial(pack_kernel, plan, bool(adapters))
+        specs = [VMEM] * (2 + len(adapters)) + [ANY] * len(after)
+        outs = call(kernel, name, out_shape, inputs, specs)
+    return [outs[len(kinds) * c : len(kinds) * (c + 1)] for c in range(len(CHUNKS))], outs[-1]
+
+
+def route_kernel(mine_ref, across_ref, got_ref, *refs):
+    chip_ref, send_ref = refs[-2:]
+    half, extra = 2 * HEAD_WIDTH, mine_ref.shape[1] % (2 * HEAD_WIDTH)
+    half = mine_ref.shape[1] - extra
+    chip_ref[rows(0, 1), :] = mine_ref[...]
+    chip_ref[rows(1, 1), :half] = got_ref[:, :half]
+    send_ref[rows(0, 1), :] = across_ref[...]
+    send_ref[rows(1, 1), :half] = got_ref[:, half : 2 * half]
+    if extra:
+        for out in (chip_ref, send_ref):
+            out[rows(1, 1), half:] = got_ref[:, 2 * half :]
+
+
+def route(name, mine, across, got, after=()):
+    shape = jax.ShapeDtypeStruct((2 * BLK, mine.shape[1]), mine.dtype)
+    specs = [VMEM] * 3 + [ANY] * len(after)
+    return call(route_kernel, name, [shape, shape], [mine, across, got, *after], specs)
 
 
 def mask_kernel(lists_ref, counts_ref, _, mask_ref):
@@ -184,27 +185,26 @@
 
 def compute_kernel(c, mask_ref, *refs):
     first, count = spans()[c]
-    kv_refs, qg_refs, (near_ref, far_ref) = refs[:TEAM], refs[TEAM : 2 * TEAM], refs[2 * TEAM : 2 * TEAM + 2]
+    kv, halo, qg = refs[:2], refs[2:4], refs[4:6]
     if c == 0:
-        own_ref, a_ref, b_ref, term_ref, adapt, kw, vw, qs, gs, pm, dm = refs[2 * TEAM + 2 :]
+        own_ref, a_ref, b_ref, term_ref, adapt, kw, vw, qs, gs, pm, dm = refs[6:]
     else:
-        adapt, own_ref, a_ref, b_ref, term_ref, kw, vw, qs, gs, pm, dm = refs[2 * TEAM + 2 :]
+        adapt, own_ref, a_ref, b_ref, term_ref, kw, vw, qs, gs, pm, dm = refs[6:]
     kind = adapt.dtype
     member, team = place()
     even = lax.rem(team, 2) == 0
-    kv, qg, halo, places = [], [], [], []
+    places = []
     for j in range(TEAM):
-        span = (0, HEADS) if j < 2 else (first, count)
-        kv.append(Tiles(kv_refs[j], span))
-        qg.append(Tiles(qg_refs[j], span))
-        halo.append(Tiles(near_ref if j < 2 else far_ref, (first, count), j % 2))
         owner = jnp.bitwise_xor(member, j)
         places.append((owner, owner + REACH, lax.rem(owner + REACH + TEAM, WINDOW)))
 
+    def tile(refs, j, h, part):
+        return refs[j // 2][rows(j % 2, 1), cols(part * count + h, 1)]
+
     if c == 0:
         for j, (_, near, far) in enumerate(places):
-            adapt[:, rows(near, 1)] = kv[j].tile(0, 2)
-            adapt[:, rows(far, 1)] = halo[j].tile(0, 2)
+            adapt[:, rows(near, 1)] = tile(kv, j, 0, 2)
+            adapt[:, rows(far, 1)] = tile(halo, j, 0, 2)
 
     zero = jnp.zeros((BLK, BLK), kind)
     for index in range(count * 2):
@@ -218,14 +218,13 @@
         return lax.dot_general(left, right, dims, preferred_element_type=jnp.float32)
 
     def load(h):
-        head = first + h
         for j, (owner, near, far) in enumerate(places):
-            kw[h, rows(near, 1), :] = kv[j].tile(head, 0)
-            vw[h, rows(near, 1), :] = kv[j].tile(head, 1)
-            kw[h, rows(far, 1), :] = halo[j].tile(head, 0)
-            vw[h, rows(far, 1), :] = halo[j].tile(head, 1)
-            qs[h, rows(owner, 1), :] = qg[j].tile(head, 0)
-            gs[h, rows(owner, 1), :] = qg[j].tile(head, 1)
+            kw[h, rows(near, 1), :] = tile(kv, j, h, 0)
+            vw[h, rows(near, 1), :] = tile(kv, j, h, 1)
+            kw[h, rows(far, 1), :] = tile(halo, j, h, 0)
+            vw[h, rows(far, 1), :] = tile(halo, j, h, 1)
+            qs[h, rows(owner, 1), :] = tile(qg, j, h, 0)
+            gs[h, rows(owner, 1), :] = tile(qg, j, h, 1)
 
     def scored(h, pair):
         span, two = rows(2 * pair, TILES + 1), rows(2 * pair, 2)
@@ -287,9 +286,9 @@
             adds = []
 
 
-def compute(c, mask, kv, qg, near, far, adapt):
+def compute(c, mask, kv, halo, qg, adapt):
     count = CHUNKS[c]
-    kind = near.dtype
+    kind = kv[0].dtype
     width = 2 * count * HEAD_WIDTH
     tall, team = WINDOW * BLK, TEAM * BLK
     out_shape = [
@@ -298,7 +297,7 @@
         jax.ShapeDtypeStruct((REACH * BLK, width), kind),
         jax.ShapeDtypeStruct((2 * RANK, count * HEAD_WIDTH), jnp.float32),
     ]
-    inputs = [mask, *kv, *qg, near, far]
+    inputs = [mask, *kv, *halo, *qg]
     if c == 0:
         out_shape.append(jax.ShapeDtypeStruct((2 * RANK, tall), kind))
     else:
@@ -350,7 +349,8 @@
 
 
 def unpack_kernel(*refs):
-    outs, other, blocks = refs[-2:], refs[-3], refs[:-3]
+    outs, other, blocks = refs[-3:-1], refs[-4], refs[:-4]
+    refs[-1][...] = jnp.zeros_like(refs[-1])
     member, _ = place()
     before = 0
     for c, (first, count) in enumerate(spans()):
@@ -365,7 +365,7 @@
 def unpack(home, other):
     flat = [block for chunk in home for block in chunk] + [other]
     shape = jax.ShapeDtypeStruct((1, BLK, HEAD_COUNT * HEAD_WIDTH), other.dtype)
-    return call(unpack_kernel, "unpack", [shape, shape], flat)
+    return call(unpack_kernel, "unpack", [shape, shape, MARK], flat)
 
 
 def bit_value(axis, bit, unit):
@@ -400,7 +400,7 @@
             out[...] = held_ref[pl.ds(first, half)] + got_ref[pl.ds(first, half)]
 
 
-def final_kernel(first_ref, second_ref, key_ref, value_ref):
+def final_kernel(first_ref, second_ref, _, key_ref, value_ref):
     key_ref[...] = first_ref[0, :RANK, :] + second_ref[0, :RANK, :]
     value_ref[...] = first_ref[0, RANK:, :] + second_ref[0, RANK:, :]
 
@@ -431,7 +431,7 @@
         self.held, self.sent = call(kernel, f"fold_{index}", [shape, shape], inputs, specs)
         self.index += 1
 
-    def finish(self):
+    def finish(self, after):
         arrived = []
         for flip, piece in enumerate((self.held, self.sent)):
             route = []
@@ -442,7 +442,7 @@
                     route.append((source, position % TEAM * self.pieces + index))
             arrived.append(lax.ppermute(piece, ("dp", "seq"), route))
         shape = jax.ShapeDtypeStruct((RANK, self.width), jnp.float32)
-        return call(final_kernel, "final", [shape, shape], arrived)
+        return call(final_kernel, "final", [shape, shape], [*arrived, after], [VMEM, VMEM, ANY])
 
 
 def body(
@@ -478,24 +478,25 @@
     lists = key_block_lists.transpose(2, 1, 0)
     counts = live_block_counts.T
     adapters = (key_adapter_input.transpose(0, 2, 1), value_adapter_input.transpose(0, 2, 1))
-    def spread(packed):
-        own, other, across, diagonal = packed
-        return [own, partner(other, 1), [partner(x, 2) for x in across], [partner(x, 3) for x in diagonal]]
-
-    kv_out = pack(head_keys, head_values, adapters)
-    kv = spread(kv_out)
-    qg_out = pack(head_queries, output_gradient, after=kv_out[:1])
-    qg = spread(qg_out)
-    mask = make_mask(lists, counts, kv_out[0])
-    near, far = [], []
-    for c, span in enumerate(spans()):
-        near.append(lax.ppermute(stack(kv[0], kv[1], f"near_{c}", span, [mask, qg[1]]), "seq", near_route))
-        far.append(lax.ppermute(stack(kv[2][c], kv[3][c], f"far_{c}"), "seq", far_route))
-
+    sides, mark = pack("pack_side", (SIDE,), head_keys, head_values, adapters, at_once=True)
+    kv_side = [partner(side, 1) for (side,) in sides]
+    kv_out, _ = pack("pack_kv", (OWN, ACROSS), head_keys, head_values, adapters, [mark])
+    mask = make_mask(lists, counts, kv_out[0][0])
+    qg_out, _ = pack("pack_qg", (SIDE, OWN, ACROSS), head_queries, output_gradient, after=[mask])
+    qg_side = [partner(side, 1) for side, _, _ in qg_out]
+    kv, halo, qg = [], [], []
+    for c in range(len(CHUNKS)):
+        (mine, across), got = kv_out[c], kv_side[c]
+        chip, send = route(f"route_kv_{c}", mine, across, got)
+        kv.append((chip, partner(send, 2)))
+    for c in range(len(CHUNKS)):
+        (_, mine, across), got = qg_out[c], qg_side[c]
+        chip, send = route(f"route_qg_{c}", mine, across, got, [kv[0][1]])
+        qg.append((chip, partner(send, 2)))
+        halo.append((lax.ppermute(kv[c][0], "seq", near_route), lax.ppermute(kv[c][1], "seq", far_route)))
     adapt, parts, terms = None, [], []
     for c in range(len(CHUNKS)):
-        kv_c, qg_c = ([x[0], x[1], x[2][c], x[3][c]] for x in (kv, qg))
-        own, to_a, to_b, term, *more = compute(c, mask, kv_c, qg_c, near[c], far[c], adapt)
+        own, to_a, to_b, term, *more = compute(c, mask, kv[c], halo[c], qg[c], adapt)
         adapt = more[0] if more else adapt
         terms.append(term)
         parts.append((own, lax.ppermute(to_a, "seq", swaps[0]), lax.ppermute(to_b, "seq", swaps[1])))
@@ -513,8 +514,8 @@
                 after.append(reduction.held)
     while reduction.index + 1 < len(reduction.rounds):
         reduction.step()
-    key_term, value_term = reduction.finish()
-    key_gradient, value_gradient = unpack(home, partner(others[-1], 1))
+    key_gradient, value_gradient, mark = unpack(home, partner(others[-1], 1))
+    key_term, value_term = reduction.finish(mark)
     return key_gradient, value_gradient, key_term.T, value_term.T
 
 

time: 94.4 us -> 85.6 us (0.907); the launches traced: 92.7 us -> 84.8 us
  waiting for transfers between devices: 33.4 us -> 26 us
  local copies, waits for them, and re-layouts: 1.83 us -> 0.72 us
    ppermute x15 -> x13, waiting for transfers between devices: 23.7 us -> 19.4 us  [partner(): lax.ppermute(block, 'seq', [(i, i ^ k) for i in range(seq)])]
    ppermute x2, waiting for transfers between devices: 2.73 us -> 0.01 us  [finish(): arrived.append(lax.ppermute(piece, ('dp', 'seq'), route))]
    ppermute x4, waiting for transfers between devices: 1.23 us -> 0.01 us  [the longest x2 0.01 us: body(): lax.ppermute(kv[c][1], 'seq', far_route)]
    unnamed x20 -> x18, local copies, waits for them, and re-layouts: 1.83 us -> 0.72 us
    ppermute x15 -> x13, starting transfers between devices: 14.4 us -> 15.3 us  [partner(): lax.ppermute(block, 'seq', [(i, i ^ k) for i in range(seq)])]
    pallas_call x16 -> x17, Pallas kernels: 17.2 us -> 17 us  [call(): pl.pallas_call(kernel, out_shape=out_shape, in_specs=in_specs or [VMEM] *...]
  transfers between devices with their start and end apart: 27 -> 25, of which waited for: 11 -> 7; matrix products, arithmetic and copies ran while one was open for 0% -> 0% of each run, Pallas kernels for 14% -> 16%
where the time goes in v3:
time: 85.6 us; the launch traced here: 84.8 us
  starting transfers between devices  40 us (47%)
  waiting for transfers between devices  26 us (30%)
  Pallas kernels  17 us (20%)
  between operations  0.99 us (1%)
    ppermute x13, waiting for transfers between devices, partner(): lax.ppermute(block, 'seq', [(i, i ^ k) for i in range(seq)])  19.4 us
    pallas_call x17, Pallas kernels, call(): pl.pallas_call(kernel, out_shape=out_shape, in_specs=in_specs or [VMEM] *...  17 us
    ppermute x13, starting transfers between devices, partner(): lax.ppermute(block, 'seq', [(i, i ^ k) for i in range(seq)])  15.3 us
    ppermute x2, starting transfers between devices, body(): lax.ppermute(kv[c][0], 'seq', near_route)  6.88 us
    ppermute x2, waiting for transfers between devices, step(): got = lax.ppermute(self.sent, axis, route)  6.64 us
    ppermute x2, starting transfers between devices, finish(): arrived.append(lax.ppermute(piece, ('dp', 'seq'), route))  6.44 us
    ppermute x2, starting transfers between devices, step(): got = lax.ppermute(self.sent, axis, route)  3.75 us
    ppermute x2, starting transfers between devices, body(): lax.ppermute(to_a, 'seq', swaps[0])  3.7 us
  transfers between devices with their start and end apart: 25, of which 7 were waited for; matrix products, arithmetic and copies ran while one was open for 0% of the time, Pallas kernels for 16%

profile of v3, /device:TPU:5, one launch (start us, length us, event | category | flops | bytes accessed | tf_op | source)
XLA Modules:
  0.0 84.8 jit_solution(8183721854734619457)
XLA Ops:
  0.7 2.6 %pack_side.1 = (bf16[128,1664]{1,0:T(8,128)(2,1)}, bf16[128,1536]{1,0:T(8,128)(2,1)}, f32[8,128]{1,0:T(8,128)}) custom-call(bf16[1,128,3072]{2,1,0:T(8,128)(2,1)} %a_ref.2, bf16[1,128,3072]{2,1,0:T(8,128)(2,1)} %b_ref.2, bf16[1,64,128]{2,1,0:T(8,128)(2,1)} %bitcast.6, bf16[1,64,128]{2,1,0:T(8,128)(2,1)} %bitcast.8), custom_call_target="tpu_custom_call" | custom-call | flops 1 | bytes 1 | tf_op jit(solution)/shard_map/pack_side/pallas_call | solution.py:31
  5.8 1.8 %mask.1.refs_0_.mask_ref = f32[120,128]{1,0:T(8,128)S(1)} custom-call(s32[5,16,24]{2,1,0:T(8,128)S(1)} %bitcast.10, s32[16,24]{1,0:T(8,128)S(1)} %bitcast.11, bf16[128,896]{1,0:T(8,128)(2,1)S(1)} %get-tuple-element.54._.mine_ref), custom_call_target="tpu_custom_call" | custom-call | flops 1 | bytes 1 | tf_op jit(solution)/shard_map/mask/pallas_call | solution.py:31
  8.2 3.7 %collective-permute-start.2 = (bf16[256,896]{1,0:T(8,128)(2,1)S(1)}, bf16[256,896]{1,0:T(8,128)(2,1)S(1)}, u32[]{:S(2)}, u32[]{:S(2)}) collective-permute-start(bf16[256,896]{1,0:T(8,128)(2,1)S(1)} %get-tuple-element.57.refs_0_), channel_id=1, source_target_pairs={{2,6},{3,7},{4,0},{5,1},{6,10},{7,11},{8,4},{9,5},{10,14},{11,15},... | collective-permute-start | bytes 1376264 | tf_op jit(solution)/shard_map/ppermute | solution.py:496
  12.4 5.1 %collective-permute-done.1.refs_0_.refs_1_ = bf16[256,896]{1,0:T(8,128)(2,1)S(1)} collective-permute-done((bf16[256,896]{1,0:T(8,128)(2,1)S(1)}, bf16[256,896]{1,0:T(8,128)(2,1)S(1)}, u32[]{:S(2)}, u32[]{:S(2)}) %collective-permute-start.1) | collective-permute-done | bytes 458784 | tf_op jit(solution)/shard_map/ppermute | solution.py:462
  17.5 1.3 %collective-permute-start.3 = (bf16[256,896]{1,0:T(8,128)(2,1)S(1)}, bf16[256,896]{1,0:T(8,128)(2,1)S(1)}, u32[]{:S(2)}, u32[]{:S(2)}) collective-permute-start(bf16[256,896]{1,0:T(8,128)(2,1)S(1)} %collective-permute-done.1.refs_0_.refs_1_), channel_id=1, source_target_pairs={{6,2},{7,3},{0,4},{1,5},{10,6},{11,7},{4,8},{5,9},{14,10},{15,11},... | collective-permute-start | bytes 1376264 | tf_op jit(solution)/shard_map/ppermute | solution.py:496
  18.9 2.2 %collective-permute-start.5 = (bf16[256,768]{1,0:T(8,128)(2,1)S(1)}, bf16[256,768]{1,0:T(8,128)(2,1)S(1)}, u32[]{:S(2)}, u32[]{:S(2)}) collective-permute-start(bf16[256,768]{1,0:T(8,128)(2,1)S(1)} %get-tuple-element.63), channel_id=1, source_target_pairs={{0,2},{1,3},{2,0},{3,1},{4,6},{5,7},{6,4},{7,5},{8,10},{9,11},{10,... | collective-permute-start | bytes 1179656 | tf_op jit(solution)/shard_map/ppermute | solution.py:462
  21.1 3.2 %collective-permute-start.12 = (bf16[256,768]{1,0:T(8,128)(2,1)S(1)}, bf16[256,768]{1,0:T(8,128)(2,1)S(1)}, u32[]{:S(2)}, u32[]{:S(2)}) collective-permute-start(bf16[256,768]{1,0:T(8,128)(2,1)S(1)} %get-tuple-element.73.refs_0_), channel_id=1, source_target_pairs={{2,6},{3,7},{4,0},{5,1},{6,10},{7,11},{8,4},{9,5},{10,14},{11,15},... | collective-permute-start | bytes 1179656 | tf_op jit(solution)/shard_map/ppermute | solution.py:496
  24.3 1.6 %collective-permute-done.11.refs_1_ = bf16[256,768]{1,0:T(8,128)(2,1)S(1)} collective-permute-done((bf16[256,768]{1,0:T(8,128)(2,1)S(1)}, bf16[256,768]{1,0:T(8,128)(2,1)S(1)}, u32[]{:S(2)}, u32[]{:S(2)}) %collective-permute-start.11) | collective-permute-done | bytes 393248 | tf_op jit(solution)/shard_map/ppermute | solution.py:462
  27.3 2.2 %collective-permute-start.15 = (bf16[256,768]{1,0:T(8,128)(2,1)S(1)}, bf16[256,768]{1,0:T(8,128)(2,1)S(1)}, u32[]{:S(2)}, u32[]{:S(2)}) collective-permute-start(bf16[256,768]{1,0:T(8,128)(2,1)S(1)} %get-tuple-element.79), channel_id=1, source_target_pairs={{0,2},{1,3},{2,0},{3,1},{4,6},{5,7},{6,4},{7,5},{8,10},{9,11},{10,... | collective-permute-start | bytes 1179656 | tf_op jit(solution)/shard_map/ppermute | solution.py:462
  29.5 4.8 %collective-permute-done.5.refs_5_ = bf16[256,768]{1,0:T(8,128)(2,1)S(1)} collective-permute-done((bf16[256,768]{1,0:T(8,128)(2,1)S(1)}, bf16[256,768]{1,0:T(8,128)(2,1)S(1)}, u32[]{:S(2)}, u32[]{:S(2)}) %collective-permute-start.5) | collective-permute-done | bytes 393248 | tf_op jit(solution)/shard_map/ppermute | solution.py:462
  34.4 4.8 %gradients_0.1 = (f32[512,768]{1,0:T(8,128)S(1)}, bf16[256,768]{1,0:T(8,128)(2,1)S(1)}, bf16[256,768]{1,0:T(8,128)(2,1)S(1)}, f32[128,384]{1,0:T(8,128)S(1)}, bf16[128,1024]{1,0:T(8,128)(2,1)S(1)}) custom-call(f32[120,128]{1,0:T(8,128)S(1)} %mask.1.refs_0_.mask_ref, bf16[256,896]{1,0:T(8,128)(2,1)S(1)} %get-tuple-element.57.refs_0_, ...), custom_call_target="tpu_custom_call" | custom-call | flops 1 | bytes 1 | tf_op jit(solution)/shard_map/gradients_0/pallas_call | solution.py:31
  39.2 1.4 %collective-permute-start.6 = (bf16[256,768]{1,0:T(8,128)(2,1)S(1)}, bf16[256,768]{1,0:T(8,128)(2,1)S(1)}, u32[]{:S(2)}, u32[]{:S(2)}) collective-permute-start(bf16[256,768]{1,0:T(8,128)(2,1)S(1)} %get-tuple-element.65), channel_id=1, source_target_pairs={{0,4},{4,0},{1,5},{5,1},{2,6},{6,2},{3,7},{7,3},{8,12},{12,8},{9,1... | collective-permute-start | bytes 1179656 | tf_op jit(solution)/shard_map/ppermute | solution.py:502
  41.2 1.6 %collective-permute-done.15.refs_5_ = bf16[256,768]{1,0:T(8,128)(2,1)S(1)} collective-permute-done((bf16[256,768]{1,0:T(8,128)(2,1)S(1)}, bf16[256,768]{1,0:T(8,128)(2,1)S(1)}, u32[]{:S(2)}, u32[]{:S(2)}) %collective-permute-start.15) | collective-permute-done | bytes 393248 | tf_op jit(solution)/shard_map/ppermute | solution.py:462
  42.8 4.7 %gradients_1.1 = (f32[512,768]{1,0:T(8,128)S(1)}, bf16[256,768]{1,0:T(8,128)(2,1)S(1)}, bf16[256,768]{1,0:T(8,128)(2,1)S(1)}, f32[128,384]{1,0:T(8,128)S(1)}) custom-call(f32[120,128]{1,0:T(8,128)S(1)} %mask.1.refs_0_.mask_ref, bf16[256,768]{1,0:T(8,128)(2,1)S(1)} %get-tuple-element.73.refs_0_, bf16[256,768]{1,0:T(8,128)(2,1)S(1)} %collective-permute-done.11.refs_1_, ...), custom_call_target="tpu_custom_call" | custom-call | flops 1 | bytes 1 | tf_op jit(solution)/shard_map/gradients_1/pallas_call | solution.py:31
  47.5 2.3 %collective-permute-start.16 = (bf16[256,768]{1,0:T(8,128)(2,1)S(1)}, bf16[256,768]{1,0:T(8,128)(2,1)S(1)}, u32[]{:S(2)}, u32[]{:S(2)}) collective-permute-start(bf16[256,768]{1,0:T(8,128)(2,1)S(1)} %get-tuple-element.82), channel_id=1, source_target_pairs={{0,4},{4,0},{1,5},{5,1},{2,6},{6,2},{3,7},{7,3},{8,12},{12,8},{9,1... | collective-permute-start | bytes 1179656 | tf_op jit(solution)/shard_map/ppermute | solution.py:502
  52.4 4.5 %collective-permute-start.9 = (bf16[128,768]{1,0:T(8,128)(2,1)S(1)}, bf16[128,768]{1,0:T(8,128)(2,1)S(1)}, u32[]{:S(2)}, u32[]{:S(2)}) collective-permute-start(bf16[128,768]{1,0:T(8,128)(2,1)S(1)} %get-tuple-element.69), channel_id=1, source_target_pairs={{0,3},{1,2},{2,1},{3,0},{4,7},{5,6},{6,5},{7,4},{8,11},{9,10},{10,... | collective-permute-start | bytes 589832 | tf_op jit(solution)/shard_map/ppermute | solution.py:462
  57.2 2.5 %collective-permute-start.19 = (f32[2,128,96]{2,1,0:T(8,128)S(1)}, f32[2,128,96]{2,1,0:T(8,128)S(1)}, u32[]{:S(2)}, u32[]{:S(2)}) collective-permute-start(f32[2,128,96]{2,1,0:T(8,128)S(1)} %get-tuple-element.90), channel_id=1, source_target_pairs={{0,8},{1,9},{2,10},{3,11},{4,12},{5,13},{6,14},{7,15},{8,0},{9,1},... | collective-permute-start | bytes 294920 | tf_op jit(solution)/shard_map/ppermute | solution.py:426
  59.7 6.6 %collective-permute-done.19.got_ref = f32[2,128,96]{2,1,0:T(8,128)S(1)} collective-permute-done((f32[2,128,96]{2,1,0:T(8,128)S(1)}, f32[2,128,96]{2,1,0:T(8,128)S(1)}, u32[]{:S(2)}, u32[]{:S(2)}) %collective-permute-start.19) | collective-permute-done | bytes 98336 | tf_op jit(solution)/shard_map/ppermute | solution.py:426
  66.6 2.6 %collective-permute-start.22 = (bf16[128,1536]{1,0:T(8,128)(2,1)S(1)}, bf16[128,1536]{1,0:T(8,128)(2,1)S(1)}, u32[]{:S(2)}, u32[]{:S(2)}) collective-permute-start(bf16[128,1536]{1,0:T(8,128)(2,1)S(1)} %get-tuple-element.95), channel_id=1, source_target_pairs={{0,1},{1,0},{2,3},{3,2},{4,5},{5,4},{6,7},{7,6},{8,9},{9,8},{10,11... | collective-permute-start | bytes 1179656 | tf_op jit(solution)/shard_map/ppermute | solution.py:462
  69.4 1.5 %collective-permute-start.21 = (bf16[128,768]{1,0:T(8,128)(2,1)S(1)}, bf16[128,768]{1,0:T(8,128)(2,1)S(1)}, u32[]{:S(2)}, u32[]{:S(2)}) collective-permute-start(bf16[128,768]{1,0:T(8,128)(2,1)S(1)} %get-tuple-element.94), channel_id=1, source_target_pairs={{0,3},{1,2},{2,1},{3,0},{4,7},{5,6},{6,5},{7,4},{8,11},{9,10},{10,... | collective-permute-start | bytes 589832 | tf_op jit(solution)/shard_map/ppermute | solution.py:462
  70.9 2.8 %collective-permute-start.23 = (f32[1,128,96]{2,1,0:T(8,128)S(1)}, f32[1,128,96]{2,1,0:T(8,128)S(1)}, u32[]{:S(2)}, u32[]{:S(2)}) collective-permute-start(f32[1,128,96]{2,1,0:T(8,128)S(1)} %get-tuple-element.91.refs_4_), channel_id=1, source_target_pairs={{0,0},{1,8},{2,16},{3,24},{4,1},{5,9},{6,17},{7,25},{8,2},{9,10},{... | collective-permute-start | bytes 147464 | tf_op jit(solution)/shard_map/ppermute | solution.py:443
  73.7 3.6 %collective-permute-start.24 = (f32[1,128,96]{2,1,0:T(8,128)S(1)}, f32[1,128,96]{2,1,0:T(8,128)S(1)}, u32[]{:S(2)}, u32[]{:S(2)}) collective-permute-start(f32[1,128,96]{2,1,0:T(8,128)S(1)} %get-tuple-element.98), channel_id=1, source_target_pairs={{0,1},{1,9},{2,17},{3,25},{4,0},{5,8},{6,16},{7,24},{8,3},{9,11},{... | collective-permute-start | bytes 147464 | tf_op jit(solution)/shard_map/ppermute | solution.py:443
  77.4 5.5 %collective-permute-done.21.refs_5_ = bf16[128,768]{1,0:T(8,128)(2,1)S(1)} collective-permute-done((bf16[128,768]{1,0:T(8,128)(2,1)S(1)}, bf16[128,768]{1,0:T(8,128)(2,1)S(1)}, u32[]{:S(2)}, u32[]{:S(2)}) %collective-permute-start.21) | collective-permute-done | bytes 196640 | tf_op jit(solution)/shard_map/ppermute | solution.py:462
  82.9 1.3 %unpack.1 = (bf16[1,128,3072]{2,1,0:T(8,128)(2,1)}, bf16[1,128,3072]{2,1,0:T(8,128)(2,1)}, f32[8,128]{1,0:T(8,128)S(1)}) custom-call(bf16[128,768]{1,0:T(8,128)(2,1)S(1)} %get-tuple-element.67.refs_0_, bf16[128,768]{1,0:T(8,128)(2,1)S(1)} %collective-permute-done.8.refs_1_, bf16[128,768]{1,0:T(8,128)(2,1)S(1)} %collective-permute-done.9.refs_2_, ...), custom_call_target="tpu_custom_call" | custom-call | flops 1 | bytes 1 | tf_op jit(solution)/shard_map/unpack/pallas_call | solution.py:31
  (61 shorter events, 9.6 us)
Async XLA Ops:
  4.0 8.3 %collective-permute-start.10 = (bf16[128,1536]{1,0:T(8,128)(2,1)}, bf16[128,1536]{1,0:T(8,128)(2,1)S(1)}, u32[]{:S(2)}, u32[]{:S(2)}) collective-permute-start(bf16[128,1536]{1,0:T(8,128)(2,1)} %get-tuple-element.72), channel_id=1, source_target_pairs={{0,1},{1,0},{2,3},{3,2},{4,5},{5,4},{6,7},{7,6},{8,9},{9,8},{10,11... | collective-permute-start | bytes 1179656 | tf_op jit(solution)/shard_map/ppermute | solution.py:462
  5.7 11.8 %collective-permute-start.1 = (bf16[256,896]{1,0:T(8,128)(2,1)S(1)}, bf16[256,896]{1,0:T(8,128)(2,1)S(1)}, u32[]{:S(2)}, u32[]{:S(2)}) collective-permute-start(bf16[256,896]{1,0:T(8,128)(2,1)S(1)} %get-tuple-element.58), channel_id=1, source_target_pairs={{0,2},{1,3},{2,0},{3,1},{4,6},{5,7},{6,4},{7,5},{8,10},{9,11},{10,... | collective-permute-start | bytes 1376264 | tf_op jit(solution)/shard_map/ppermute | solution.py:462
  7.8 11.0 %collective-permute-start.4 = (bf16[128,1536]{1,0:T(8,128)(2,1)S(1)}, bf16[128,1536]{1,0:T(8,128)(2,1)S(1)}, u32[]{:S(2)}, u32[]{:S(2)}) collective-permute-start(bf16[128,1536]{1,0:T(8,128)(2,1)S(1)} %get-tuple-element.61), channel_id=1, source_target_pairs={{0,1},{1,0},{2,3},{3,2},{4,5},{5,4},{6,7},{7,6},{8,9},{9,8},{10,11... | collective-permute-start | bytes 1179656 | tf_op jit(solution)/shard_map/ppermute | solution.py:462
  8.2 19.1 %collective-permute-start.2 = (bf16[256,896]{1,0:T(8,128)(2,1)S(1)}, bf16[256,896]{1,0:T(8,128)(2,1)S(1)}, u32[]{:S(2)}, u32[]{:S(2)}) collective-permute-start(bf16[256,896]{1,0:T(8,128)(2,1)S(1)} %get-tuple-element.57.refs_0_), channel_id=1, source_target_pairs={{2,6},{3,7},{4,0},{5,1},{6,10},{7,11},{8,4},{9,5},{10,14},{11,15},... | collective-permute-start | bytes 1376264 | tf_op jit(solution)/shard_map/ppermute | solution.py:496
  11.9 9.2 %collective-permute-start.14 = (bf16[128,1536]{1,0:T(8,128)(2,1)S(1)}, bf16[128,1536]{1,0:T(8,128)(2,1)S(1)}, u32[]{:S(2)}, u32[]{:S(2)}) collective-permute-start(bf16[128,1536]{1,0:T(8,128)(2,1)S(1)} %get-tuple-element.77), channel_id=1, source_target_pairs={{0,1},{1,0},{2,3},{3,2},{4,5},{5,4},{6,7},{7,6},{8,9},{9,8},{10,11... | collective-permute-start | bytes 1179656 | tf_op jit(solution)/shard_map/ppermute | solution.py:462
  12.4 13.6 %collective-permute-start.11 = (bf16[256,768]{1,0:T(8,128)(2,1)S(1)}, bf16[256,768]{1,0:T(8,128)(2,1)S(1)}, u32[]{:S(2)}, u32[]{:S(2)}) collective-permute-start(bf16[256,768]{1,0:T(8,128)(2,1)S(1)} %get-tuple-element.74), channel_id=1, source_target_pairs={{0,2},{1,3},{2,0},{3,1},{4,6},{5,7},{6,4},{7,5},{8,10},{9,11},{10,... | collective-permute-start | bytes 1179656 | tf_op jit(solution)/shard_map/ppermute | solution.py:462
  17.5 16.9 %collective-permute-start.3 = (bf16[256,896]{1,0:T(8,128)(2,1)S(1)}, bf16[256,896]{1,0:T(8,128)(2,1)S(1)}, u32[]{:S(2)}, u32[]{:S(2)}) collective-permute-start(bf16[256,896]{1,0:T(8,128)(2,1)S(1)} %collective-permute-done.1.refs_0_.refs_1_), channel_id=1, source_target_pairs={{6,2},{7,3},{0,4},{1,5},{10,6},{11,7},{4,8},{5,9},{14,10},{15,11},... | collective-permute-start | bytes 1376264 | tf_op jit(solution)/shard_map/ppermute | solution.py:496
  18.9 15.5 %collective-permute-start.5 = (bf16[256,768]{1,0:T(8,128)(2,1)S(1)}, bf16[256,768]{1,0:T(8,128)(2,1)S(1)}, u32[]{:S(2)}, u32[]{:S(2)}) collective-permute-start(bf16[256,768]{1,0:T(8,128)(2,1)S(1)} %get-tuple-element.63), channel_id=1, source_target_pairs={{0,2},{1,3},{2,0},{3,1},{4,6},{5,7},{6,4},{7,5},{8,10},{9,11},{10,... | collective-permute-start | bytes 1179656 | tf_op jit(solution)/shard_map/ppermute | solution.py:462
  21.1 20.1 %collective-permute-start.12 = (bf16[256,768]{1,0:T(8,128)(2,1)S(1)}, bf16[256,768]{1,0:T(8,128)(2,1)S(1)}, u32[]{:S(2)}, u32[]{:S(2)}) collective-permute-start(bf16[256,768]{1,0:T(8,128)(2,1)S(1)} %get-tuple-element.73.refs_0_), channel_id=1, source_target_pairs={{2,6},{3,7},{4,0},{5,1},{6,10},{7,11},{8,4},{9,5},{10,14},{11,15},... | collective-permute-start | bytes 1179656 | tf_op jit(solution)/shard_map/ppermute | solution.py:496
  25.9 15.3 %collective-permute-start.13 = (bf16[256,768]{1,0:T(8,128)(2,1)S(1)}, bf16[256,768]{1,0:T(8,128)(2,1)S(1)}, u32[]{:S(2)}, u32[]{:S(2)}) collective-permute-start(bf16[256,768]{1,0:T(8,128)(2,1)S(1)} %collective-permute-done.11.refs_1_), channel_id=1, source_target_pairs={{6,2},{7,3},{0,4},{1,5},{10,6},{11,7},{4,8},{5,9},{14,10},{15,11},... | collective-permute-start | bytes 1179656 | tf_op jit(solution)/shard_map/ppermute | solution.py:496
  27.3 15.5 %collective-permute-start.15 = (bf16[256,768]{1,0:T(8,128)(2,1)S(1)}, bf16[256,768]{1,0:T(8,128)(2,1)S(1)}, u32[]{:S(2)}, u32[]{:S(2)}) collective-permute-start(bf16[256,768]{1,0:T(8,128)(2,1)S(1)} %get-tuple-element.79), channel_id=1, source_target_pairs={{0,2},{1,3},{2,0},{3,1},{4,6},{5,7},{6,4},{7,5},{8,10},{9,11},{10,... | collective-permute-start | bytes 1179656 | tf_op jit(solution)/shard_map/ppermute | solution.py:462
  39.2 12.7 %collective-permute-start.6 = (bf16[256,768]{1,0:T(8,128)(2,1)S(1)}, bf16[256,768]{1,0:T(8,128)(2,1)S(1)}, u32[]{:S(2)}, u32[]{:S(2)}) collective-permute-start(bf16[256,768]{1,0:T(8,128)(2,1)S(1)} %get-tuple-element.65), channel_id=1, source_target_pairs={{0,4},{4,0},{1,5},{5,1},{2,6},{6,2},{3,7},{7,3},{8,12},{12,8},{9,1... | collective-permute-start | bytes 1179656 | tf_op jit(solution)/shard_map/ppermute | solution.py:502
  40.5 11.4 %collective-permute-start.7 = (bf16[256,768]{1,0:T(8,128)(2,1)S(1)}, bf16[256,768]{1,0:T(8,128)(2,1)S(1)}, u32[]{:S(2)}, u32[]{:S(2)}) collective-permute-start(bf16[256,768]{1,0:T(8,128)(2,1)S(1)} %get-tuple-element.66), channel_id=1, source_target_pairs={{4,8},{8,4},{5,9},{9,5},{6,10},{10,6},{7,11},{11,7},{20,24},{24,20... | collective-permute-start | bytes 1179656 | tf_op jit(solution)/shard_map/ppermute | solution.py:502
  47.5 18.8 %collective-permute-start.16 = (bf16[256,768]{1,0:T(8,128)(2,1)S(1)}, bf16[256,768]{1,0:T(8,128)(2,1)S(1)}, u32[]{:S(2)}, u32[]{:S(2)}) collective-permute-start(bf16[256,768]{1,0:T(8,128)(2,1)S(1)} %get-tuple-element.82), channel_id=1, source_target_pairs={{0,4},{4,0},{1,5},{5,1},{2,6},{6,2},{3,7},{7,3},{8,12},{12,8},{9,1... | collective-permute-start | bytes 1179656 | tf_op jit(solution)/shard_map/ppermute | solution.py:502
  49.9 16.5 %collective-permute-start.17 = (bf16[256,768]{1,0:T(8,128)(2,1)S(1)}, bf16[256,768]{1,0:T(8,128)(2,1)S(1)}, u32[]{:S(2)}, u32[]{:S(2)}) collective-permute-start(bf16[256,768]{1,0:T(8,128)(2,1)S(1)} %get-tuple-element.83), channel_id=1, source_target_pairs={{4,8},{8,4},{5,9},{9,5},{6,10},{10,6},{7,11},{11,7},{20,24},{24,20... | collective-permute-start | bytes 1179656 | tf_op jit(solution)/shard_map/ppermute | solution.py:502
  50.6 6.3 %collective-permute-start.18 = (f32[128,384]{1,0:T(8,128)S(1)}, f32[128,384]{1,0:T(8,128)S(1)}, u32[]{:S(2)}, u32[]{:S(2)}) collective-permute-start(f32[128,384]{1,0:T(8,128)S(1)} %get-tuple-element.88), channel_id=1, source_target_pairs={{0,16},{16,0},{1,17},{17,1},{2,18},{18,2},{3,19},{19,3},{4,20},{20... | collective-permute-start | bytes 589832 | tf_op jit(solution)/shard_map/ppermute | solution.py:426
  52.1 14.3 %collective-permute-start.8 = (bf16[128,768]{1,0:T(8,128)(2,1)S(1)}, bf16[128,768]{1,0:T(8,128)(2,1)S(1)}, u32[]{:S(2)}, u32[]{:S(2)}) collective-permute-start(bf16[128,768]{1,0:T(8,128)(2,1)S(1)} %get-tuple-element.68), channel_id=1, source_target_pairs={{0,2},{1,3},{2,0},{3,1},{4,6},{5,7},{6,4},{7,5},{8,10},{9,11},{10,... | collective-permute-start | bytes 589832 | tf_op jit(solution)/shard_map/ppermute | solution.py:462
  52.4 14.0 %collective-permute-start.9 = (bf16[128,768]{1,0:T(8,128)(2,1)S(1)}, bf16[128,768]{1,0:T(8,128)(2,1)S(1)}, u32[]{:S(2)}, u32[]{:S(2)}) collective-permute-start(bf16[128,768]{1,0:T(8,128)(2,1)S(1)} %get-tuple-element.69), channel_id=1, source_target_pairs={{0,3},{1,2},{2,1},{3,0},{4,7},{5,6},{6,5},{7,4},{8,11},{9,10},{10,... | collective-permute-start | bytes 589832 | tf_op jit(solution)/shard_map/ppermute | solution.py:462
  57.2 9.1 %collective-permute-start.19 = (f32[2,128,96]{2,1,0:T(8,128)S(1)}, f32[2,128,96]{2,1,0:T(8,128)S(1)}, u32[]{:S(2)}, u32[]{:S(2)}) collective-permute-start(f32[2,128,96]{2,1,0:T(8,128)S(1)} %get-tuple-element.90), channel_id=1, source_target_pairs={{0,8},{1,9},{2,10},{3,11},{4,12},{5,13},{6,14},{7,15},{8,0},{9,1},... | collective-permute-start | bytes 294920 | tf_op jit(solution)/shard_map/ppermute | solution.py:426
  66.6 16.2 %collective-permute-start.22 = (bf16[128,1536]{1,0:T(8,128)(2,1)S(1)}, bf16[128,1536]{1,0:T(8,128)(2,1)S(1)}, u32[]{:S(2)}, u32[]{:S(2)}) collective-permute-start(bf16[128,1536]{1,0:T(8,128)(2,1)S(1)} %get-tuple-element.95), channel_id=1, source_target_pairs={{0,1},{1,0},{2,3},{3,2},{4,5},{5,4},{6,7},{7,6},{8,9},{9,8},{10,11... | collective-permute-start | bytes 1179656 | tf_op jit(solution)/shard_map/ppermute | solution.py:462
  69.2 8.2 %collective-permute-start.20 = (bf16[128,768]{1,0:T(8,128)(2,1)S(1)}, bf16[128,768]{1,0:T(8,128)(2,1)S(1)}, u32[]{:S(2)}, u32[]{:S(2)}) collective-permute-start(bf16[128,768]{1,0:T(8,128)(2,1)S(1)} %get-tuple-element.93), channel_id=1, source_target_pairs={{0,2},{1,3},{2,0},{3,1},{4,6},{5,7},{6,4},{7,5},{8,10},{9,11},{10,... | collective-permute-start | bytes 589832 | tf_op jit(solution)/shard_map/ppermute | solution.py:462
  69.4 13.4 %collective-permute-start.21 = (bf16[128,768]{1,0:T(8,128)(2,1)S(1)}, bf16[128,768]{1,0:T(8,128)(2,1)S(1)}, u32[]{:S(2)}, u32[]{:S(2)}) collective-permute-start(bf16[128,768]{1,0:T(8,128)(2,1)S(1)} %get-tuple-element.94), channel_id=1, source_target_pairs={{0,3},{1,2},{2,1},{3,0},{4,7},{5,6},{6,5},{7,4},{8,11},{9,10},{10,... | collective-permute-start | bytes 589832 | tf_op jit(solution)/shard_map/ppermute | solution.py:462
  70.9 13.3 %collective-permute-start.23 = (f32[1,128,96]{2,1,0:T(8,128)S(1)}, f32[1,128,96]{2,1,0:T(8,128)S(1)}, u32[]{:S(2)}, u32[]{:S(2)}) collective-permute-start(f32[1,128,96]{2,1,0:T(8,128)S(1)} %get-tuple-element.91.refs_4_), channel_id=1, source_target_pairs={{0,0},{1,8},{2,16},{3,24},{4,1},{5,9},{6,17},{7,25},{8,2},{9,10},{... | collective-permute-start | bytes 147464 | tf_op jit(solution)/shard_map/ppermute | solution.py:443
  73.7 10.4 %collective-permute-start.24 = (f32[1,128,96]{2,1,0:T(8,128)S(1)}, f32[1,128,96]{2,1,0:T(8,128)S(1)}, u32[]{:S(2)}, u32[]{:S(2)}) collective-permute-start(f32[1,128,96]{2,1,0:T(8,128)S(1)} %get-tuple-element.98), channel_id=1, source_target_pairs={{0,1},{1,9},{2,17},{3,25},{4,0},{5,8},{6,16},{7,24},{8,3},{9,11},{... | collective-permute-start | bytes 147464 | tf_op jit(solution)/shard_map/ppermute | solution.py:443
  (10 other events, 30.7 us)

commit v4 on v3

--- a/solution.py
+++ b/solution.py
@@ -16,7 +16,6 @@
 TEAM = 4
 HEADS = HEAD_COUNT // TEAM
 CHUNKS = (3, 3)
-LOADS = 4
 WINDOW = TEAM + 2 * REACH
 SCALING = HEAD_WIDTH**-0.5
 LOG2E = 1.4426950408889634
@@ -56,6 +55,14 @@
     return pl.ds(first, count * BLK)
 
 
+def padded(columns):
+    return pl.cdiv(columns, HEAD_WIDTH) * HEAD_WIDTH
+
+
+def first_head(c, member):
+    return (c * TEAM + member) * CHUNKS[c]
+
+
 def place():
     position = lax.axis_index("seq")
     return lax.rem(position, TEAM), position // TEAM
@@ -76,7 +83,7 @@
     member, _ = place()
     for ((first, count), owners, _), out in zip(plan, outs):
         for index, k in enumerate(owners):
-            head = jnp.bitwise_xor(member, k) * HEADS + first
+            head = first_head(first // count, jnp.bitwise_xor(member, k))
             out[part, cols(2 * index * count, count)] = a_ref[part, cols(head, count)]
             out[part, cols((2 * index + 1) * count, count)] = b_ref[part, cols(head, count)]
 
@@ -90,25 +97,23 @@
 
 
 def pack_first_kernel(plan, keys, values, key_in, value_in, *refs):
-    outs, (mark, tall, small, sems) = refs[:-4], refs[-4:]
-    mark[...] = jnp.zeros_like(mark)
-    size = BLK // LOADS
-    copies = []
-    for part in range(LOADS):
-        for index, source in enumerate((keys, values)):
-            piece = pl.ds(part * size, size)
-            copies.append((source.at[0, piece, :], tall.at[index, piece, :]))
-    copies += [(key_in.at[0], small.at[0]), (value_in.at[0], small.at[1])]
+    outs, (small, sems) = refs[:-2], refs[-2:]
+    member, _ = place()
+    copies = [(key_in.at[0], small.at[0]), (value_in.at[0], small.at[1])]
+    for ((first, count), owners, _), out in zip(plan, outs):
+        for index, k in enumerate(owners):
+            head = first_head(first // count, jnp.bitwise_xor(member, k))
+            for part, source in enumerate((keys, values)):
+                target = out.at[:, cols((2 * index + part) * count, count)]
+                copies.append((source.at[0, :, cols(head, count)], target))
     copies = [pltpu.make_async_copy(*pair, sems.at[i]) for i, pair in enumerate(copies)]
     for copy in copies:
         copy.start()
-    for part in range(LOADS):
-        for copy in copies[2 * part : 2 * part + 2]:
-            copy.wait()
-        fill(plan, tall.at[0], tall.at[1], outs, pl.ds(part * size, size))
-    for copy in copies[2 * LOADS :]:
+    for copy in copies[:2]:
         copy.wait()
     fill_adapters(plan, small[0], small[1], outs)
+    for copy in copies[2:]:
+        copy.wait()
 
 
 def pack_kernel(plan, adapters, a_ref, b_ref, *refs):
@@ -128,18 +133,16 @@
     inputs = [first, second, *adapters, *after]
     if at_once:
         scratch = [
-            pltpu.VMEM((2, BLK, HEAD_COUNT * HEAD_WIDTH), kind),
             pltpu.VMEM((2, RANK, BLK), kind),
-            pltpu.SemaphoreType.DMA((2 * LOADS + 2,)),
+            pltpu.SemaphoreType.DMA((2 + sum(2 * len(owners) for _, owners, _ in plan),)),
         ]
         kernel = functools.partial(pack_first_kernel, plan)
-        out_shape.append(MARK)
         outs = call(kernel, name, out_shape, inputs, [ANY] * 4, scratch, PACK_VMEM)
     else:
         kernel = functools.partial(pack_kernel, plan, bool(adapters))
         specs = [VMEM] * (2 + len(adapters)) + [ANY] * len(after)
         outs = call(kernel, name, out_shape, inputs, specs)
-    return [outs[len(kinds) * c : len(kinds) * (c + 1)] for c in range(len(CHUNKS))], outs[-1]
+    return [outs[len(kinds) * c : len(kinds) * (c + 1)] for c in range(len(CHUNKS))]
 
 
 def route_kernel(mine_ref, across_ref, got_ref, *refs):
@@ -164,7 +167,7 @@
 def mask_kernel(lists_ref, counts_ref, _, mask_ref):
     member, team = place()
     for h in range(HEADS):
-        head = member * HEADS + h
+        head = first_head(h // CHUNKS[0], member) + h % CHUNKS[0]
         for b in range(TEAM):
             block = team * TEAM + b
             used = counts_ref[block, head]
@@ -185,11 +188,12 @@
 
 def compute_kernel(c, mask_ref, *refs):
     first, count = spans()[c]
-    kv, halo, qg = refs[:2], refs[2:4], refs[4:6]
+    kv, halo, qg, rest = refs[:2], refs[2:4], refs[4:6], refs[6:]
+    kw, vw, qs, gs, pm, dm, term = rest[-7:]
     if c == 0:
-        own_ref, a_ref, b_ref, term_ref, adapt, kw, vw, qs, gs, pm, dm = refs[6:]
+        own_ref, a_ref, b_ref, keep_ref, clip_ref, both_ref, adapt = rest[:-7]
     else:
-        adapt, own_ref, a_ref, b_ref, term_ref, kw, vw, qs, gs, pm, dm = refs[6:]
+        adapt, *earlier, own_ref, a_ref, b_ref, keep_ref, clip_ref, both_ref = rest[:-7]
     kind = adapt.dtype
     member, team = place()
     even = lax.rem(team, 2) == 0
@@ -269,7 +273,7 @@
             a_ref[:, column] = jnp.where(even, upper, lower)
             b_ref[:, column] = jnp.where(even, lower, upper)
             window = jnp.concatenate([lower, middle.astype(kind), upper], axis=0)
-            term_ref[half : half + RANK, cols(h, 1)] = product(adapt[half : half + RANK, :], window)
+            term[half : half + RANK, cols(h, 1)] = product(adapt[half : half + RANK, :], window)
 
     items = [(h, pair) for h in range(count) for pair in range(TEAM // 2)]
     for h in range(count):
@@ -284,24 +288,46 @@
         if len(adds) == TEAM // 2:
             finish(item[0], adds)
             adds = []
-
-
-def compute(c, mask, kv, halo, qg, adapt):
+    width = term.shape[1] // 4
+    quarters = [term[:, i * width : (i + 1) * width] for i in range(4)]
+    upper = bit_value("dp", lax.axis_size("dp") // 2, 1) == 1
+
+    def quarter(other_team, other_clip):
+        odd, high = jnp.logical_not(even) ^ other_team, upper ^ other_clip
+        return jnp.where(odd, jnp.where(high, *quarters[3:1:-1]), jnp.where(high, *quarters[1::-1]))
+
+    keep_ref[:, :width] = quarter(False, False)
+    leave = quarter(True, False)
+    whole = leave.astype(kind)
+    place_ = pl.ds(2 * count * HEAD_WIDTH, width)
+    a_ref[rows(0, 1), place_] = whole
+    a_ref[rows(1, 1), place_] = (leave - whole.astype(jnp.float32)).astype(kind)
+    for out, part in ((clip_ref, quarter(False, True)), (both_ref, quarter(True, True))):
+        if c == 0:
+            out[:, :width] = part
+        else:
+            out[1, :, :width] = part
+    if c == 1:
+        clip_ref[0] = earlier[0][...]
+        both_ref[0] = earlier[1][...]
+
+
+def compute(c, mask, kv, halo, qg, earlier):
     count = CHUNKS[c]
     kind = kv[0].dtype
     width = 2 * count * HEAD_WIDTH
     tall, team = WINDOW * BLK, TEAM * BLK
     out_shape = [
         jax.ShapeDtypeStruct((team, width), jnp.float32),
+        jax.ShapeDtypeStruct((REACH * BLK, width + HEAD_WIDTH), kind),
         jax.ShapeDtypeStruct((REACH * BLK, width), kind),
-        jax.ShapeDtypeStruct((REACH * BLK, width), kind),
-        jax.ShapeDtypeStruct((2 * RANK, count * HEAD_WIDTH), jnp.float32),
     ]
-    inputs = [mask, *kv, *halo, *qg]
+    part = (2 * RANK, padded(count * HEAD_WIDTH // 4))
+    many = part if c == 0 else (2, *part)
+    out_shape += [jax.ShapeDtypeStruct(shape, jnp.float32) for shape in (part, many, many)]
     if c == 0:
         out_shape.append(jax.ShapeDtypeStruct((2 * RANK, tall), kind))
-    else:
-        inputs.append(adapt)
+    inputs = [mask, *kv, *halo, *qg, *earlier]
     scratch = [
         pltpu.VMEM((count, tall, HEAD_WIDTH), kind),
         pltpu.VMEM((count, tall, HEAD_WIDTH), kind),
@@ -309,22 +335,21 @@
         pltpu.VMEM((count, team, HEAD_WIDTH), kind),
         pltpu.VMEM((count * 2, (TILES + 1) * BLK, 2 * BLK), kind),
         pltpu.VMEM((count * 2, (TILES + 1) * BLK, 2 * BLK), kind),
+        pltpu.VMEM((2 * RANK, count * HEAD_WIDTH), jnp.float32),
     ]
     return call(
         functools.partial(compute_kernel, c), f"gradients_{c}", out_shape, inputs, scratch=scratch, vmem=16
     )
 
 
-def combine_kernel(earlier, own_ref, a_ref, b_ref, *refs):
-    outs = refs[-TEAM:]
+def combine_kernel(last, bit, own_ref, a_ref, b_ref, keep_ref, *refs):
+    outs = refs[-5 - last : -1 - last]
     member, team = place()
     even = lax.rem(team, 2)
     width = own_ref.shape[1]
     start = outs[1].shape[1] - width
-    for index in range(earlier):
-        ref = refs[index]
-        before = sum(refs[i].shape[1] for i in range(index))
-        outs[1][:, before : before + ref.shape[1]] = ref[...]
+    if last:
+        outs[1][:, :start] = refs[0][...]
     for k in range(TEAM):
         owner = jnp.bitwise_xor(member, k)
         row = rows(lax.rem(owner, 2), 1)
@@ -332,117 +357,113 @@
         column = slice(start, start + width) if k == 1 else slice(None)
 
         def add(part_ref, out=outs[k], owner=owner, row=row, column=column):
-            part = part_ref[row, :].astype(jnp.float32)
+            part = part_ref[row, :width].astype(jnp.float32)
             out[:, column] = (own_ref[rows(owner, 1), :] + part).astype(out.dtype)
 
         pl.when(from_a)(functools.partial(add, a_ref))
         pl.when(jnp.logical_not(from_a))(functools.partial(add, b_ref))
-
-
-def combine(c, own, a, b, earlier, after):
+    got = [a_ref[rows(row, 1), pl.ds(width, keep_ref.shape[1])].astype(jnp.float32) for row in range(2)]
+    total = keep_ref[...] + got[0] + got[1]
+    if last:
+        earlier, clip_ref, both_ref = refs[1:4]
+        first = earlier[...] + clip_ref[0] + both_ref[0]
+        second = total + clip_ref[1] + both_ref[1]
+        upper = bit_value(*bit) == 1
+        refs[-2][...] = jnp.where(upper, second, first)
+        refs[-1][...] = jnp.where(upper, first, second)
+    else:
+        refs[-1][...] = total
+
+
+def combine(c, bit, own, a, b, keep, earlier, after):
+    last = int(c + 1 == len(CHUNKS))
     block = jax.ShapeDtypeStruct((BLK, own.shape[1]), a.dtype)
-    wide = jax.ShapeDtypeStruct((BLK, own.shape[1] + sum(x.shape[1] for x in earlier)), a.dtype)
-    specs = [VMEM] * (3 + len(earlier)) + [ANY] * len(after)
-    kernel = functools.partial(combine_kernel, len(earlier))
-    inputs = [own, a, b, *earlier, *after]
-    return call(kernel, f"combine_{c}", [block, wide, block, block], inputs, specs)
+    wide = jax.ShapeDtypeStruct((BLK, own.shape[1] + (earlier[0].shape[1] if last else 0)), a.dtype)
+    term = jax.ShapeDtypeStruct(keep.shape, keep.dtype)
+    specs = [VMEM] * (4 + len(earlier)) + [ANY] * len(after)
+    inputs = [own, a, b, keep, *earlier, *after]
+    kernel = functools.partial(combine_kernel, last, bit)
+    return call(kernel, f"combine_{c}", [block, wide, block, block] + [term] * (1 + last), inputs, specs)
 
 
 def unpack_kernel(*refs):
-    outs, other, blocks = refs[-3:-1], refs[-4], refs[:-4]
-    refs[-1][...] = jnp.zeros_like(refs[-1])
+    blocks, other, arrived = refs[: 3 * len(CHUNKS)], refs[3 * len(CHUNKS)], refs[3 * len(CHUNKS) + 1 : -4]
+    outs, terms = refs[-4:-2], refs[-2:]
     member, _ = place()
     before = 0
-    for c, (first, count) in enumerate(spans()):
+    for c, (_, count) in enumerate(spans()):
         sources = [(0, blocks[3 * c], 0), (1, other, before), (2, blocks[3 * c + 1], 0), (3, blocks[3 * c + 2], 0)]
         for k, ref, column in sources:
-            head = jnp.bitwise_xor(member, k) * HEADS + first
+            head = first_head(c, jnp.bitwise_xor(member, k))
             for part, out in enumerate(outs):
                 out[0, :, cols(head, count)] = ref[:, cols(column + part * count, count)]
         before += 2 * count
-
-
-def unpack(home, other):
-    flat = [block for chunk in home for block in chunk] + [other]
+    if len(arrived[0].shape) == 3:
+        arrived = [ref.at[0] for ref in arrived]
+    for half, term in zip((slice(0, RANK), slice(RANK, 2 * RANK)), terms):
+        term[...] = sum(ref[half, : term.shape[1]] for ref in arrived)
+
+
+def unpack(home, other, arrived, width):
+    flat = [block for chunk in home for block in chunk] + [other, *arrived]
     shape = jax.ShapeDtypeStruct((1, BLK, HEAD_COUNT * HEAD_WIDTH), other.dtype)
-    return call(unpack_kernel, "unpack", [shape, shape, MARK], flat)
+    term = jax.ShapeDtypeStruct((RANK, width), jnp.float32)
+    return call(unpack_kernel, "unpack", [shape, shape, term, term], flat)
 
 
 def bit_value(axis, bit, unit):
     return lax.rem(lax.axis_index(axis) // (bit * unit), 2)
 
 
-def pieces_kernel(bit, *refs):
-    terms = refs[: len(CHUNKS)]
-    keep_ref, send_ref, whole = refs[len(CHUNKS) :]
-    for (first, count), term in zip(spans(), terms):
-        whole[:, cols(first, count)] = term[...]
-    upper = bit_value(*bit) == 1
-    half = whole.shape[1] // 2
-    low, high = whole[:, :half], whole[:, half:]
-    keep_ref[...] = jnp.where(upper, high, low)
-    send_ref[...] = jnp.where(upper, low, high)
-
-
-def fold_kernel(bit, held_ref, got_ref, *refs):
-    keep_ref, send_ref = refs[-2:]
-    half, width = keep_ref.shape[0], keep_ref.shape[2]
+def fold_kernel(bit, width, held_ref, got_ref, keep_ref, send_ref):
+    half = keep_ref.shape[0]
     value = bit_value(*bit)
     if len(held_ref.shape) == 2:
-        total = held_ref[...] + got_ref[...]
         for j in range(half):
-            low = total[:, j * width : (j + 1) * width]
-            high = total[:, (half + j) * width : (half + j + 1) * width]
-            keep_ref[j] = jnp.where(value == 1, high, low)
-            send_ref[j] = jnp.where(value == 1, low, high)
+            low, high = (slice(i * width, (i + 1) * width) for i in (j, half + j))
+            low, high = (held_ref[:, part] + got_ref[:, part] for part in (low, high))
+            keep_ref[j, :, :width] = jnp.where(value == 1, high, low)
+            send_ref[j, :, :width] = jnp.where(value == 1, low, high)
     else:
         for out, first in ((keep_ref, value * half), (send_ref, (1 - value) * half)):
             out[...] = held_ref[pl.ds(first, half)] + got_ref[pl.ds(first, half)]
 
 
-def final_kernel(first_ref, second_ref, _, key_ref, value_ref):
-    key_ref[...] = first_ref[0, :RANK, :] + second_ref[0, :RANK, :]
-    value_ref[...] = first_ref[0, RANK:, :] + second_ref[0, RANK:, :]
-
-
-class Reduction:
-    def __init__(self, terms):
-        self.clips, seq = lax.axis_size("dp"), lax.axis_size("seq")
-        self.teams = seq // TEAM
-        self.pieces = self.clips * self.teams
-        self.rounds = [("dp", self.clips >> s, 1) for s in range(1, self.clips.bit_length())]
-        self.rounds += [("seq", self.teams >> s, TEAM) for s in range(1, self.teams.bit_length())]
-        self.width = HEADS * HEAD_WIDTH // self.pieces
-        shape = jax.ShapeDtypeStruct((2 * RANK, HEADS * HEAD_WIDTH // 2), jnp.float32)
-        scratch = [pltpu.VMEM((2 * RANK, HEADS * HEAD_WIDTH), jnp.float32)]
-        kernel = functools.partial(pieces_kernel, self.rounds[0])
-        self.held, self.sent = call(kernel, "pieces", [shape, shape], terms, scratch=scratch)
-        self.index = 0
-
-    def step(self, after=()):
-        index = self.index
-        axis, bit, unit = self.rounds[index]
+def later_rounds():
+    clips, teams = lax.axis_size("dp"), lax.axis_size("seq") // TEAM
+    clip_bits = [clips >> s for s in range(2, clips.bit_length())]
+    team_bits = [teams >> s for s in range(1, teams.bit_length() - 1)]
+    return [("dp", bit, 1) for bit in clip_bits] + [("seq", bit, TEAM) for bit in team_bits]
+
+
+def reduce_terms(held, sent):
+    clips, seq = lax.axis_size("dp"), lax.axis_size("seq")
+    teams = seq // TEAM
+    pieces = clips * teams
+    width = HEADS * HEAD_WIDTH // pieces
+    rounds = later_rounds()
+
+    def piece_of(clip, team):
+        bits = [(clip if axis == "dp" else team) // bit % 2 for axis, bit, _ in rounds]
+        bits[1:1] = [team % 2, clip // (clips // 2) % 2]
+        return functools.reduce(lambda value, bit: 2 * value + bit, bits, 0)
+
+    for index, (axis, bit, unit) in enumerate(rounds[:-1]):
         route = [(i, i ^ (bit * unit)) for i in range(lax.axis_size(axis))]
-        got = lax.ppermute(self.sent, axis, route)
-        shape = jax.ShapeDtypeStruct((self.pieces >> (index + 2), 2 * RANK, self.width), jnp.float32)
-        specs = [VMEM] * 2 + [ANY] * len(after)
-        kernel = functools.partial(fold_kernel, self.rounds[index + 1])
-        inputs = [self.held, got, *after]
-        self.held, self.sent = call(kernel, f"fold_{index}", [shape, shape], inputs, specs)
-        self.index += 1
-
-    def finish(self, after):
-        arrived = []
-        for flip, piece in enumerate((self.held, self.sent)):
-            route = []
-            for clip in range(self.clips):
-                for position in range(self.teams * TEAM):
-                    index = (clip * self.teams + position // TEAM) ^ flip
-                    source = clip * self.teams * TEAM + position
-                    route.append((source, position % TEAM * self.pieces + index))
-            arrived.append(lax.ppermute(piece, ("dp", "seq"), route))
-        shape = jax.ShapeDtypeStruct((RANK, self.width), jnp.float32)
-        return call(final_kernel, "final", [shape, shape], [*arrived, after], [VMEM, VMEM, ANY])
+        got = lax.ppermute(sent, axis, route)
+        shape = jax.ShapeDtypeStruct((pieces >> (index + 4), 2 * RANK, padded(width)), jnp.float32)
+        kernel = functools.partial(fold_kernel, rounds[index + 1], width)
+        held, sent = call(kernel, f"fold_{index}", [shape, shape], [held, got])
+    arrived = []
+    for flip, piece in enumerate((held, sent)):
+        route = []
+        for clip in range(clips):
+            for position in range(seq):
+                other = flip * (pieces // 2 if len(rounds) == 1 else 1)
+                c, index = divmod(piece_of(clip, position // TEAM) ^ other, pieces // 2)
+                route.append((clip * seq + position, (c * TEAM + position % TEAM) * pieces // 2 + index))
+        arrived.append(lax.ppermute(piece, ("dp", "seq"), route))
+    return arrived, width
 
 
 def body(
@@ -478,11 +499,11 @@
     lists = key_block_lists.transpose(2, 1, 0)
     counts = live_block_counts.T
     adapters = (key_adapter_input.transpose(0, 2, 1), value_adapter_input.transpose(0, 2, 1))
-    sides, mark = pack("pack_side", (SIDE,), head_keys, head_values, adapters, at_once=True)
+    sides = pack("pack_side", (SIDE,), head_keys, head_values, adapters, at_once=True)
     kv_side = [partner(side, 1) for (side,) in sides]
-    kv_out, _ = pack("pack_kv", (OWN, ACROSS), head_keys, head_values, adapters, [mark])
+    kv_out = pack("pack_kv", (OWN, ACROSS), head_keys, head_values, adapters)
     mask = make_mask(lists, counts, kv_out[0][0])
-    qg_out, _ = pack("pack_qg", (SIDE, OWN, ACROSS), head_queries, output_gradient, after=[mask])
+    qg_out = pack("pack_qg", (SIDE, OWN, ACROSS), head_queries, output_gradient, after=[mask])
     qg_side = [partner(side, 1) for side, _, _ in qg_out]
     kv, halo, qg = [], [], []
     for c in range(len(CHUNKS)):
@@ -494,28 +515,27 @@
         chip, send = route(f"route_qg_{c}", mine, across, got, [kv[0][1]])
         qg.append((chip, partner(send, 2)))
         halo.append((lax.ppermute(kv[c][0], "seq", near_route), lax.ppermute(kv[c][1], "seq", far_route)))
-    adapt, parts, terms = None, [], []
+    earlier, parts = [], []
     for c in range(len(CHUNKS)):
-        own, to_a, to_b, term, *more = compute(c, mask, kv[c], halo[c], qg[c], adapt)
-        adapt = more[0] if more else adapt
-        terms.append(term)
-        parts.append((own, lax.ppermute(to_a, "seq", swaps[0]), lax.ppermute(to_b, "seq", swaps[1])))
-    reduction = Reduction(terms)
-    home, others, after = [], [], []
+        own, to_a, to_b, keep, to_clip, to_both, *more = compute(c, mask, kv[c], halo[c], qg[c], earlier)
+        earlier = [*more, to_clip, to_both]
+        parts.append((own, lax.ppermute(to_a, "seq", swaps[0]), lax.ppermute(to_b, "seq", swaps[1]), keep))
+    clips = lax.axis_size("dp")
+    from_clip = lax.ppermute(to_clip, "dp", [(i, i ^ (clips // 2)) for i in range(clips)])
+    both = []
+    for clip in range(clips):
+        both += [(clip * seq + p, (clip ^ (clips // 2)) * seq + (p ^ TEAM)) for p in range(seq)]
+    from_both = lax.ppermute(to_both, ("dp", "seq"), both)
+    home, earlier, after = [], [], []
     for c, part in enumerate(parts):
         last = c + 1 == len(CHUNKS)
-        blocks = combine(c, *part, others if last else [], after)
-        others.append(blocks[1])
+        given = [*earlier, from_clip, from_both] if last else []
+        blocks = combine(c, later_rounds()[0], *part, given, after)
         home.append([blocks[0], partner(blocks[2], 2), partner(blocks[3], 3)])
-        after = home[-1][1:]
-        for _ in range(2):
-            if not last and reduction.index + 1 < len(reduction.rounds):
-                reduction.step(blocks[:1])
-                after.append(reduction.held)
-    while reduction.index + 1 < len(reduction.rounds):
-        reduction.step()
-    key_gradient, value_gradient, mark = unpack(home, partner(others[-1], 1))
-    key_term, value_term = reduction.finish(mark)
+        earlier, after = [blocks[1], blocks[4]], home[-1][1:]
+    key_gradient, value_gradient, key_term, value_term = unpack(
+        home, partner(blocks[1], 1), *reduce_terms(blocks[4], blocks[5])
+    )
     return key_gradient, value_gradient, key_term.T, value_term.T
 
 

time: 85.6 us -> 82 us (0.958)
  starting transfers between devices: 40 us -> 37.5 us
    ppermute x4, waiting for transfers between devices: 6.64 us -> 10.9 us  [the longest x2 6.2 us: reduce_terms(): arrived.append(lax.ppermute(piece, ('dp', 'seq'), route))]
    ppermute x13, waiting for transfers between devices: 19.4 us -> 15.9 us  [partner(): lax.ppermute(block, 'seq', [(i, i ^ k) for i in range(seq)])]
    ppermute x13, starting transfers between devices: 15.3 us -> 13.7 us  [partner(): lax.ppermute(block, 'seq', [(i, i ^ k) for i in range(seq)])]
    ppermute x4, starting transfers between devices: 10.2 us -> 9.14 us  [the longest x2 6.36 us: reduce_terms(): arrived.append(lax.ppermute(piece, ('dp', 'seq'), route))]
    pallas_call x17 -> x13, Pallas kernels: 17 us -> 16.4 us  [call(): pl.pallas_call(kernel, out_shape=out_shape, in_specs=in_specs or [VMEM] *...]
  transfers between devices with their start and end apart: 25 -> 25, of which waited for: 7 -> 9; matrix products, arithmetic and copies ran while one was open for 0% -> 0% of each run, Pallas kernels for 16% -> 15%
where the time goes in v4:
time: 82 us; the launch traced here: 81.7 us
  starting transfers between devices  37.5 us (46%)
  waiting for transfers between devices  26.8 us (33%)
  Pallas kernels  16.4 us (20%)
  between operations  0.92 us (1%)
    pallas_call x13, Pallas kernels, call(): pl.pallas_call(kernel, out_shape=out_shape, in_specs=in_specs or [VMEM] *...  16.4 us
    ppermute x13, waiting for transfers between devices, partner(): lax.ppermute(block, 'seq', [(i, i ^ k) for i in range(seq)])  15.9 us
    ppermute x13, starting transfers between devices, partner(): lax.ppermute(block, 'seq', [(i, i ^ k) for i in range(seq)])  13.7 us
    ppermute x2, starting transfers between devices, body(): lax.ppermute(kv[c][0], 'seq', near_route)  6.88 us
    ppermute x2, starting transfers between devices, reduce_terms(): arrived.append(lax.ppermute(piece, ('dp', 'seq'), route))  6.36 us
    ppermute x2, waiting for transfers between devices, reduce_terms(): arrived.append(lax.ppermute(piece, ('dp', 'seq'), route))  6.2 us
    ppermute x1, waiting for transfers between devices, body(): from_both = lax.ppermute(to_both, ('dp', 'seq'), both)  4.69 us
    ppermute x2, starting transfers between devices, body(): lax.ppermute(to_a, 'seq', swaps[0])  3.86 us
  transfers between devices with their start and end apart: 25, of which 9 were waited for; matrix products, arithmetic and copies ran while one was open for 0% of the time, Pallas kernels for 15%

profile of v4, /device:TPU:5, one launch (start us, length us, event | category | flops | bytes accessed | tf_op | source)
XLA Modules:
  0.0 81.7 jit_solution(631967599114602257)
XLA Ops:
  0.7 2.3 %pack_side.1 = (bf16[128,1664]{1,0:T(8,128)(2,1)}, bf16[128,1536]{1,0:T(8,128)(2,1)}) custom-call(bf16[1,128,3072]{2,1,0:T(8,128)(2,1)} %keys.1, bf16[1,128,3072]{2,1,0:T(8,128)(2,1)} %values.1, bf16[1,64,128]{2,1,0:T(8,128)(2,1)} %bitcast.6, bf16[1,64,128]{2,1,0:T(8,128)(2,1)} %bitcast.8), custom_call_target="tpu_custom_call" | custom-call | flops 1 | bytes 1 | tf_op jit(solution)/shard_map/pack_side/pallas_call | solution.py:30
  4.0 1.4 %collective-permute-done.got_ref = bf16[128,1664]{1,0:T(8,128)(2,1)S(1)} collective-permute-done((bf16[128,1664]{1,0:T(8,128)(2,1)}, bf16[128,1664]{1,0:T(8,128)(2,1)S(1)}, u32[]{:S(2)}, u32[]{:S(2)}) %collective-permute-start) | collective-permute-done | bytes 426016 | tf_op jit(solution)/shard_map/ppermute | solution.py:483
  5.6 1.8 %mask.1.refs_0_.mask_ref = f32[120,128]{1,0:T(8,128)S(1)} custom-call(s32[5,16,24]{2,1,0:T(8,128)S(1)} %bitcast.10, s32[16,24]{1,0:T(8,128)S(1)} %bitcast.11, bf16[128,896]{1,0:T(8,128)(2,1)S(1)} %get-tuple-element.52._.mine_ref), custom_call_target="tpu_custom_call" | custom-call | flops 1 | bytes 1 | tf_op jit(solution)/shard_map/mask/pallas_call | solution.py:30
  8.0 3.7 %collective-permute-start.2 = (bf16[256,896]{1,0:T(8,128)(2,1)S(1)}, bf16[256,896]{1,0:T(8,128)(2,1)S(1)}, u32[]{:S(2)}, u32[]{:S(2)}) collective-permute-start(bf16[256,896]{1,0:T(8,128)(2,1)S(1)} %get-tuple-element.55.refs_0_), channel_id=1, source_target_pairs={{2,6},{3,7},{4,0},{5,1},{6,10},{7,11},{8,4},{9,5},{10,14},{11,15},... | collective-permute-start | bytes 1376264 | tf_op jit(solution)/shard_map/ppermute | solution.py:517
  12.2 5.1 %collective-permute-done.1.refs_0_.refs_1_ = bf16[256,896]{1,0:T(8,128)(2,1)S(1)} collective-permute-done((bf16[256,896]{1,0:T(8,128)(2,1)S(1)}, bf16[256,896]{1,0:T(8,128)(2,1)S(1)}, u32[]{:S(2)}, u32[]{:S(2)}) %collective-permute-start.1) | collective-permute-done | bytes 458784 | tf_op jit(solution)/shard_map/ppermute | solution.py:483
  18.6 2.2 %collective-permute-start.5 = (bf16[256,768]{1,0:T(8,128)(2,1)S(1)}, bf16[256,768]{1,0:T(8,128)(2,1)S(1)}, u32[]{:S(2)}, u32[]{:S(2)}) collective-permute-start(bf16[256,768]{1,0:T(8,128)(2,1)S(1)} %get-tuple-element.61), channel_id=1, source_target_pairs={{0,2},{1,3},{2,0},{3,1},{4,6},{5,7},{6,4},{7,5},{8,10},{9,11},{10,... | collective-permute-start | bytes 1179656 | tf_op jit(solution)/shard_map/ppermute | solution.py:483
  20.9 3.2 %collective-permute-start.12 = (bf16[256,768]{1,0:T(8,128)(2,1)S(1)}, bf16[256,768]{1,0:T(8,128)(2,1)S(1)}, u32[]{:S(2)}, u32[]{:S(2)}) collective-permute-start(bf16[256,768]{1,0:T(8,128)(2,1)S(1)} %get-tuple-element.72.refs_0_), channel_id=1, source_target_pairs={{2,6},{3,7},{4,0},{5,1},{6,10},{7,11},{8,4},{9,5},{10,14},{11,15},... | collective-permute-start | bytes 1179656 | tf_op jit(solution)/shard_map/ppermute | solution.py:517
  24.1 1.6 %collective-permute-done.11.refs_1_ = bf16[256,768]{1,0:T(8,128)(2,1)S(1)} collective-permute-done((bf16[256,768]{1,0:T(8,128)(2,1)S(1)}, bf16[256,768]{1,0:T(8,128)(2,1)S(1)}, u32[]{:S(2)}, u32[]{:S(2)}) %collective-permute-start.11) | collective-permute-done | bytes 393248 | tf_op jit(solution)/shard_map/ppermute | solution.py:483
  27.0 2.2 %collective-permute-start.15 = (bf16[256,768]{1,0:T(8,128)(2,1)S(1)}, bf16[256,768]{1,0:T(8,128)(2,1)S(1)}, u32[]{:S(2)}, u32[]{:S(2)}) collective-permute-start(bf16[256,768]{1,0:T(8,128)(2,1)S(1)} %get-tuple-element.78), channel_id=1, source_target_pairs={{0,2},{1,3},{2,0},{3,1},{4,6},{5,7},{6,4},{7,5},{8,10},{9,11},{10,... | collective-permute-start | bytes 1179656 | tf_op jit(solution)/shard_map/ppermute | solution.py:483
  29.3 4.8 %collective-permute-done.5.refs_5_ = bf16[256,768]{1,0:T(8,128)(2,1)S(1)} collective-permute-done((bf16[256,768]{1,0:T(8,128)(2,1)S(1)}, bf16[256,768]{1,0:T(8,128)(2,1)S(1)}, u32[]{:S(2)}, u32[]{:S(2)}) %collective-permute-start.5) | collective-permute-done | bytes 393248 | tf_op jit(solution)/shard_map/ppermute | solution.py:483
  34.1 5.0 %gradients_0.1 = (f32[512,768]{1,0:T(8,128)S(1)}, bf16[256,896]{1,0:T(8,128)(2,1)S(1)}, bf16[256,768]{1,0:T(8,128)(2,1)S(1)}, f32[128,128]{1,0:T(8,128)S(1)}, f3...) custom-call(f32[120,128]{1,0:T(8,128)S(1)} %mask.1.refs_0_.mask_ref, ...), custom_call_target="tpu_custom_call" | custom-call | flops 1 | bytes 1 | tf_op jit(solution)/shard_map/gradients_0/pallas_call | solution.py:30
  39.2 1.3 %collective-permute-start.6 = (bf16[256,896]{1,0:T(8,128)(2,1)S(1)}, bf16[256,896]{1,0:T(8,128)(2,1)S(1)}, u32[]{:S(2)}, u32[]{:S(2)}) collective-permute-start(bf16[256,896]{1,0:T(8,128)(2,1)S(1)} %get-tuple-element.63), channel_id=1, source_target_pairs={{0,4},{4,0},{1,5},{5,1},{2,6},{6,2},{3,7},{7,3},{8,12},{12,8},{9,1... | collective-permute-start | bytes 1376264 | tf_op jit(solution)/shard_map/ppermute | solution.py:522
  41.2 1.3 %collective-permute-done.15.refs_5_ = bf16[256,768]{1,0:T(8,128)(2,1)S(1)} collective-permute-done((bf16[256,768]{1,0:T(8,128)(2,1)S(1)}, bf16[256,768]{1,0:T(8,128)(2,1)S(1)}, u32[]{:S(2)}, u32[]{:S(2)}) %collective-permute-start.15) | collective-permute-done | bytes 393248 | tf_op jit(solution)/shard_map/ppermute | solution.py:483
  42.5 5.0 %gradients_1.1 = (f32[512,768]{1,0:T(8,128)S(1)}, bf16[256,896]{1,0:T(8,128)(2,1)S(1)}, bf16[256,768]{1,0:T(8,128)(2,1)S(1)}, f32[128,128]{1,0:T(8,128)S(1)}, f3...) custom-call(f32[120,128]{1,0:T(8,128)S(1)} %mask.1.refs_0_.mask_ref, ...), custom_call_target="tpu_custom_call" | custom-call | flops 1 | bytes 1 | tf_op jit(solution)/shard_map/gradients_1/pallas_call | solution.py:30
  47.5 2.5 %collective-permute-start.16 = (bf16[256,896]{1,0:T(8,128)(2,1)S(1)}, bf16[256,896]{1,0:T(8,128)(2,1)S(1)}, u32[]{:S(2)}, u32[]{:S(2)}) collective-permute-start(bf16[256,896]{1,0:T(8,128)(2,1)S(1)} %get-tuple-element.83), channel_id=1, source_target_pairs={{0,4},{4,0},{1,5},{5,1},{2,6},{6,2},{3,7},{7,3},{8,12},{12,8},{9,1... | collective-permute-start | bytes 1376264 | tf_op jit(solution)/shard_map/ppermute | solution.py:522
  52.5 4.5 %collective-permute-start.9 = (bf16[128,768]{1,0:T(8,128)(2,1)S(1)}, bf16[128,768]{1,0:T(8,128)(2,1)S(1)}, u32[]{:S(2)}, u32[]{:S(2)}) collective-permute-start(bf16[128,768]{1,0:T(8,128)(2,1)S(1)} %get-tuple-element.68), channel_id=1, source_target_pairs={{0,3},{1,2},{2,1},{3,0},{4,7},{5,6},{6,5},{7,4},{8,11},{9,10},{10,... | collective-permute-start | bytes 589832 | tf_op jit(solution)/shard_map/ppermute | solution.py:483
  57.1 1.5 %collective-permute-start.19 = (f32[2,128,128]{2,1,0:T(8,128)S(1)}, f32[2,128,128]{2,1,0:T(8,128)S(1)}, u32[]{:S(2)}, u32[]{:S(2)}) collective-permute-start(f32[2,128,128]{2,1,0:T(8,128)S(1)} %get-tuple-element.89), channel_id=1, source_target_pairs={{0,20},{1,21},{2,22},{3,23},{4,16},{5,17},{6,18},{7,19},{8,28},{9,... | collective-permute-start | bytes 393224 | tf_op jit(solution)/shard_map/ppermute | solution.py:528
  58.6 4.7 %collective-permute-done.19.refs_3_ = f32[2,128,128]{2,1,0:T(8,128)S(1)} collective-permute-done((f32[2,128,128]{2,1,0:T(8,128)S(1)}, f32[2,128,128]{2,1,0:T(8,128)S(1)}, u32[]{:S(2)}, u32[]{:S(2)}) %collective-permute-start.19) | collective-permute-done | bytes 131104 | tf_op jit(solution)/shard_map/ppermute | solution.py:528
  63.3 1.6 %collective-permute-done.9.refs_5_.refs_2_ = bf16[128,768]{1,0:T(8,128)(2,1)S(1)} collective-permute-done((bf16[128,768]{1,0:T(8,128)(2,1)S(1)}, bf16[128,768]{1,0:T(8,128)(2,1)S(1)}, u32[]{:S(2)}, u32[]{:S(2)}) %collective-permute-start.9) | collective-permute-done | bytes 196640 | tf_op jit(solution)/shard_map/ppermute | solution.py:483
  66.3 1.5 %collective-permute-start.21 = (bf16[128,768]{1,0:T(8,128)(2,1)S(1)}, bf16[128,768]{1,0:T(8,128)(2,1)S(1)}, u32[]{:S(2)}, u32[]{:S(2)}) collective-permute-start(bf16[128,768]{1,0:T(8,128)(2,1)S(1)} %get-tuple-element.92), channel_id=1, source_target_pairs={{0,3},{1,2},{2,1},{3,0},{4,7},{5,6},{6,5},{7,4},{8,11},{9,10},{10,... | collective-permute-start | bytes 589832 | tf_op jit(solution)/shard_map/ppermute | solution.py:483
  67.8 5.2 %collective-permute-start.23 = (f32[128,128]{1,0:T(8,128)S(1)}, f32[128,128]{1,0:T(8,128)S(1)}, u32[]{:S(2)}, u32[]{:S(2)}) collective-permute-start(f32[128,128]{1,0:T(8,128)S(1)} %get-tuple-element.94), channel_id=1, source_target_pairs={{0,0},{1,4},{2,8},{3,12},{4,2},{5,6},{6,10},{7,14},{8,16},{9,20},{... | collective-permute-start | bytes 196616 | tf_op jit(solution)/shard_map/ppermute | solution.py:465
  74.2 1.5 %collective-permute-done.23.refs_7_ = f32[128,128]{1,0:T(8,128)S(1)} collective-permute-done((f32[128,128]{1,0:T(8,128)S(1)}, f32[128,128]{1,0:T(8,128)S(1)}, u32[]{:S(2)}, u32[]{:S(2)}) %collective-permute-start.23) | collective-permute-done | bytes 65568 | tf_op jit(solution)/shard_map/ppermute | solution.py:465
  75.6 4.7 %collective-permute-done.24.refs_8_ = f32[128,128]{1,0:T(8,128)S(1)} collective-permute-done((f32[128,128]{1,0:T(8,128)S(1)}, f32[128,128]{1,0:T(8,128)S(1)}, u32[]{:S(2)}, u32[]{:S(2)}) %collective-permute-start.24) | collective-permute-done | bytes 65568 | tf_op jit(solution)/shard_map/ppermute | solution.py:465
  80.4 1.3 %unpack.1 = (bf16[1,128,3072]{2,1,0:T(8,128)(2,1)}, bf16[1,128,3072]{2,1,0:T(8,128)(2,1)}, f32[64,96]{1,0:T(8,128)}, f32[64,96]{1,0:T(8,128)}) custom-call(bf16[128,768]{1,0:T(8,128)(2,1)S(1)} %get-tuple-element.66.refs_0_, bf16[128,768]{1,0:T(8,128)(2,1)S(1)} %collective-permute-done.8.refs_4_.refs_1_, ...), custom_call_target="tpu_custom_call" | custom-call | flops 1 | bytes 1 | tf_op jit(solution)/shard_map/unpack/pallas_call | solution.py:30
  (55 shorter events, 10.6 us)
Async XLA Ops:
  3.8 8.3 %collective-permute-start.10 = (bf16[128,1536]{1,0:T(8,128)(2,1)}, bf16[128,1536]{1,0:T(8,128)(2,1)S(1)}, u32[]{:S(2)}, u32[]{:S(2)}) collective-permute-start(bf16[128,1536]{1,0:T(8,128)(2,1)} %get-tuple-element.71), channel_id=1, source_target_pairs={{0,1},{1,0},{2,3},{3,2},{4,5},{5,4},{6,7},{7,6},{8,9},{9,8},{10,11... | collective-permute-start | bytes 1179656 | tf_op jit(solution)/shard_map/ppermute | solution.py:483
  5.5 11.8 %collective-permute-start.1 = (bf16[256,896]{1,0:T(8,128)(2,1)S(1)}, bf16[256,896]{1,0:T(8,128)(2,1)S(1)}, u32[]{:S(2)}, u32[]{:S(2)}) collective-permute-start(bf16[256,896]{1,0:T(8,128)(2,1)S(1)} %get-tuple-element.56), channel_id=1, source_target_pairs={{0,2},{1,3},{2,0},{3,1},{4,6},{5,7},{6,4},{7,5},{8,10},{9,11},{10,... | collective-permute-start | bytes 1376264 | tf_op jit(solution)/shard_map/ppermute | solution.py:483
  7.6 11.0 %collective-permute-start.4 = (bf16[128,1536]{1,0:T(8,128)(2,1)S(1)}, bf16[128,1536]{1,0:T(8,128)(2,1)S(1)}, u32[]{:S(2)}, u32[]{:S(2)}) collective-permute-start(bf16[128,1536]{1,0:T(8,128)(2,1)S(1)} %get-tuple-element.59), channel_id=1, source_target_pairs={{0,1},{1,0},{2,3},{3,2},{4,5},{5,4},{6,7},{7,6},{8,9},{9,8},{10,11... | collective-permute-start | bytes 1179656 | tf_op jit(solution)/shard_map/ppermute | solution.py:483
  8.0 19.0 %collective-permute-start.2 = (bf16[256,896]{1,0:T(8,128)(2,1)S(1)}, bf16[256,896]{1,0:T(8,128)(2,1)S(1)}, u32[]{:S(2)}, u32[]{:S(2)}) collective-permute-start(bf16[256,896]{1,0:T(8,128)(2,1)S(1)} %get-tuple-element.55.refs_0_), channel_id=1, source_target_pairs={{2,6},{3,7},{4,0},{5,1},{6,10},{7,11},{8,4},{9,5},{10,14},{11,15},... | collective-permute-start | bytes 1376264 | tf_op jit(solution)/shard_map/ppermute | solution.py:517
  11.7 9.2 %collective-permute-start.14 = (bf16[128,1536]{1,0:T(8,128)(2,1)S(1)}, bf16[128,1536]{1,0:T(8,128)(2,1)S(1)}, u32[]{:S(2)}, u32[]{:S(2)}) collective-permute-start(bf16[128,1536]{1,0:T(8,128)(2,1)S(1)} %get-tuple-element.76), channel_id=1, source_target_pairs={{0,1},{1,0},{2,3},{3,2},{4,5},{5,4},{6,7},{7,6},{8,9},{9,8},{10,11... | collective-permute-start | bytes 1179656 | tf_op jit(solution)/shard_map/ppermute | solution.py:483
  12.1 13.6 %collective-permute-start.11 = (bf16[256,768]{1,0:T(8,128)(2,1)S(1)}, bf16[256,768]{1,0:T(8,128)(2,1)S(1)}, u32[]{:S(2)}, u32[]{:S(2)}) collective-permute-start(bf16[256,768]{1,0:T(8,128)(2,1)S(1)} %get-tuple-element.73), channel_id=1, source_target_pairs={{0,2},{1,3},{2,0},{3,1},{4,6},{5,7},{6,4},{7,5},{8,10},{9,11},{10,... | collective-permute-start | bytes 1179656 | tf_op jit(solution)/shard_map/ppermute | solution.py:483
  17.3 16.9 %collective-permute-start.3 = (bf16[256,896]{1,0:T(8,128)(2,1)S(1)}, bf16[256,896]{1,0:T(8,128)(2,1)S(1)}, u32[]{:S(2)}, u32[]{:S(2)}) collective-permute-start(bf16[256,896]{1,0:T(8,128)(2,1)S(1)} %collective-permute-done.1.refs_0_.refs_1_), channel_id=1, source_target_pairs={{6,2},{7,3},{0,4},{1,5},{10,6},{11,7},{4,8},{5,9},{14,10},{15,11},... | collective-permute-start | bytes 1376264 | tf_op jit(solution)/shard_map/ppermute | solution.py:517
  18.6 15.5 %collective-permute-start.5 = (bf16[256,768]{1,0:T(8,128)(2,1)S(1)}, bf16[256,768]{1,0:T(8,128)(2,1)S(1)}, u32[]{:S(2)}, u32[]{:S(2)}) collective-permute-start(bf16[256,768]{1,0:T(8,128)(2,1)S(1)} %get-tuple-element.61), channel_id=1, source_target_pairs={{0,2},{1,3},{2,0},{3,1},{4,6},{5,7},{6,4},{7,5},{8,10},{9,11},{10,... | collective-permute-start | bytes 1179656 | tf_op jit(solution)/shard_map/ppermute | solution.py:483
  20.9 20.3 %collective-permute-start.12 = (bf16[256,768]{1,0:T(8,128)(2,1)S(1)}, bf16[256,768]{1,0:T(8,128)(2,1)S(1)}, u32[]{:S(2)}, u32[]{:S(2)}) collective-permute-start(bf16[256,768]{1,0:T(8,128)(2,1)S(1)} %get-tuple-element.72.refs_0_), channel_id=1, source_target_pairs={{2,6},{3,7},{4,0},{5,1},{6,10},{7,11},{8,4},{9,5},{10,14},{11,15},... | collective-permute-start | bytes 1179656 | tf_op jit(solution)/shard_map/ppermute | solution.py:517
  25.7 15.5 %collective-permute-start.13 = (bf16[256,768]{1,0:T(8,128)(2,1)S(1)}, bf16[256,768]{1,0:T(8,128)(2,1)S(1)}, u32[]{:S(2)}, u32[]{:S(2)}) collective-permute-start(bf16[256,768]{1,0:T(8,128)(2,1)S(1)} %collective-permute-done.11.refs_1_), channel_id=1, source_target_pairs={{6,2},{7,3},{0,4},{1,5},{10,6},{11,7},{4,8},{5,9},{14,10},{15,11},... | collective-permute-start | bytes 1179656 | tf_op jit(solution)/shard_map/ppermute | solution.py:517
  27.0 15.5 %collective-permute-start.15 = (bf16[256,768]{1,0:T(8,128)(2,1)S(1)}, bf16[256,768]{1,0:T(8,128)(2,1)S(1)}, u32[]{:S(2)}, u32[]{:S(2)}) collective-permute-start(bf16[256,768]{1,0:T(8,128)(2,1)S(1)} %get-tuple-element.78), channel_id=1, source_target_pairs={{0,2},{1,3},{2,0},{3,1},{4,6},{5,7},{6,4},{7,5},{8,10},{9,11},{10,... | collective-permute-start | bytes 1179656 | tf_op jit(solution)/shard_map/ppermute | solution.py:483
  39.2 12.9 %collective-permute-start.6 = (bf16[256,896]{1,0:T(8,128)(2,1)S(1)}, bf16[256,896]{1,0:T(8,128)(2,1)S(1)}, u32[]{:S(2)}, u32[]{:S(2)}) collective-permute-start(bf16[256,896]{1,0:T(8,128)(2,1)S(1)} %get-tuple-element.63), channel_id=1, source_target_pairs={{0,4},{4,0},{1,5},{5,1},{2,6},{6,2},{3,7},{7,3},{8,12},{12,8},{9,1... | collective-permute-start | bytes 1376264 | tf_op jit(solution)/shard_map/ppermute | solution.py:522
  40.5 11.5 %collective-permute-start.7 = (bf16[256,768]{1,0:T(8,128)(2,1)S(1)}, bf16[256,768]{1,0:T(8,128)(2,1)S(1)}, u32[]{:S(2)}, u32[]{:S(2)}) collective-permute-start(bf16[256,768]{1,0:T(8,128)(2,1)S(1)} %get-tuple-element.64), channel_id=1, source_target_pairs={{4,8},{8,4},{5,9},{9,5},{6,10},{10,6},{7,11},{11,7},{20,24},{24,20... | collective-permute-start | bytes 1179656 | tf_op jit(solution)/shard_map/ppermute | solution.py:522
  47.5 15.7 %collective-permute-start.16 = (bf16[256,896]{1,0:T(8,128)(2,1)S(1)}, bf16[256,896]{1,0:T(8,128)(2,1)S(1)}, u32[]{:S(2)}, u32[]{:S(2)}) collective-permute-start(bf16[256,896]{1,0:T(8,128)(2,1)S(1)} %get-tuple-element.83), channel_id=1, source_target_pairs={{0,4},{4,0},{1,5},{5,1},{2,6},{6,2},{3,7},{7,3},{8,12},{12,8},{9,1... | collective-permute-start | bytes 1376264 | tf_op jit(solution)/shard_map/ppermute | solution.py:522
  50.1 13.2 %collective-permute-start.17 = (bf16[256,768]{1,0:T(8,128)(2,1)S(1)}, bf16[256,768]{1,0:T(8,128)(2,1)S(1)}, u32[]{:S(2)}, u32[]{:S(2)}) collective-permute-start(bf16[256,768]{1,0:T(8,128)(2,1)S(1)} %get-tuple-element.84), channel_id=1, source_target_pairs={{4,8},{8,4},{5,9},{9,5},{6,10},{10,6},{7,11},{11,7},{20,24},{24,20... | collective-permute-start | bytes 1179656 | tf_op jit(solution)/shard_map/ppermute | solution.py:522
  50.7 6.3 %collective-permute-start.18 = (f32[2,128,128]{2,1,0:T(8,128)S(1)}, f32[2,128,128]{2,1,0:T(8,128)S(1)}, u32[]{:S(2)}, u32[]{:S(2)}) collective-permute-start(f32[2,128,128]{2,1,0:T(8,128)S(1)} %get-tuple-element.88), channel_id=1, source_target_pairs={{0,16},{16,0},{1,17},{17,1},{2,18},{18,2},{3,19},{19,3},{4,20},{20... | collective-permute-start | bytes 393224 | tf_op jit(solution)/shard_map/ppermute | solution.py:524
  52.2 11.0 %collective-permute-start.8 = (bf16[128,768]{1,0:T(8,128)(2,1)S(1)}, bf16[128,768]{1,0:T(8,128)(2,1)S(1)}, u32[]{:S(2)}, u32[]{:S(2)}) collective-permute-start(bf16[128,768]{1,0:T(8,128)(2,1)S(1)} %get-tuple-element.67), channel_id=1, source_target_pairs={{0,2},{1,3},{2,0},{3,1},{4,6},{5,7},{6,4},{7,5},{8,10},{9,11},{10,... | collective-permute-start | bytes 589832 | tf_op jit(solution)/shard_map/ppermute | solution.py:483
  52.5 12.3 %collective-permute-start.9 = (bf16[128,768]{1,0:T(8,128)(2,1)S(1)}, bf16[128,768]{1,0:T(8,128)(2,1)S(1)}, u32[]{:S(2)}, u32[]{:S(2)}) collective-permute-start(bf16[128,768]{1,0:T(8,128)(2,1)S(1)} %get-tuple-element.68), channel_id=1, source_target_pairs={{0,3},{1,2},{2,1},{3,0},{4,7},{5,6},{6,5},{7,4},{8,11},{9,10},{10,... | collective-permute-start | bytes 589832 | tf_op jit(solution)/shard_map/ppermute | solution.py:483
  57.1 6.2 %collective-permute-start.19 = (f32[2,128,128]{2,1,0:T(8,128)S(1)}, f32[2,128,128]{2,1,0:T(8,128)S(1)}, u32[]{:S(2)}, u32[]{:S(2)}) collective-permute-start(f32[2,128,128]{2,1,0:T(8,128)S(1)} %get-tuple-element.89), channel_id=1, source_target_pairs={{0,20},{1,21},{2,22},{3,23},{4,16},{5,17},{6,18},{7,19},{8,28},{9,... | collective-permute-start | bytes 393224 | tf_op jit(solution)/shard_map/ppermute | solution.py:528
  65.1 15.2 %collective-permute-start.22 = (bf16[128,1536]{1,0:T(8,128)(2,1)S(1)}, bf16[128,1536]{1,0:T(8,128)(2,1)S(1)}, u32[]{:S(2)}, u32[]{:S(2)}) collective-permute-start(bf16[128,1536]{1,0:T(8,128)(2,1)S(1)} %get-tuple-element.93), channel_id=1, source_target_pairs={{0,1},{1,0},{2,3},{3,2},{4,5},{5,4},{6,7},{7,6},{8,9},{9,8},{10,11... | collective-permute-start | bytes 1179656 | tf_op jit(solution)/shard_map/ppermute | solution.py:483
  66.1 14.3 %collective-permute-start.20 = (bf16[128,768]{1,0:T(8,128)(2,1)S(1)}, bf16[128,768]{1,0:T(8,128)(2,1)S(1)}, u32[]{:S(2)}, u32[]{:S(2)}) collective-permute-start(bf16[128,768]{1,0:T(8,128)(2,1)S(1)} %get-tuple-element.91), channel_id=1, source_target_pairs={{0,2},{1,3},{2,0},{3,1},{4,6},{5,7},{6,4},{7,5},{8,10},{9,11},{10,... | collective-permute-start | bytes 589832 | tf_op jit(solution)/shard_map/ppermute | solution.py:483
  66.3 14.0 %collective-permute-start.21 = (bf16[128,768]{1,0:T(8,128)(2,1)S(1)}, bf16[128,768]{1,0:T(8,128)(2,1)S(1)}, u32[]{:S(2)}, u32[]{:S(2)}) collective-permute-start(bf16[128,768]{1,0:T(8,128)(2,1)S(1)} %get-tuple-element.92), channel_id=1, source_target_pairs={{0,3},{1,2},{2,1},{3,0},{4,7},{5,6},{6,5},{7,4},{8,11},{9,10},{10,... | collective-permute-start | bytes 589832 | tf_op jit(solution)/shard_map/ppermute | solution.py:483
  67.8 7.8 %collective-permute-start.23 = (f32[128,128]{1,0:T(8,128)S(1)}, f32[128,128]{1,0:T(8,128)S(1)}, u32[]{:S(2)}, u32[]{:S(2)}) collective-permute-start(f32[128,128]{1,0:T(8,128)S(1)} %get-tuple-element.94), channel_id=1, source_target_pairs={{0,0},{1,4},{2,8},{3,12},{4,2},{5,6},{6,10},{7,14},{8,16},{9,20},{... | collective-permute-start | bytes 196616 | tf_op jit(solution)/shard_map/ppermute | solution.py:465
  73.0 7.3 %collective-permute-start.24 = (f32[128,128]{1,0:T(8,128)S(1)}, f32[128,128]{1,0:T(8,128)S(1)}, u32[]{:S(2)}, u32[]{:S(2)}) collective-permute-start(f32[128,128]{1,0:T(8,128)S(1)} %get-tuple-element.95), channel_id=1, source_target_pairs={{0,16},{1,20},{2,24},{3,28},{4,18},{5,22},{6,26},{7,30},{8,0},{9,4... | collective-permute-start | bytes 196616 | tf_op jit(solution)/shard_map/ppermute | solution.py:465
  (9 other events, 29.0 us)

commit v5 on v4

--- a/solution.py
+++ b/solution.py
@@ -75,8 +75,8 @@
 SIDE, OWN, ACROSS = (1, 3), (0,), (2,)
 
 
-def pack_plan(kinds, adapters):
-    return [(span, owners, bool(adapters) and span[0] == 0) for span in spans() for owners in kinds]
+def pack_plan(kinds, adapters, chunks):
+    return [(span, owners, bool(adapters) and span[0] == 0) for span in chunks for owners in kinds]
 
 
 def fill(plan, a_ref, b_ref, outs, part):
@@ -123,15 +123,16 @@
         fill_adapters(plan, refs[0][0], refs[1][0], outs)
 
 
-def pack(name, kinds, first, second, adapters=(), after=(), at_once=False):
-    plan = pack_plan(kinds, adapters)
+def pack(name, kinds, first, second, adapters=(), after=(), only=None):
+    chunks = spans() if only is None else [spans()[only]]
+    plan = pack_plan(kinds, adapters, chunks)
     kind = first.dtype
     out_shape = [
         jax.ShapeDtypeStruct((BLK, (2 * count * len(owners) + adapted) * HEAD_WIDTH), kind)
         for (_, count), owners, adapted in plan
     ]
     inputs = [first, second, *adapters, *after]
-    if at_once:
+    if only is not None:
         scratch = [
             pltpu.VMEM((2, RANK, BLK), kind),
             pltpu.SemaphoreType.DMA((2 + sum(2 * len(owners) for _, owners, _ in plan),)),
@@ -142,7 +143,7 @@
         kernel = functools.partial(pack_kernel, plan, bool(adapters))
         specs = [VMEM] * (2 + len(adapters)) + [ANY] * len(after)
         outs = call(kernel, name, out_shape, inputs, specs)
-    return [outs[len(kinds) * c : len(kinds) * (c + 1)] for c in range(len(CHUNKS))]
+    return [outs[len(kinds) * c : len(kinds) * (c + 1)] for c in range(len(chunks))]
 
 
 def route_kernel(mine_ref, across_ref, got_ref, *refs):
@@ -304,9 +305,9 @@
     a_ref[rows(1, 1), place_] = (leave - whole.astype(jnp.float32)).astype(kind)
     for out, part in ((clip_ref, quarter(False, True)), (both_ref, quarter(True, True))):
         if c == 0:
-            out[:, :width] = part
+            out[:, :width] = part.astype(kind)
         else:
-            out[1, :, :width] = part
+            out[1, :, :width] = part.astype(kind)
     if c == 1:
         clip_ref[0] = earlier[0][...]
         both_ref[0] = earlier[1][...]
@@ -324,7 +325,8 @@
     ]
     part = (2 * RANK, padded(count * HEAD_WIDTH // 4))
     many = part if c == 0 else (2, *part)
-    out_shape += [jax.ShapeDtypeStruct(shape, jnp.float32) for shape in (part, many, many)]
+    out_shape.append(jax.ShapeDtypeStruct(part, jnp.float32))
+    out_shape += [jax.ShapeDtypeStruct(many, kind)] * 2
     if c == 0:
         out_shape.append(jax.ShapeDtypeStruct((2 * RANK, tall), kind))
     inputs = [mask, *kv, *halo, *qg, *earlier]
@@ -366,11 +368,12 @@
     total = keep_ref[...] + got[0] + got[1]
     if last:
         earlier, clip_ref, both_ref = refs[1:4]
-        first = earlier[...] + clip_ref[0] + both_ref[0]
-        second = total + clip_ref[1] + both_ref[1]
+        clip, both = clip_ref[...].astype(jnp.float32), both_ref[...].astype(jnp.float32)
+        first = earlier[...] + clip[0] + both[0]
+        second = total + clip[1] + both[1]
         upper = bit_value(*bit) == 1
-        refs[-2][...] = jnp.where(upper, second, first)
-        refs[-1][...] = jnp.where(upper, first, second)
+        refs[-2][...] = jnp.where(upper, second, first).astype(refs[-2].dtype)
+        refs[-1][...] = jnp.where(upper, first, second).astype(refs[-1].dtype)
     else:
         refs[-1][...] = total
 
@@ -379,7 +382,7 @@
     last = int(c + 1 == len(CHUNKS))
     block = jax.ShapeDtypeStruct((BLK, own.shape[1]), a.dtype)
     wide = jax.ShapeDtypeStruct((BLK, own.shape[1] + (earlier[0].shape[1] if last else 0)), a.dtype)
-    term = jax.ShapeDtypeStruct(keep.shape, keep.dtype)
+    term = jax.ShapeDtypeStruct(keep.shape, a.dtype if last and len(later_rounds()) == 1 else keep.dtype)
     specs = [VMEM] * (4 + len(earlier)) + [ANY] * len(after)
     inputs = [own, a, b, keep, *earlier, *after]
     kernel = functools.partial(combine_kernel, last, bit)
@@ -387,28 +390,23 @@
 
 
 def unpack_kernel(*refs):
-    blocks, other, arrived = refs[: 3 * len(CHUNKS)], refs[3 * len(CHUNKS)], refs[3 * len(CHUNKS) + 1 : -4]
-    outs, terms = refs[-4:-2], refs[-2:]
+    outs, other, blocks = refs[-3:-1], refs[-4], refs[:-4]
+    refs[-1][...] = jnp.zeros_like(refs[-1])
     member, _ = place()
     before = 0
-    for c, (_, count) in enumerate(spans()):
+    for c, (first, count) in enumerate(spans()):
         sources = [(0, blocks[3 * c], 0), (1, other, before), (2, blocks[3 * c + 1], 0), (3, blocks[3 * c + 2], 0)]
         for k, ref, column in sources:
             head = first_head(c, jnp.bitwise_xor(member, k))
             for part, out in enumerate(outs):
                 out[0, :, cols(head, count)] = ref[:, cols(column + part * count, count)]
         before += 2 * count
-    if len(arrived[0].shape) == 3:
-        arrived = [ref.at[0] for ref in arrived]
-    for half, term in zip((slice(0, RANK), slice(RANK, 2 * RANK)), terms):
-        term[...] = sum(ref[half, : term.shape[1]] for ref in arrived)
-
-
-def unpack(home, other, arrived, width):
-    flat = [block for chunk in home for block in chunk] + [other, *arrived]
+
+
+def unpack(home, other):
+    flat = [block for chunk in home for block in chunk] + [other]
     shape = jax.ShapeDtypeStruct((1, BLK, HEAD_COUNT * HEAD_WIDTH), other.dtype)
-    term = jax.ShapeDtypeStruct((RANK, width), jnp.float32)
-    return call(unpack_kernel, "unpack", [shape, shape, term, term], flat)
+    return call(unpack_kernel, "unpack", [shape, shape, MARK], flat)
 
 
 def bit_value(axis, bit, unit):
@@ -422,11 +420,19 @@
         for j in range(half):
             low, high = (slice(i * width, (i + 1) * width) for i in (j, half + j))
             low, high = (held_ref[:, part] + got_ref[:, part] for part in (low, high))
-            keep_ref[j, :, :width] = jnp.where(value == 1, high, low)
-            send_ref[j, :, :width] = jnp.where(value == 1, low, high)
+            keep_ref[j, :, :width] = jnp.where(value == 1, high, low).astype(keep_ref.dtype)
+            send_ref[j, :, :width] = jnp.where(value == 1, low, high).astype(send_ref.dtype)
     else:
         for out, first in ((keep_ref, value * half), (send_ref, (1 - value) * half)):
-            out[...] = held_ref[pl.ds(first, half)] + got_ref[pl.ds(first, half)]
+            out[...] = (held_ref[pl.ds(first, half)] + got_ref[pl.ds(first, half)]).astype(out.dtype)
+
+
+def final_kernel(first_ref, second_ref, _, key_ref, value_ref):
+    width = key_ref.shape[1]
+    if len(first_ref.shape) == 3:
+        first_ref, second_ref = first_ref.at[0], second_ref.at[0]
+    for half, out in ((slice(0, RANK), key_ref), (slice(RANK, 2 * RANK), value_ref)):
+        out[...] = first_ref[half, :width].astype(jnp.float32) + second_ref[half, :width].astype(jnp.float32)
 
 
 def later_rounds():
@@ -436,7 +442,7 @@
     return [("dp", bit, 1) for bit in clip_bits] + [("seq", bit, TEAM) for bit in team_bits]
 
 
-def reduce_terms(held, sent):
+def reduce_terms(held, sent, after):
     clips, seq = lax.axis_size("dp"), lax.axis_size("seq")
     teams = seq // TEAM
     pieces = clips * teams
@@ -451,7 +457,8 @@
     for index, (axis, bit, unit) in enumerate(rounds[:-1]):
         route = [(i, i ^ (bit * unit)) for i in range(lax.axis_size(axis))]
         got = lax.ppermute(sent, axis, route)
-        shape = jax.ShapeDtypeStruct((pieces >> (index + 4), 2 * RANK, padded(width)), jnp.float32)
+        kind = jnp.bfloat16 if index + 2 == len(rounds) else jnp.float32
+        shape = jax.ShapeDtypeStruct((pieces >> (index + 4), 2 * RANK, padded(width)), kind)
         kernel = functools.partial(fold_kernel, rounds[index + 1], width)
         held, sent = call(kernel, f"fold_{index}", [shape, shape], [held, got])
     arrived = []
@@ -463,7 +470,8 @@
                 c, index = divmod(piece_of(clip, position // TEAM) ^ other, pieces // 2)
                 route.append((clip * seq + position, (c * TEAM + position % TEAM) * pieces // 2 + index))
         arrived.append(lax.ppermute(piece, ("dp", "seq"), route))
-    return arrived, width
+    shape = jax.ShapeDtypeStruct((RANK, width), jnp.float32)
+    return call(final_kernel, "final", [shape, shape], [*arrived, after], [VMEM, VMEM, ANY])
 
 
 def body(
@@ -499,15 +507,15 @@
     lists = key_block_lists.transpose(2, 1, 0)
     counts = live_block_counts.T
     adapters = (key_adapter_input.transpose(0, 2, 1), value_adapter_input.transpose(0, 2, 1))
-    sides = pack("pack_side", (SIDE,), head_keys, head_values, adapters, at_once=True)
-    kv_side = [partner(side, 1) for (side,) in sides]
-    kv_out = pack("pack_kv", (OWN, ACROSS), head_keys, head_values, adapters)
-    mask = make_mask(lists, counts, kv_out[0][0])
+    ((side,),) = pack("pack_side", (SIDE,), head_keys, head_values, adapters, only=0)
+    kv_out = pack("pack_kv", (SIDE, OWN, ACROSS), head_keys, head_values, adapters)
+    kv_side = [partner(side if c == 0 else kv_out[c][0], 1) for c in range(len(CHUNKS))]
+    mask = make_mask(lists, counts, kv_out[0][1])
     qg_out = pack("pack_qg", (SIDE, OWN, ACROSS), head_queries, output_gradient, after=[mask])
     qg_side = [partner(side, 1) for side, _, _ in qg_out]
     kv, halo, qg = [], [], []
     for c in range(len(CHUNKS)):
-        (mine, across), got = kv_out[c], kv_side[c]
+        (_, mine, across), got = kv_out[c], kv_side[c]
         chip, send = route(f"route_kv_{c}", mine, across, got)
         kv.append((chip, partner(send, 2)))
     for c in range(len(CHUNKS)):
@@ -533,9 +541,8 @@
         blocks = combine(c, later_rounds()[0], *part, given, after)
         home.append([blocks[0], partner(blocks[2], 2), partner(blocks[3], 3)])
         earlier, after = [blocks[1], blocks[4]], home[-1][1:]
-    key_gradient, value_gradient, key_term, value_term = unpack(
-        home, partner(blocks[1], 1), *reduce_terms(blocks[4], blocks[5])
-    )
+    key_gradient, value_gradient, mark = unpack(home, partner(blocks[1], 1))
+    key_term, value_term = reduce_terms(blocks[4], blocks[5], mark)
     return key_gradient, value_gradient, key_term.T, value_term.T
 
 

time: 82 us -> 80.1 us (0.977)
  waiting for transfers between devices: 26.8 us -> 22.3 us
  Pallas kernels: 16.4 us -> 17.7 us
  starting transfers between devices: 37.5 us -> 38.8 us
    ppermute x2, waiting for transfers between devices: 6.2 us -> 1.65 us  [reduce_terms(): arrived.append(lax.ppermute(piece, ('dp', 'seq'), route))]
    ppermute x1, waiting for transfers between devices: 4.69 us -> 2.42 us  [body(): from_both = lax.ppermute(to_both, ('dp', 'seq'), both)]
    ppermute x1, waiting for transfers between devices: 0.01 us -> 2.24 us  [body(): lax.ppermute(to_clip, 'dp', [(i, i ^ clips // 2) for i in range(clips)])]
    pallas_call x13 -> x14, Pallas kernels: 16.4 us -> 17.7 us  [call(): pl.pallas_call(kernel, out_shape=out_shape, in_specs=in_specs or [VMEM] *...]
    ppermute x2, starting transfers between devices: 6.36 us -> 7.31 us  [reduce_terms(): arrived.append(lax.ppermute(piece, ('dp', 'seq'), route))]
    ppermute x1, starting transfers between devices: 1.49 us -> 2.37 us  [body(): from_both = lax.ppermute(to_both, ('dp', 'seq'), both)]
  transfers between devices with their start and end apart: 25 -> 25, of which waited for: 9 -> 9; matrix products, arithmetic and copies ran while one was open for 0% -> 0% of each run, Pallas kernels for 15% -> 19%
where the time goes in v5:
time: 80.1 us; the launch traced here: 79.8 us
  starting transfers between devices  38.8 us (48%)
  waiting for transfers between devices  22.3 us (28%)
  Pallas kernels  17.7 us (22%)
  between operations  0.94 us (1%)
    pallas_call x14, Pallas kernels, call(): pl.pallas_call(kernel, out_shape=out_shape, in_specs=in_specs or [VMEM] *...  17.7 us
    ppermute x13, waiting for transfers between devices, partner(): lax.ppermute(block, 'seq', [(i, i ^ k) for i in range(seq)])  16 us
    ppermute x13, starting transfers between devices, partner(): lax.ppermute(block, 'seq', [(i, i ^ k) for i in range(seq)])  13.1 us
    ppermute x2, starting transfers between devices, reduce_terms(): arrived.append(lax.ppermute(piece, ('dp', 'seq'), route))  7.31 us
    ppermute x2, starting transfers between devices, body(): lax.ppermute(kv[c][0], 'seq', near_route)  6.88 us
    ppermute x2, starting transfers between devices, body(): lax.ppermute(to_a, 'seq', swaps[0])  3.96 us
    ppermute x2, starting transfers between devices, body(): lax.ppermute(kv[c][1], 'seq', far_route)  2.56 us
    ppermute x1, waiting for transfers between devices, body(): from_both = lax.ppermute(to_both, ('dp', 'seq'), both)  2.42 us
  transfers between devices with their start and end apart: 25, of which 9 were waited for; matrix products, arithmetic and copies ran while one was open for 0% of the time, Pallas kernels for 19%

profile of v5, /device:TPU:5, one launch (start us, length us, event | category | flops | bytes accessed | tf_op | source)
XLA Modules:
  0.0 79.8 jit_solution(16423284071283038706)
XLA Ops:
  0.7 2.0 %pack_side.1 = bf16[128,1664]{1,0:T(8,128)(2,1)} custom-call(bf16[1,128,3072]{2,1,0:T(8,128)(2,1)} %keys.1, bf16[1,128,3072]{2,1,0:T(8,128)(2,1)} %values.1, bf16[1,64,128]{2,1,0:T(8,128)(2,1)} %bitcast.6, bf16[1,64,128]{2,1,0:T(8,128)(2,1)} %bitcast.8), custom_call_target="tpu_custom_call" | custom-call | flops 1 | bytes 1 | tf_op jit(solution)/shard_map/pack_side/pallas_call | solution.py:30
  5.2 1.8 %mask.1.refs_0_.mask_ref = f32[120,128]{1,0:T(8,128)S(1)} custom-call(s32[5,16,24]{2,1,0:T(8,128)S(1)} %bitcast.10, s32[16,24]{1,0:T(8,128)S(1)} %bitcast.11, bf16[128,896]{1,0:T(8,128)(2,1)S(1)} %get-tuple-element.52._.mine_ref), custom_call_target="tpu_custom_call" | custom-call | flops 1 | bytes 1 | tf_op jit(solution)/shard_map/mask/pallas_call | solution.py:30
  7.7 3.7 %collective-permute-start.2 = (bf16[256,896]{1,0:T(8,128)(2,1)S(1)}, bf16[256,896]{1,0:T(8,128)(2,1)S(1)}, u32[]{:S(2)}, u32[]{:S(2)}) collective-permute-start(bf16[256,896]{1,0:T(8,128)(2,1)S(1)} %get-tuple-element.54.refs_0_), channel_id=1, source_target_pairs={{2,6},{3,7},{4,0},{5,1},{6,10},{7,11},{8,4},{9,5},{10,14},{11,15},... | collective-permute-start | bytes 1376264 | tf_op jit(solution)/shard_map/ppermute | solution.py:525
  11.9 5.1 %collective-permute-done.1.refs_0_.refs_1_ = bf16[256,896]{1,0:T(8,128)(2,1)S(1)} collective-permute-done((bf16[256,896]{1,0:T(8,128)(2,1)S(1)}, bf16[256,896]{1,0:T(8,128)(2,1)S(1)}, u32[]{:S(2)}, u32[]{:S(2)}) %collective-permute-start.1) | collective-permute-done | bytes 458784 | tf_op jit(solution)/shard_map/ppermute | solution.py:491
  16.9 1.3 %collective-permute-start.3 = (bf16[256,896]{1,0:T(8,128)(2,1)S(1)}, bf16[256,896]{1,0:T(8,128)(2,1)S(1)}, u32[]{:S(2)}, u32[]{:S(2)}) collective-permute-start(bf16[256,896]{1,0:T(8,128)(2,1)S(1)} %collective-permute-done.1.refs_0_.refs_1_), channel_id=1, source_target_pairs={{6,2},{7,3},{0,4},{1,5},{10,6},{11,7},{4,8},{5,9},{14,10},{15,11},... | collective-permute-start | bytes 1376264 | tf_op jit(solution)/shard_map/ppermute | solution.py:525
  18.3 2.2 %collective-permute-start.5 = (bf16[256,768]{1,0:T(8,128)(2,1)S(1)}, bf16[256,768]{1,0:T(8,128)(2,1)S(1)}, u32[]{:S(2)}, u32[]{:S(2)}) collective-permute-start(bf16[256,768]{1,0:T(8,128)(2,1)S(1)} %get-tuple-element.60), channel_id=1, source_target_pairs={{0,2},{1,3},{2,0},{3,1},{4,6},{5,7},{6,4},{7,5},{8,10},{9,11},{10,... | collective-permute-start | bytes 1179656 | tf_op jit(solution)/shard_map/ppermute | solution.py:491
  20.5 3.2 %collective-permute-start.12 = (bf16[256,768]{1,0:T(8,128)(2,1)S(1)}, bf16[256,768]{1,0:T(8,128)(2,1)S(1)}, u32[]{:S(2)}, u32[]{:S(2)}) collective-permute-start(bf16[256,768]{1,0:T(8,128)(2,1)S(1)} %get-tuple-element.71.refs_0_), channel_id=1, source_target_pairs={{2,6},{3,7},{4,0},{5,1},{6,10},{7,11},{8,4},{9,5},{10,14},{11,15},... | collective-permute-start | bytes 1179656 | tf_op jit(solution)/shard_map/ppermute | solution.py:525
  23.7 1.6 %collective-permute-done.11.refs_1_ = bf16[256,768]{1,0:T(8,128)(2,1)S(1)} collective-permute-done((bf16[256,768]{1,0:T(8,128)(2,1)S(1)}, bf16[256,768]{1,0:T(8,128)(2,1)S(1)}, u32[]{:S(2)}, u32[]{:S(2)}) %collective-permute-start.11) | collective-permute-done | bytes 393248 | tf_op jit(solution)/shard_map/ppermute | solution.py:491
  25.4 1.3 %collective-permute-start.13 = (bf16[256,768]{1,0:T(8,128)(2,1)S(1)}, bf16[256,768]{1,0:T(8,128)(2,1)S(1)}, u32[]{:S(2)}, u32[]{:S(2)}) collective-permute-start(bf16[256,768]{1,0:T(8,128)(2,1)S(1)} %collective-permute-done.11.refs_1_), channel_id=1, source_target_pairs={{6,2},{7,3},{0,4},{1,5},{10,6},{11,7},{4,8},{5,9},{14,10},{15,11},... | collective-permute-start | bytes 1179656 | tf_op jit(solution)/shard_map/ppermute | solution.py:525
  26.7 2.2 %collective-permute-start.15 = (bf16[256,768]{1,0:T(8,128)(2,1)S(1)}, bf16[256,768]{1,0:T(8,128)(2,1)S(1)}, u32[]{:S(2)}, u32[]{:S(2)}) collective-permute-start(bf16[256,768]{1,0:T(8,128)(2,1)S(1)} %get-tuple-element.77), channel_id=1, source_target_pairs={{0,2},{1,3},{2,0},{3,1},{4,6},{5,7},{6,4},{7,5},{8,10},{9,11},{10,... | collective-permute-start | bytes 1179656 | tf_op jit(solution)/shard_map/ppermute | solution.py:491
  29.0 4.8 %collective-permute-done.5.refs_5_ = bf16[256,768]{1,0:T(8,128)(2,1)S(1)} collective-permute-done((bf16[256,768]{1,0:T(8,128)(2,1)S(1)}, bf16[256,768]{1,0:T(8,128)(2,1)S(1)}, u32[]{:S(2)}, u32[]{:S(2)}) %collective-permute-start.5) | collective-permute-done | bytes 393248 | tf_op jit(solution)/shard_map/ppermute | solution.py:491
  33.8 5.1 %gradients_0.1 = (f32[512,768]{1,0:T(8,128)S(1)}, bf16[256,896]{1,0:T(8,128)(2,1)S(1)}, bf16[256,768]{1,0:T(8,128)(2,1)S(1)}, f32[128,128]{1,0:T(8,128)S(1)}, bf...) custom-call(f32[120,128]{1,0:T(8,128)S(1)} %mask.1.refs_0_.mask_ref, ...), custom_call_target="tpu_custom_call" | custom-call | flops 1 | bytes 1 | tf_op jit(solution)/shard_map/gradients_0/pallas_call | solution.py:30
  38.9 1.3 %collective-permute-start.6 = (bf16[256,896]{1,0:T(8,128)(2,1)S(1)}, bf16[256,896]{1,0:T(8,128)(2,1)S(1)}, u32[]{:S(2)}, u32[]{:S(2)}) collective-permute-start(bf16[256,896]{1,0:T(8,128)(2,1)S(1)} %get-tuple-element.62), channel_id=1, source_target_pairs={{0,4},{4,0},{1,5},{5,1},{2,6},{6,2},{3,7},{7,3},{8,12},{12,8},{9,1... | collective-permute-start | bytes 1376264 | tf_op jit(solution)/shard_map/ppermute | solution.py:530
  42.2 5.1 %gradients_1.1 = (f32[512,768]{1,0:T(8,128)S(1)}, bf16[256,896]{1,0:T(8,128)(2,1)S(1)}, bf16[256,768]{1,0:T(8,128)(2,1)S(1)}, f32[128,128]{1,0:T(8,128)S(1)}, bf...) custom-call(f32[120,128]{1,0:T(8,128)S(1)} %mask.1.refs_0_.mask_ref, ...), custom_call_target="tpu_custom_call" | custom-call | flops 1 | bytes 1 | tf_op jit(solution)/shard_map/gradients_1/pallas_call | solution.py:30
  47.3 2.6 %collective-permute-start.16 = (bf16[256,896]{1,0:T(8,128)(2,1)S(1)}, bf16[256,896]{1,0:T(8,128)(2,1)S(1)}, u32[]{:S(2)}, u32[]{:S(2)}) collective-permute-start(bf16[256,896]{1,0:T(8,128)(2,1)S(1)} %get-tuple-element.82), channel_id=1, source_target_pairs={{0,4},{4,0},{1,5},{5,1},{2,6},{6,2},{3,7},{7,3},{8,12},{12,8},{9,1... | collective-permute-start | bytes 1376264 | tf_op jit(solution)/shard_map/ppermute | solution.py:530
  51.2 4.3 %collective-permute-start.9 = (bf16[128,768]{1,0:T(8,128)(2,1)S(1)}, bf16[128,768]{1,0:T(8,128)(2,1)S(1)}, u32[]{:S(2)}, u32[]{:S(2)}) collective-permute-start(bf16[128,768]{1,0:T(8,128)(2,1)S(1)} %get-tuple-element.67), channel_id=1, source_target_pairs={{0,3},{1,2},{2,1},{3,0},{4,7},{5,6},{6,5},{7,4},{8,11},{9,10},{10,... | collective-permute-start | bytes 589832 | tf_op jit(solution)/shard_map/ppermute | solution.py:491
  56.6 2.2 %collective-permute-done.18.refs_2_ = bf16[2,128,128]{2,1,0:T(8,128)(2,1)S(1)} collective-permute-done((bf16[2,128,128]{2,1,0:T(8,128)(2,1)S(1)}, bf16[2,128,128]{2,1,0:T(8,128)(2,1)S(1)}, u32[]{:S(2)}, u32[]{:S(2)}) %collective-permute-start.18) | collective-permute-done | bytes 65568 | tf_op jit(solution)/shard_map/ppermute | solution.py:532
  58.9 2.4 %collective-permute-start.19 = (bf16[2,128,128]{2,1,0:T(8,128)(2,1)S(1)}, bf16[2,128,128]{2,1,0:T(8,128)(2,1)S(1)}, u32[]{:S(2)}, u32[]{:S(2)}) collective-permute-start(bf16[2,128,128]{2,1,0:T(8,128)(2,1)S(1)} %get-tuple-element.88), channel_id=1, source_target_pairs={{0,20},{1,21},{2,22},{3,23},{4,16},{5,17},{6,18},{7,19},{8,28},{9,... | collective-permute-start | bytes 196616 | tf_op jit(solution)/shard_map/ppermute | solution.py:536
  61.2 2.4 %collective-permute-done.19.refs_3_ = bf16[2,128,128]{2,1,0:T(8,128)(2,1)S(1)} collective-permute-done((bf16[2,128,128]{2,1,0:T(8,128)(2,1)S(1)}, bf16[2,128,128]{2,1,0:T(8,128)(2,1)S(1)}, u32[]{:S(2)}, u32[]{:S(2)}) %collective-permute-start.19) | collective-permute-done | bytes 65568 | tf_op jit(solution)/shard_map/ppermute | solution.py:536
  66.3 5.8 %collective-permute-start.23 = (bf16[128,128]{1,0:T(8,128)(2,1)S(1)}, bf16[128,128]{1,0:T(8,128)(2,1)S(1)}, u32[]{:S(2)}, u32[]{:S(2)}) collective-permute-start(bf16[128,128]{1,0:T(8,128)(2,1)S(1)} %get-tuple-element.95), channel_id=1, source_target_pairs={{0,0},{1,4},{2,8},{3,12},{4,2},{5,6},{6,10},{7,14},{8,16},{9,20},{... | collective-permute-start | bytes 98312 | tf_op jit(solution)/shard_map/ppermute | solution.py:472
  72.1 1.5 %collective-permute-start.24 = (bf16[128,128]{1,0:T(8,128)(2,1)S(1)}, bf16[128,128]{1,0:T(8,128)(2,1)S(1)}, u32[]{:S(2)}, u32[]{:S(2)}) collective-permute-start(bf16[128,128]{1,0:T(8,128)(2,1)S(1)} %get-tuple-element.96), channel_id=1, source_target_pairs={{0,16},{1,20},{2,24},{3,28},{4,18},{5,22},{6,26},{7,30},{8,0},{9,4... | collective-permute-start | bytes 98312 | tf_op jit(solution)/shard_map/ppermute | solution.py:472
  73.7 2.5 %collective-permute-done.21.refs_5_ = bf16[128,768]{1,0:T(8,128)(2,1)S(1)} collective-permute-done((bf16[128,768]{1,0:T(8,128)(2,1)S(1)}, bf16[128,768]{1,0:T(8,128)(2,1)S(1)}, u32[]{:S(2)}, u32[]{:S(2)}) %collective-permute-start.21) | collective-permute-done | bytes 196640 | tf_op jit(solution)/shard_map/ppermute | solution.py:491
  76.2 1.3 %unpack.1 = (bf16[1,128,3072]{2,1,0:T(8,128)(2,1)}, bf16[1,128,3072]{2,1,0:T(8,128)(2,1)}, f32[8,128]{1,0:T(8,128)S(1)}) custom-call(bf16[128,768]{1,0:T(8,128)(2,1)S(1)} %get-tuple-element.65.refs_0_, bf16[128,768]{1,0:T(8,128)(2,1)S(1)} %collective-permute-done.8.refs_4_.refs_1_, bf16[128,768]{1,0:T(8,128)(2,1)S(1)} %collective-permute-done.9.refs_5_.refs_2_, ...), custom_call_target="tpu_custom_call" | custom-call | flops 1 | bytes 1 | tf_op jit(solution)/shard_map/unpack/pallas_call | solution.py:30
  77.5 1.7 %collective-permute-done.24.second_ref = bf16[128,128]{1,0:T(8,128)(2,1)S(1)} collective-permute-done((bf16[128,128]{1,0:T(8,128)(2,1)S(1)}, bf16[128,128]{1,0:T(8,128)(2,1)S(1)}, u32[]{:S(2)}, u32[]{:S(2)}) %collective-permute-start.24) | collective-permute-done | bytes 32800 | tf_op jit(solution)/shard_map/ppermute | solution.py:472
  (56 shorter events, 11.3 us)
Async XLA Ops:
  4.4 7.3 %collective-permute-start.10 = (bf16[128,1536]{1,0:T(8,128)(2,1)S(1)}, bf16[128,1536]{1,0:T(8,128)(2,1)S(1)}, u32[]{:S(2)}, u32[]{:S(2)}) collective-permute-start(bf16[128,1536]{1,0:T(8,128)(2,1)S(1)} %get-tuple-element.70), channel_id=1, source_target_pairs={{0,1},{1,0},{2,3},{3,2},{4,5},{5,4},{6,7},{7,6},{8,9},{9,8},{10,11... | collective-permute-start | bytes 1179656 | tf_op jit(solution)/shard_map/ppermute | solution.py:491
  5.1 11.8 %collective-permute-start.1 = (bf16[256,896]{1,0:T(8,128)(2,1)S(1)}, bf16[256,896]{1,0:T(8,128)(2,1)S(1)}, u32[]{:S(2)}, u32[]{:S(2)}) collective-permute-start(bf16[256,896]{1,0:T(8,128)(2,1)S(1)} %get-tuple-element.55), channel_id=1, source_target_pairs={{0,2},{1,3},{2,0},{3,1},{4,6},{5,7},{6,4},{7,5},{8,10},{9,11},{10,... | collective-permute-start | bytes 1376264 | tf_op jit(solution)/shard_map/ppermute | solution.py:491
  7.2 11.0 %collective-permute-start.4 = (bf16[128,1536]{1,0:T(8,128)(2,1)S(1)}, bf16[128,1536]{1,0:T(8,128)(2,1)S(1)}, u32[]{:S(2)}, u32[]{:S(2)}) collective-permute-start(bf16[128,1536]{1,0:T(8,128)(2,1)S(1)} %get-tuple-element.58), channel_id=1, source_target_pairs={{0,1},{1,0},{2,3},{3,2},{4,5},{5,4},{6,7},{7,6},{8,9},{9,8},{10,11... | collective-permute-start | bytes 1179656 | tf_op jit(solution)/shard_map/ppermute | solution.py:491
  7.7 19.0 %collective-permute-start.2 = (bf16[256,896]{1,0:T(8,128)(2,1)S(1)}, bf16[256,896]{1,0:T(8,128)(2,1)S(1)}, u32[]{:S(2)}, u32[]{:S(2)}) collective-permute-start(bf16[256,896]{1,0:T(8,128)(2,1)S(1)} %get-tuple-element.54.refs_0_), channel_id=1, source_target_pairs={{2,6},{3,7},{4,0},{5,1},{6,10},{7,11},{8,4},{9,5},{10,14},{11,15},... | collective-permute-start | bytes 1376264 | tf_op jit(solution)/shard_map/ppermute | solution.py:525
  11.4 9.2 %collective-permute-start.14 = (bf16[128,1536]{1,0:T(8,128)(2,1)S(1)}, bf16[128,1536]{1,0:T(8,128)(2,1)S(1)}, u32[]{:S(2)}, u32[]{:S(2)}) collective-permute-start(bf16[128,1536]{1,0:T(8,128)(2,1)S(1)} %get-tuple-element.75), channel_id=1, source_target_pairs={{0,1},{1,0},{2,3},{3,2},{4,5},{5,4},{6,7},{7,6},{8,9},{9,8},{10,11... | collective-permute-start | bytes 1179656 | tf_op jit(solution)/shard_map/ppermute | solution.py:491
  11.8 13.6 %collective-permute-start.11 = (bf16[256,768]{1,0:T(8,128)(2,1)S(1)}, bf16[256,768]{1,0:T(8,128)(2,1)S(1)}, u32[]{:S(2)}, u32[]{:S(2)}) collective-permute-start(bf16[256,768]{1,0:T(8,128)(2,1)S(1)} %get-tuple-element.72), channel_id=1, source_target_pairs={{0,2},{1,3},{2,0},{3,1},{4,6},{5,7},{6,4},{7,5},{8,10},{9,11},{10,... | collective-permute-start | bytes 1179656 | tf_op jit(solution)/shard_map/ppermute | solution.py:491
  16.9 16.9 %collective-permute-start.3 = (bf16[256,896]{1,0:T(8,128)(2,1)S(1)}, bf16[256,896]{1,0:T(8,128)(2,1)S(1)}, u32[]{:S(2)}, u32[]{:S(2)}) collective-permute-start(bf16[256,896]{1,0:T(8,128)(2,1)S(1)} %collective-permute-done.1.refs_0_.refs_1_), channel_id=1, source_target_pairs={{6,2},{7,3},{0,4},{1,5},{10,6},{11,7},{4,8},{5,9},{14,10},{15,11},... | collective-permute-start | bytes 1376264 | tf_op jit(solution)/shard_map/ppermute | solution.py:525
  18.3 15.5 %collective-permute-start.5 = (bf16[256,768]{1,0:T(8,128)(2,1)S(1)}, bf16[256,768]{1,0:T(8,128)(2,1)S(1)}, u32[]{:S(2)}, u32[]{:S(2)}) collective-permute-start(bf16[256,768]{1,0:T(8,128)(2,1)S(1)} %get-tuple-element.60), channel_id=1, source_target_pairs={{0,2},{1,3},{2,0},{3,1},{4,6},{5,7},{6,4},{7,5},{8,10},{9,11},{10,... | collective-permute-start | bytes 1179656 | tf_op jit(solution)/shard_map/ppermute | solution.py:491
  20.5 20.4 %collective-permute-start.12 = (bf16[256,768]{1,0:T(8,128)(2,1)S(1)}, bf16[256,768]{1,0:T(8,128)(2,1)S(1)}, u32[]{:S(2)}, u32[]{:S(2)}) collective-permute-start(bf16[256,768]{1,0:T(8,128)(2,1)S(1)} %get-tuple-element.71.refs_0_), channel_id=1, source_target_pairs={{2,6},{3,7},{4,0},{5,1},{6,10},{7,11},{8,4},{9,5},{10,14},{11,15},... | collective-permute-start | bytes 1179656 | tf_op jit(solution)/shard_map/ppermute | solution.py:525
  25.4 15.6 %collective-permute-start.13 = (bf16[256,768]{1,0:T(8,128)(2,1)S(1)}, bf16[256,768]{1,0:T(8,128)(2,1)S(1)}, u32[]{:S(2)}, u32[]{:S(2)}) collective-permute-start(bf16[256,768]{1,0:T(8,128)(2,1)S(1)} %collective-permute-done.11.refs_1_), channel_id=1, source_target_pairs={{6,2},{7,3},{0,4},{1,5},{10,6},{11,7},{4,8},{5,9},{14,10},{15,11},... | collective-permute-start | bytes 1179656 | tf_op jit(solution)/shard_map/ppermute | solution.py:525
  26.7 15.5 %collective-permute-start.15 = (bf16[256,768]{1,0:T(8,128)(2,1)S(1)}, bf16[256,768]{1,0:T(8,128)(2,1)S(1)}, u32[]{:S(2)}, u32[]{:S(2)}) collective-permute-start(bf16[256,768]{1,0:T(8,128)(2,1)S(1)} %get-tuple-element.77), channel_id=1, source_target_pairs={{0,2},{1,3},{2,0},{3,1},{4,6},{5,7},{6,4},{7,5},{8,10},{9,11},{10,... | collective-permute-start | bytes 1179656 | tf_op jit(solution)/shard_map/ppermute | solution.py:491
  38.9 11.7 %collective-permute-start.6 = (bf16[256,896]{1,0:T(8,128)(2,1)S(1)}, bf16[256,896]{1,0:T(8,128)(2,1)S(1)}, u32[]{:S(2)}, u32[]{:S(2)}) collective-permute-start(bf16[256,896]{1,0:T(8,128)(2,1)S(1)} %get-tuple-element.62), channel_id=1, source_target_pairs={{0,4},{4,0},{1,5},{5,1},{2,6},{6,2},{3,7},{7,3},{8,12},{12,8},{9,1... | collective-permute-start | bytes 1376264 | tf_op jit(solution)/shard_map/ppermute | solution.py:530
  40.3 10.4 %collective-permute-start.7 = (bf16[256,768]{1,0:T(8,128)(2,1)S(1)}, bf16[256,768]{1,0:T(8,128)(2,1)S(1)}, u32[]{:S(2)}, u32[]{:S(2)}) collective-permute-start(bf16[256,768]{1,0:T(8,128)(2,1)S(1)} %get-tuple-element.63), channel_id=1, source_target_pairs={{4,8},{8,4},{5,9},{9,5},{6,10},{10,6},{7,11},{11,7},{20,24},{24,20... | collective-permute-start | bytes 1179656 | tf_op jit(solution)/shard_map/ppermute | solution.py:530
  47.3 16.3 %collective-permute-start.16 = (bf16[256,896]{1,0:T(8,128)(2,1)S(1)}, bf16[256,896]{1,0:T(8,128)(2,1)S(1)}, u32[]{:S(2)}, u32[]{:S(2)}) collective-permute-start(bf16[256,896]{1,0:T(8,128)(2,1)S(1)} %get-tuple-element.82), channel_id=1, source_target_pairs={{0,4},{4,0},{1,5},{5,1},{2,6},{6,2},{3,7},{7,3},{8,12},{12,8},{9,1... | collective-permute-start | bytes 1376264 | tf_op jit(solution)/shard_map/ppermute | solution.py:530
  49.9 13.7 %collective-permute-start.17 = (bf16[256,768]{1,0:T(8,128)(2,1)S(1)}, bf16[256,768]{1,0:T(8,128)(2,1)S(1)}, u32[]{:S(2)}, u32[]{:S(2)}) collective-permute-start(bf16[256,768]{1,0:T(8,128)(2,1)S(1)} %get-tuple-element.83), channel_id=1, source_target_pairs={{4,8},{8,4},{5,9},{9,5},{6,10},{10,6},{7,11},{11,7},{20,24},{24,20... | collective-permute-start | bytes 1179656 | tf_op jit(solution)/shard_map/ppermute | solution.py:530
  50.9 12.8 %collective-permute-start.8 = (bf16[128,768]{1,0:T(8,128)(2,1)S(1)}, bf16[128,768]{1,0:T(8,128)(2,1)S(1)}, u32[]{:S(2)}, u32[]{:S(2)}) collective-permute-start(bf16[128,768]{1,0:T(8,128)(2,1)S(1)} %get-tuple-element.66), channel_id=1, source_target_pairs={{0,2},{1,3},{2,0},{3,1},{4,6},{5,7},{6,4},{7,5},{8,10},{9,11},{10,... | collective-permute-start | bytes 589832 | tf_op jit(solution)/shard_map/ppermute | solution.py:491
  51.2 12.5 %collective-permute-start.9 = (bf16[128,768]{1,0:T(8,128)(2,1)S(1)}, bf16[128,768]{1,0:T(8,128)(2,1)S(1)}, u32[]{:S(2)}, u32[]{:S(2)}) collective-permute-start(bf16[128,768]{1,0:T(8,128)(2,1)S(1)} %get-tuple-element.67), channel_id=1, source_target_pairs={{0,3},{1,2},{2,1},{3,0},{4,7},{5,6},{6,5},{7,4},{8,11},{9,10},{10,... | collective-permute-start | bytes 589832 | tf_op jit(solution)/shard_map/ppermute | solution.py:491
  55.4 3.5 %collective-permute-start.18 = (bf16[2,128,128]{2,1,0:T(8,128)(2,1)S(1)}, bf16[2,128,128]{2,1,0:T(8,128)(2,1)S(1)}, u32[]{:S(2)}, u32[]{:S(2)}) collective-permute-start(bf16[2,128,128]{2,1,0:T(8,128)(2,1)S(1)} %get-tuple-element.87), channel_id=1, source_target_pairs={{0,16},{16,0},{1,17},{17,1},{2,18},{18,2},{3,19},{19,3},{4,20},{20... | collective-permute-start | bytes 196616 | tf_op jit(solution)/shard_map/ppermute | solution.py:532
  58.9 4.8 %collective-permute-start.19 = (bf16[2,128,128]{2,1,0:T(8,128)(2,1)S(1)}, bf16[2,128,128]{2,1,0:T(8,128)(2,1)S(1)}, u32[]{:S(2)}, u32[]{:S(2)}) collective-permute-start(bf16[2,128,128]{2,1,0:T(8,128)(2,1)S(1)} %get-tuple-element.88), channel_id=1, source_target_pairs={{0,20},{1,21},{2,22},{3,23},{4,16},{5,17},{6,18},{7,19},{8,28},{9,... | collective-permute-start | bytes 196616 | tf_op jit(solution)/shard_map/ppermute | solution.py:536
  63.9 12.3 %collective-permute-start.22 = (bf16[128,1536]{1,0:T(8,128)(2,1)S(1)}, bf16[128,1536]{1,0:T(8,128)(2,1)S(1)}, u32[]{:S(2)}, u32[]{:S(2)}) collective-permute-start(bf16[128,1536]{1,0:T(8,128)(2,1)S(1)} %get-tuple-element.92), channel_id=1, source_target_pairs={{0,1},{1,0},{2,3},{3,2},{4,5},{5,4},{6,7},{7,6},{8,9},{9,8},{10,11... | collective-permute-start | bytes 1179656 | tf_op jit(solution)/shard_map/ppermute | solution.py:491
  64.6 9.0 %collective-permute-start.20 = (bf16[128,768]{1,0:T(8,128)(2,1)S(1)}, bf16[128,768]{1,0:T(8,128)(2,1)S(1)}, u32[]{:S(2)}, u32[]{:S(2)}) collective-permute-start(bf16[128,768]{1,0:T(8,128)(2,1)S(1)} %get-tuple-element.90), channel_id=1, source_target_pairs={{0,2},{1,3},{2,0},{3,1},{4,6},{5,7},{6,4},{7,5},{8,10},{9,11},{10,... | collective-permute-start | bytes 589832 | tf_op jit(solution)/shard_map/ppermute | solution.py:491
  65.7 10.5 %collective-permute-start.21 = (bf16[128,768]{1,0:T(8,128)(2,1)S(1)}, bf16[128,768]{1,0:T(8,128)(2,1)S(1)}, u32[]{:S(2)}, u32[]{:S(2)}) collective-permute-start(bf16[128,768]{1,0:T(8,128)(2,1)S(1)} %get-tuple-element.91), channel_id=1, source_target_pairs={{0,3},{1,2},{2,1},{3,0},{4,7},{5,6},{6,5},{7,4},{8,11},{9,10},{10,... | collective-permute-start | bytes 589832 | tf_op jit(solution)/shard_map/ppermute | solution.py:491
  66.3 11.1 %collective-permute-start.23 = (bf16[128,128]{1,0:T(8,128)(2,1)S(1)}, bf16[128,128]{1,0:T(8,128)(2,1)S(1)}, u32[]{:S(2)}, u32[]{:S(2)}) collective-permute-start(bf16[128,128]{1,0:T(8,128)(2,1)S(1)} %get-tuple-element.95), channel_id=1, source_target_pairs={{0,0},{1,4},{2,8},{3,12},{4,2},{5,6},{6,10},{7,14},{8,16},{9,20},{... | collective-permute-start | bytes 98312 | tf_op jit(solution)/shard_map/ppermute | solution.py:472
  72.1 7.0 %collective-permute-start.24 = (bf16[128,128]{1,0:T(8,128)(2,1)S(1)}, bf16[128,128]{1,0:T(8,128)(2,1)S(1)}, u32[]{:S(2)}, u32[]{:S(2)}) collective-permute-start(bf16[128,128]{1,0:T(8,128)(2,1)S(1)} %get-tuple-element.96), channel_id=1, source_target_pairs={{0,16},{1,20},{2,24},{3,28},{4,18},{5,22},{6,26},{7,30},{8,0},{9,4... | collective-permute-start | bytes 98312 | tf_op jit(solution)/shard_map/ppermute | solution.py:472
  (9 other events, 27.4 us)

commit v6 on v5

--- a/solution.py
+++ b/solution.py
@@ -192,7 +192,7 @@
     kv, halo, qg, rest = refs[:2], refs[2:4], refs[4:6], refs[6:]
     kw, vw, qs, gs, pm, dm, term = rest[-7:]
     if c == 0:
-        own_ref, a_ref, b_ref, keep_ref, clip_ref, both_ref, adapt = rest[:-7]
+        own_ref, a_ref, b_ref, keep_ref, team_ref, clip_ref, both_ref, adapt = rest[:-7]
     else:
         adapt, *earlier, own_ref, a_ref, b_ref, keep_ref, clip_ref, both_ref = rest[:-7]
     kind = adapt.dtype
@@ -279,11 +279,11 @@
     items = [(h, pair) for h in range(count) for pair in range(TEAM // 2)]
     for h in range(count):
         load(h)
-    waiting, adds = scored(*items[0]), []
+    ahead, adds = [scored(*item) for item in items[:2]], []
     for index, item in enumerate(items):
-        current = waiting
-        if index + 1 < len(items):
-            waiting = scored(*items[index + 1])
+        current = ahead.pop(0)
+        if index + 2 < len(items):
+            ahead.append(scored(*items[index + 2]))
         soften(*item, *current)
         adds.append(spread(*item))
         if len(adds) == TEAM // 2:
@@ -298,19 +298,21 @@
         return jnp.where(odd, jnp.where(high, *quarters[3:1:-1]), jnp.where(high, *quarters[1::-1]))
 
     keep_ref[:, :width] = quarter(False, False)
-    leave = quarter(True, False)
-    whole = leave.astype(kind)
-    place_ = pl.ds(2 * count * HEAD_WIDTH, width)
-    a_ref[rows(0, 1), place_] = whole
-    a_ref[rows(1, 1), place_] = (leave - whole.astype(jnp.float32)).astype(kind)
+    leave = quarter(True, False).astype(kind)
+    if c == 0:
+        team_ref[:, :width] = leave
+    else:
+        column = pl.ds(2 * count * HEAD_WIDTH, width)
+        a_ref[rows(0, 1), column] = earlier[0][:, :width]
+        a_ref[rows(1, 1), column] = leave
     for out, part in ((clip_ref, quarter(False, True)), (both_ref, quarter(True, True))):
         if c == 0:
             out[:, :width] = part.astype(kind)
         else:
             out[1, :, :width] = part.astype(kind)
     if c == 1:
-        clip_ref[0] = earlier[0][...]
-        both_ref[0] = earlier[1][...]
+        clip_ref[0] = earlier[1][...]
+        both_ref[0] = earlier[2][...]
 
 
 def compute(c, mask, kv, halo, qg, earlier):
@@ -320,12 +322,14 @@
     tall, team = WINDOW * BLK, TEAM * BLK
     out_shape = [
         jax.ShapeDtypeStruct((team, width), jnp.float32),
-        jax.ShapeDtypeStruct((REACH * BLK, width + HEAD_WIDTH), kind),
+        jax.ShapeDtypeStruct((REACH * BLK, width + (HEAD_WIDTH if c else 0)), kind),
         jax.ShapeDtypeStruct((REACH * BLK, width), kind),
     ]
     part = (2 * RANK, padded(count * HEAD_WIDTH // 4))
     many = part if c == 0 else (2, *part)
     out_shape.append(jax.ShapeDtypeStruct(part, jnp.float32))
+    if c == 0:
+        out_shape.append(jax.ShapeDtypeStruct(part, kind))
     out_shape += [jax.ShapeDtypeStruct(many, kind)] * 2
     if c == 0:
         out_shape.append(jax.ShapeDtypeStruct((2 * RANK, tall), kind))
@@ -345,7 +349,7 @@
 
 
 def combine_kernel(last, bit, own_ref, a_ref, b_ref, keep_ref, *refs):
-    outs = refs[-5 - last : -1 - last]
+    outs = refs[-6:-2] if last else refs[-4:]
     member, team = place()
     even = lax.rem(team, 2)
     width = own_ref.shape[1]
@@ -364,18 +368,15 @@
 
         pl.when(from_a)(functools.partial(add, a_ref))
         pl.when(jnp.logical_not(from_a))(functools.partial(add, b_ref))
-    got = [a_ref[rows(row, 1), pl.ds(width, keep_ref.shape[1])].astype(jnp.float32) for row in range(2)]
-    total = keep_ref[...] + got[0] + got[1]
     if last:
         earlier, clip_ref, both_ref = refs[1:4]
-        clip, both = clip_ref[...].astype(jnp.float32), both_ref[...].astype(jnp.float32)
-        first = earlier[...] + clip[0] + both[0]
-        second = total + clip[1] + both[1]
+        totals = []
+        for index, keep in enumerate((earlier, keep_ref)):
+            got = a_ref[rows(index, 1), pl.ds(width, keep.shape[1])].astype(jnp.float32)
+            totals.append(keep[...] + got + clip_ref[index].astype(jnp.float32) + both_ref[index].astype(jnp.float32))
         upper = bit_value(*bit) == 1
-        refs[-2][...] = jnp.where(upper, second, first).astype(refs[-2].dtype)
-        refs[-1][...] = jnp.where(upper, first, second).astype(refs[-1].dtype)
-    else:
-        refs[-1][...] = total
+        refs[-2][...] = jnp.where(upper, *totals[::-1]).astype(refs[-2].dtype)
+        refs[-1][...] = jnp.where(upper, *totals).astype(refs[-1].dtype)
 
 
 def combine(c, bit, own, a, b, keep, earlier, after):
@@ -386,27 +387,48 @@
     specs = [VMEM] * (4 + len(earlier)) + [ANY] * len(after)
     inputs = [own, a, b, keep, *earlier, *after]
     kernel = functools.partial(combine_kernel, last, bit)
-    return call(kernel, f"combine_{c}", [block, wide, block, block] + [term] * (1 + last), inputs, specs)
-
-
-def unpack_kernel(*refs):
-    outs, other, blocks = refs[-3:-1], refs[-4], refs[:-4]
-    refs[-1][...] = jnp.zeros_like(refs[-1])
+    return call(kernel, f"combine_{c}", [block, wide, block, block] + [term] * (2 * last), inputs, specs)
+
+
+def unpack_kernel(c, *refs):
+    count = CHUNKS[c]
+    own_ref, across_ref, diagonal_ref, other_ref = refs[:4]
+    last = c + 1 == len(CHUNKS)
+    outs = refs[-4:-2] if last else refs[-2:]
     member, _ = place()
-    before = 0
-    for c, (first, count) in enumerate(spans()):
-        sources = [(0, blocks[3 * c], 0), (1, other, before), (2, blocks[3 * c + 1], 0), (3, blocks[3 * c + 2], 0)]
-        for k, ref, column in sources:
-            head = first_head(c, jnp.bitwise_xor(member, k))
-            for part, out in enumerate(outs):
-                out[0, :, cols(head, count)] = ref[:, cols(column + part * count, count)]
-        before += 2 * count
-
-
-def unpack(home, other):
-    flat = [block for chunk in home for block in chunk] + [other]
+    before = 2 * sum(CHUNKS[:c])
+    for k, ref, column in ((0, own_ref, 0), (1, other_ref, before), (2, across_ref, 0), (3, diagonal_ref, 0)):
+        head = jnp.bitwise_xor(member, k) * count
+        for part, out in enumerate(outs):
+            out[0, :, cols(head, count)] = ref[:, cols(column + part * count, count)]
+    if last:
+        arrived = refs[4:6]
+        if len(arrived[0].shape) == 3:
+            arrived = [ref.at[0] for ref in arrived]
+        for half, term in zip((slice(0, RANK), slice(RANK, 2 * RANK)), refs[-2:]):
+            term[...] = sum(ref[half, : term.shape[1]].astype(jnp.float32) for ref in arrived)
+
+
+def unpack(c, home, other, arrived, width, earlier):
+    last = c + 1 == len(CHUNKS)
+    block = (1, BLK, TEAM * CHUNKS[c] * HEAD_WIDTH)
     shape = jax.ShapeDtypeStruct((1, BLK, HEAD_COUNT * HEAD_WIDTH), other.dtype)
-    return call(unpack_kernel, "unpack", [shape, shape, MARK], flat)
+    out_shape, out_specs = [shape] * 2, [pl.BlockSpec(block, lambda i: (0, 0, c))] * 2
+    if last:
+        out_shape += [jax.ShapeDtypeStruct((RANK, width), jnp.float32)] * 2
+        out_specs += [pl.BlockSpec((RANK, width), lambda i: (0, 0))] * 2
+    inputs = [*home, other, *arrived]
+    return pl.pallas_call(
+        functools.partial(unpack_kernel, c),
+        grid=(1,),
+        out_shape=out_shape,
+        in_specs=[VMEM] * len(inputs) + [ANY] * len(earlier),
+        out_specs=out_specs,
+        input_output_aliases={len(inputs) + i: i for i in range(len(earlier))},
+        compiler_params=pltpu.CompilerParams(vmem_limit_bytes=8 << 20),
+        cost_estimate=pl.CostEstimate(flops=1, bytes_accessed=1, transcendentals=0),
+        name=f"unpack_{c}",
+    )(*inputs, *earlier)
 
 
 def bit_value(axis, bit, unit):
@@ -427,14 +449,6 @@
             out[...] = (held_ref[pl.ds(first, half)] + got_ref[pl.ds(first, half)]).astype(out.dtype)
 
 
-def final_kernel(first_ref, second_ref, _, key_ref, value_ref):
-    width = key_ref.shape[1]
-    if len(first_ref.shape) == 3:
-        first_ref, second_ref = first_ref.at[0], second_ref.at[0]
-    for half, out in ((slice(0, RANK), key_ref), (slice(RANK, 2 * RANK), value_ref)):
-        out[...] = first_ref[half, :width].astype(jnp.float32) + second_ref[half, :width].astype(jnp.float32)
-
-
 def later_rounds():
     clips, teams = lax.axis_size("dp"), lax.axis_size("seq") // TEAM
     clip_bits = [clips >> s for s in range(2, clips.bit_length())]
@@ -442,7 +456,7 @@
     return [("dp", bit, 1) for bit in clip_bits] + [("seq", bit, TEAM) for bit in team_bits]
 
 
-def reduce_terms(held, sent, after):
+def reduce_terms(held, sent):
     clips, seq = lax.axis_size("dp"), lax.axis_size("seq")
     teams = seq // TEAM
     pieces = clips * teams
@@ -470,8 +484,7 @@
                 c, index = divmod(piece_of(clip, position // TEAM) ^ other, pieces // 2)
                 route.append((clip * seq + position, (c * TEAM + position % TEAM) * pieces // 2 + index))
         arrived.append(lax.ppermute(piece, ("dp", "seq"), route))
-    shape = jax.ShapeDtypeStruct((RANK, width), jnp.float32)
-    return call(final_kernel, "final", [shape, shape], [*arrived, after], [VMEM, VMEM, ANY])
+    return arrived, width
 
 
 def body(
@@ -525,9 +538,13 @@
         halo.append((lax.ppermute(kv[c][0], "seq", near_route), lax.ppermute(kv[c][1], "seq", far_route)))
     earlier, parts = [], []
     for c in range(len(CHUNKS)):
-        own, to_a, to_b, keep, to_clip, to_both, *more = compute(c, mask, kv[c], halo[c], qg[c], earlier)
-        earlier = [*more, to_clip, to_both]
-        parts.append((own, lax.ppermute(to_a, "seq", swaps[0]), lax.ppermute(to_b, "seq", swaps[1]), keep))
+        own, to_a, to_b, keep, *quarters = compute(c, mask, kv[c], halo[c], qg[c], earlier)
+        if c == 0:
+            to_team, to_clip, to_both, adapt = quarters
+            earlier = [adapt, to_team, to_clip, to_both]
+        from_b = lax.ppermute(to_b, "seq", swaps[1])
+        parts.append((own, lax.ppermute(to_a, "seq", swaps[0]), from_b, keep))
+    to_clip, to_both = quarters
     clips = lax.axis_size("dp")
     from_clip = lax.ppermute(to_clip, "dp", [(i, i ^ (clips // 2)) for i in range(clips)])
     both = []
@@ -540,9 +557,12 @@
         given = [*earlier, from_clip, from_both] if last else []
         blocks = combine(c, later_rounds()[0], *part, given, after)
         home.append([blocks[0], partner(blocks[2], 2), partner(blocks[3], 3)])
-        earlier, after = [blocks[1], blocks[4]], home[-1][1:]
-    key_gradient, value_gradient, mark = unpack(home, partner(blocks[1], 1))
-    key_term, value_term = reduce_terms(blocks[4], blocks[5], mark)
+        earlier, after = [blocks[1], part[-1]], home[-1][1:]
+    other, (arrived, width) = partner(blocks[1], 1), reduce_terms(blocks[4], blocks[5])
+    results = []
+    for c in range(len(CHUNKS)):
+        results = unpack(c, home[c], other, arrived if c + 1 == len(CHUNKS) else [], width, results)
+    key_gradient, value_gradient, key_term, value_term = results
     return key_gradient, value_gradient, key_term.T, value_term.T
 
 

time: 80.1 us -> 79.2 us (0.989)
    pallas_call x14 -> x12, Pallas kernels: 17.7 us -> 15.3 us  [call(): pl.pallas_call(kernel, out_shape=out_shape, in_specs=in_specs or [VMEM] *...]
    ppermute x13, waiting for transfers between devices: 16 us -> 13.7 us  [partner(): lax.ppermute(block, 'seq', [(i, i ^ k) for i in range(seq)])]
    ppermute x2, waiting for transfers between devices: 1.65 us -> 3.87 us  [reduce_terms(): arrived.append(lax.ppermute(piece, ('dp', 'seq'), route))]
    pallas_call x0 -> x2, Pallas kernels: none -> 1.92 us  [unpack(): pl.pallas_call(functools.partial(unpack_kernel, c), grid=(1,), out_shape=...]
  transfers between devices with their start and end apart: 25 -> 25, of which waited for: 9 -> 8; matrix products, arithmetic and copies ran while one was open for 0% -> 0% of each run, Pallas kernels for 19% -> 18%
where the time goes in v6:
time: 79.2 us; the launch traced here: 79 us
  starting transfers between devices  38.3 us (48%)
  waiting for transfers between devices  22.4 us (28%)
  Pallas kernels  17.2 us (22%)
  between operations  0.94 us (1%)
    pallas_call x12, Pallas kernels, call(): pl.pallas_call(kernel, out_shape=out_shape, in_specs=in_specs or [VMEM] *...  15.3 us
    ppermute x13, waiting for transfers between devices, partner(): lax.ppermute(block, 'seq', [(i, i ^ k) for i in range(seq)])  13.7 us
    ppermute x13, starting transfers between devices, partner(): lax.ppermute(block, 'seq', [(i, i ^ k) for i in range(seq)])  13 us
    ppermute x2, starting transfers between devices, reduce_terms(): arrived.append(lax.ppermute(piece, ('dp', 'seq'), route))  7.04 us
    ppermute x2, starting transfers between devices, body(): lax.ppermute(kv[c][0], 'seq', near_route)  6.88 us
    ppermute x2, waiting for transfers between devices, reduce_terms(): arrived.append(lax.ppermute(piece, ('dp', 'seq'), route))  3.87 us
    ppermute x2, starting transfers between devices, body(): parts.append((own, lax.ppermute(to_a, 'seq', swaps[0]), from_b, keep))  3.71 us
    ppermute x1, starting transfers between devices, body(): from_both = lax.ppermute(to_both, ('dp', 'seq'), both)  2.62 us
  transfers between devices with their start and end apart: 25, of which 8 were waited for; matrix products, arithmetic and copies ran while one was open for 0% of the time, Pallas kernels for 18%

profile of v6, /device:TPU:5, one launch (start us, length us, event | category | flops | bytes accessed | tf_op | source)
XLA Modules:
  0.0 79.0 jit_solution(4507813853306774990)
XLA Ops:
  0.7 2.0 %pack_side.1 = bf16[128,1664]{1,0:T(8,128)(2,1)} custom-call(bf16[1,128,3072]{2,1,0:T(8,128)(2,1)} %keys.1, bf16[1,128,3072]{2,1,0:T(8,128)(2,1)} %values.1, bf16[1,64,128]{2,1,0:T(8,128)(2,1)} %bitcast.6, bf16[1,64,128]{2,1,0:T(8,128)(2,1)} %bitcast.8), custom_call_target="tpu_custom_call" | custom-call | flops 1 | bytes 1 | tf_op jit(solution)/shard_map/pack_side/pallas_call | solution.py:30
  5.2 1.8 %mask.1.refs_0_.mask_ref = f32[120,128]{1,0:T(8,128)S(1)} custom-call(s32[5,16,24]{2,1,0:T(8,128)S(1)} %bitcast.10, s32[16,24]{1,0:T(8,128)S(1)} %bitcast.11, bf16[128,896]{1,0:T(8,128)(2,1)S(1)} %get-tuple-element.53._.mine_ref), custom_call_target="tpu_custom_call" | custom-call | flops 1 | bytes 1 | tf_op jit(solution)/shard_map/mask/pallas_call | solution.py:30
  7.7 3.7 %collective-permute-start.8 = (bf16[256,896]{1,0:T(8,128)(2,1)S(1)}, bf16[256,896]{1,0:T(8,128)(2,1)S(1)}, u32[]{:S(2)}, u32[]{:S(2)}) collective-permute-start(bf16[256,896]{1,0:T(8,128)(2,1)S(1)} %get-tuple-element.66.refs_0_), channel_id=1, source_target_pairs={{2,6},{3,7},{4,0},{5,1},{6,10},{7,11},{8,4},{9,5},{10,14},{11,15},... | collective-permute-start | bytes 1376264 | tf_op jit(solution)/shard_map/ppermute | solution.py:538
  11.9 5.1 %collective-permute-done.6.refs_0_.refs_1_ = bf16[256,896]{1,0:T(8,128)(2,1)S(1)} collective-permute-done((bf16[256,896]{1,0:T(8,128)(2,1)S(1)}, bf16[256,896]{1,0:T(8,128)(2,1)S(1)}, u32[]{:S(2)}, u32[]{:S(2)}) %collective-permute-start.6) | collective-permute-done | bytes 458784 | tf_op jit(solution)/shard_map/ppermute | solution.py:504
  16.9 1.3 %collective-permute-start.9 = (bf16[256,896]{1,0:T(8,128)(2,1)S(1)}, bf16[256,896]{1,0:T(8,128)(2,1)S(1)}, u32[]{:S(2)}, u32[]{:S(2)}) collective-permute-start(bf16[256,896]{1,0:T(8,128)(2,1)S(1)} %collective-permute-done.6.refs_0_.refs_1_), channel_id=1, source_target_pairs={{6,2},{7,3},{0,4},{1,5},{10,6},{11,7},{4,8},{5,9},{14,10},{15,11},... | collective-permute-start | bytes 1376264 | tf_op jit(solution)/shard_map/ppermute | solution.py:538
  18.3 2.2 %collective-permute-start.11 = (bf16[256,768]{1,0:T(8,128)(2,1)S(1)}, bf16[256,768]{1,0:T(8,128)(2,1)S(1)}, u32[]{:S(2)}, u32[]{:S(2)}) collective-permute-start(bf16[256,768]{1,0:T(8,128)(2,1)S(1)} %get-tuple-element.71), channel_id=1, source_target_pairs={{0,2},{1,3},{2,0},{3,1},{4,6},{5,7},{6,4},{7,5},{8,10},{9,11},{10,... | collective-permute-start | bytes 1179656 | tf_op jit(solution)/shard_map/ppermute | solution.py:504
  20.5 3.2 %collective-permute-start.2 = (bf16[256,768]{1,0:T(8,128)(2,1)S(1)}, bf16[256,768]{1,0:T(8,128)(2,1)S(1)}, u32[]{:S(2)}, u32[]{:S(2)}) collective-permute-start(bf16[256,768]{1,0:T(8,128)(2,1)S(1)} %get-tuple-element.57.refs_0_), channel_id=1, source_target_pairs={{2,6},{3,7},{4,0},{5,1},{6,10},{7,11},{8,4},{9,5},{10,14},{11,15},... | collective-permute-start | bytes 1179656 | tf_op jit(solution)/shard_map/ppermute | solution.py:538
  23.7 1.6 %collective-permute-done.1.refs_1_ = bf16[256,768]{1,0:T(8,128)(2,1)S(1)} collective-permute-done((bf16[256,768]{1,0:T(8,128)(2,1)S(1)}, bf16[256,768]{1,0:T(8,128)(2,1)S(1)}, u32[]{:S(2)}, u32[]{:S(2)}) %collective-permute-start.1) | collective-permute-done | bytes 393248 | tf_op jit(solution)/shard_map/ppermute | solution.py:504
  25.4 1.3 %collective-permute-start.3 = (bf16[256,768]{1,0:T(8,128)(2,1)S(1)}, bf16[256,768]{1,0:T(8,128)(2,1)S(1)}, u32[]{:S(2)}, u32[]{:S(2)}) collective-permute-start(bf16[256,768]{1,0:T(8,128)(2,1)S(1)} %collective-permute-done.1.refs_1_), channel_id=1, source_target_pairs={{6,2},{7,3},{0,4},{1,5},{10,6},{11,7},{4,8},{5,9},{14,10},{15,11},... | collective-permute-start | bytes 1179656 | tf_op jit(solution)/shard_map/ppermute | solution.py:538
  26.7 2.2 %collective-permute-start.7 = (bf16[256,768]{1,0:T(8,128)(2,1)S(1)}, bf16[256,768]{1,0:T(8,128)(2,1)S(1)}, u32[]{:S(2)}, u32[]{:S(2)}) collective-permute-start(bf16[256,768]{1,0:T(8,128)(2,1)S(1)} %get-tuple-element.65), channel_id=1, source_target_pairs={{0,2},{1,3},{2,0},{3,1},{4,6},{5,7},{6,4},{7,5},{8,10},{9,11},{10,... | collective-permute-start | bytes 1179656 | tf_op jit(solution)/shard_map/ppermute | solution.py:504
  29.0 4.8 %collective-permute-done.11.refs_5_ = bf16[256,768]{1,0:T(8,128)(2,1)S(1)} collective-permute-done((bf16[256,768]{1,0:T(8,128)(2,1)S(1)}, bf16[256,768]{1,0:T(8,128)(2,1)S(1)}, u32[]{:S(2)}, u32[]{:S(2)}) %collective-permute-start.11) | collective-permute-done | bytes 393248 | tf_op jit(solution)/shard_map/ppermute | solution.py:504
  33.8 4.9 %gradients_0.1 = (f32[512,768]{1,0:T(8,128)S(1)}, bf16[256,768]{1,0:T(8,128)(2,1)S(1)}, bf16[256,768]{1,0:T(8,128)(2,1)S(1)}, f32[128,128]{1,0:T(8,128)S(1)}, bf...) custom-call(f32[120,128]{1,0:T(8,128)S(1)} %mask.1.refs_0_.mask_ref,, ...), custom_call_target="tpu_custom_call" | custom-call | flops 1 | bytes 1 | tf_op jit(solution)/shard_map/gradients_0/pallas_call | solution.py:30
  38.7 1.3 %collective-permute-start.14 = (bf16[256,768]{1,0:T(8,128)(2,1)S(1)}, bf16[256,768]{1,0:T(8,128)(2,1)S(1)}, u32[]{:S(2)}, u32[]{:S(2)}) collective-permute-start(bf16[256,768]{1,0:T(8,128)(2,1)S(1)} %get-tuple-element.81), channel_id=1, source_target_pairs={{0,4},{4,0},{1,5},{5,1},{2,6},{6,2},{3,7},{7,3},{8,12},{12,8},{9,1... | collective-permute-start | bytes 1179656 | tf_op jit(solution)/shard_map/ppermute | solution.py:546
  40.7 1.5 %collective-permute-done.7.refs_5_ = bf16[256,768]{1,0:T(8,128)(2,1)S(1)} collective-permute-done((bf16[256,768]{1,0:T(8,128)(2,1)S(1)}, bf16[256,768]{1,0:T(8,128)(2,1)S(1)}, u32[]{:S(2)}, u32[]{:S(2)}) %collective-permute-start.7) | collective-permute-done | bytes 393248 | tf_op jit(solution)/shard_map/ppermute | solution.py:504
  42.2 4.8 %gradients_1.1 = (f32[512,768]{1,0:T(8,128)S(1)}, bf16[256,896]{1,0:T(8,128)(2,1)S(1)}, bf16[256,768]{1,0:T(8,128)(2,1)S(1)}, f32[128,128]{1,0:T(8,128)S(1)}, bf...) custom-call(f32[120,128]{1,0:T(8,128)S(1)} %mask.1.refs_0_.mask_ref, ...), custom_call_target="tpu_custom_call" | custom-call | flops 1 | bytes 1 | tf_op jit(solution)/shard_map/gradients_1/pallas_call | solution.py:30
  47.1 2.4 %collective-permute-start.12 = (bf16[256,896]{1,0:T(8,128)(2,1)S(1)}, bf16[256,896]{1,0:T(8,128)(2,1)S(1)}, u32[]{:S(2)}, u32[]{:S(2)}) collective-permute-start(bf16[256,896]{1,0:T(8,128)(2,1)S(1)} %get-tuple-element.77), channel_id=1, source_target_pairs={{0,4},{4,0},{1,5},{5,1},{2,6},{6,2},{3,7},{7,3},{8,12},{12,8},{9,1... | collective-permute-start | bytes 1376264 | tf_op jit(solution)/shard_map/ppermute | solution.py:546
  50.7 4.2 %collective-permute-start.19 = (bf16[128,768]{1,0:T(8,128)(2,1)S(1)}, bf16[128,768]{1,0:T(8,128)(2,1)S(1)}, u32[]{:S(2)}, u32[]{:S(2)}) collective-permute-start(bf16[128,768]{1,0:T(8,128)(2,1)S(1)} %get-tuple-element.88), channel_id=1, source_target_pairs={{0,3},{1,2},{2,1},{3,0},{4,7},{5,6},{6,5},{7,4},{8,11},{9,10},{10,... | collective-permute-start | bytes 589832 | tf_op jit(solution)/shard_map/ppermute | solution.py:504
  54.9 1.2 %collective-permute-start.16 = (bf16[2,128,128]{2,1,0:T(8,128)(2,1)S(1)}, bf16[2,128,128]{2,1,0:T(8,128)(2,1)S(1)}, u32[]{:S(2)}, u32[]{:S(2)}) collective-permute-start(bf16[2,128,128]{2,1,0:T(8,128)(2,1)S(1)} %get-tuple-element.85), channel_id=1, source_target_pairs={{0,16},{16,0},{1,17},{17,1},{2,18},{18,2},{3,19},{19,3},{4,20},{20... | collective-permute-start | bytes 196616 | tf_op jit(solution)/shard_map/ppermute | solution.py:549
  56.1 2.2 %collective-permute-done.16.refs_2_ = bf16[2,128,128]{2,1,0:T(8,128)(2,1)S(1)} collective-permute-done((bf16[2,128,128]{2,1,0:T(8,128)(2,1)S(1)}, bf16[2,128,128]{2,1,0:T(8,128)(2,1)S(1)}, u32[]{:S(2)}, u32[]{:S(2)}) %collective-permute-start.16) | collective-permute-done | bytes 65568 | tf_op jit(solution)/shard_map/ppermute | solution.py:549
  58.4 2.6 %collective-permute-start.17 = (bf16[2,128,128]{2,1,0:T(8,128)(2,1)S(1)}, bf16[2,128,128]{2,1,0:T(8,128)(2,1)S(1)}, u32[]{:S(2)}, u32[]{:S(2)}) collective-permute-start(bf16[2,128,128]{2,1,0:T(8,128)(2,1)S(1)} %get-tuple-element.86), channel_id=1, source_target_pairs={{0,20},{1,21},{2,22},{3,23},{4,16},{5,17},{6,18},{7,19},{8,28},{9,... | collective-permute-start | bytes 196616 | tf_op jit(solution)/shard_map/ppermute | solution.py:553
  61.0 2.6 %collective-permute-done.17.refs_3_ = bf16[2,128,128]{2,1,0:T(8,128)(2,1)S(1)} collective-permute-done((bf16[2,128,128]{2,1,0:T(8,128)(2,1)S(1)}, bf16[2,128,128]{2,1,0:T(8,128)(2,1)S(1)}, u32[]{:S(2)}, u32[]{:S(2)}) %collective-permute-start.17) | collective-permute-done | bytes 65568 | tf_op jit(solution)/shard_map/ppermute | solution.py:553
  66.1 4.6 %collective-permute-start.23 = (bf16[128,128]{1,0:T(8,128)(2,1)S(1)}, bf16[128,128]{1,0:T(8,128)(2,1)S(1)}, u32[]{:S(2)}, u32[]{:S(2)}) collective-permute-start(bf16[128,128]{1,0:T(8,128)(2,1)S(1)} %get-tuple-element.93), channel_id=1, source_target_pairs={{0,0},{1,4},{2,8},{3,12},{4,2},{5,6},{6,10},{7,14},{8,16},{9,20},{... | collective-permute-start | bytes 98312 | tf_op jit(solution)/shard_map/ppermute | solution.py:486
  70.7 2.4 %collective-permute-start.24 = (bf16[128,128]{1,0:T(8,128)(2,1)S(1)}, bf16[128,128]{1,0:T(8,128)(2,1)S(1)}, u32[]{:S(2)}, u32[]{:S(2)}) collective-permute-start(bf16[128,128]{1,0:T(8,128)(2,1)S(1)} %get-tuple-element.94), channel_id=1, source_target_pairs={{0,16},{1,20},{2,24},{3,28},{4,18},{5,22},{6,26},{7,30},{8,0},{9,4... | collective-permute-start | bytes 98312 | tf_op jit(solution)/shard_map/ppermute | solution.py:486
  74.1 3.9 %collective-permute-done.24.refs_5_ = bf16[128,128]{1,0:T(8,128)(2,1)S(1)} collective-permute-done((bf16[128,128]{1,0:T(8,128)(2,1)S(1)}, bf16[128,128]{1,0:T(8,128)(2,1)S(1)}, u32[]{:S(2)}, u32[]{:S(2)}) %collective-permute-start.24) | collective-permute-done | bytes 32800 | tf_op jit(solution)/shard_map/ppermute | solution.py:486
  (56 shorter events, 10.0 us)
Async XLA Ops:
  4.4 7.3 %collective-permute-start = (bf16[128,1536]{1,0:T(8,128)(2,1)S(1)}, bf16[128,1536]{1,0:T(8,128)(2,1)S(1)}, u32[]{:S(2)}, u32[]{:S(2)}) collective-permute-start(bf16[128,1536]{1,0:T(8,128)(2,1)S(1)} %get-tuple-element.56), channel_id=1, source_target_pairs={{0,1},{1,0},{2,3},{3,2},{4,5},{5,4},{6,7},{7,6},{8,9},{9,8},{10,11... | collective-permute-start | bytes 1179656 | tf_op jit(solution)/shard_map/ppermute | solution.py:504
  5.1 11.8 %collective-permute-start.6 = (bf16[256,896]{1,0:T(8,128)(2,1)S(1)}, bf16[256,896]{1,0:T(8,128)(2,1)S(1)}, u32[]{:S(2)}, u32[]{:S(2)}) collective-permute-start(bf16[256,896]{1,0:T(8,128)(2,1)S(1)} %get-tuple-element.63), channel_id=1, source_target_pairs={{0,2},{1,3},{2,0},{3,1},{4,6},{5,7},{6,4},{7,5},{8,10},{9,11},{10,... | collective-permute-start | bytes 1376264 | tf_op jit(solution)/shard_map/ppermute | solution.py:504
  7.2 11.0 %collective-permute-start.10 = (bf16[128,1536]{1,0:T(8,128)(2,1)S(1)}, bf16[128,1536]{1,0:T(8,128)(2,1)S(1)}, u32[]{:S(2)}, u32[]{:S(2)}) collective-permute-start(bf16[128,1536]{1,0:T(8,128)(2,1)S(1)} %get-tuple-element.69), channel_id=1, source_target_pairs={{0,1},{1,0},{2,3},{3,2},{4,5},{5,4},{6,7},{7,6},{8,9},{9,8},{10,11... | collective-permute-start | bytes 1179656 | tf_op jit(solution)/shard_map/ppermute | solution.py:504
  7.7 19.0 %collective-permute-start.8 = (bf16[256,896]{1,0:T(8,128)(2,1)S(1)}, bf16[256,896]{1,0:T(8,128)(2,1)S(1)}, u32[]{:S(2)}, u32[]{:S(2)}) collective-permute-start(bf16[256,896]{1,0:T(8,128)(2,1)S(1)} %get-tuple-element.66.refs_0_), channel_id=1, source_target_pairs={{2,6},{3,7},{4,0},{5,1},{6,10},{7,11},{8,4},{9,5},{10,14},{11,15},... | collective-permute-start | bytes 1376264 | tf_op jit(solution)/shard_map/ppermute | solution.py:538
  11.4 9.2 %collective-permute-start.4 = (bf16[128,1536]{1,0:T(8,128)(2,1)S(1)}, bf16[128,1536]{1,0:T(8,128)(2,1)S(1)}, u32[]{:S(2)}, u32[]{:S(2)}) collective-permute-start(bf16[128,1536]{1,0:T(8,128)(2,1)S(1)} %get-tuple-element.61), channel_id=1, source_target_pairs={{0,1},{1,0},{2,3},{3,2},{4,5},{5,4},{6,7},{7,6},{8,9},{9,8},{10,11... | collective-permute-start | bytes 1179656 | tf_op jit(solution)/shard_map/ppermute | solution.py:504
  11.8 13.6 %collective-permute-start.1 = (bf16[256,768]{1,0:T(8,128)(2,1)S(1)}, bf16[256,768]{1,0:T(8,128)(2,1)S(1)}, u32[]{:S(2)}, u32[]{:S(2)}) collective-permute-start(bf16[256,768]{1,0:T(8,128)(2,1)S(1)} %get-tuple-element.58), channel_id=1, source_target_pairs={{0,2},{1,3},{2,0},{3,1},{4,6},{5,7},{6,4},{7,5},{8,10},{9,11},{10,... | collective-permute-start | bytes 1179656 | tf_op jit(solution)/shard_map/ppermute | solution.py:504
  16.9 16.9 %collective-permute-start.9 = (bf16[256,896]{1,0:T(8,128)(2,1)S(1)}, bf16[256,896]{1,0:T(8,128)(2,1)S(1)}, u32[]{:S(2)}, u32[]{:S(2)}) collective-permute-start(bf16[256,896]{1,0:T(8,128)(2,1)S(1)} %collective-permute-done.6.refs_0_.refs_1_), channel_id=1, source_target_pairs={{6,2},{7,3},{0,4},{1,5},{10,6},{11,7},{4,8},{5,9},{14,10},{15,11},... | collective-permute-start | bytes 1376264 | tf_op jit(solution)/shard_map/ppermute | solution.py:538
  18.3 15.5 %collective-permute-start.11 = (bf16[256,768]{1,0:T(8,128)(2,1)S(1)}, bf16[256,768]{1,0:T(8,128)(2,1)S(1)}, u32[]{:S(2)}, u32[]{:S(2)}) collective-permute-start(bf16[256,768]{1,0:T(8,128)(2,1)S(1)} %get-tuple-element.71), channel_id=1, source_target_pairs={{0,2},{1,3},{2,0},{3,1},{4,6},{5,7},{6,4},{7,5},{8,10},{9,11},{10,... | collective-permute-start | bytes 1179656 | tf_op jit(solution)/shard_map/ppermute | solution.py:504
  20.5 20.2 %collective-permute-start.2 = (bf16[256,768]{1,0:T(8,128)(2,1)S(1)}, bf16[256,768]{1,0:T(8,128)(2,1)S(1)}, u32[]{:S(2)}, u32[]{:S(2)}) collective-permute-start(bf16[256,768]{1,0:T(8,128)(2,1)S(1)} %get-tuple-element.57.refs_0_), channel_id=1, source_target_pairs={{2,6},{3,7},{4,0},{5,1},{6,10},{7,11},{8,4},{9,5},{10,14},{11,15},... | collective-permute-start | bytes 1179656 | tf_op jit(solution)/shard_map/ppermute | solution.py:538
  25.4 15.3 %collective-permute-start.3 = (bf16[256,768]{1,0:T(8,128)(2,1)S(1)}, bf16[256,768]{1,0:T(8,128)(2,1)S(1)}, u32[]{:S(2)}, u32[]{:S(2)}) collective-permute-start(bf16[256,768]{1,0:T(8,128)(2,1)S(1)} %collective-permute-done.1.refs_1_), channel_id=1, source_target_pairs={{6,2},{7,3},{0,4},{1,5},{10,6},{11,7},{4,8},{5,9},{14,10},{15,11},... | collective-permute-start | bytes 1179656 | tf_op jit(solution)/shard_map/ppermute | solution.py:538
  26.7 15.5 %collective-permute-start.7 = (bf16[256,768]{1,0:T(8,128)(2,1)S(1)}, bf16[256,768]{1,0:T(8,128)(2,1)S(1)}, u32[]{:S(2)}, u32[]{:S(2)}) collective-permute-start(bf16[256,768]{1,0:T(8,128)(2,1)S(1)} %get-tuple-element.65), channel_id=1, source_target_pairs={{0,2},{1,3},{2,0},{3,1},{4,6},{5,7},{6,4},{7,5},{8,10},{9,11},{10,... | collective-permute-start | bytes 1179656 | tf_op jit(solution)/shard_map/ppermute | solution.py:504
  38.7 11.4 %collective-permute-start.14 = (bf16[256,768]{1,0:T(8,128)(2,1)S(1)}, bf16[256,768]{1,0:T(8,128)(2,1)S(1)}, u32[]{:S(2)}, u32[]{:S(2)}) collective-permute-start(bf16[256,768]{1,0:T(8,128)(2,1)S(1)} %get-tuple-element.81), channel_id=1, source_target_pairs={{0,4},{4,0},{1,5},{5,1},{2,6},{6,2},{3,7},{7,3},{8,12},{12,8},{9,1... | collective-permute-start | bytes 1179656 | tf_op jit(solution)/shard_map/ppermute | solution.py:546
  40.0 10.1 %collective-permute-start.15 = (bf16[256,768]{1,0:T(8,128)(2,1)S(1)}, bf16[256,768]{1,0:T(8,128)(2,1)S(1)}, u32[]{:S(2)}, u32[]{:S(2)}) collective-permute-start(bf16[256,768]{1,0:T(8,128)(2,1)S(1)} %get-tuple-element.82), channel_id=1, source_target_pairs={{4,8},{8,4},{5,9},{9,5},{6,10},{10,6},{7,11},{11,7},{20,24},{24,20... | collective-permute-start | bytes 1179656 | tf_op jit(solution)/shard_map/ppermute | solution.py:545
  47.1 16.5 %collective-permute-start.12 = (bf16[256,896]{1,0:T(8,128)(2,1)S(1)}, bf16[256,896]{1,0:T(8,128)(2,1)S(1)}, u32[]{:S(2)}, u32[]{:S(2)}) collective-permute-start(bf16[256,896]{1,0:T(8,128)(2,1)S(1)} %get-tuple-element.77), channel_id=1, source_target_pairs={{0,4},{4,0},{1,5},{5,1},{2,6},{6,2},{3,7},{7,3},{8,12},{12,8},{9,1... | collective-permute-start | bytes 1376264 | tf_op jit(solution)/shard_map/ppermute | solution.py:546
  49.4 14.2 %collective-permute-start.13 = (bf16[256,768]{1,0:T(8,128)(2,1)S(1)}, bf16[256,768]{1,0:T(8,128)(2,1)S(1)}, u32[]{:S(2)}, u32[]{:S(2)}) collective-permute-start(bf16[256,768]{1,0:T(8,128)(2,1)S(1)} %get-tuple-element.78), channel_id=1, source_target_pairs={{4,8},{8,4},{5,9},{9,5},{6,10},{10,6},{7,11},{11,7},{20,24},{24,20... | collective-permute-start | bytes 1179656 | tf_op jit(solution)/shard_map/ppermute | solution.py:545
  50.4 13.2 %collective-permute-start.18 = (bf16[128,768]{1,0:T(8,128)(2,1)S(1)}, bf16[128,768]{1,0:T(8,128)(2,1)S(1)}, u32[]{:S(2)}, u32[]{:S(2)}) collective-permute-start(bf16[128,768]{1,0:T(8,128)(2,1)S(1)} %get-tuple-element.87), channel_id=1, source_target_pairs={{0,2},{1,3},{2,0},{3,1},{4,6},{5,7},{6,4},{7,5},{8,10},{9,11},{10,... | collective-permute-start | bytes 589832 | tf_op jit(solution)/shard_map/ppermute | solution.py:504
  50.7 12.9 %collective-permute-start.19 = (bf16[128,768]{1,0:T(8,128)(2,1)S(1)}, bf16[128,768]{1,0:T(8,128)(2,1)S(1)}, u32[]{:S(2)}, u32[]{:S(2)}) collective-permute-start(bf16[128,768]{1,0:T(8,128)(2,1)S(1)} %get-tuple-element.88), channel_id=1, source_target_pairs={{0,3},{1,2},{2,1},{3,0},{4,7},{5,6},{6,5},{7,4},{8,11},{9,10},{10,... | collective-permute-start | bytes 589832 | tf_op jit(solution)/shard_map/ppermute | solution.py:504
  54.9 3.5 %collective-permute-start.16 = (bf16[2,128,128]{2,1,0:T(8,128)(2,1)S(1)}, bf16[2,128,128]{2,1,0:T(8,128)(2,1)S(1)}, u32[]{:S(2)}, u32[]{:S(2)}) collective-permute-start(bf16[2,128,128]{2,1,0:T(8,128)(2,1)S(1)} %get-tuple-element.85), channel_id=1, source_target_pairs={{0,16},{16,0},{1,17},{17,1},{2,18},{18,2},{3,19},{19,3},{4,20},{20... | collective-permute-start | bytes 196616 | tf_op jit(solution)/shard_map/ppermute | solution.py:549
  58.4 5.2 %collective-permute-start.17 = (bf16[2,128,128]{2,1,0:T(8,128)(2,1)S(1)}, bf16[2,128,128]{2,1,0:T(8,128)(2,1)S(1)}, u32[]{:S(2)}, u32[]{:S(2)}) collective-permute-start(bf16[2,128,128]{2,1,0:T(8,128)(2,1)S(1)} %get-tuple-element.86), channel_id=1, source_target_pairs={{0,20},{1,21},{2,22},{3,23},{4,16},{5,17},{6,18},{7,19},{8,28},{9,... | collective-permute-start | bytes 196616 | tf_op jit(solution)/shard_map/ppermute | solution.py:553
  63.9 9.3 %collective-permute-start.22 = (bf16[128,1536]{1,0:T(8,128)(2,1)S(1)}, bf16[128,1536]{1,0:T(8,128)(2,1)S(1)}, u32[]{:S(2)}, u32[]{:S(2)}) collective-permute-start(bf16[128,1536]{1,0:T(8,128)(2,1)S(1)} %get-tuple-element.92), channel_id=1, source_target_pairs={{0,1},{1,0},{2,3},{3,2},{4,5},{5,4},{6,7},{7,6},{8,9},{9,8},{10,11... | collective-permute-start | bytes 1179656 | tf_op jit(solution)/shard_map/ppermute | solution.py:504
  64.3 13.7 %collective-permute-start.20 = (bf16[128,768]{1,0:T(8,128)(2,1)S(1)}, bf16[128,768]{1,0:T(8,128)(2,1)S(1)}, u32[]{:S(2)}, u32[]{:S(2)}) collective-permute-start(bf16[128,768]{1,0:T(8,128)(2,1)S(1)} %get-tuple-element.90), channel_id=1, source_target_pairs={{0,2},{1,3},{2,0},{3,1},{4,6},{5,7},{6,4},{7,5},{8,10},{9,11},{10,... | collective-permute-start | bytes 589832 | tf_op jit(solution)/shard_map/ppermute | solution.py:504
  65.2 12.8 %collective-permute-start.21 = (bf16[128,768]{1,0:T(8,128)(2,1)S(1)}, bf16[128,768]{1,0:T(8,128)(2,1)S(1)}, u32[]{:S(2)}, u32[]{:S(2)}) collective-permute-start(bf16[128,768]{1,0:T(8,128)(2,1)S(1)} %get-tuple-element.91), channel_id=1, source_target_pairs={{0,3},{1,2},{2,1},{3,0},{4,7},{5,6},{6,5},{7,4},{8,11},{9,10},{10,... | collective-permute-start | bytes 589832 | tf_op jit(solution)/shard_map/ppermute | solution.py:504
  66.1 8.0 %collective-permute-start.23 = (bf16[128,128]{1,0:T(8,128)(2,1)S(1)}, bf16[128,128]{1,0:T(8,128)(2,1)S(1)}, u32[]{:S(2)}, u32[]{:S(2)}) collective-permute-start(bf16[128,128]{1,0:T(8,128)(2,1)S(1)} %get-tuple-element.93), channel_id=1, source_target_pairs={{0,0},{1,4},{2,8},{3,12},{4,2},{5,6},{6,10},{7,14},{8,16},{9,20},{... | collective-permute-start | bytes 98312 | tf_op jit(solution)/shard_map/ppermute | solution.py:486
  70.7 7.3 %collective-permute-start.24 = (bf16[128,128]{1,0:T(8,128)(2,1)S(1)}, bf16[128,128]{1,0:T(8,128)(2,1)S(1)}, u32[]{:S(2)}, u32[]{:S(2)}) collective-permute-start(bf16[128,128]{1,0:T(8,128)(2,1)S(1)} %get-tuple-element.94), channel_id=1, source_target_pairs={{0,16},{1,20},{2,24},{3,28},{4,18},{5,22},{6,26},{7,30},{8,0},{9,4... | collective-permute-start | bytes 98312 | tf_op jit(solution)/shard_map/ppermute | solution.py:486
  (9 other events, 27.5 us)

commit v7 on v6

--- a/solution.py
+++ b/solution.py
@@ -190,11 +190,11 @@
 def compute_kernel(c, mask_ref, *refs):
     first, count = spans()[c]
     kv, halo, qg, rest = refs[:2], refs[2:4], refs[4:6], refs[6:]
-    kw, vw, qs, gs, pm, dm, term = rest[-7:]
+    kw, vw, qs, gs, pm, dm, term, parts = rest[-8:]
     if c == 0:
-        own_ref, a_ref, b_ref, keep_ref, team_ref, clip_ref, both_ref, adapt = rest[:-7]
+        own_ref, a_ref, b_ref, keep_ref, team_ref, clip_ref, both_ref, adapt = rest[:-8]
     else:
-        adapt, *earlier, own_ref, a_ref, b_ref, keep_ref, clip_ref, both_ref = rest[:-7]
+        adapt, *earlier, own_ref, a_ref, b_ref, keep_ref, clip_ref, both_ref = rest[:-8]
     kind = adapt.dtype
     member, team = place()
     even = lax.rem(team, 2) == 0
@@ -290,12 +290,13 @@
             finish(item[0], adds)
             adds = []
     width = term.shape[1] // 4
-    quarters = [term[:, i * width : (i + 1) * width] for i in range(4)]
-    upper = bit_value("dp", lax.axis_size("dp") // 2, 1) == 1
+    for i in range(4):
+        parts[i, :, :width] = term[:, i * width : (i + 1) * width]
+    odd, high = lax.rem(team, 2), bit_value("dp", lax.axis_size("dp") // 2, 1)
 
     def quarter(other_team, other_clip):
-        odd, high = jnp.logical_not(even) ^ other_team, upper ^ other_clip
-        return jnp.where(odd, jnp.where(high, *quarters[3:1:-1]), jnp.where(high, *quarters[1::-1]))
+        index = 2 * jnp.bitwise_xor(odd, int(other_team)) + jnp.bitwise_xor(high, int(other_clip))
+        return parts[index, :, :width]
 
     keep_ref[:, :width] = quarter(False, False)
     leave = quarter(True, False).astype(kind)
@@ -342,6 +343,7 @@
         pltpu.VMEM((count * 2, (TILES + 1) * BLK, 2 * BLK), kind),
         pltpu.VMEM((count * 2, (TILES + 1) * BLK, 2 * BLK), kind),
         pltpu.VMEM((2 * RANK, count * HEAD_WIDTH), jnp.float32),
+        pltpu.VMEM((4, *part), jnp.float32),
     ]
     return call(
         functools.partial(compute_kernel, c), f"gradients_{c}", out_shape, inputs, scratch=scratch, vmem=16

time: 79.2 us -> 79.1 us (level)
  transfers between devices with their start and end apart: 25 -> 25, of which waited for: 8 -> 8; matrix products, arithmetic and copies ran while one was open for 0% -> 0% of each run, Pallas kernels for 18% -> 17%
where the time goes in v7:
time: 79.1 us; the launch traced here: 78.8 us
  starting transfers between devices  38.3 us (48%)
  waiting for transfers between devices  22.8 us (29%)
  Pallas kernels  16.7 us (21%)
  between operations  0.95 us (1%)
    pallas_call x12, Pallas kernels, call(): pl.pallas_call(kernel, out_shape=out_shape, in_specs=in_specs or [VMEM] *...  14.8 us
    ppermute x13, waiting for transfers between devices, partner(): lax.ppermute(block, 'seq', [(i, i ^ k) for i in range(seq)])  13.9 us
    ppermute x13, starting transfers between devices, partner(): lax.ppermute(block, 'seq', [(i, i ^ k) for i in range(seq)])  13 us
    ppermute x2, starting transfers between devices, reduce_terms(): arrived.append(lax.ppermute(piece, ('dp', 'seq'), route))  6.9 us
    ppermute x2, starting transfers between devices, body(): lax.ppermute(kv[c][0], 'seq', near_route)  6.88 us
    ppermute x2, waiting for transfers between devices, reduce_terms(): arrived.append(lax.ppermute(piece, ('dp', 'seq'), route))  4.07 us
    ppermute x2, starting transfers between devices, body(): parts.append((own, lax.ppermute(to_a, 'seq', swaps[0]), from_b, keep))  3.58 us
    ppermute x1, starting transfers between devices, body(): from_both = lax.ppermute(to_both, ('dp', 'seq'), both)  2.81 us
  transfers between devices with their start and end apart: 25, of which 8 were waited for; matrix products, arithmetic and copies ran while one was open for 0% of the time, Pallas kernels for 17%

profile of v7, /device:TPU:5, one launch (start us, length us, event | category | flops | bytes accessed | tf_op | source)
XLA Modules:
  0.0 78.8 jit_solution(11322007430839284140)
XLA Ops:
  0.7 2.0 %pack_side.1 = bf16[128,1664]{1,0:T(8,128)(2,1)} custom-call(bf16[1,128,3072]{2,1,0:T(8,128)(2,1)} %keys.1, bf16[1,128,3072]{2,1,0:T(8,128)(2,1)} %values.1, bf16[1,64,128]{2,1,0:T(8,128)(2,1)} %bitcast.6, bf16[1,64,128]{2,1,0:T(8,128)(2,1)} %bitcast.8), custom_call_target="tpu_custom_call" | custom-call | flops 1 | bytes 1 | tf_op jit(solution)/shard_map/pack_side/pallas_call | solution.py:30
  5.2 1.8 %mask.1.refs_0_.mask_ref = f32[120,128]{1,0:T(8,128)S(1)} custom-call(s32[5,16,24]{2,1,0:T(8,128)S(1)} %bitcast.10, s32[16,24]{1,0:T(8,128)S(1)} %bitcast.11, bf16[128,896]{1,0:T(8,128)(2,1)S(1)} %get-tuple-element.53._.mine_ref), custom_call_target="tpu_custom_call" | custom-call | flops 1 | bytes 1 | tf_op jit(solution)/shard_map/mask/pallas_call | solution.py:30
  7.7 3.7 %collective-permute-start.8 = (bf16[256,896]{1,0:T(8,128)(2,1)S(1)}, bf16[256,896]{1,0:T(8,128)(2,1)S(1)}, u32[]{:S(2)}, u32[]{:S(2)}) collective-permute-start(bf16[256,896]{1,0:T(8,128)(2,1)S(1)} %get-tuple-element.66.refs_0_), channel_id=1, source_target_pairs={{2,6},{3,7},{4,0},{5,1},{6,10},{7,11},{8,4},{9,5},{10,14},{11,15},... | collective-permute-start | bytes 1376264 | tf_op jit(solution)/shard_map/ppermute | solution.py:540
  11.9 5.1 %collective-permute-done.6.refs_0_.refs_1_ = bf16[256,896]{1,0:T(8,128)(2,1)S(1)} collective-permute-done((bf16[256,896]{1,0:T(8,128)(2,1)S(1)}, bf16[256,896]{1,0:T(8,128)(2,1)S(1)}, u32[]{:S(2)}, u32[]{:S(2)}) %collective-permute-start.6) | collective-permute-done | bytes 458784 | tf_op jit(solution)/shard_map/ppermute | solution.py:506
  16.9 1.3 %collective-permute-start.9 = (bf16[256,896]{1,0:T(8,128)(2,1)S(1)}, bf16[256,896]{1,0:T(8,128)(2,1)S(1)}, u32[]{:S(2)}, u32[]{:S(2)}) collective-permute-start(bf16[256,896]{1,0:T(8,128)(2,1)S(1)} %collective-permute-done.6.refs_0_.refs_1_), channel_id=1, source_target_pairs={{6,2},{7,3},{0,4},{1,5},{10,6},{11,7},{4,8},{5,9},{14,10},{15,11},... | collective-permute-start | bytes 1376264 | tf_op jit(solution)/shard_map/ppermute | solution.py:540
  18.3 2.2 %collective-permute-start.11 = (bf16[256,768]{1,0:T(8,128)(2,1)S(1)}, bf16[256,768]{1,0:T(8,128)(2,1)S(1)}, u32[]{:S(2)}, u32[]{:S(2)}) collective-permute-start(bf16[256,768]{1,0:T(8,128)(2,1)S(1)} %get-tuple-element.71), channel_id=1, source_target_pairs={{0,2},{1,3},{2,0},{3,1},{4,6},{5,7},{6,4},{7,5},{8,10},{9,11},{10,... | collective-permute-start | bytes 1179656 | tf_op jit(solution)/shard_map/ppermute | solution.py:506
  20.5 3.2 %collective-permute-start.2 = (bf16[256,768]{1,0:T(8,128)(2,1)S(1)}, bf16[256,768]{1,0:T(8,128)(2,1)S(1)}, u32[]{:S(2)}, u32[]{:S(2)}) collective-permute-start(bf16[256,768]{1,0:T(8,128)(2,1)S(1)} %get-tuple-element.57.refs_0_), channel_id=1, source_target_pairs={{2,6},{3,7},{4,0},{5,1},{6,10},{7,11},{8,4},{9,5},{10,14},{11,15},... | collective-permute-start | bytes 1179656 | tf_op jit(solution)/shard_map/ppermute | solution.py:540
  23.7 1.6 %collective-permute-done.1.refs_1_ = bf16[256,768]{1,0:T(8,128)(2,1)S(1)} collective-permute-done((bf16[256,768]{1,0:T(8,128)(2,1)S(1)}, bf16[256,768]{1,0:T(8,128)(2,1)S(1)}, u32[]{:S(2)}, u32[]{:S(2)}) %collective-permute-start.1) | collective-permute-done | bytes 393248 | tf_op jit(solution)/shard_map/ppermute | solution.py:506
  25.4 1.3 %collective-permute-start.3 = (bf16[256,768]{1,0:T(8,128)(2,1)S(1)}, bf16[256,768]{1,0:T(8,128)(2,1)S(1)}, u32[]{:S(2)}, u32[]{:S(2)}) collective-permute-start(bf16[256,768]{1,0:T(8,128)(2,1)S(1)} %collective-permute-done.1.refs_1_), channel_id=1, source_target_pairs={{6,2},{7,3},{0,4},{1,5},{10,6},{11,7},{4,8},{5,9},{14,10},{15,11},... | collective-permute-start | bytes 1179656 | tf_op jit(solution)/shard_map/ppermute | solution.py:540
  26.7 2.2 %collective-permute-start.7 = (bf16[256,768]{1,0:T(8,128)(2,1)S(1)}, bf16[256,768]{1,0:T(8,128)(2,1)S(1)}, u32[]{:S(2)}, u32[]{:S(2)}) collective-permute-start(bf16[256,768]{1,0:T(8,128)(2,1)S(1)} %get-tuple-element.65), channel_id=1, source_target_pairs={{0,2},{1,3},{2,0},{3,1},{4,6},{5,7},{6,4},{7,5},{8,10},{9,11},{10,... | collective-permute-start | bytes 1179656 | tf_op jit(solution)/shard_map/ppermute | solution.py:506
  29.0 4.8 %collective-permute-done.11.refs_5_ = bf16[256,768]{1,0:T(8,128)(2,1)S(1)} collective-permute-done((bf16[256,768]{1,0:T(8,128)(2,1)S(1)}, bf16[256,768]{1,0:T(8,128)(2,1)S(1)}, u32[]{:S(2)}, u32[]{:S(2)}) %collective-permute-start.11) | collective-permute-done | bytes 393248 | tf_op jit(solution)/shard_map/ppermute | solution.py:506
  33.8 4.7 %gradients_0.1 = (f32[512,768]{1,0:T(8,128)S(1)}, bf16[256,768]{1,0:T(8,128)(2,1)S(1)}, bf16[256,768]{1,0:T(8,128)(2,1)S(1)}, f32[128,128]{1,0:T(8,128)S(1)}, bf...) custom-call(f32[120,128]{1,0:T(8,128)S(1)} %mask.1.refs_0_.mask_ref,, ...), custom_call_target="tpu_custom_call" | custom-call | flops 1 | bytes 1 | tf_op jit(solution)/shard_map/gradients_0/pallas_call | solution.py:30
  38.5 1.4 %collective-permute-start.14 = (bf16[256,768]{1,0:T(8,128)(2,1)S(1)}, bf16[256,768]{1,0:T(8,128)(2,1)S(1)}, u32[]{:S(2)}, u32[]{:S(2)}) collective-permute-start(bf16[256,768]{1,0:T(8,128)(2,1)S(1)} %get-tuple-element.81), channel_id=1, source_target_pairs={{0,4},{4,0},{1,5},{5,1},{2,6},{6,2},{3,7},{7,3},{8,12},{12,8},{9,1... | collective-permute-start | bytes 1179656 | tf_op jit(solution)/shard_map/ppermute | solution.py:548
  40.5 1.7 %collective-permute-done.7.refs_5_ = bf16[256,768]{1,0:T(8,128)(2,1)S(1)} collective-permute-done((bf16[256,768]{1,0:T(8,128)(2,1)S(1)}, bf16[256,768]{1,0:T(8,128)(2,1)S(1)}, u32[]{:S(2)}, u32[]{:S(2)}) %collective-permute-start.7) | collective-permute-done | bytes 393248 | tf_op jit(solution)/shard_map/ppermute | solution.py:506
  42.2 4.6 %gradients_1.1 = (f32[512,768]{1,0:T(8,128)S(1)}, bf16[256,896]{1,0:T(8,128)(2,1)S(1)}, bf16[256,768]{1,0:T(8,128)(2,1)S(1)}, f32[128,128]{1,0:T(8,128)S(1)}, bf...) custom-call(f32[120,128]{1,0:T(8,128)S(1)} %mask.1.refs_0_.mask_ref, ...), custom_call_target="tpu_custom_call" | custom-call | flops 1 | bytes 1 | tf_op jit(solution)/shard_map/gradients_1/pallas_call | solution.py:30
  46.8 2.2 %collective-permute-start.12 = (bf16[256,896]{1,0:T(8,128)(2,1)S(1)}, bf16[256,896]{1,0:T(8,128)(2,1)S(1)}, u32[]{:S(2)}, u32[]{:S(2)}) collective-permute-start(bf16[256,896]{1,0:T(8,128)(2,1)S(1)} %get-tuple-element.77), channel_id=1, source_target_pairs={{0,4},{4,0},{1,5},{5,1},{2,6},{6,2},{3,7},{7,3},{8,12},{12,8},{9,1... | collective-permute-start | bytes 1376264 | tf_op jit(solution)/shard_map/ppermute | solution.py:548
  50.3 4.3 %collective-permute-start.19 = (bf16[128,768]{1,0:T(8,128)(2,1)S(1)}, bf16[128,768]{1,0:T(8,128)(2,1)S(1)}, u32[]{:S(2)}, u32[]{:S(2)}) collective-permute-start(bf16[128,768]{1,0:T(8,128)(2,1)S(1)} %get-tuple-element.88), channel_id=1, source_target_pairs={{0,3},{1,2},{2,1},{3,0},{4,7},{5,6},{6,5},{7,4},{8,11},{9,10},{10,... | collective-permute-start | bytes 589832 | tf_op jit(solution)/shard_map/ppermute | solution.py:506
  54.5 1.2 %collective-permute-start.16 = (bf16[2,128,128]{2,1,0:T(8,128)(2,1)S(1)}, bf16[2,128,128]{2,1,0:T(8,128)(2,1)S(1)}, u32[]{:S(2)}, u32[]{:S(2)}) collective-permute-start(bf16[2,128,128]{2,1,0:T(8,128)(2,1)S(1)} %get-tuple-element.85), channel_id=1, source_target_pairs={{0,16},{16,0},{1,17},{17,1},{2,18},{18,2},{3,19},{19,3},{4,20},{20... | collective-permute-start | bytes 196616 | tf_op jit(solution)/shard_map/ppermute | solution.py:551
  55.7 2.3 %collective-permute-done.16.refs_2_ = bf16[2,128,128]{2,1,0:T(8,128)(2,1)S(1)} collective-permute-done((bf16[2,128,128]{2,1,0:T(8,128)(2,1)S(1)}, bf16[2,128,128]{2,1,0:T(8,128)(2,1)S(1)}, u32[]{:S(2)}, u32[]{:S(2)}) %collective-permute-start.16) | collective-permute-done | bytes 65568 | tf_op jit(solution)/shard_map/ppermute | solution.py:551
  58.0 2.8 %collective-permute-start.17 = (bf16[2,128,128]{2,1,0:T(8,128)(2,1)S(1)}, bf16[2,128,128]{2,1,0:T(8,128)(2,1)S(1)}, u32[]{:S(2)}, u32[]{:S(2)}) collective-permute-start(bf16[2,128,128]{2,1,0:T(8,128)(2,1)S(1)} %get-tuple-element.86), channel_id=1, source_target_pairs={{0,20},{1,21},{2,22},{3,23},{4,16},{5,17},{6,18},{7,19},{8,28},{9,... | collective-permute-start | bytes 196616 | tf_op jit(solution)/shard_map/ppermute | solution.py:555
  60.8 2.6 %collective-permute-done.17.refs_3_ = bf16[2,128,128]{2,1,0:T(8,128)(2,1)S(1)} collective-permute-done((bf16[2,128,128]{2,1,0:T(8,128)(2,1)S(1)}, bf16[2,128,128]{2,1,0:T(8,128)(2,1)S(1)}, u32[]{:S(2)}, u32[]{:S(2)}) %collective-permute-start.17) | collective-permute-done | bytes 65568 | tf_op jit(solution)/shard_map/ppermute | solution.py:555
  65.9 4.7 %collective-permute-start.23 = (bf16[128,128]{1,0:T(8,128)(2,1)S(1)}, bf16[128,128]{1,0:T(8,128)(2,1)S(1)}, u32[]{:S(2)}, u32[]{:S(2)}) collective-permute-start(bf16[128,128]{1,0:T(8,128)(2,1)S(1)} %get-tuple-element.93), channel_id=1, source_target_pairs={{0,0},{1,4},{2,8},{3,12},{4,2},{5,6},{6,10},{7,14},{8,16},{9,20},{... | collective-permute-start | bytes 98312 | tf_op jit(solution)/shard_map/ppermute | solution.py:488
  70.5 2.2 %collective-permute-start.24 = (bf16[128,128]{1,0:T(8,128)(2,1)S(1)}, bf16[128,128]{1,0:T(8,128)(2,1)S(1)}, u32[]{:S(2)}, u32[]{:S(2)}) collective-permute-start(bf16[128,128]{1,0:T(8,128)(2,1)S(1)} %get-tuple-element.94), channel_id=1, source_target_pairs={{0,16},{1,20},{2,24},{3,28},{4,18},{5,22},{6,26},{7,30},{8,0},{9,4... | collective-permute-start | bytes 98312 | tf_op jit(solution)/shard_map/ppermute | solution.py:488
  73.7 4.1 %collective-permute-done.24.refs_5_ = bf16[128,128]{1,0:T(8,128)(2,1)S(1)} collective-permute-done((bf16[128,128]{1,0:T(8,128)(2,1)S(1)}, bf16[128,128]{1,0:T(8,128)(2,1)S(1)}, u32[]{:S(2)}, u32[]{:S(2)}) %collective-permute-start.24) | collective-permute-done | bytes 32800 | tf_op jit(solution)/shard_map/ppermute | solution.py:488
  (56 shorter events, 10.0 us)
Async XLA Ops:
  4.4 7.3 %collective-permute-start = (bf16[128,1536]{1,0:T(8,128)(2,1)S(1)}, bf16[128,1536]{1,0:T(8,128)(2,1)S(1)}, u32[]{:S(2)}, u32[]{:S(2)}) collective-permute-start(bf16[128,1536]{1,0:T(8,128)(2,1)S(1)} %get-tuple-element.56), channel_id=1, source_target_pairs={{0,1},{1,0},{2,3},{3,2},{4,5},{5,4},{6,7},{7,6},{8,9},{9,8},{10,11... | collective-permute-start | bytes 1179656 | tf_op jit(solution)/shard_map/ppermute | solution.py:506
  5.1 11.8 %collective-permute-start.6 = (bf16[256,896]{1,0:T(8,128)(2,1)S(1)}, bf16[256,896]{1,0:T(8,128)(2,1)S(1)}, u32[]{:S(2)}, u32[]{:S(2)}) collective-permute-start(bf16[256,896]{1,0:T(8,128)(2,1)S(1)} %get-tuple-element.63), channel_id=1, source_target_pairs={{0,2},{1,3},{2,0},{3,1},{4,6},{5,7},{6,4},{7,5},{8,10},{9,11},{10,... | collective-permute-start | bytes 1376264 | tf_op jit(solution)/shard_map/ppermute | solution.py:506
  7.2 11.0 %collective-permute-start.10 = (bf16[128,1536]{1,0:T(8,128)(2,1)S(1)}, bf16[128,1536]{1,0:T(8,128)(2,1)S(1)}, u32[]{:S(2)}, u32[]{:S(2)}) collective-permute-start(bf16[128,1536]{1,0:T(8,128)(2,1)S(1)} %get-tuple-element.69), channel_id=1, source_target_pairs={{0,1},{1,0},{2,3},{3,2},{4,5},{5,4},{6,7},{7,6},{8,9},{9,8},{10,11... | collective-permute-start | bytes 1179656 | tf_op jit(solution)/shard_map/ppermute | solution.py:506
  7.7 19.0 %collective-permute-start.8 = (bf16[256,896]{1,0:T(8,128)(2,1)S(1)}, bf16[256,896]{1,0:T(8,128)(2,1)S(1)}, u32[]{:S(2)}, u32[]{:S(2)}) collective-permute-start(bf16[256,896]{1,0:T(8,128)(2,1)S(1)} %get-tuple-element.66.refs_0_), channel_id=1, source_target_pairs={{2,6},{3,7},{4,0},{5,1},{6,10},{7,11},{8,4},{9,5},{10,14},{11,15},... | collective-permute-start | bytes 1376264 | tf_op jit(solution)/shard_map/ppermute | solution.py:540
  11.4 9.2 %collective-permute-start.4 = (bf16[128,1536]{1,0:T(8,128)(2,1)S(1)}, bf16[128,1536]{1,0:T(8,128)(2,1)S(1)}, u32[]{:S(2)}, u32[]{:S(2)}) collective-permute-start(bf16[128,1536]{1,0:T(8,128)(2,1)S(1)} %get-tuple-element.61), channel_id=1, source_target_pairs={{0,1},{1,0},{2,3},{3,2},{4,5},{5,4},{6,7},{7,6},{8,9},{9,8},{10,11... | collective-permute-start | bytes 1179656 | tf_op jit(solution)/shard_map/ppermute | solution.py:506
  11.8 13.6 %collective-permute-start.1 = (bf16[256,768]{1,0:T(8,128)(2,1)S(1)}, bf16[256,768]{1,0:T(8,128)(2,1)S(1)}, u32[]{:S(2)}, u32[]{:S(2)}) collective-permute-start(bf16[256,768]{1,0:T(8,128)(2,1)S(1)} %get-tuple-element.58), channel_id=1, source_target_pairs={{0,2},{1,3},{2,0},{3,1},{4,6},{5,7},{6,4},{7,5},{8,10},{9,11},{10,... | collective-permute-start | bytes 1179656 | tf_op jit(solution)/shard_map/ppermute | solution.py:506
  16.9 16.9 %collective-permute-start.9 = (bf16[256,896]{1,0:T(8,128)(2,1)S(1)}, bf16[256,896]{1,0:T(8,128)(2,1)S(1)}, u32[]{:S(2)}, u32[]{:S(2)}) collective-permute-start(bf16[256,896]{1,0:T(8,128)(2,1)S(1)} %collective-permute-done.6.refs_0_.refs_1_), channel_id=1, source_target_pairs={{6,2},{7,3},{0,4},{1,5},{10,6},{11,7},{4,8},{5,9},{14,10},{15,11},... | collective-permute-start | bytes 1376264 | tf_op jit(solution)/shard_map/ppermute | solution.py:540
  18.3 15.5 %collective-permute-start.11 = (bf16[256,768]{1,0:T(8,128)(2,1)S(1)}, bf16[256,768]{1,0:T(8,128)(2,1)S(1)}, u32[]{:S(2)}, u32[]{:S(2)}) collective-permute-start(bf16[256,768]{1,0:T(8,128)(2,1)S(1)} %get-tuple-element.71), channel_id=1, source_target_pairs={{0,2},{1,3},{2,0},{3,1},{4,6},{5,7},{6,4},{7,5},{8,10},{9,11},{10,... | collective-permute-start | bytes 1179656 | tf_op jit(solution)/shard_map/ppermute | solution.py:506
  20.5 20.0 %collective-permute-start.2 = (bf16[256,768]{1,0:T(8,128)(2,1)S(1)}, bf16[256,768]{1,0:T(8,128)(2,1)S(1)}, u32[]{:S(2)}, u32[]{:S(2)}) collective-permute-start(bf16[256,768]{1,0:T(8,128)(2,1)S(1)} %get-tuple-element.57.refs_0_), channel_id=1, source_target_pairs={{2,6},{3,7},{4,0},{5,1},{6,10},{7,11},{8,4},{9,5},{10,14},{11,15},... | collective-permute-start | bytes 1179656 | tf_op jit(solution)/shard_map/ppermute | solution.py:540
  25.4 15.2 %collective-permute-start.3 = (bf16[256,768]{1,0:T(8,128)(2,1)S(1)}, bf16[256,768]{1,0:T(8,128)(2,1)S(1)}, u32[]{:S(2)}, u32[]{:S(2)}) collective-permute-start(bf16[256,768]{1,0:T(8,128)(2,1)S(1)} %collective-permute-done.1.refs_1_), channel_id=1, source_target_pairs={{6,2},{7,3},{0,4},{1,5},{10,6},{11,7},{4,8},{5,9},{14,10},{15,11},... | collective-permute-start | bytes 1179656 | tf_op jit(solution)/shard_map/ppermute | solution.py:540
  26.7 15.5 %collective-permute-start.7 = (bf16[256,768]{1,0:T(8,128)(2,1)S(1)}, bf16[256,768]{1,0:T(8,128)(2,1)S(1)}, u32[]{:S(2)}, u32[]{:S(2)}) collective-permute-start(bf16[256,768]{1,0:T(8,128)(2,1)S(1)} %get-tuple-element.65), channel_id=1, source_target_pairs={{0,2},{1,3},{2,0},{3,1},{4,6},{5,7},{6,4},{7,5},{8,10},{9,11},{10,... | collective-permute-start | bytes 1179656 | tf_op jit(solution)/shard_map/ppermute | solution.py:506
  38.5 11.3 %collective-permute-start.14 = (bf16[256,768]{1,0:T(8,128)(2,1)S(1)}, bf16[256,768]{1,0:T(8,128)(2,1)S(1)}, u32[]{:S(2)}, u32[]{:S(2)}) collective-permute-start(bf16[256,768]{1,0:T(8,128)(2,1)S(1)} %get-tuple-element.81), channel_id=1, source_target_pairs={{0,4},{4,0},{1,5},{5,1},{2,6},{6,2},{3,7},{7,3},{8,12},{12,8},{9,1... | collective-permute-start | bytes 1179656 | tf_op jit(solution)/shard_map/ppermute | solution.py:548
  39.8 9.9 %collective-permute-start.15 = (bf16[256,768]{1,0:T(8,128)(2,1)S(1)}, bf16[256,768]{1,0:T(8,128)(2,1)S(1)}, u32[]{:S(2)}, u32[]{:S(2)}) collective-permute-start(bf16[256,768]{1,0:T(8,128)(2,1)S(1)} %get-tuple-element.82), channel_id=1, source_target_pairs={{4,8},{8,4},{5,9},{9,5},{6,10},{10,6},{7,11},{11,7},{20,24},{24,20... | collective-permute-start | bytes 1179656 | tf_op jit(solution)/shard_map/ppermute | solution.py:547
  46.8 16.5 %collective-permute-start.12 = (bf16[256,896]{1,0:T(8,128)(2,1)S(1)}, bf16[256,896]{1,0:T(8,128)(2,1)S(1)}, u32[]{:S(2)}, u32[]{:S(2)}) collective-permute-start(bf16[256,896]{1,0:T(8,128)(2,1)S(1)} %get-tuple-element.77), channel_id=1, source_target_pairs={{0,4},{4,0},{1,5},{5,1},{2,6},{6,2},{3,7},{7,3},{8,12},{12,8},{9,1... | collective-permute-start | bytes 1376264 | tf_op jit(solution)/shard_map/ppermute | solution.py:548
  49.0 14.3 %collective-permute-start.13 = (bf16[256,768]{1,0:T(8,128)(2,1)S(1)}, bf16[256,768]{1,0:T(8,128)(2,1)S(1)}, u32[]{:S(2)}, u32[]{:S(2)}) collective-permute-start(bf16[256,768]{1,0:T(8,128)(2,1)S(1)} %get-tuple-element.78), channel_id=1, source_target_pairs={{4,8},{8,4},{5,9},{9,5},{6,10},{10,6},{7,11},{11,7},{20,24},{24,20... | collective-permute-start | bytes 1179656 | tf_op jit(solution)/shard_map/ppermute | solution.py:547
  50.0 13.4 %collective-permute-start.18 = (bf16[128,768]{1,0:T(8,128)(2,1)S(1)}, bf16[128,768]{1,0:T(8,128)(2,1)S(1)}, u32[]{:S(2)}, u32[]{:S(2)}) collective-permute-start(bf16[128,768]{1,0:T(8,128)(2,1)S(1)} %get-tuple-element.87), channel_id=1, source_target_pairs={{0,2},{1,3},{2,0},{3,1},{4,6},{5,7},{6,4},{7,5},{8,10},{9,11},{10,... | collective-permute-start | bytes 589832 | tf_op jit(solution)/shard_map/ppermute | solution.py:506
  50.3 13.1 %collective-permute-start.19 = (bf16[128,768]{1,0:T(8,128)(2,1)S(1)}, bf16[128,768]{1,0:T(8,128)(2,1)S(1)}, u32[]{:S(2)}, u32[]{:S(2)}) collective-permute-start(bf16[128,768]{1,0:T(8,128)(2,1)S(1)} %get-tuple-element.88), channel_id=1, source_target_pairs={{0,3},{1,2},{2,1},{3,0},{4,7},{5,6},{6,5},{7,4},{8,11},{9,10},{10,... | collective-permute-start | bytes 589832 | tf_op jit(solution)/shard_map/ppermute | solution.py:506
  54.5 3.5 %collective-permute-start.16 = (bf16[2,128,128]{2,1,0:T(8,128)(2,1)S(1)}, bf16[2,128,128]{2,1,0:T(8,128)(2,1)S(1)}, u32[]{:S(2)}, u32[]{:S(2)}) collective-permute-start(bf16[2,128,128]{2,1,0:T(8,128)(2,1)S(1)} %get-tuple-element.85), channel_id=1, source_target_pairs={{0,16},{16,0},{1,17},{17,1},{2,18},{18,2},{3,19},{19,3},{4,20},{20... | collective-permute-start | bytes 196616 | tf_op jit(solution)/shard_map/ppermute | solution.py:551
  58.0 5.4 %collective-permute-start.17 = (bf16[2,128,128]{2,1,0:T(8,128)(2,1)S(1)}, bf16[2,128,128]{2,1,0:T(8,128)(2,1)S(1)}, u32[]{:S(2)}, u32[]{:S(2)}) collective-permute-start(bf16[2,128,128]{2,1,0:T(8,128)(2,1)S(1)} %get-tuple-element.86), channel_id=1, source_target_pairs={{0,20},{1,21},{2,22},{3,23},{4,16},{5,17},{6,18},{7,19},{8,28},{9,... | collective-permute-start | bytes 196616 | tf_op jit(solution)/shard_map/ppermute | solution.py:555
  63.6 9.1 %collective-permute-start.22 = (bf16[128,1536]{1,0:T(8,128)(2,1)S(1)}, bf16[128,1536]{1,0:T(8,128)(2,1)S(1)}, u32[]{:S(2)}, u32[]{:S(2)}) collective-permute-start(bf16[128,1536]{1,0:T(8,128)(2,1)S(1)} %get-tuple-element.92), channel_id=1, source_target_pairs={{0,1},{1,0},{2,3},{3,2},{4,5},{5,4},{6,7},{7,6},{8,9},{9,8},{10,11... | collective-permute-start | bytes 1179656 | tf_op jit(solution)/shard_map/ppermute | solution.py:506
  64.1 13.7 %collective-permute-start.20 = (bf16[128,768]{1,0:T(8,128)(2,1)S(1)}, bf16[128,768]{1,0:T(8,128)(2,1)S(1)}, u32[]{:S(2)}, u32[]{:S(2)}) collective-permute-start(bf16[128,768]{1,0:T(8,128)(2,1)S(1)} %get-tuple-element.90), channel_id=1, source_target_pairs={{0,2},{1,3},{2,0},{3,1},{4,6},{5,7},{6,4},{7,5},{8,10},{9,11},{10,... | collective-permute-start | bytes 589832 | tf_op jit(solution)/shard_map/ppermute | solution.py:506
  65.0 12.9 %collective-permute-start.21 = (bf16[128,768]{1,0:T(8,128)(2,1)S(1)}, bf16[128,768]{1,0:T(8,128)(2,1)S(1)}, u32[]{:S(2)}, u32[]{:S(2)}) collective-permute-start(bf16[128,768]{1,0:T(8,128)(2,1)S(1)} %get-tuple-element.91), channel_id=1, source_target_pairs={{0,3},{1,2},{2,1},{3,0},{4,7},{5,6},{6,5},{7,4},{8,11},{9,10},{10,... | collective-permute-start | bytes 589832 | tf_op jit(solution)/shard_map/ppermute | solution.py:506
  65.9 7.9 %collective-permute-start.23 = (bf16[128,128]{1,0:T(8,128)(2,1)S(1)}, bf16[128,128]{1,0:T(8,128)(2,1)S(1)}, u32[]{:S(2)}, u32[]{:S(2)}) collective-permute-start(bf16[128,128]{1,0:T(8,128)(2,1)S(1)} %get-tuple-element.93), channel_id=1, source_target_pairs={{0,0},{1,4},{2,8},{3,12},{4,2},{5,6},{6,10},{7,14},{8,16},{9,20},{... | collective-permute-start | bytes 98312 | tf_op jit(solution)/shard_map/ppermute | solution.py:488
  70.5 7.3 %collective-permute-start.24 = (bf16[128,128]{1,0:T(8,128)(2,1)S(1)}, bf16[128,128]{1,0:T(8,128)(2,1)S(1)}, u32[]{:S(2)}, u32[]{:S(2)}) collective-permute-start(bf16[128,128]{1,0:T(8,128)(2,1)S(1)} %get-tuple-element.94), channel_id=1, source_target_pairs={{0,16},{1,20},{2,24},{3,28},{4,18},{5,22},{6,26},{7,30},{8,0},{9,4... | collective-permute-start | bytes 98312 | tf_op jit(solution)/shard_map/ppermute | solution.py:488
  (9 other events, 27.5 us)

commit v8 on v7

--- a/solution.py
+++ b/solution.py
@@ -258,7 +258,8 @@
             for weight, tile in zip(weights, tiles):
                 probs = weight * inverse
                 pm[index, tile, lanes] = probs.astype(kind)
-                dm[index, tile, lanes] = (probs * (dprobs[tile, lanes] - delta)).astype(kind)
+            for weight, tile in zip(weights, tiles):
+                dm[index, tile, lanes] = (weight * inverse * (dprobs[tile, lanes] - delta)).astype(kind)
 
     def spread(h, pair):
         index, two = h * 2 + pair, rows(2 * pair, 2)

time: 79.1 us -> 79.1 us (level)
  no operation moved by 1% of the time
where the time goes in v8:
time: 79.1 us; the launch traced here: 78.8 us
  starting transfers between devices  38.3 us (48%)
  waiting for transfers between devices  22.8 us (29%)
  Pallas kernels  16.7 us (21%)
  between operations  0.95 us (1%)
    pallas_call x12, Pallas kernels, call(): pl.pallas_call(kernel, out_shape=out_shape, in_specs=in_specs or [VMEM] *...  14.8 us
    ppermute x13, waiting for transfers between devices, partner(): lax.ppermute(block, 'seq', [(i, i ^ k) for i in range(seq)])  13.9 us
    ppermute x13, starting transfers between devices, partner(): lax.ppermute(block, 'seq', [(i, i ^ k) for i in range(seq)])  13 us
    ppermute x2, starting transfers between devices, reduce_terms(): arrived.append(lax.ppermute(piece, ('dp', 'seq'), route))  6.9 us
    ppermute x2, starting transfers between devices, body(): lax.ppermute(kv[c][0], 'seq', near_route)  6.88 us
    ppermute x2, waiting for transfers between devices, reduce_terms(): arrived.append(lax.ppermute(piece, ('dp', 'seq'), route))  4.07 us
    ppermute x2, starting transfers between devices, body(): parts.append((own, lax.ppermute(to_a, 'seq', swaps[0]), from_b, keep))  3.58 us
    ppermute x1, starting transfers between devices, body(): from_both = lax.ppermute(to_both, ('dp', 'seq'), both)  2.81 us
  transfers between devices with their start and end apart: 25, of which 8 were waited for; matrix products, arithmetic and copies ran while one was open for 0% of the time, Pallas kernels for 17%

profile of v8, /device:TPU:5, one launch (start us, length us, event | category | flops | bytes accessed | tf_op | source)
XLA Modules:
  0.0 78.8 jit_solution(11322007430839284140)
XLA Ops:
  0.7 2.0 %pack_side.1 = bf16[128,1664]{1,0:T(8,128)(2,1)} custom-call(bf16[1,128,3072]{2,1,0:T(8,128)(2,1)} %keys.1, bf16[1,128,3072]{2,1,0:T(8,128)(2,1)} %values.1, bf16[1,64,128]{2,1,0:T(8,128)(2,1)} %bitcast.6, bf16[1,64,128]{2,1,0:T(8,128)(2,1)} %bitcast.8), custom_call_target="tpu_custom_call" | custom-call | flops 1 | bytes 1 | tf_op jit(solution)/shard_map/pack_side/pallas_call | solution.py:30
  5.2 1.8 %mask.1.refs_0_.mask_ref = f32[120,128]{1,0:T(8,128)S(1)} custom-call(s32[5,16,24]{2,1,0:T(8,128)S(1)} %bitcast.10, s32[16,24]{1,0:T(8,128)S(1)} %bitcast.11, bf16[128,896]{1,0:T(8,128)(2,1)S(1)} %get-tuple-element.53._.mine_ref), custom_call_target="tpu_custom_call" | custom-call | flops 1 | bytes 1 | tf_op jit(solution)/shard_map/mask/pallas_call | solution.py:30
  7.7 3.7 %collective-permute-start.8 = (bf16[256,896]{1,0:T(8,128)(2,1)S(1)}, bf16[256,896]{1,0:T(8,128)(2,1)S(1)}, u32[]{:S(2)}, u32[]{:S(2)}) collective-permute-start(bf16[256,896]{1,0:T(8,128)(2,1)S(1)} %get-tuple-element.66.refs_0_), channel_id=1, source_target_pairs={{2,6},{3,7},{4,0},{5,1},{6,10},{7,11},{8,4},{9,5},{10,14},{11,15},... | collective-permute-start | bytes 1376264 | tf_op jit(solution)/shard_map/ppermute | solution.py:541
  11.9 5.1 %collective-permute-done.6.refs_0_.refs_1_ = bf16[256,896]{1,0:T(8,128)(2,1)S(1)} collective-permute-done((bf16[256,896]{1,0:T(8,128)(2,1)S(1)}, bf16[256,896]{1,0:T(8,128)(2,1)S(1)}, u32[]{:S(2)}, u32[]{:S(2)}) %collective-permute-start.6) | collective-permute-done | bytes 458784 | tf_op jit(solution)/shard_map/ppermute | solution.py:507
  16.9 1.3 %collective-permute-start.9 = (bf16[256,896]{1,0:T(8,128)(2,1)S(1)}, bf16[256,896]{1,0:T(8,128)(2,1)S(1)}, u32[]{:S(2)}, u32[]{:S(2)}) collective-permute-start(bf16[256,896]{1,0:T(8,128)(2,1)S(1)} %collective-permute-done.6.refs_0_.refs_1_), channel_id=1, source_target_pairs={{6,2},{7,3},{0,4},{1,5},{10,6},{11,7},{4,8},{5,9},{14,10},{15,11},... | collective-permute-start | bytes 1376264 | tf_op jit(solution)/shard_map/ppermute | solution.py:541
  18.3 2.2 %collective-permute-start.11 = (bf16[256,768]{1,0:T(8,128)(2,1)S(1)}, bf16[256,768]{1,0:T(8,128)(2,1)S(1)}, u32[]{:S(2)}, u32[]{:S(2)}) collective-permute-start(bf16[256,768]{1,0:T(8,128)(2,1)S(1)} %get-tuple-element.71), channel_id=1, source_target_pairs={{0,2},{1,3},{2,0},{3,1},{4,6},{5,7},{6,4},{7,5},{8,10},{9,11},{10,... | collective-permute-start | bytes 1179656 | tf_op jit(solution)/shard_map/ppermute | solution.py:507
  20.5 3.2 %collective-permute-start.2 = (bf16[256,768]{1,0:T(8,128)(2,1)S(1)}, bf16[256,768]{1,0:T(8,128)(2,1)S(1)}, u32[]{:S(2)}, u32[]{:S(2)}) collective-permute-start(bf16[256,768]{1,0:T(8,128)(2,1)S(1)} %get-tuple-element.57.refs_0_), channel_id=1, source_target_pairs={{2,6},{3,7},{4,0},{5,1},{6,10},{7,11},{8,4},{9,5},{10,14},{11,15},... | collective-permute-start | bytes 1179656 | tf_op jit(solution)/shard_map/ppermute | solution.py:541
  23.7 1.6 %collective-permute-done.1.refs_1_ = bf16[256,768]{1,0:T(8,128)(2,1)S(1)} collective-permute-done((bf16[256,768]{1,0:T(8,128)(2,1)S(1)}, bf16[256,768]{1,0:T(8,128)(2,1)S(1)}, u32[]{:S(2)}, u32[]{:S(2)}) %collective-permute-start.1) | collective-permute-done | bytes 393248 | tf_op jit(solution)/shard_map/ppermute | solution.py:507
  25.4 1.3 %collective-permute-start.3 = (bf16[256,768]{1,0:T(8,128)(2,1)S(1)}, bf16[256,768]{1,0:T(8,128)(2,1)S(1)}, u32[]{:S(2)}, u32[]{:S(2)}) collective-permute-start(bf16[256,768]{1,0:T(8,128)(2,1)S(1)} %collective-permute-done.1.refs_1_), channel_id=1, source_target_pairs={{6,2},{7,3},{0,4},{1,5},{10,6},{11,7},{4,8},{5,9},{14,10},{15,11},... | collective-permute-start | bytes 1179656 | tf_op jit(solution)/shard_map/ppermute | solution.py:541
  26.7 2.2 %collective-permute-start.7 = (bf16[256,768]{1,0:T(8,128)(2,1)S(1)}, bf16[256,768]{1,0:T(8,128)(2,1)S(1)}, u32[]{:S(2)}, u32[]{:S(2)}) collective-permute-start(bf16[256,768]{1,0:T(8,128)(2,1)S(1)} %get-tuple-element.65), channel_id=1, source_target_pairs={{0,2},{1,3},{2,0},{3,1},{4,6},{5,7},{6,4},{7,5},{8,10},{9,11},{10,... | collective-permute-start | bytes 1179656 | tf_op jit(solution)/shard_map/ppermute | solution.py:507
  29.0 4.8 %collective-permute-done.11.refs_5_ = bf16[256,768]{1,0:T(8,128)(2,1)S(1)} collective-permute-done((bf16[256,768]{1,0:T(8,128)(2,1)S(1)}, bf16[256,768]{1,0:T(8,128)(2,1)S(1)}, u32[]{:S(2)}, u32[]{:S(2)}) %collective-permute-start.11) | collective-permute-done | bytes 393248 | tf_op jit(solution)/shard_map/ppermute | solution.py:507
  33.8 4.7 %gradients_0.1 = (f32[512,768]{1,0:T(8,128)S(1)}, bf16[256,768]{1,0:T(8,128)(2,1)S(1)}, bf16[256,768]{1,0:T(8,128)(2,1)S(1)}, f32[128,128]{1,0:T(8,128)S(1)}, bf...) custom-call(f32[120,128]{1,0:T(8,128)S(1)} %mask.1.refs_0_.mask_ref,, ...), custom_call_target="tpu_custom_call" | custom-call | flops 1 | bytes 1 | tf_op jit(solution)/shard_map/gradients_0/pallas_call | solution.py:30
  38.5 1.4 %collective-permute-start.14 = (bf16[256,768]{1,0:T(8,128)(2,1)S(1)}, bf16[256,768]{1,0:T(8,128)(2,1)S(1)}, u32[]{:S(2)}, u32[]{:S(2)}) collective-permute-start(bf16[256,768]{1,0:T(8,128)(2,1)S(1)} %get-tuple-element.81), channel_id=1, source_target_pairs={{0,4},{4,0},{1,5},{5,1},{2,6},{6,2},{3,7},{7,3},{8,12},{12,8},{9,1... | collective-permute-start | bytes 1179656 | tf_op jit(solution)/shard_map/ppermute | solution.py:549
  40.5 1.7 %collective-permute-done.7.refs_5_ = bf16[256,768]{1,0:T(8,128)(2,1)S(1)} collective-permute-done((bf16[256,768]{1,0:T(8,128)(2,1)S(1)}, bf16[256,768]{1,0:T(8,128)(2,1)S(1)}, u32[]{:S(2)}, u32[]{:S(2)}) %collective-permute-start.7) | collective-permute-done | bytes 393248 | tf_op jit(solution)/shard_map/ppermute | solution.py:507
  42.2 4.6 %gradients_1.1 = (f32[512,768]{1,0:T(8,128)S(1)}, bf16[256,896]{1,0:T(8,128)(2,1)S(1)}, bf16[256,768]{1,0:T(8,128)(2,1)S(1)}, f32[128,128]{1,0:T(8,128)S(1)}, bf...) custom-call(f32[120,128]{1,0:T(8,128)S(1)} %mask.1.refs_0_.mask_ref, ...), custom_call_target="tpu_custom_call" | custom-call | flops 1 | bytes 1 | tf_op jit(solution)/shard_map/gradients_1/pallas_call | solution.py:30
  46.8 2.2 %collective-permute-start.12 = (bf16[256,896]{1,0:T(8,128)(2,1)S(1)}, bf16[256,896]{1,0:T(8,128)(2,1)S(1)}, u32[]{:S(2)}, u32[]{:S(2)}) collective-permute-start(bf16[256,896]{1,0:T(8,128)(2,1)S(1)} %get-tuple-element.77), channel_id=1, source_target_pairs={{0,4},{4,0},{1,5},{5,1},{2,6},{6,2},{3,7},{7,3},{8,12},{12,8},{9,1... | collective-permute-start | bytes 1376264 | tf_op jit(solution)/shard_map/ppermute | solution.py:549
  50.3 4.3 %collective-permute-start.19 = (bf16[128,768]{1,0:T(8,128)(2,1)S(1)}, bf16[128,768]{1,0:T(8,128)(2,1)S(1)}, u32[]{:S(2)}, u32[]{:S(2)}) collective-permute-start(bf16[128,768]{1,0:T(8,128)(2,1)S(1)} %get-tuple-element.88), channel_id=1, source_target_pairs={{0,3},{1,2},{2,1},{3,0},{4,7},{5,6},{6,5},{7,4},{8,11},{9,10},{10,... | collective-permute-start | bytes 589832 | tf_op jit(solution)/shard_map/ppermute | solution.py:507
  54.5 1.2 %collective-permute-start.16 = (bf16[2,128,128]{2,1,0:T(8,128)(2,1)S(1)}, bf16[2,128,128]{2,1,0:T(8,128)(2,1)S(1)}, u32[]{:S(2)}, u32[]{:S(2)}) collective-permute-start(bf16[2,128,128]{2,1,0:T(8,128)(2,1)S(1)} %get-tuple-element.85), channel_id=1, source_target_pairs={{0,16},{16,0},{1,17},{17,1},{2,18},{18,2},{3,19},{19,3},{4,20},{20... | collective-permute-start | bytes 196616 | tf_op jit(solution)/shard_map/ppermute | solution.py:552
  55.7 2.3 %collective-permute-done.16.refs_2_ = bf16[2,128,128]{2,1,0:T(8,128)(2,1)S(1)} collective-permute-done((bf16[2,128,128]{2,1,0:T(8,128)(2,1)S(1)}, bf16[2,128,128]{2,1,0:T(8,128)(2,1)S(1)}, u32[]{:S(2)}, u32[]{:S(2)}) %collective-permute-start.16) | collective-permute-done | bytes 65568 | tf_op jit(solution)/shard_map/ppermute | solution.py:552
  58.0 2.8 %collective-permute-start.17 = (bf16[2,128,128]{2,1,0:T(8,128)(2,1)S(1)}, bf16[2,128,128]{2,1,0:T(8,128)(2,1)S(1)}, u32[]{:S(2)}, u32[]{:S(2)}) collective-permute-start(bf16[2,128,128]{2,1,0:T(8,128)(2,1)S(1)} %get-tuple-element.86), channel_id=1, source_target_pairs={{0,20},{1,21},{2,22},{3,23},{4,16},{5,17},{6,18},{7,19},{8,28},{9,... | collective-permute-start | bytes 196616 | tf_op jit(solution)/shard_map/ppermute | solution.py:556
  60.8 2.6 %collective-permute-done.17.refs_3_ = bf16[2,128,128]{2,1,0:T(8,128)(2,1)S(1)} collective-permute-done((bf16[2,128,128]{2,1,0:T(8,128)(2,1)S(1)}, bf16[2,128,128]{2,1,0:T(8,128)(2,1)S(1)}, u32[]{:S(2)}, u32[]{:S(2)}) %collective-permute-start.17) | collective-permute-done | bytes 65568 | tf_op jit(solution)/shard_map/ppermute | solution.py:556
  65.9 4.7 %collective-permute-start.23 = (bf16[128,128]{1,0:T(8,128)(2,1)S(1)}, bf16[128,128]{1,0:T(8,128)(2,1)S(1)}, u32[]{:S(2)}, u32[]{:S(2)}) collective-permute-start(bf16[128,128]{1,0:T(8,128)(2,1)S(1)} %get-tuple-element.93), channel_id=1, source_target_pairs={{0,0},{1,4},{2,8},{3,12},{4,2},{5,6},{6,10},{7,14},{8,16},{9,20},{... | collective-permute-start | bytes 98312 | tf_op jit(solution)/shard_map/ppermute | solution.py:489
  70.5 2.2 %collective-permute-start.24 = (bf16[128,128]{1,0:T(8,128)(2,1)S(1)}, bf16[128,128]{1,0:T(8,128)(2,1)S(1)}, u32[]{:S(2)}, u32[]{:S(2)}) collective-permute-start(bf16[128,128]{1,0:T(8,128)(2,1)S(1)} %get-tuple-element.94), channel_id=1, source_target_pairs={{0,16},{1,20},{2,24},{3,28},{4,18},{5,22},{6,26},{7,30},{8,0},{9,4... | collective-permute-start | bytes 98312 | tf_op jit(solution)/shard_map/ppermute | solution.py:489
  73.7 4.1 %collective-permute-done.24.refs_5_ = bf16[128,128]{1,0:T(8,128)(2,1)S(1)} collective-permute-done((bf16[128,128]{1,0:T(8,128)(2,1)S(1)}, bf16[128,128]{1,0:T(8,128)(2,1)S(1)}, u32[]{:S(2)}, u32[]{:S(2)}) %collective-permute-start.24) | collective-permute-done | bytes 32800 | tf_op jit(solution)/shard_map/ppermute | solution.py:489
  (56 shorter events, 10.0 us)
Async XLA Ops:
  4.4 7.3 %collective-permute-start = (bf16[128,1536]{1,0:T(8,128)(2,1)S(1)}, bf16[128,1536]{1,0:T(8,128)(2,1)S(1)}, u32[]{:S(2)}, u32[]{:S(2)}) collective-permute-start(bf16[128,1536]{1,0:T(8,128)(2,1)S(1)} %get-tuple-element.56), channel_id=1, source_target_pairs={{0,1},{1,0},{2,3},{3,2},{4,5},{5,4},{6,7},{7,6},{8,9},{9,8},{10,11... | collective-permute-start | bytes 1179656 | tf_op jit(solution)/shard_map/ppermute | solution.py:507
  5.1 11.8 %collective-permute-start.6 = (bf16[256,896]{1,0:T(8,128)(2,1)S(1)}, bf16[256,896]{1,0:T(8,128)(2,1)S(1)}, u32[]{:S(2)}, u32[]{:S(2)}) collective-permute-start(bf16[256,896]{1,0:T(8,128)(2,1)S(1)} %get-tuple-element.63), channel_id=1, source_target_pairs={{0,2},{1,3},{2,0},{3,1},{4,6},{5,7},{6,4},{7,5},{8,10},{9,11},{10,... | collective-permute-start | bytes 1376264 | tf_op jit(solution)/shard_map/ppermute | solution.py:507
  7.2 11.0 %collective-permute-start.10 = (bf16[128,1536]{1,0:T(8,128)(2,1)S(1)}, bf16[128,1536]{1,0:T(8,128)(2,1)S(1)}, u32[]{:S(2)}, u32[]{:S(2)}) collective-permute-start(bf16[128,1536]{1,0:T(8,128)(2,1)S(1)} %get-tuple-element.69), channel_id=1, source_target_pairs={{0,1},{1,0},{2,3},{3,2},{4,5},{5,4},{6,7},{7,6},{8,9},{9,8},{10,11... | collective-permute-start | bytes 1179656 | tf_op jit(solution)/shard_map/ppermute | solution.py:507
  7.7 19.0 %collective-permute-start.8 = (bf16[256,896]{1,0:T(8,128)(2,1)S(1)}, bf16[256,896]{1,0:T(8,128)(2,1)S(1)}, u32[]{:S(2)}, u32[]{:S(2)}) collective-permute-start(bf16[256,896]{1,0:T(8,128)(2,1)S(1)} %get-tuple-element.66.refs_0_), channel_id=1, source_target_pairs={{2,6},{3,7},{4,0},{5,1},{6,10},{7,11},{8,4},{9,5},{10,14},{11,15},... | collective-permute-start | bytes 1376264 | tf_op jit(solution)/shard_map/ppermute | solution.py:541
  11.4 9.2 %collective-permute-start.4 = (bf16[128,1536]{1,0:T(8,128)(2,1)S(1)}, bf16[128,1536]{1,0:T(8,128)(2,1)S(1)}, u32[]{:S(2)}, u32[]{:S(2)}) collective-permute-start(bf16[128,1536]{1,0:T(8,128)(2,1)S(1)} %get-tuple-element.61), channel_id=1, source_target_pairs={{0,1},{1,0},{2,3},{3,2},{4,5},{5,4},{6,7},{7,6},{8,9},{9,8},{10,11... | collective-permute-start | bytes 1179656 | tf_op jit(solution)/shard_map/ppermute | solution.py:507
  11.8 13.6 %collective-permute-start.1 = (bf16[256,768]{1,0:T(8,128)(2,1)S(1)}, bf16[256,768]{1,0:T(8,128)(2,1)S(1)}, u32[]{:S(2)}, u32[]{:S(2)}) collective-permute-start(bf16[256,768]{1,0:T(8,128)(2,1)S(1)} %get-tuple-element.58), channel_id=1, source_target_pairs={{0,2},{1,3},{2,0},{3,1},{4,6},{5,7},{6,4},{7,5},{8,10},{9,11},{10,... | collective-permute-start | bytes 1179656 | tf_op jit(solution)/shard_map/ppermute | solution.py:507
  16.9 16.9 %collective-permute-start.9 = (bf16[256,896]{1,0:T(8,128)(2,1)S(1)}, bf16[256,896]{1,0:T(8,128)(2,1)S(1)}, u32[]{:S(2)}, u32[]{:S(2)}) collective-permute-start(bf16[256,896]{1,0:T(8,128)(2,1)S(1)} %collective-permute-done.6.refs_0_.refs_1_), channel_id=1, source_target_pairs={{6,2},{7,3},{0,4},{1,5},{10,6},{11,7},{4,8},{5,9},{14,10},{15,11},... | collective-permute-start | bytes 1376264 | tf_op jit(solution)/shard_map/ppermute | solution.py:541
  18.3 15.5 %collective-permute-start.11 = (bf16[256,768]{1,0:T(8,128)(2,1)S(1)}, bf16[256,768]{1,0:T(8,128)(2,1)S(1)}, u32[]{:S(2)}, u32[]{:S(2)}) collective-permute-start(bf16[256,768]{1,0:T(8,128)(2,1)S(1)} %get-tuple-element.71), channel_id=1, source_target_pairs={{0,2},{1,3},{2,0},{3,1},{4,6},{5,7},{6,4},{7,5},{8,10},{9,11},{10,... | collective-permute-start | bytes 1179656 | tf_op jit(solution)/shard_map/ppermute | solution.py:507
  20.5 20.0 %collective-permute-start.2 = (bf16[256,768]{1,0:T(8,128)(2,1)S(1)}, bf16[256,768]{1,0:T(8,128)(2,1)S(1)}, u32[]{:S(2)}, u32[]{:S(2)}) collective-permute-start(bf16[256,768]{1,0:T(8,128)(2,1)S(1)} %get-tuple-element.57.refs_0_), channel_id=1, source_target_pairs={{2,6},{3,7},{4,0},{5,1},{6,10},{7,11},{8,4},{9,5},{10,14},{11,15},... | collective-permute-start | bytes 1179656 | tf_op jit(solution)/shard_map/ppermute | solution.py:541
  25.4 15.2 %collective-permute-start.3 = (bf16[256,768]{1,0:T(8,128)(2,1)S(1)}, bf16[256,768]{1,0:T(8,128)(2,1)S(1)}, u32[]{:S(2)}, u32[]{:S(2)}) collective-permute-start(bf16[256,768]{1,0:T(8,128)(2,1)S(1)} %collective-permute-done.1.refs_1_), channel_id=1, source_target_pairs={{6,2},{7,3},{0,4},{1,5},{10,6},{11,7},{4,8},{5,9},{14,10},{15,11},... | collective-permute-start | bytes 1179656 | tf_op jit(solution)/shard_map/ppermute | solution.py:541
  26.7 15.5 %collective-permute-start.7 = (bf16[256,768]{1,0:T(8,128)(2,1)S(1)}, bf16[256,768]{1,0:T(8,128)(2,1)S(1)}, u32[]{:S(2)}, u32[]{:S(2)}) collective-permute-start(bf16[256,768]{1,0:T(8,128)(2,1)S(1)} %get-tuple-element.65), channel_id=1, source_target_pairs={{0,2},{1,3},{2,0},{3,1},{4,6},{5,7},{6,4},{7,5},{8,10},{9,11},{10,... | collective-permute-start | bytes 1179656 | tf_op jit(solution)/shard_map/ppermute | solution.py:507
  38.5 11.3 %collective-permute-start.14 = (bf16[256,768]{1,0:T(8,128)(2,1)S(1)}, bf16[256,768]{1,0:T(8,128)(2,1)S(1)}, u32[]{:S(2)}, u32[]{:S(2)}) collective-permute-start(bf16[256,768]{1,0:T(8,128)(2,1)S(1)} %get-tuple-element.81), channel_id=1, source_target_pairs={{0,4},{4,0},{1,5},{5,1},{2,6},{6,2},{3,7},{7,3},{8,12},{12,8},{9,1... | collective-permute-start | bytes 1179656 | tf_op jit(solution)/shard_map/ppermute | solution.py:549
  39.8 9.9 %collective-permute-start.15 = (bf16[256,768]{1,0:T(8,128)(2,1)S(1)}, bf16[256,768]{1,0:T(8,128)(2,1)S(1)}, u32[]{:S(2)}, u32[]{:S(2)}) collective-permute-start(bf16[256,768]{1,0:T(8,128)(2,1)S(1)} %get-tuple-element.82), channel_id=1, source_target_pairs={{4,8},{8,4},{5,9},{9,5},{6,10},{10,6},{7,11},{11,7},{20,24},{24,20... | collective-permute-start | bytes 1179656 | tf_op jit(solution)/shard_map/ppermute | solution.py:548
  46.8 16.5 %collective-permute-start.12 = (bf16[256,896]{1,0:T(8,128)(2,1)S(1)}, bf16[256,896]{1,0:T(8,128)(2,1)S(1)}, u32[]{:S(2)}, u32[]{:S(2)}) collective-permute-start(bf16[256,896]{1,0:T(8,128)(2,1)S(1)} %get-tuple-element.77), channel_id=1, source_target_pairs={{0,4},{4,0},{1,5},{5,1},{2,6},{6,2},{3,7},{7,3},{8,12},{12,8},{9,1... | collective-permute-start | bytes 1376264 | tf_op jit(solution)/shard_map/ppermute | solution.py:549
  49.0 14.3 %collective-permute-start.13 = (bf16[256,768]{1,0:T(8,128)(2,1)S(1)}, bf16[256,768]{1,0:T(8,128)(2,1)S(1)}, u32[]{:S(2)}, u32[]{:S(2)}) collective-permute-start(bf16[256,768]{1,0:T(8,128)(2,1)S(1)} %get-tuple-element.78), channel_id=1, source_target_pairs={{4,8},{8,4},{5,9},{9,5},{6,10},{10,6},{7,11},{11,7},{20,24},{24,20... | collective-permute-start | bytes 1179656 | tf_op jit(solution)/shard_map/ppermute | solution.py:548
  50.0 13.4 %collective-permute-start.18 = (bf16[128,768]{1,0:T(8,128)(2,1)S(1)}, bf16[128,768]{1,0:T(8,128)(2,1)S(1)}, u32[]{:S(2)}, u32[]{:S(2)}) collective-permute-start(bf16[128,768]{1,0:T(8,128)(2,1)S(1)} %get-tuple-element.87), channel_id=1, source_target_pairs={{0,2},{1,3},{2,0},{3,1},{4,6},{5,7},{6,4},{7,5},{8,10},{9,11},{10,... | collective-permute-start | bytes 589832 | tf_op jit(solution)/shard_map/ppermute | solution.py:507
  50.3 13.1 %collective-permute-start.19 = (bf16[128,768]{1,0:T(8,128)(2,1)S(1)}, bf16[128,768]{1,0:T(8,128)(2,1)S(1)}, u32[]{:S(2)}, u32[]{:S(2)}) collective-permute-start(bf16[128,768]{1,0:T(8,128)(2,1)S(1)} %get-tuple-element.88), channel_id=1, source_target_pairs={{0,3},{1,2},{2,1},{3,0},{4,7},{5,6},{6,5},{7,4},{8,11},{9,10},{10,... | collective-permute-start | bytes 589832 | tf_op jit(solution)/shard_map/ppermute | solution.py:507
  54.5 3.5 %collective-permute-start.16 = (bf16[2,128,128]{2,1,0:T(8,128)(2,1)S(1)}, bf16[2,128,128]{2,1,0:T(8,128)(2,1)S(1)}, u32[]{:S(2)}, u32[]{:S(2)}) collective-permute-start(bf16[2,128,128]{2,1,0:T(8,128)(2,1)S(1)} %get-tuple-element.85), channel_id=1, source_target_pairs={{0,16},{16,0},{1,17},{17,1},{2,18},{18,2},{3,19},{19,3},{4,20},{20... | collective-permute-start | bytes 196616 | tf_op jit(solution)/shard_map/ppermute | solution.py:552
  58.0 5.4 %collective-permute-start.17 = (bf16[2,128,128]{2,1,0:T(8,128)(2,1)S(1)}, bf16[2,128,128]{2,1,0:T(8,128)(2,1)S(1)}, u32[]{:S(2)}, u32[]{:S(2)}) collective-permute-start(bf16[2,128,128]{2,1,0:T(8,128)(2,1)S(1)} %get-tuple-element.86), channel_id=1, source_target_pairs={{0,20},{1,21},{2,22},{3,23},{4,16},{5,17},{6,18},{7,19},{8,28},{9,... | collective-permute-start | bytes 196616 | tf_op jit(solution)/shard_map/ppermute | solution.py:556
  63.6 9.1 %collective-permute-start.22 = (bf16[128,1536]{1,0:T(8,128)(2,1)S(1)}, bf16[128,1536]{1,0:T(8,128)(2,1)S(1)}, u32[]{:S(2)}, u32[]{:S(2)}) collective-permute-start(bf16[128,1536]{1,0:T(8,128)(2,1)S(1)} %get-tuple-element.92), channel_id=1, source_target_pairs={{0,1},{1,0},{2,3},{3,2},{4,5},{5,4},{6,7},{7,6},{8,9},{9,8},{10,11... | collective-permute-start | bytes 1179656 | tf_op jit(solution)/shard_map/ppermute | solution.py:507
  64.1 13.7 %collective-permute-start.20 = (bf16[128,768]{1,0:T(8,128)(2,1)S(1)}, bf16[128,768]{1,0:T(8,128)(2,1)S(1)}, u32[]{:S(2)}, u32[]{:S(2)}) collective-permute-start(bf16[128,768]{1,0:T(8,128)(2,1)S(1)} %get-tuple-element.90), channel_id=1, source_target_pairs={{0,2},{1,3},{2,0},{3,1},{4,6},{5,7},{6,4},{7,5},{8,10},{9,11},{10,... | collective-permute-start | bytes 589832 | tf_op jit(solution)/shard_map/ppermute | solution.py:507
  65.0 12.9 %collective-permute-start.21 = (bf16[128,768]{1,0:T(8,128)(2,1)S(1)}, bf16[128,768]{1,0:T(8,128)(2,1)S(1)}, u32[]{:S(2)}, u32[]{:S(2)}) collective-permute-start(bf16[128,768]{1,0:T(8,128)(2,1)S(1)} %get-tuple-element.91), channel_id=1, source_target_pairs={{0,3},{1,2},{2,1},{3,0},{4,7},{5,6},{6,5},{7,4},{8,11},{9,10},{10,... | collective-permute-start | bytes 589832 | tf_op jit(solution)/shard_map/ppermute | solution.py:507
  65.9 7.9 %collective-permute-start.23 = (bf16[128,128]{1,0:T(8,128)(2,1)S(1)}, bf16[128,128]{1,0:T(8,128)(2,1)S(1)}, u32[]{:S(2)}, u32[]{:S(2)}) collective-permute-start(bf16[128,128]{1,0:T(8,128)(2,1)S(1)} %get-tuple-element.93), channel_id=1, source_target_pairs={{0,0},{1,4},{2,8},{3,12},{4,2},{5,6},{6,10},{7,14},{8,16},{9,20},{... | collective-permute-start | bytes 98312 | tf_op jit(solution)/shard_map/ppermute | solution.py:489
  70.5 7.3 %collective-permute-start.24 = (bf16[128,128]{1,0:T(8,128)(2,1)S(1)}, bf16[128,128]{1,0:T(8,128)(2,1)S(1)}, u32[]{:S(2)}, u32[]{:S(2)}) collective-permute-start(bf16[128,128]{1,0:T(8,128)(2,1)S(1)} %get-tuple-element.94), channel_id=1, source_target_pairs={{0,16},{1,20},{2,24},{3,28},{4,18},{5,22},{6,26},{7,30},{8,0},{9,4... | collective-permute-start | bytes 98312 | tf_op jit(solution)/shard_map/ppermute | solution.py:489
  (9 other events, 27.5 us)
